TPU v7x, 32 devices: a whole 2x2x4 slice. The times are simulated.
32 devices in a mesh: blk: 8 (over y, x, core), rep: 4 (over z).
Axes of the slice: x: 2, y: 2, z: 4, core: 2. Of those that a mesh axis runs over, the one named last changes fastest.
Arguments:
- coords: float32 [192, 4096], P('rep', 'blk'), may hold values from -4 to 4
- eigvecs: float32 [128, 4096], P(None, ('blk', 'rep')), may hold values from -0.36 to 0.36
- nbr_list: int32 [32, 8], P('blk'), may hold values from 0 to 31, as said below
- nbr_count: int32 [32], P('blk'), may hold values from 2 to 8, as said below
Outputs:
- smoothed: float32 [128, 4096], P(None, ('blk', 'rep'))
Inputs may be any that keep to these rules, and one draw needn't show every extreme that they name: `nbr_count`: the largest count is exactly 8 in every draw; counts differ from block to block. `nbr_list`: the first nbr_count entries of a row are distinct block indices; entries after them are not used.
All inputs are finite; a program needn't handle non-finite values.
Results may differ from a plain program's by a relative error of at most 0.0003.
Values sent between devices are 32-bit elements; how exact they have to be, the bound alone decides.
No kernel may reach another device: no remote copies, remote signals or barrier semaphores. Data moves between devices by JAX's collectives and lax.ppermute only.
A program may use at most 64 MiB of HBM per device.

v0:
```python
import jax
import jax.numpy as jnp
from jax import lax
from jax.sharding import PartitionSpec as P


def from_behind(value, axis, steps):
    count = lax.axis_size(axis)
    pairs = [(source, (source + steps) % count) for source in range(count)]
    return lax.ppermute(value, axis, pairs)


def shards(coords, eigvecs, nbr_list, nbr_count):
    cycle_size = lax.axis_size("blk")
    rep_size = lax.axis_size("rep")
    blk_index = lax.axis_index("blk")
    rep_index = lax.axis_index("rep")
    gathered = lax.all_gather(coords, "rep", axis=0, tiled=True)
    feat_count, group_width = gathered.shape
    group_blocks, slot_count = nbr_list.shape
    block_width = group_width // group_blocks
    eig_count, own_width = eigvecs.shape
    per_device = own_width // block_width
    kernel_scale = feat_count * 1.0
    batch_rows = 4
    row_tiles = gathered.reshape(feat_count, group_blocks, block_width)
    row_norms = jnp.sum(row_tiles * row_tiles, axis=0)
    owner_dev = nbr_list // per_device
    source_blk = owner_dev // rep_size
    source_rep = owner_dev % rep_size
    local_column = nbr_list % per_device
    slot_ids = jnp.arange(slot_count, dtype=jnp.int32)
    usable = (slot_ids[None, :] < nbr_count[:, None]) & (source_rep == rep_index)
    distance = (blk_index - source_blk) % cycle_size
    key_count = cycle_size * per_device
    slot_keys = jnp.where(usable, distance * per_device + local_column, key_count).reshape(-1)
    ordering = jnp.argsort(slot_keys, stable=True)
    sorted_keys = slot_keys[ordering]
    sorted_rows = jnp.concatenate([ordering // slot_count, jnp.zeros((batch_rows,), jnp.int32)])
    starts = jnp.searchsorted(sorted_keys, jnp.arange(key_count + 1, dtype=jnp.int32))

    def run_key(slot_key, col_coords, col_vecs, totals):
        first_slot = starts[slot_key]
        live_count = starts[slot_key + 1] - first_slot
        group_total = (live_count + batch_rows - 1) // batch_rows
        col_norms = jnp.sum(col_coords * col_coords, axis=0)

        def keep_going(state):
            return state[0] < group_total

        def one_group(state):
            done_groups, running = state
            first_pick = done_groups * batch_rows
            picked = lax.dynamic_slice_in_dim(sorted_rows, first_slot + first_pick, batch_rows)
            live_mask = first_pick + jnp.arange(batch_rows, dtype=jnp.int32) < live_count
            row_block = jnp.take(row_tiles, picked, axis=1)
            row_sq = jnp.take(row_norms, picked, axis=0)
            inner_prod = jnp.einsum(
                "fgt,fu->gtu", row_block, col_coords, precision=lax.Precision.HIGHEST
            )
            dist_sq = row_sq[:, :, None] + col_norms[None, None, :] - 2.0 * inner_prod
            weight = jnp.where(live_mask[:, None, None], jnp.exp(-dist_sq / kernel_scale), 0.0)
            contrib = jnp.einsum("gtu,eu->egt", weight, col_vecs, precision=lax.Precision.HIGHEST)
            return (done_groups + 1, running.at[:, picked, :].add(contrib))

        return lax.while_loop(keep_going, one_group, (jnp.int32(0), totals))[1]

    def use_panel(distance_now, panel, totals):
        col_coords = panel[:feat_count, 0:block_width]
        col_vecs = panel[feat_count:, 0:block_width]
        totals = run_key(distance_now * per_device + 0, col_coords, col_vecs, totals)
        return totals

    own_coords = lax.dynamic_slice_in_dim(gathered, rep_index * own_width, own_width, 1)
    panel = jnp.concatenate([own_coords, eigvecs], axis=0)
    totals = jnp.zeros((eig_count, group_blocks, block_width), jnp.float32)
    totals = use_panel(jnp.int32(0), panel, totals)

    def onward_turn(step_no, state):
        moving, running = state
        moving = from_behind(moving, "blk", 1)
        return (moving, use_panel(step_no, moving, running))

    totals = lax.fori_loop(1, cycle_size, onward_turn, (panel, totals))[1]
    partial_value = totals.reshape(eig_count, group_blocks * block_width)
    return lax.psum_scatter(partial_value, "rep", scatter_dimension=1, tiled=True)


def solution(mesh):
    return jax.shard_map(
        shards,
        mesh=mesh,
        in_specs=(P("rep", "blk"), P(None, ("blk", "rep")), P("blk", None), P("blk")),
        out_specs=P(None, ("blk", "rep")),
        check_vma=False,
    )
```

profile of v0, /device:TPU:0, one launch (start us, length us, event | category | flops | bytes accessed | tf_op | source)
XLA Modules:
  0.0 124.7 jit_solution(3957476991007546950)
XLA Ops:
  6.5 0.7 copy-done.2
  7.4 1.6 %sort.17 = (s32[32]{0:T(128)}, s32[32]{0:T(128)S(1)}) sort(s32[32]{0:T(128)S(1)} %reshape.35, s32[32]{0:T(128)S(1)} %iota.21), dimensions={0}, to_apply=%region_0.0 | sort | flops 160 | bytes 512 | tf_op jit(solution)/shard_map/jit(argsort)/sort | solution.py:37
  9.0 0.7 gather_fusion.5
  9.7 4.3 %while.96 = (s32[]{:T(128)}, u32[9]{0:T(128)S(1)}, u32[9]{0:T(128)S(1)}, s32[32]{0:T(128)S(1)}, s32[]{:T(128)}, /*index=5*/s32[]{:T(128)}, s32[]{}) while((s32[]{:T(128)}, u32[9]{0:T(128)S(1)}, u32[9]{0:T(128)S(1)}, s32[32]{0:T(128)S(1)}, s32[]{:T(128)}, /*index=5*/s32[]{:T(128)}, s32[]{}) %tuple.133), condition=%wide.region_2.3_spmd.clone, body=%wide.region_1.2_spmd.clone.sunk | while | flops 1145 | bytes 4628 | solution.py:40
  9.8 0.7 gather_fusion.2
  10.5 0.7 gather_fusion.2
  11.2 0.7 gather_fusion.2
  11.9 0.7 gather_fusion.2
  12.7 0.7 gather_fusion.2
  13.4 0.7 gather_fusion.2
  14.1 0.6 fusion.37
  15.9 16.2 %all_gather.3 = f32[192,512]{1,0:T(8,128)S(1)} all-gather(f32[48,512]{1,0:T(8,128)S(1)} %copy-done.1), channel_id=1, replica_groups=mesh['blk'=8,'rep'=4] {'rep'}, dimensions={0}, use_global_device_ids=true | all-gather | bytes 491520 | tf_op jit(solution)/shard_map/all_gather | solution.py:18
  32.3 0.8 copy-done
  33.2 4.3 %while.93 = (s32[]{:T(128)}, f32[128,4,128]{2,0,1:T(8,128)S(1)}, s32[]{:T(128)}, s32[]{:T(128)}, s32[36]{0:T(128)S(1)}, /*index=5*/s32[]{:T(128)}, f32[4,128]{1,...) while((s32[]{:T(128)}, f32[128,4,128]{2,0,1:T(8,128)S(1)}, ...), condition=%wide.region_7.10_spmd, body=%wide.region_5.9_spmd.sunk | while | flops 252216864 | bytes 3455815 | solution.py:66
  33.8 0.6 gather_fusion.1
  34.5 0.6 gather_fusion
  35.1 1.1 fusion.59
  36.1 0.4 convolution_bitcast_fusion.4
  36.5 0.1 copy.22
  36.7 0.8 scatter_fusion
  37.4 59.0 %while.95 = (s32[]{:T(128)}, f32[320,128]{1,0:T(8,128)S(1)}, f32[128,4,128]{2,0,1:T(8,128)S(1)}, s32[9]{0:T(128)S(1)}, s32[36]{0:T(128)S(1)}, /*index=5*/f32[4,1...) while((s32[]{:T(128)}, f32[320,128]{1,0:T(8,128)S(1)}, ...), condition=%wide.region_13.16_spmd, body=%wide.region_8.15_spmd.sunk | while | flops 252265920 | bytes 4767666 | solution.py:84
  37.5 0.7 fusion.60
  39.5 3.6 %collective-permute-done = f32[320,128]{1,0:T(8,128)S(1)} collective-permute-done((f32[320,128]{1,0:T(8,128)S(1)}, f32[320,128]{1,0:T(8,128)S(1)}, u32[]{:S(2)}, u32[]{:S(2)}) %collective-permute-start) | collective-permute-done | bytes 163872 | tf_op jit(solution)/shard_map/while/body/eval_jaxpr/ppermute | solution.py:10
  43.2 4.4 %while.97 = (s32[]{:T(128)}, f32[128,4,128]{2,0,1:T(8,128)S(1)}, s32[]{:T(128)}, s32[]{:T(128)}, s32[36]{0:T(128)S(1)}, /*index=5*/s32[]{:T(128)}, f32[4,128]{1,...) while((s32[]{:T(128)}, f32[128,4,128]{2,0,1:T(8,128)S(1)}, ...), condition=%wide.region_12.14_spmd, body=%wide.region_10.13_spmd.sunk | while | flops 252216864 | bytes 3455815 | solution.py:66
  44.0 0.6 gather_fusion.4
  44.6 0.6 gather_fusion.3
  45.2 1.1 fusion.67
  46.3 0.4 convolution_bitcast_fusion.5
  46.7 0.1 copy.23
  46.8 0.8 scatter_fusion.1
  47.7 0.7 fusion.60
  49.7 3.6 %collective-permute-done = f32[320,128]{1,0:T(8,128)S(1)} collective-permute-done((f32[320,128]{1,0:T(8,128)S(1)}, f32[320,128]{1,0:T(8,128)S(1)}, u32[]{:S(2)}, u32[]{:S(2)}) %collective-permute-start) | collective-permute-done | bytes 163872 | tf_op jit(solution)/shard_map/while/body/eval_jaxpr/ppermute | solution.py:10
  53.5 0.7 fusion.60
  55.5 3.6 %collective-permute-done = f32[320,128]{1,0:T(8,128)S(1)} collective-permute-done((f32[320,128]{1,0:T(8,128)S(1)}, f32[320,128]{1,0:T(8,128)S(1)}, u32[]{:S(2)}, u32[]{:S(2)}) %collective-permute-start) | collective-permute-done | bytes 163872 | tf_op jit(solution)/shard_map/while/body/eval_jaxpr/ppermute | solution.py:10
  59.1 4.4 %while.97 = (s32[]{:T(128)}, f32[128,4,128]{2,0,1:T(8,128)S(1)}, s32[]{:T(128)}, s32[]{:T(128)}, s32[36]{0:T(128)S(1)}, /*index=5*/s32[]{:T(128)}, f32[4,128]{1,...) while((s32[]{:T(128)}, f32[128,4,128]{2,0,1:T(8,128)S(1)}, ...), condition=%wide.region_12.14_spmd, body=%wide.region_10.13_spmd.sunk | while | flops 252216864 | bytes 3455815 | solution.py:66
  59.9 0.6 gather_fusion.4
  60.6 0.6 gather_fusion.3
  61.1 1.1 fusion.67
  62.2 0.4 convolution_bitcast_fusion.5
  62.6 0.1 copy.23
  62.7 0.8 scatter_fusion.1
  63.6 0.7 fusion.60
  65.6 3.6 %collective-permute-done = f32[320,128]{1,0:T(8,128)S(1)} collective-permute-done((f32[320,128]{1,0:T(8,128)S(1)}, f32[320,128]{1,0:T(8,128)S(1)}, u32[]{:S(2)}, u32[]{:S(2)}) %collective-permute-start) | collective-permute-done | bytes 163872 | tf_op jit(solution)/shard_map/while/body/eval_jaxpr/ppermute | solution.py:10
  69.4 0.7 fusion.60
  71.4 4.6 %collective-permute-done = f32[320,128]{1,0:T(8,128)S(1)} collective-permute-done((f32[320,128]{1,0:T(8,128)S(1)}, f32[320,128]{1,0:T(8,128)S(1)}, u32[]{:S(2)}, u32[]{:S(2)}) %collective-permute-start) | collective-permute-done | bytes 163872 | tf_op jit(solution)/shard_map/while/body/eval_jaxpr/ppermute | solution.py:10
  76.1 4.4 %while.97 = (s32[]{:T(128)}, f32[128,4,128]{2,0,1:T(8,128)S(1)}, s32[]{:T(128)}, s32[]{:T(128)}, s32[36]{0:T(128)S(1)}, /*index=5*/s32[]{:T(128)}, f32[4,128]{1,...) while((s32[]{:T(128)}, f32[128,4,128]{2,0,1:T(8,128)S(1)}, ...), condition=%wide.region_12.14_spmd, body=%wide.region_10.13_spmd.sunk | while | flops 252216864 | bytes 3455815 | solution.py:66
  76.9 0.6 gather_fusion.4
  77.5 0.6 gather_fusion.3
  78.1 1.1 fusion.67
  79.2 0.4 convolution_bitcast_fusion.5
  79.6 0.1 copy.23
  79.7 0.7 scatter_fusion.1
  80.6 0.7 fusion.60
  82.6 3.6 %collective-permute-done = f32[320,128]{1,0:T(8,128)S(1)} collective-permute-done((f32[320,128]{1,0:T(8,128)S(1)}, f32[320,128]{1,0:T(8,128)S(1)}, u32[]{:S(2)}, u32[]{:S(2)}) %collective-permute-start) | collective-permute-done | bytes 163872 | tf_op jit(solution)/shard_map/while/body/eval_jaxpr/ppermute | solution.py:10
  86.2 4.4 %while.97 = (s32[]{:T(128)}, f32[128,4,128]{2,0,1:T(8,128)S(1)}, s32[]{:T(128)}, s32[]{:T(128)}, s32[36]{0:T(128)S(1)}, /*index=5*/s32[]{:T(128)}, f32[4,128]{1,...) while((s32[]{:T(128)}, f32[128,4,128]{2,0,1:T(8,128)S(1)}, ...), condition=%wide.region_12.14_spmd, body=%wide.region_10.13_spmd.sunk | while | flops 252216864 | bytes 3455815 | solution.py:66
  87.0 0.6 gather_fusion.4
  87.7 0.6 gather_fusion.3
  88.2 1.1 fusion.67
  89.3 0.4 convolution_bitcast_fusion.5
  89.8 0.7 scatter_fusion.1
  90.7 0.7 fusion.60
  92.7 3.6 %collective-permute-done = f32[320,128]{1,0:T(8,128)S(1)} collective-permute-done((f32[320,128]{1,0:T(8,128)S(1)}, f32[320,128]{1,0:T(8,128)S(1)}, u32[]{:S(2)}, u32[]{:S(2)}) %collective-permute-start) | collective-permute-done | bytes 163872 | tf_op jit(solution)/shard_map/while/body/eval_jaxpr/ppermute | solution.py:10
  96.4 0.7 copy_bitcast_fusion.1
  97.2 20.7 %reduce-scatter.2.cloned.1.call-done = f32[128,128]{1,0:T(8,128)} async-done(((f32[128,512]{1,0:T(8,128)}), f32[128,128]{1,0:T(8,128)}) %reduce-scatter.2.cloned.1.call-update) | async-done | bytes 65552 | tf_op jit(solution)/shard_map/reduce_scatter | solution.py:86
  (87 shorter events, 2.3 us)
Async XLA Ops:
  6.5 111.3 %reduce-scatter.2.cloned.1.call-start = ((), (), s32[]{:S(2)}) async-start(), calls=%async_computation.1 | async-start | bytes 327680 | tf_op jit(solution)/shard_map/reduce_scatter | solution.py:86
  6.5 0.7 copy-start.2
  6.5 0.7 copy-start.3
  9.7 6.2 %copy-start.1 = (f32[48,512]{1,0:T(8,128)S(1)}, f32[48,512]{1,0:T(8,128)}, u32[]{:S(2)}) copy-start(f32[48,512]{1,0:T(8,128)} %param.16) | copy-start | bytes 294916
  32.3 0.8 copy-start
  37.4 5.7 %collective-permute-start = (f32[320,128]{1,0:T(8,128)S(1)}, f32[320,128]{1,0:T(8,128)S(1)}, u32[]{:S(2)}, u32[]{:S(2)}) collective-permute-start(f32[320,128]{1,0:T(8,128)S(1)} %get-tuple-element.1044), channel_id=1, source_target_pairs={{0,4},{4,8},{8,12},{12,16},{16,20},{20,24},{24,28},{28,0},{1,5},{5... | collective-permute-start | bytes 491528 | tf_op jit(solution)/shard_map/while/body/eval_jaxpr/ppermute | solution.py:10
  47.6 5.7 %collective-permute-start = (f32[320,128]{1,0:T(8,128)S(1)}, f32[320,128]{1,0:T(8,128)S(1)}, u32[]{:S(2)}, u32[]{:S(2)}) collective-permute-start(f32[320,128]{1,0:T(8,128)S(1)} %get-tuple-element.1044), channel_id=1, source_target_pairs={{0,4},{4,8},{8,12},{12,16},{16,20},{20,24},{24,28},{28,0},{1,5},{5... | collective-permute-start | bytes 491528 | tf_op jit(solution)/shard_map/while/body/eval_jaxpr/ppermute | solution.py:10
  53.4 5.7 %collective-permute-start = (f32[320,128]{1,0:T(8,128)S(1)}, f32[320,128]{1,0:T(8,128)S(1)}, u32[]{:S(2)}, u32[]{:S(2)}) collective-permute-start(f32[320,128]{1,0:T(8,128)S(1)} %get-tuple-element.1044), channel_id=1, source_target_pairs={{0,4},{4,8},{8,12},{12,16},{16,20},{20,24},{24,28},{28,0},{1,5},{5... | collective-permute-start | bytes 491528 | tf_op jit(solution)/shard_map/while/body/eval_jaxpr/ppermute | solution.py:10
  63.5 5.7 %collective-permute-start = (f32[320,128]{1,0:T(8,128)S(1)}, f32[320,128]{1,0:T(8,128)S(1)}, u32[]{:S(2)}, u32[]{:S(2)}) collective-permute-start(f32[320,128]{1,0:T(8,128)S(1)} %get-tuple-element.1044), channel_id=1, source_target_pairs={{0,4},{4,8},{8,12},{12,16},{16,20},{20,24},{24,28},{28,0},{1,5},{5... | collective-permute-start | bytes 491528 | tf_op jit(solution)/shard_map/while/body/eval_jaxpr/ppermute | solution.py:10
  69.3 6.7 %collective-permute-start = (f32[320,128]{1,0:T(8,128)S(1)}, f32[320,128]{1,0:T(8,128)S(1)}, u32[]{:S(2)}, u32[]{:S(2)}) collective-permute-start(f32[320,128]{1,0:T(8,128)S(1)} %get-tuple-element.1044), channel_id=1, source_target_pairs={{0,4},{4,8},{8,12},{12,16},{16,20},{20,24},{24,28},{28,0},{1,5},{5... | collective-permute-start | bytes 491528 | tf_op jit(solution)/shard_map/while/body/eval_jaxpr/ppermute | solution.py:10
  80.5 5.7 %collective-permute-start = (f32[320,128]{1,0:T(8,128)S(1)}, f32[320,128]{1,0:T(8,128)S(1)}, u32[]{:S(2)}, u32[]{:S(2)}) collective-permute-start(f32[320,128]{1,0:T(8,128)S(1)} %get-tuple-element.1044), channel_id=1, source_target_pairs={{0,4},{4,8},{8,12},{12,16},{16,20},{20,24},{24,28},{28,0},{1,5},{5... | collective-permute-start | bytes 491528 | tf_op jit(solution)/shard_map/while/body/eval_jaxpr/ppermute | solution.py:10
  90.6 5.7 %collective-permute-start = (f32[320,128]{1,0:T(8,128)S(1)}, f32[320,128]{1,0:T(8,128)S(1)}, u32[]{:S(2)}, u32[]{:S(2)}) collective-permute-start(f32[320,128]{1,0:T(8,128)S(1)} %get-tuple-element.1044), channel_id=1, source_target_pairs={{0,4},{4,8},{8,12},{12,16},{16,20},{20,24},{24,28},{28,0},{1,5},{5... | collective-permute-start | bytes 491528 | tf_op jit(solution)/shard_map/while/body/eval_jaxpr/ppermute | solution.py:10
Sparse Core Ops, SparseCore 0:
  97.3 20.5 reduce-scatter.1
where the time goes:
time: 126 us; the launch traced here: 125 us
  waiting for transfers between devices  46.9 us (37%)
  local copies, waits for them, and re-layouts  18.7 us (15%)
  blocking collectives  16.2 us (13%)
  between operations  14.7 us (12%)
  loops' own time  13.6 us (11%)
  matrix products  7.29 us (6%)
  other arithmetic  6.85 us (5%)
    ppermute x7, waiting for transfers between devices, from_behind(): return lax.ppermute(value, axis, pairs)  26.2 us
    reduce_scatter x1, waiting for transfers between devices, shards(): lax.psum_scatter(partial_value, 'rep', scatter_dimension=1, tiled=True)  20.7 us
    all_gather x1, blocking collectives, shards(): gathered = lax.all_gather(coords, 'rep', axis=0, tiled=True)  16.2 us
    another operation x1, loops' own time, shards(): totals = lax.fori_loop(1, cycle_size, onward_turn, (panel, totals))[1]  9.79 us
    dot_general x5, matrix products, one_group(): jnp.einsum('fgt,fu->gtu', row_block, col_coords, precision=lax.Precision....  5.4 us
    dynamic_slice x8, local copies, waits for them, and re-layouts, run_key(): first_slot = starts[slot_key]  5.33 us
    gather x6, local copies, waits for them, and re-layouts, shards(): jnp.searchsorted(sorted_keys, jnp.arange(key_count + 1, dtype=jnp.int32))  3.95 us
    scatter-add x5, other arithmetic, one_group(): return (done_groups + 1, running.at[:, picked, :].add(contrib))  3.75 us
  transfers between devices with their start and end apart: 8, of which 8 were waited for; matrix products, arithmetic and copies ran while one was open for 4% of the time, Pallas kernels for 0%

commit v1 on v0

v1 whole, which is shorter than its diff:
```python
import functools

import jax
import jax.numpy as jnp
from jax import lax
from jax.experimental import pallas as pl
from jax.experimental.pallas import tpu as pltpu
from jax.sharding import PartitionSpec as P


def halves(value):
    high = value.astype(jnp.bfloat16)
    return high, (value - high.astype(jnp.float32)).astype(jnp.bfloat16)


def three_pass(lhs, rhs, dims):
    lhs_high, lhs_low = lhs
    rhs_high, rhs_low = rhs
    mul = functools.partial(
        lax.dot_general, dimension_numbers=(dims, ((), ())), preferred_element_type=jnp.float32
    )
    return mul(lhs_high, rhs_high) + (mul(lhs_high, rhs_low) + mul(lhs_low, rhs_high))


def apply_kernel(row_ref, mask_ref, *refs):
    panels, out_ref = refs[:-1], refs[-1]
    rows = row_ref[...]
    feat_count = rows.shape[0]
    row_scale = jnp.exp(jnp.sum(rows * rows, axis=0, keepdims=True) * (-1.0 / feat_count))
    row_halves = halves(rows * (2.0 / feat_count))
    total = None
    for place, panel in enumerate(panels):
        cols = panel[:feat_count, :]
        vecs = panel[feat_count:, :]
        col_scale = jnp.exp(jnp.sum(cols * cols, axis=0, keepdims=True) * (-1.0 / feat_count))
        inner = three_pass(halves(cols), row_halves, ((0,), (0,)))
        weight = jnp.exp(inner) * mask_ref[place : place + 1, :]
        part = three_pass(halves(vecs * col_scale), halves(weight), ((1,), (0,)))
        total = part if total is None else total + part
    out_ref[...] = total * row_scale


def swapped(value, step):
    count = lax.axis_size("blk")
    return lax.ppermute(value, "blk", [(source, source ^ step) for source in range(count)])


def shards(coords, eigvecs, nbr_list, nbr_count):
    cycle_size = lax.axis_size("blk")
    rep_size = lax.axis_size("rep")
    blk_index = lax.axis_index("blk")
    rep_index = lax.axis_index("rep")
    group_blocks, slot_count = nbr_list.shape
    eig_count, own_width = eigvecs.shape

    steps = jnp.arange(cycle_size, dtype=jnp.int32)
    columns = (blk_index ^ steps) * rep_size + rep_index
    used = jnp.arange(slot_count, dtype=jnp.int32)[None, :] < nbr_count[:, None]
    listed = jnp.any((nbr_list[None] == columns[:, None, None]) & used[None], axis=2)
    mask = jnp.repeat(listed.astype(jnp.float32), own_width, axis=1)

    gathered = lax.all_gather(coords, "rep", axis=0, tiled=True)
    own_coords = lax.dynamic_slice_in_dim(gathered, rep_index * own_width, own_width, 1)
    panels = {0: jnp.concatenate([own_coords, eigvecs], axis=0)}
    for step in range(2, cycle_size, 2):
        panels[step] = swapped(panels[0], step)
    for step in range(0, cycle_size, 2):
        panels[step + 1] = swapped(panels[step], 1)

    partial_value = pl.pallas_call(
        apply_kernel,
        out_shape=jax.ShapeDtypeStruct((eig_count, group_blocks * own_width), jnp.float32),
        compiler_params=pltpu.CompilerParams(vmem_limit_bytes=48 * 1024 * 1024),
    )(gathered, mask, *[panels[step] for step in range(cycle_size)])

    pieces = partial_value.reshape(eig_count, group_blocks, own_width).transpose(1, 0, 2)
    arrived = lax.all_to_all(pieces, "rep", 0, 0)
    return jnp.sum(arrived, axis=0)


def solution(mesh):
    return jax.shard_map(
        shards,
        mesh=mesh,
        in_specs=(P("rep", "blk"), P(None, ("blk", "rep")), P("blk", None), P("blk")),
        out_specs=P(None, ("blk", "rep")),
        check_vma=False,
    )
```

time: 126 us -> 45.4 us (0.36)
  waiting for transfers between devices: 46.9 us -> 4.69 us
  local copies, waits for them, and re-layouts: 18.7 us -> 2.18 us
  between operations: 14.7 us -> 0.04 us
  blocking collectives: 16.2 us -> 30.2 us
  loops' own time: 13.6 us -> 0 us
  matrix products: 7.29 us -> 0 us
  other arithmetic: 6.85 us -> 0.95 us
  starting transfers between devices: 0.41 us -> 4.07 us
  Pallas kernels: 0 us -> 3.04 us
    ppermute x7, waiting for transfers between devices: 26.2 us -> 4.69 us  [swapped(): lax.ppermute(value, 'blk', [(source, source ^ step) for source in range(c...]
    reduce_scatter x1 -> x0, waiting for transfers between devices: 20.7 us -> none  [shards(): lax.psum_scatter(partial_value, 'rep', scatter_dimension=1, tiled=True)]
    all_to_all x0 -> x1, blocking collectives: none -> 13.8 us  [shards(): arrived = lax.all_to_all(pieces, 'rep', 0, 0)]
    another operation x10 -> x0, loops' own time: 13.6 us -> none  [the longest x1 9.79 us: shards(): totals = lax.fori_loop(1, cycle_size, onward_turn, (panel, totals))[1]]
    gather x17 -> x0, local copies, waits for them, and re-layouts: 10.3 us -> none  [the longest x6 3.95 us: shards(): jnp.searchsorted(sorted_keys, jnp.arange(key_count + 1, dtype=jnp.int32))]
    dot_general x10 -> x0, matrix products: 7.29 us -> none  [the longest x5 5.4 us: one_group(): jnp.einsum('fgt,fu->gtu', row_block, col_coords, precision=lax.Precision....]
    dynamic_slice x8 -> x1, local copies, waits for them, and re-layouts: 5.33 us -> 0.01 us  [shards(): lax.dynamic_slice_in_dim(gathered, rep_index * own_width, own_width, 1)]
    scatter-add x5 -> x0, other arithmetic: 3.75 us -> none  [one_group(): return (done_groups + 1, running.at[:, picked, :].add(contrib))]
  transfers between devices with their start and end apart: 8 -> 7, of which waited for: 8 -> 4; matrix products, arithmetic and copies ran while one was open for 4% -> 1% of each run, Pallas kernels for 0% -> 0%
where the time goes in v1:
time: 45.4 us; the launch traced here: 45.2 us
  blocking collectives  30.2 us (67%)
  waiting for transfers between devices  4.69 us (10%)
  starting transfers between devices  4.07 us (9%)
  Pallas kernels  3.04 us (7%)
  local copies, waits for them, and re-layouts  2.18 us (5%)
  other arithmetic  0.95 us (2%)
    all_gather x1, blocking collectives, shards(): gathered = lax.all_gather(coords, 'rep', axis=0, tiled=True)  16.4 us
    all_to_all x1, blocking collectives, shards(): arrived = lax.all_to_all(pieces, 'rep', 0, 0)  13.8 us
    ppermute x7, waiting for transfers between devices, swapped(): lax.ppermute(value, 'blk', [(source, source ^ step) for source in range(c...  4.69 us
    ppermute x7, starting transfers between devices, swapped(): lax.ppermute(value, 'blk', [(source, source ^ step) for source in range(c...  4.07 us
    pallas_call x1, Pallas kernels, shards(): pl.pallas_call(apply_kernel, out_shape=jax.ShapeDtypeStruct((eig_count, g...  3.04 us
    unnamed x6, local copies, waits for them, and re-layouts  2.08 us
  transfers between devices with their start and end apart: 7, of which 4 were waited for; matrix products, arithmetic and copies ran while one was open for 1% of the time, Pallas kernels for 0%

profile of v1, /device:TPU:0, one launch (start us, length us, event | category | flops | bytes accessed | tf_op | source)
XLA Modules:
  0.0 45.2 jit_solution(778829706452137838)
XLA Ops:
  0.0 16.4 %all_gather.3.row_ref = f32[192,512]{1,0:T(8,128)S(1)} all-gather(f32[48,512]{1,0:T(8,128)} %param.4), channel_id=1, replica_groups=mesh['blk'=8,'rep'=4] {'rep'}, dimensions={0}, use_global_device_ids=true | all-gather | bytes 491520 | tf_op jit(solution)/shard_map/all_gather | solution.py:62
  16.4 0.0 copy-start
  16.5 0.8 %copy-done = f32[128,128]{1,0:T(8,128)S(1)} copy-done((f32[128,128]{1,0:T(8,128)S(1)}, f32[128,128]{1,0:T(8,128)}, u32[]{:S(2)}) %copy-start) | copy-done | bytes 65560
  17.3 2.5 %collective-permute-start.5 = (f32[320,128]{1,0:T(8,128)S(1)}, f32[320,128]{1,0:T(8,128)S(1)}, u32[]{:S(2)}, u32[]{:S(2)}) collective-permute-start(f32[320,128]{1,0:T(8,128)S(1)} %pad_maximum_fusion.refs_0_), channel_id=1, source_target_pairs={{0,24},{4,28},{8,16},{12,20},{16,8},{20,12},{24,0},{28,4},{1,25},{... | collective-permute-start | bytes 491528 | tf_op jit(solution)/shard_map/ppermute | solution.py:45
  19.8 0.5 %collective-permute-start.3 = (f32[320,128]{1,0:T(8,128)S(1)}, f32[320,128]{1,0:T(8,128)S(1)}, u32[]{:S(2)}, u32[]{:S(2)}) collective-permute-start(f32[320,128]{1,0:T(8,128)S(1)} %pad_maximum_fusion.refs_0_), channel_id=1, source_target_pairs={{0,16},{4,20},{8,24},{12,28},{16,0},{20,4},{24,8},{28,12},{1,17},{... | collective-permute-start | bytes 491528 | tf_op jit(solution)/shard_map/ppermute | solution.py:45
  20.3 0.5 %collective-permute-start.1 = (f32[320,128]{1,0:T(8,128)S(1)}, f32[320,128]{1,0:T(8,128)S(1)}, u32[]{:S(2)}, u32[]{:S(2)}) collective-permute-start(f32[320,128]{1,0:T(8,128)S(1)} %pad_maximum_fusion.refs_0_), channel_id=1, source_target_pairs={{0,8},{4,12},{8,0},{12,4},{16,24},{20,28},{24,16},{28,20},{1,9},{5... | collective-permute-start | bytes 491528 | tf_op jit(solution)/shard_map/ppermute | solution.py:45
  20.8 0.0 collective-permute-start
  20.8 0.0 copy-start.2
  20.9 0.7 %copy-done.2 = s32[4]{0:T(128)S(1)} copy-done((s32[4]{0:T(128)S(1)}, s32[4]{0:T(128)}, u32[]{:S(2)}) %copy-start.2) | copy-done | bytes 40
  21.5 0.0 copy-start.1
  21.5 0.1 iota_compare_fusion
  21.6 0.6 %copy-done.1 = s32[4,8]{1,0:T(4,128)S(1)} copy-done((s32[4,8]{1,0:T(4,128)S(1)}, s32[4,8]{1,0:T(4,128)}, u32[]{:S(2)}) %copy-start.1) | copy-done | bytes 152
  22.2 0.2 and_reduce_fusion
  22.4 2.5 %collective-permute-done.5.refs_6_ = f32[320,128]{1,0:T(8,128)S(1)} collective-permute-done((f32[320,128]{1,0:T(8,128)S(1)}, f32[320,128]{1,0:T(8,128)S(1)}, u32[]{:S(2)}, u32[]{:S(2)}) %collective-permute-start.5) | collective-permute-done | bytes 163872 | tf_op jit(solution)/shard_map/ppermute | solution.py:45
  24.9 0.0 collective-permute-start.6
  24.9 1.1 %collective-permute-done.3.refs_4_ = f32[320,128]{1,0:T(8,128)S(1)} collective-permute-done((f32[320,128]{1,0:T(8,128)S(1)}, f32[320,128]{1,0:T(8,128)S(1)}, u32[]{:S(2)}, u32[]{:S(2)}) %collective-permute-start.3) | collective-permute-done | bytes 163872 | tf_op jit(solution)/shard_map/ppermute | solution.py:45
  26.1 0.0 collective-permute-start.4
  26.1 0.0 collective-permute-done.1.refs_2_
  26.1 0.5 %collective-permute-start.2 = (f32[320,128]{1,0:T(8,128)S(1)}, f32[320,128]{1,0:T(8,128)S(1)}, u32[]{:S(2)}, u32[]{:S(2)}) collective-permute-start(f32[320,128]{1,0:T(8,128)S(1)} %collective-permute-done.1.refs_2_), channel_id=1, source_target_pairs={{0,4},{4,0},{8,12},{12,8},{16,20},{20,16},{24,28},{28,24},{1,5},{5... | collective-permute-start | bytes 491528 | tf_op jit(solution)/shard_map/ppermute | solution.py:45
  26.6 0.1 broadcast_bitcast_fusion.mask_ref
  26.6 0.0 collective-permute-done.refs_1_
  26.6 0.0 collective-permute-done.6.refs_7_
  26.7 0.8 %collective-permute-done.4.refs_5_ = f32[320,128]{1,0:T(8,128)S(1)} collective-permute-done((f32[320,128]{1,0:T(8,128)S(1)}, f32[320,128]{1,0:T(8,128)S(1)}, u32[]{:S(2)}, u32[]{:S(2)}) %collective-permute-start.4) | collective-permute-done | bytes 163872 | tf_op jit(solution)/shard_map/ppermute | solution.py:45
  27.5 0.2 collective-permute-done.2.refs_3_
  27.7 3.0 %shard_map.46 = f32[128,512]{1,0:T(8,128)S(1)} custom-call(f32[192,512]{1,0:T(8,128)S(1)} %all_gather.3.row_ref, f32[8,512]{1,0:T(8,128)S(1)} %broadcast_bitcast_fusion.mask_ref, f32[320,128]{1,0:T(8,128)S(1)} %pad_maximum_fusion.refs_0_, f32[320,128]{1,0:T(8,128)S(1)} %collective-permute-done.refs_1_, f32[320,128]{1,0:T(8,128)S(1)} %collective-permute-done.1.refs_2_, ...), custom_call_target="tpu_custom_call" | custom-call | tf_op jit(solution)/shard_map/pallas_call | solution.py:70
  30.8 13.8 %all_to_all.5 = f32[4,128,128]{2,1,0:T(8,128)S(1)} all-to-all(f32[4,128,128]{2,1,0:T(8,128)S(1)} %bitcast_bitcast_fusion), channel_id=1, replica_groups=mesh['blk'=8,'rep'=4] {'rep'}, dimensions={0} | all-to-all | bytes 524288 | tf_op jit(solution)/shard_map/all_to_all | solution.py:77
  44.5 0.6 %reduce_sum.9 = f32[128,128]{1,0:T(8,128)} reduce(f32[4,128,128]{2,1,0:T(8,128)S(1)} %all_to_all.5, f32[]{:T(128)} %constant.20.clone.1), dimensions={0}, to_apply=%region_1.0 | reduce | flops 49152 | bytes 327684 | tf_op jit(solution)/shard_map/reduce_sum | solution.py:78
  (5 shorter events, 0.1 us)
Async XLA Ops:
  16.4 0.8 %copy-start = (f32[128,128]{1,0:T(8,128)S(1)}, f32[128,128]{1,0:T(8,128)}, u32[]{:S(2)}) copy-start(f32[128,128]{1,0:T(8,128)} %param.5) | copy-start | bytes 196612
  17.3 7.7 %collective-permute-start.5 = (f32[320,128]{1,0:T(8,128)S(1)}, f32[320,128]{1,0:T(8,128)S(1)}, u32[]{:S(2)}, u32[]{:S(2)}) collective-permute-start(f32[320,128]{1,0:T(8,128)S(1)} %pad_maximum_fusion.refs_0_), channel_id=1, source_target_pairs={{0,24},{4,28},{8,16},{12,20},{16,8},{20,12},{24,0},{28,4},{1,25},{... | collective-permute-start | bytes 491528 | tf_op jit(solution)/shard_map/ppermute | solution.py:45
  19.8 6.3 %collective-permute-start.3 = (f32[320,128]{1,0:T(8,128)S(1)}, f32[320,128]{1,0:T(8,128)S(1)}, u32[]{:S(2)}, u32[]{:S(2)}) collective-permute-start(f32[320,128]{1,0:T(8,128)S(1)} %pad_maximum_fusion.refs_0_), channel_id=1, source_target_pairs={{0,16},{4,20},{8,24},{12,28},{16,0},{20,4},{24,8},{28,12},{1,17},{... | collective-permute-start | bytes 491528 | tf_op jit(solution)/shard_map/ppermute | solution.py:45
  20.3 5.8 %collective-permute-start.1 = (f32[320,128]{1,0:T(8,128)S(1)}, f32[320,128]{1,0:T(8,128)S(1)}, u32[]{:S(2)}, u32[]{:S(2)}) collective-permute-start(f32[320,128]{1,0:T(8,128)S(1)} %pad_maximum_fusion.refs_0_), channel_id=1, source_target_pairs={{0,8},{4,12},{8,0},{12,4},{16,24},{20,28},{24,16},{28,20},{1,9},{5... | collective-permute-start | bytes 491528 | tf_op jit(solution)/shard_map/ppermute | solution.py:45
  20.8 5.8 %collective-permute-start = (f32[320,128]{1,0:T(8,128)S(1)}, f32[320,128]{1,0:T(8,128)S(1)}, u32[]{:S(2)}, u32[]{:S(2)}) collective-permute-start(f32[320,128]{1,0:T(8,128)S(1)} %pad_maximum_fusion.refs_0_), channel_id=1, source_target_pairs={{0,4},{4,0},{8,12},{12,8},{16,20},{20,16},{24,28},{28,24},{1,5},{5... | collective-permute-start | bytes 491528 | tf_op jit(solution)/shard_map/ppermute | solution.py:45
  20.8 0.7 %copy-start.2 = (s32[4]{0:T(128)S(1)}, s32[4]{0:T(128)}, u32[]{:S(2)}) copy-start(s32[4]{0:T(128)} %param.7) | copy-start | bytes 52
  21.5 0.7 %copy-start.1 = (s32[4,8]{1,0:T(4,128)S(1)}, s32[4,8]{1,0:T(4,128)}, u32[]{:S(2)}) copy-start(s32[4,8]{1,0:T(4,128)} %param.6) | copy-start | bytes 388
  24.9 1.7 %collective-permute-start.6 = (f32[320,128]{1,0:T(8,128)S(1)}, f32[320,128]{1,0:T(8,128)S(1)}, u32[]{:S(2)}, u32[]{:S(2)}) collective-permute-start(f32[320,128]{1,0:T(8,128)S(1)} %collective-permute-done.5.refs_6_), channel_id=1, source_target_pairs={{0,4},{4,0},{8,12},{12,8},{16,20},{20,16},{24,28},{28,24},{1,5},{5... | collective-permute-start | bytes 491528 | tf_op jit(solution)/shard_map/ppermute | solution.py:45
  26.1 1.4 %collective-permute-start.4 = (f32[320,128]{1,0:T(8,128)S(1)}, f32[320,128]{1,0:T(8,128)S(1)}, u32[]{:S(2)}, u32[]{:S(2)}) collective-permute-start(f32[320,128]{1,0:T(8,128)S(1)} %collective-permute-done.3.refs_4_), channel_id=1, source_target_pairs={{0,4},{4,0},{8,12},{12,8},{16,20},{20,16},{24,28},{28,24},{1,5},{5... | collective-permute-start | bytes 491528 | tf_op jit(solution)/shard_map/ppermute | solution.py:45
  26.1 1.6 %collective-permute-start.2 = (f32[320,128]{1,0:T(8,128)S(1)}, f32[320,128]{1,0:T(8,128)S(1)}, u32[]{:S(2)}, u32[]{:S(2)}) collective-permute-start(f32[320,128]{1,0:T(8,128)S(1)} %collective-permute-done.1.refs_2_), channel_id=1, source_target_pairs={{0,4},{4,0},{8,12},{12,8},{16,20},{20,16},{24,28},{28,24},{1,5},{5... | collective-permute-start | bytes 491528 | tf_op jit(solution)/shard_map/ppermute | solution.py:45

commit v2 on v1

v2 whole, which is shorter than its diff:
```python
import functools

import jax
import jax.numpy as jnp
from jax import lax
from jax.experimental import pallas as pl
from jax.experimental.pallas import tpu as pltpu
from jax.sharding import PartitionSpec as P


TRANSFER_FLOPS = 3 * 10**9


def halves(value):
    high = value.astype(jnp.bfloat16)
    return high, (value - high.astype(jnp.float32)).astype(jnp.bfloat16)


def three_pass(lhs, rhs, dims):
    lhs_high, lhs_low = lhs
    rhs_high, rhs_low = rhs
    mul = functools.partial(
        lax.dot_general, dimension_numbers=(dims, ((), ())), preferred_element_type=jnp.float32
    )
    return mul(lhs_high, rhs_high) + (mul(lhs_high, rhs_low) + mul(lhs_low, rhs_high))


def lists_kernel(list_ref, count_ref, out_ref):
    rank = lax.axis_index("rep")
    for slot in range(out_ref.shape[0]):
        listed = jnp.where(slot < count_ref[rank], list_ref[rank, slot], -1)
        out_ref[slot : slot + 1, :] = jnp.full((1, out_ref.shape[1]), listed.astype(jnp.float32))


def columns_kernel(*refs):
    piece_refs, (high_ref, low_ref, scale_ref) = refs[:-3], refs[-3:]
    cols = jnp.concatenate([ref[...] for ref in piece_refs], axis=0)
    scale_ref[...] = jnp.exp(jnp.sum(cols * cols, axis=0, keepdims=True) * (-1.0 / cols.shape[0]))
    high_ref[...], low_ref[...] = halves(cols.T)


def rows_kernel(feat_count, *refs):
    panel_refs, (high_ref, low_ref, scale_ref, mask_ref) = refs[:-4], refs[-4:]
    width = panel_refs[0].shape[1]
    group_blocks = mask_ref.shape[0] // 2
    blk_index = lax.axis_index("blk")
    for place, ref in enumerate(panel_refs):
        span = slice(place * width, (place + 1) * width)
        rows = ref[:feat_count, :]
        scale_ref[:, span] = jnp.exp(jnp.sum(rows * rows, axis=0, keepdims=True) * (-1.0 / feat_count))
        high_ref[:, span], low_ref[:, span] = halves(rows * (2.0 / feat_count))
        lists = ref[feat_count:, :]
        for spot in range(2 * group_blocks):
            column = (blk_index ^ (spot // group_blocks)) * group_blocks + spot % group_blocks
            hits = jnp.where(lists == column.astype(jnp.float32), 1.0, 0.0)
            mask_ref[spot : spot + 1, span] = jnp.max(hits, axis=0, keepdims=True)


def vectors_kernel(before_ref, own_ref, sibling_ref, own_scale, sibling_scale, high_ref, low_ref):
    eig_count, group_cols = high_ref.shape[0], own_scale.shape[1]
    width = own_ref.shape[1]
    rank = lax.axis_index("rep")
    for group, (vec_ref, scale_ref) in enumerate(((own_ref, own_scale), (sibling_ref, sibling_scale))):
        for spot in range(group_cols // width):
            start = pl.multiple_of((rank ^ spot) * width, width)
            block = vec_ref[spot * eig_count : (spot + 1) * eig_count, :] * scale_ref[:, pl.ds(start, width)]
            there = pl.ds(group * group_cols + start, width)
            high_ref[:, there], low_ref[:, there] = halves(block)


def apply_kernel(first, count, before_ref, row_high, row_low, row_scale, mask_ref, *refs):
    own_high, own_low, sibling_high, sibling_low, vec_high, vec_low, *out_refs = refs
    width = out_refs[0].shape[1]
    group_cols = own_high.shape[0]
    span = slice(first * width, (first + count) * width)
    row_halves = row_high[:, span], row_low[:, span]
    total = None
    for group, (col_high, col_low) in enumerate(((own_high, own_low), (sibling_high, sibling_low))):
        for start in range(0, group_cols, 2 * width):
            part = slice(start, start + 2 * width)
            inner = three_pass((col_high[part, :], col_low[part, :]), row_halves, ((1,), (0,)))
            at = (group * group_cols + start) // width
            both = [jnp.broadcast_to(mask_ref[spot : spot + 1, span], (width, count * width)) for spot in (at, at + 1)]
            weight = jnp.exp(inner) * jnp.concatenate(both, axis=0)
            there = slice(group * group_cols + start, group * group_cols + start + 2 * width)
            added = three_pass((vec_high[:, there], vec_low[:, there]), halves(weight), ((1,), (0,)))
            total = added if total is None else total + added
    total = total * row_scale[:, span]
    for spot, out_ref in enumerate(out_refs):
        out_ref[...] = total[:, spot * width : (spot + 1) * width]


def add_kernel(*refs):
    total = refs[0][...]
    for ref in refs[1:-1]:
        total = total + ref[...]
    refs[-1][...] = total


def swapped(value, axis, step):
    count = lax.axis_size(axis)
    return lax.ppermute(value, axis, [(source, source ^ step) for source in range(count)])


def shards(coords, eigvecs, nbr_list, nbr_count):
    cycle_size = lax.axis_size("blk")
    rep_size = lax.axis_size("rep")
    rep_index = lax.axis_index("rep")
    group_blocks, slot_count = nbr_list.shape
    eig_count, width = eigvecs.shape
    feat_count = rep_size * coords.shape[0]
    params = pltpu.CompilerParams(vmem_limit_bytes=(8 + group_blocks) * 1024 * 1024)
    smem = pl.BlockSpec(memory_space=pltpu.SMEM)
    vmem = pl.BlockSpec(memory_space=pltpu.VMEM)
    anywhere = pl.BlockSpec(memory_space=pl.ANY)
    hint = pl.CostEstimate(flops=TRANSFER_FLOPS, bytes_accessed=1024 * 1024, transcendentals=0)

    pieces = [coords] + [swapped(coords, "rep", step) for step in range(1, rep_size)]
    own_block = jnp.concatenate(
        [lax.dynamic_slice_in_dim(piece, rep_index * width, width, 1) for piece in pieces], axis=0
    )
    vecs = eigvecs
    bit = 1
    while bit < rep_size:
        vecs = jnp.concatenate([vecs, swapped(vecs, "rep", bit)], axis=0)
        bit *= 2

    lists = pl.pallas_call(
        lists_kernel,
        in_specs=[smem, smem],
        out_shape=jax.ShapeDtypeStruct((slot_count, width), jnp.float32),
        compiler_params=params,
    )(nbr_list, nbr_count)
    panel = jnp.concatenate([own_block, lists], axis=0)
    panels = {0: panel}
    for step in range(2, cycle_size, 2):
        panels[step] = swapped(panel, "blk", step)

    f32, bf16 = jnp.float32, jnp.bfloat16
    group_cols = group_blocks * width
    row_count = len(panels) * width

    def columns_of(group_pieces):
        shape = jax.ShapeDtypeStruct((group_cols, feat_count), bf16)
        return pl.pallas_call(
            columns_kernel,
            out_shape=[shape, shape, jax.ShapeDtypeStruct((1, group_cols), f32)],
            compiler_params=params,
        )(*group_pieces)

    sibling_cols = swapped(jnp.concatenate(pieces, axis=0), "blk", 1)
    sibling_vecs = swapped(vecs, "blk", 1)
    own_high, own_low, own_scale = columns_of(pieces)
    sibling_high, sibling_low, sibling_scale = columns_of([sibling_cols])

    steps = list(range(0, cycle_size, 2))
    high_low = jax.ShapeDtypeStruct((feat_count, row_count), bf16)
    rows = pl.pallas_call(
        functools.partial(rows_kernel, feat_count),
        out_shape=[
            high_low,
            high_low,
            jax.ShapeDtypeStruct((1, row_count), f32),
            jax.ShapeDtypeStruct((2 * group_blocks, row_count), f32),
        ],
        compiler_params=params,
        cost_estimate=hint,
    )(*[panels[step] for step in steps])
    high_low = jax.ShapeDtypeStruct((eig_count, 2 * group_cols), bf16)
    vectors = pl.pallas_call(
        vectors_kernel,
        in_specs=[anywhere] + [vmem] * 4,
        out_shape=[high_low, high_low],
        compiler_params=params,
    )(rows[2], vecs, sibling_vecs, own_scale, sibling_scale)

    half = len(steps) // 2
    tiles = {}
    before = rows[2]
    for first in (half, 0):
        done = pl.pallas_call(
            functools.partial(apply_kernel, first, half),
            in_specs=[anywhere] + [vmem] * 10,
            out_shape=[jax.ShapeDtypeStruct((eig_count, width), f32)] * half,
            compiler_params=params,
        )(before, *rows, own_high, own_low, sibling_high, sibling_low, *vectors)
        before = done[0]
        for spot in range(half):
            tiles[steps[first + spot]] = done[spot]

    arrived = [swapped(tiles[step], "blk", step) for step in steps[1:]]
    far = pl.pallas_call(
        add_kernel,
        out_shape=jax.ShapeDtypeStruct((eig_count, width), f32),
        compiler_params=params,
        cost_estimate=hint,
    )(*arrived[half - 1 :])
    total = tiles[0]
    for tile in arrived[: half - 1]:
        total = total + tile
    return total + far


def solution(mesh):
    return jax.shard_map(
        shards,
        mesh=mesh,
        in_specs=(P("rep", "blk"), P(None, ("blk", "rep")), P("blk", None), P("blk")),
        out_specs=P(None, ("blk", "rep")),
        check_vma=False,
    )
```

time: 45.4 us -> 35 us (0.77)
  blocking collectives: 30.2 us -> 0 us
  starting transfers between devices: 4.07 us -> 15.6 us
  waiting for transfers between devices: 4.69 us -> 12.1 us
  Pallas kernels: 3.04 us -> 3.77 us
  other arithmetic: 0.95 us -> 1.52 us
  local copies, waits for them, and re-layouts: 2.18 us -> 1.63 us
    all_gather x1 -> x0, blocking collectives: 16.4 us -> none  [shards(): gathered = lax.all_gather(coords, 'rep', axis=0, tiled=True)]
    all_to_all x1 -> x0, blocking collectives: 13.8 us -> none  [shards(): arrived = lax.all_to_all(pieces, 'rep', 0, 0)]
    ppermute x7 -> x13, starting transfers between devices: 4.07 us -> 15.6 us  [swapped(): lax.ppermute(value, axis, [(source, source ^ step) for source in range(co...]
    ppermute x7 -> x13, waiting for transfers between devices: 4.69 us -> 12.1 us  [swapped(): lax.ppermute(value, axis, [(source, source ^ step) for source in range(co...]
    concatenate x1 -> x2, other arithmetic: 0.01 us -> 0.87 us  [the longest x1 0.85 us: shards(): vecs = jnp.concatenate([vecs, swapped(vecs, 'rep', bit)], axis=0)]
    pallas_call x1 -> x8, Pallas kernels: 3.04 us -> 3.77 us  [the longest x2 2.43 us: shards(): pl.pallas_call(functools.partial(apply_kernel, first, half), in_specs=[an...]
    reduce_sum x1 -> x0, other arithmetic: 0.64 us -> none  [shards(): return jnp.sum(arrived, axis=0)]
    add x1, other arithmetic: 0.01 us -> 0.64 us  [shards(): return total + far]
  transfers between devices with their start and end apart: 7 -> 13, of which waited for: 4 -> 8; matrix products, arithmetic and copies ran while one was open for 1% -> 5% of each run, Pallas kernels for 0% -> 7%
where the time goes in v2:
time: 35 us; the launch traced here: 34.8 us
  starting transfers between devices  15.6 us (45%)
  waiting for transfers between devices  12.1 us (35%)
  Pallas kernels  3.77 us (11%)
  local copies, waits for them, and re-layouts  1.63 us (5%)
  other arithmetic  1.52 us (4%)
    ppermute x13, starting transfers between devices, swapped(): lax.ppermute(value, axis, [(source, source ^ step) for source in range(co...  15.6 us
    ppermute x13, waiting for transfers between devices, swapped(): lax.ppermute(value, axis, [(source, source ^ step) for source in range(co...  12.1 us
    pallas_call x2, Pallas kernels, shards(): pl.pallas_call(functools.partial(apply_kernel, first, half), in_specs=[an...  2.43 us
    unnamed x12, local copies, waits for them, and re-layouts  1.62 us
    concatenate x1, other arithmetic, shards(): vecs = jnp.concatenate([vecs, swapped(vecs, 'rep', bit)], axis=0)  0.85 us
  transfers between devices with their start and end apart: 13, of which 8 were waited for; matrix products, arithmetic and copies ran while one was open for 5% of the time, Pallas kernels for 7%

profile of v2, /device:TPU:0, one launch (start us, length us, event | category | flops | bytes accessed | tf_op | source)
XLA Modules:
  0.0 34.8 jit_solution(18069732225452552541)
XLA Ops:
  0.0 0.0 copy-start
  0.0 5.0 %collective-permute-start.2 = (f32[48,512]{1,0:T(8,128)}, f32[48,512]{1,0:T(8,128)S(1)}, u32[]{:S(2)}, u32[]{:S(2)}) collective-permute-start(f32[48,512]{1,0:T(8,128)} %refs_0_.1), channel_id=1, source_target_pairs={{0,3},{1,2},{2,1},{3,0},{4,7},{5,6},{6,5},{7,4},{8,11},{9,10},{10,... | collective-permute-start | bytes 294920 | tf_op jit(solution)/shard_map/ppermute | solution.py:102
  5.1 0.0 collective-permute-start.1
  5.1 0.6 %collective-permute-start = (f32[48,512]{1,0:T(8,128)}, f32[48,512]{1,0:T(8,128)S(1)}, u32[]{:S(2)}, u32[]{:S(2)}) collective-permute-start(f32[48,512]{1,0:T(8,128)} %refs_0_.1), channel_id=1, source_target_pairs={{0,1},{1,0},{2,3},{3,2},{4,5},{5,4},{6,7},{7,6},{8,9},{9,8},{10,11... | collective-permute-start | bytes 294920 | tf_op jit(solution)/shard_map/ppermute | solution.py:102
  5.7 1.4 %collective-permute-start.7 = (f32[128,128]{1,0:T(8,128)}, f32[128,128]{1,0:T(8,128)S(1)}, u32[]{:S(2)}, u32[]{:S(2)}) collective-permute-start(f32[128,128]{1,0:T(8,128)} %param.5), channel_id=1, source_target_pairs={{0,1},{1,0},{2,3},{3,2},{4,5},{5,4},{6,7},{7,6},{8,9},{9,8},{10,11... | collective-permute-start | bytes 196616 | tf_op jit(solution)/shard_map/ppermute | solution.py:102
  7.1 0.9 %constant_dynamic-update-slice_fusion.3 = f32[512,128]{1,0:T(8,128)S(1)} fusion(f32[128,128]{1,0:T(8,128)} %param.5), kind=kLoop, calls=%fused_computation.10 | loop fusion | bytes 131072
  8.0 0.0 copy-start.1
  8.0 0.0 copy-start.2
  8.0 0.7 %copy-done.1 = s32[4,8]{1,0:T(4,128)S(1)} copy-done((s32[4,8]{1,0:T(4,128)S(1)}, s32[4,8]{1,0:T(4,128)}, u32[]{:S(2)}) %copy-start.1) | copy-done | bytes 152
  8.6 0.0 copy-done.2
  8.6 0.6 %shard_map.46 = f32[8,128]{1,0:T(8,128)S(1)} custom-call(s32[4,8]{1,0:T(4,128)S(1)} %copy-done.1, s32[4]{0:T(128)S(1)} %copy-done.2), custom_call_target="tpu_custom_call" | custom-call | tf_op jit(solution)/shard_map/pallas_call | solution.py:128
  9.2 0.0 copy-done
  9.3 4.6 %collective-permute-done.7 = f32[128,128]{1,0:T(8,128)S(1)} collective-permute-done((f32[128,128]{1,0:T(8,128)}, f32[128,128]{1,0:T(8,128)S(1)}, u32[]{:S(2)}, u32[]{:S(2)}) %collective-permute-start.7) | collective-permute-done | bytes 65568 | tf_op jit(solution)/shard_map/ppermute | solution.py:102
  13.9 0.8 %pad_maximum_fusion.1 = f32[256,128]{1,0:T(8,128)S(1)} fusion(f32[128,128]{1,0:T(8,128)S(1)} %collective-permute-done.7, f32[128,128]{1,0:T(8,128)} %param.5), kind=kLoop, calls=%fused_computation.1 | loop fusion | flops 32768 | bytes 262144 | tf_op jit(solution)/shard_map/concatenate | solution.py:125
  14.7 1.2 %collective-permute-start.8 = (f32[256,128]{1,0:T(8,128)S(1)}, f32[256,128]{1,0:T(8,128)S(1)}, u32[]{:S(2)}, u32[]{:S(2)}) collective-permute-start(f32[256,128]{1,0:T(8,128)S(1)} %pad_maximum_fusion.1), channel_id=1, source_target_pairs={{0,2},{1,3},{2,0},{3,1},{4,6},{5,7},{6,4},{7,5},{8,10},{9,11},{10,... | collective-permute-start | bytes 393224 | tf_op jit(solution)/shard_map/ppermute | solution.py:102
  15.9 0.0 collective-permute-done.refs_1_
  16.0 0.0 collective-permute-done.1.refs_2_
  16.0 0.0 collective-permute-done.2.refs_3_
  16.0 2.5 %collective-permute-start.5 = (f32[200,128]{1,0:T(8,128)S(1)}, f32[200,128]{1,0:T(8,128)S(1)}, u32[]{:S(2)}, u32[]{:S(2)}) collective-permute-start(f32[200,128]{1,0:T(8,128)S(1)} %constant_dynamic-update-slice_fusion.refs_0_), channel_id=1, source_target_pairs={{0,24},{4,28},{8,16},{12,20},{16,8},{20,12},{24,0},{28,4},{1,25},{... | collective-permute-start | bytes 307208 | tf_op jit(solution)/shard_map/ppermute | solution.py:102
  18.5 0.5 %collective-permute-start.4 = (f32[200,128]{1,0:T(8,128)S(1)}, f32[200,128]{1,0:T(8,128)S(1)}, u32[]{:S(2)}, u32[]{:S(2)}) collective-permute-start(f32[200,128]{1,0:T(8,128)S(1)} %constant_dynamic-update-slice_fusion.refs_0_), channel_id=1, source_target_pairs={{0,16},{4,20},{8,24},{12,28},{16,0},{20,4},{24,8},{28,12},{1,17},{... | collective-permute-start | bytes 307208 | tf_op jit(solution)/shard_map/ppermute | solution.py:102
  19.0 0.5 %collective-permute-start.3 = (f32[200,128]{1,0:T(8,128)S(1)}, f32[200,128]{1,0:T(8,128)S(1)}, u32[]{:S(2)}, u32[]{:S(2)}) collective-permute-start(f32[200,128]{1,0:T(8,128)S(1)} %constant_dynamic-update-slice_fusion.refs_0_), channel_id=1, source_target_pairs={{0,8},{4,12},{8,0},{12,4},{16,24},{20,28},{24,16},{28,20},{1,9},{5... | collective-permute-start | bytes 307208 | tf_op jit(solution)/shard_map/ppermute | solution.py:102
  19.6 0.1 collective-permute-start.6
  19.7 0.2 shard_map.48
  19.9 2.7 %collective-permute-done.8 = f32[256,128]{1,0:T(8,128)S(1)} collective-permute-done((f32[256,128]{1,0:T(8,128)S(1)}, f32[256,128]{1,0:T(8,128)S(1)}, u32[]{:S(2)}, u32[]{:S(2)}) %collective-permute-start.8) | collective-permute-done | bytes 131104 | tf_op jit(solution)/shard_map/ppermute | solution.py:102
  22.6 0.1 collective-permute-start.9
  22.7 0.0 collective-permute-done.5.refs_3_
  22.7 0.8 %collective-permute-done.4.refs_2_ = f32[200,128]{1,0:T(8,128)S(1)} collective-permute-done((f32[200,128]{1,0:T(8,128)S(1)}, f32[200,128]{1,0:T(8,128)S(1)}, u32[]{:S(2)}, u32[]{:S(2)}) %collective-permute-start.4) | collective-permute-done | bytes 102432 | tf_op jit(solution)/shard_map/ppermute | solution.py:102
  23.5 0.2 collective-permute-done.3.refs_1_
  23.7 0.2 shard_map.47
  23.9 0.0 collective-permute-done.6.refs_0_
  23.9 0.2 shard_map.49
  24.1 0.1 collective-permute-done.9.sibling_ref
  24.2 0.2 shard_map.50
  24.4 1.2 %shard_map.51 = (f32[128,128]{1,0:T(8,128)S(1)}, f32[128,128]{1,0:T(8,128)S(1)}) custom-call(f32[1,512]{1,0:T(1,128)S(1)} %get-tuple-element.21.before_ref.row_scale, bf16[192,512]{1,0:T(8,128)(2,1)S(1)} %get-tuple-element.22.row_high, bf16[192,512]{1,0:T(8,128)(2,1)S(1)} %get-tuple-element.23.row_low, f32[1,512]{1,0:T(1,128)S(1)} %get-tuple-element.21.before_ref.row_scale, ...), custom_call_target="tpu_custom_call" | custom-call | tf_op jit(solution)/shard_map/pallas_call | solution.py:181
  25.6 2.5 %collective-permute-start.12 = (f32[128,128]{1,0:T(8,128)S(1)}, f32[128,128]{1,0:T(8,128)S(1)}, u32[]{:S(2)}, u32[]{:S(2)}) collective-permute-start(f32[128,128]{1,0:T(8,128)S(1)} %get-tuple-element.36), channel_id=1, source_target_pairs={{0,24},{4,28},{8,16},{12,20},{16,8},{20,12},{24,0},{28,4},{1,25},{... | collective-permute-start | bytes 196616 | tf_op jit(solution)/shard_map/ppermute | solution.py:102
  28.1 0.5 %collective-permute-start.11 = (f32[128,128]{1,0:T(8,128)S(1)}, f32[128,128]{1,0:T(8,128)S(1)}, u32[]{:S(2)}, u32[]{:S(2)}) collective-permute-start(f32[128,128]{1,0:T(8,128)S(1)} %get-tuple-element.33.before_ref), channel_id=1, source_target_pairs={{0,16},{4,20},{8,24},{12,28},{16,0},{20,4},{24,8},{28,12},{1,17},{... | collective-permute-start | bytes 196616 | tf_op jit(solution)/shard_map/ppermute | solution.py:102
  28.6 1.2 %shard_map.52 = (f32[128,128]{1,0:T(8,128)S(1)}, f32[128,128]{1,0:T(8,128)S(1)}) custom-call(f32[128,128]{1,0:T(8,128)S(1)} %get-tuple-element.33.before_ref, bf16[192,512]{1,0:T(8,128)(2,1)S(1)} %get-tuple-element.22.row_high, bf16[192,512]{1,0:T(8,128)(2,1)S(1)} %get-tuple-element.23.row_low, f32[1,512]{1,0:T(1,128)S(1)} %get-tuple-element.21.before_ref.row_scale, ...), custom_call_target="tpu_custom_call" | custom-call | tf_op jit(solution)/shard_map/pallas_call | solution.py:181
  29.8 0.6 %collective-permute-start.10 = (f32[128,128]{1,0:T(8,128)S(1)}, f32[128,128]{1,0:T(8,128)S(1)}, u32[]{:S(2)}, u32[]{:S(2)}) collective-permute-start(f32[128,128]{1,0:T(8,128)S(1)} %get-tuple-element.35), channel_id=1, source_target_pairs={{0,8},{4,12},{8,0},{12,4},{16,24},{20,28},{24,16},{28,20},{1,9},{5... | collective-permute-start | bytes 196616 | tf_op jit(solution)/shard_map/ppermute | solution.py:102
  30.4 0.4 %collective-permute-done.12.refs_1_ = f32[128,128]{1,0:T(8,128)S(1)} collective-permute-done((f32[128,128]{1,0:T(8,128)S(1)}, f32[128,128]{1,0:T(8,128)S(1)}, u32[]{:S(2)}, u32[]{:S(2)}) %collective-permute-start.12) | collective-permute-done | bytes 65568 | tf_op jit(solution)/shard_map/ppermute | solution.py:102
  30.9 1.5 %collective-permute-done.11.refs_0_ = f32[128,128]{1,0:T(8,128)S(1)} collective-permute-done((f32[128,128]{1,0:T(8,128)S(1)}, f32[128,128]{1,0:T(8,128)S(1)}, u32[]{:S(2)}, u32[]{:S(2)}) %collective-permute-start.11) | collective-permute-done | bytes 65568 | tf_op jit(solution)/shard_map/ppermute | solution.py:102
  32.4 1.8 %collective-permute-done.10 = f32[128,128]{1,0:T(8,128)S(1)} collective-permute-done((f32[128,128]{1,0:T(8,128)S(1)}, f32[128,128]{1,0:T(8,128)S(1)}, u32[]{:S(2)}, u32[]{:S(2)}) %collective-permute-start.10) | collective-permute-done | bytes 65568 | tf_op jit(solution)/shard_map/ppermute | solution.py:102
  34.2 0.6 %add_add_fusion = f32[128,128]{1,0:T(8,128)} fusion(f32[128,128]{1,0:T(8,128)S(1)} %shard_map.53, f32[128,128]{1,0:T(8,128)S(1)} %get-tuple-element.34, f32[128,128]{1,0:T(8,128)S(1)} %collective-permute-done.10), kind=kLoop, calls=%fused_computation.2 | loop fusion | flops 32768 | bytes 262144 | tf_op jit(solution)/shard_map/add | solution.py:201
  (9 shorter events, 0.1 us)
Async XLA Ops:
  0.0 9.2 %copy-start = (f32[48,512]{1,0:T(8,128)S(1)}, f32[48,512]{1,0:T(8,128)}, u32[]{:S(2)}) copy-start(f32[48,512]{1,0:T(8,128)} %refs_0_.1) | copy-start | bytes 294916
  0.0 16.0 %collective-permute-start.2 = (f32[48,512]{1,0:T(8,128)}, f32[48,512]{1,0:T(8,128)S(1)}, u32[]{:S(2)}, u32[]{:S(2)}) collective-permute-start(f32[48,512]{1,0:T(8,128)} %refs_0_.1), channel_id=1, source_target_pairs={{0,3},{1,2},{2,1},{3,0},{4,7},{5,6},{6,5},{7,4},{8,11},{9,10},{10,... | collective-permute-start | bytes 294920 | tf_op jit(solution)/shard_map/ppermute | solution.py:102
  5.1 10.9 %collective-permute-start.1 = (f32[48,512]{1,0:T(8,128)}, f32[48,512]{1,0:T(8,128)S(1)}, u32[]{:S(2)}, u32[]{:S(2)}) collective-permute-start(f32[48,512]{1,0:T(8,128)} %refs_0_.1), channel_id=1, source_target_pairs={{0,2},{1,3},{2,0},{3,1},{4,6},{5,7},{6,4},{7,5},{8,10},{9,11},{10,... | collective-permute-start | bytes 294920 | tf_op jit(solution)/shard_map/ppermute | solution.py:102
  5.1 10.9 %collective-permute-start = (f32[48,512]{1,0:T(8,128)}, f32[48,512]{1,0:T(8,128)S(1)}, u32[]{:S(2)}, u32[]{:S(2)}) collective-permute-start(f32[48,512]{1,0:T(8,128)} %refs_0_.1), channel_id=1, source_target_pairs={{0,1},{1,0},{2,3},{3,2},{4,5},{5,4},{6,7},{7,6},{8,9},{9,8},{10,11... | collective-permute-start | bytes 294920 | tf_op jit(solution)/shard_map/ppermute | solution.py:102
  5.7 8.2 %collective-permute-start.7 = (f32[128,128]{1,0:T(8,128)}, f32[128,128]{1,0:T(8,128)S(1)}, u32[]{:S(2)}, u32[]{:S(2)}) collective-permute-start(f32[128,128]{1,0:T(8,128)} %param.5), channel_id=1, source_target_pairs={{0,1},{1,0},{2,3},{3,2},{4,5},{5,4},{6,7},{7,6},{8,9},{9,8},{10,11... | collective-permute-start | bytes 196616 | tf_op jit(solution)/shard_map/ppermute | solution.py:102
  8.0 0.7 %copy-start.1 = (s32[4,8]{1,0:T(4,128)S(1)}, s32[4,8]{1,0:T(4,128)}, u32[]{:S(2)}) copy-start(s32[4,8]{1,0:T(4,128)} %list_ref.1) | copy-start | bytes 388
  8.0 0.7 %copy-start.2 = (s32[4]{0:T(128)S(1)}, s32[4]{0:T(128)}, u32[]{:S(2)}) copy-start(s32[4]{0:T(128)} %count_ref.1) | copy-start | bytes 52
  14.7 7.9 %collective-permute-start.8 = (f32[256,128]{1,0:T(8,128)S(1)}, f32[256,128]{1,0:T(8,128)S(1)}, u32[]{:S(2)}, u32[]{:S(2)}) collective-permute-start(f32[256,128]{1,0:T(8,128)S(1)} %pad_maximum_fusion.1), channel_id=1, source_target_pairs={{0,2},{1,3},{2,0},{3,1},{4,6},{5,7},{6,4},{7,5},{8,10},{9,11},{10,... | collective-permute-start | bytes 393224 | tf_op jit(solution)/shard_map/ppermute | solution.py:102
  16.0 6.7 %collective-permute-start.5 = (f32[200,128]{1,0:T(8,128)S(1)}, f32[200,128]{1,0:T(8,128)S(1)}, u32[]{:S(2)}, u32[]{:S(2)}) collective-permute-start(f32[200,128]{1,0:T(8,128)S(1)} %constant_dynamic-update-slice_fusion.refs_0_), channel_id=1, source_target_pairs={{0,24},{4,28},{8,16},{12,20},{16,8},{20,12},{24,0},{28,4},{1,25},{... | collective-permute-start | bytes 307208 | tf_op jit(solution)/shard_map/ppermute | solution.py:102
  18.5 5.0 %collective-permute-start.4 = (f32[200,128]{1,0:T(8,128)S(1)}, f32[200,128]{1,0:T(8,128)S(1)}, u32[]{:S(2)}, u32[]{:S(2)}) collective-permute-start(f32[200,128]{1,0:T(8,128)S(1)} %constant_dynamic-update-slice_fusion.refs_0_), channel_id=1, source_target_pairs={{0,16},{4,20},{8,24},{12,28},{16,0},{20,4},{24,8},{28,12},{1,17},{... | collective-permute-start | bytes 307208 | tf_op jit(solution)/shard_map/ppermute | solution.py:102
  19.0 4.7 %collective-permute-start.3 = (f32[200,128]{1,0:T(8,128)S(1)}, f32[200,128]{1,0:T(8,128)S(1)}, u32[]{:S(2)}, u32[]{:S(2)}) collective-permute-start(f32[200,128]{1,0:T(8,128)S(1)} %constant_dynamic-update-slice_fusion.refs_0_), channel_id=1, source_target_pairs={{0,8},{4,12},{8,0},{12,4},{16,24},{20,28},{24,16},{28,20},{1,9},{5... | collective-permute-start | bytes 307208 | tf_op jit(solution)/shard_map/ppermute | solution.py:102
  19.6 4.3 %collective-permute-start.6 = (f32[192,512]{1,0:T(8,128)S(1)}, f32[192,512]{1,0:T(8,128)S(1)}, u32[]{:S(2)}, u32[]{:S(2)}) collective-permute-start(f32[192,512]{1,0:T(8,128)S(1)} %pad_maximum_fusion), channel_id=1, source_target_pairs={{0,4},{4,0},{8,12},{12,8},{16,20},{20,16},{24,28},{28,24},{1,5},{5... | collective-permute-start | bytes 1179656 | tf_op jit(solution)/shard_map/ppermute | solution.py:102
  22.6 1.6 %collective-permute-start.9 = (f32[512,128]{1,0:T(8,128)S(1)}, f32[512,128]{1,0:T(8,128)S(1)}, u32[]{:S(2)}, u32[]{:S(2)}) collective-permute-start(f32[512,128]{1,0:T(8,128)S(1)} %constant_dynamic-update-slice_fusion.1.own_ref), channel_id=1, source_target_pairs={{0,4},{4,0},{8,12},{12,8},{16,20},{20,16},{24,28},{28,24},{1,5},{5... | collective-permute-start | bytes 786440 | tf_op jit(solution)/shard_map/ppermute | solution.py:102
  25.6 5.3 %collective-permute-start.12 = (f32[128,128]{1,0:T(8,128)S(1)}, f32[128,128]{1,0:T(8,128)S(1)}, u32[]{:S(2)}, u32[]{:S(2)}) collective-permute-start(f32[128,128]{1,0:T(8,128)S(1)} %get-tuple-element.36), channel_id=1, source_target_pairs={{0,24},{4,28},{8,16},{12,20},{16,8},{20,12},{24,0},{28,4},{1,25},{... | collective-permute-start | bytes 196616 | tf_op jit(solution)/shard_map/ppermute | solution.py:102
  28.1 4.3 %collective-permute-start.11 = (f32[128,128]{1,0:T(8,128)S(1)}, f32[128,128]{1,0:T(8,128)S(1)}, u32[]{:S(2)}, u32[]{:S(2)}) collective-permute-start(f32[128,128]{1,0:T(8,128)S(1)} %get-tuple-element.33.before_ref), channel_id=1, source_target_pairs={{0,16},{4,20},{8,24},{12,28},{16,0},{20,4},{24,8},{28,12},{1,17},{... | collective-permute-start | bytes 196616 | tf_op jit(solution)/shard_map/ppermute | solution.py:102
  29.8 4.3 %collective-permute-start.10 = (f32[128,128]{1,0:T(8,128)S(1)}, f32[128,128]{1,0:T(8,128)S(1)}, u32[]{:S(2)}, u32[]{:S(2)}) collective-permute-start(f32[128,128]{1,0:T(8,128)S(1)} %get-tuple-element.35), channel_id=1, source_target_pairs={{0,8},{4,12},{8,0},{12,4},{16,24},{20,28},{24,16},{28,20},{1,9},{5... | collective-permute-start | bytes 196616 | tf_op jit(solution)/shard_map/ppermute | solution.py:102

commit v3 on v1

v3 whole, which is shorter than its diff:
```python
import functools

import jax
import jax.numpy as jnp
from jax import lax
from jax.experimental import pallas as pl
from jax.experimental.pallas import tpu as pltpu
from jax.sharding import PartitionSpec as P


TRANSFER_FLOPS = 7 * 10**9


def halves(value):
    high = value.astype(jnp.bfloat16)
    return high, (value - high.astype(jnp.float32)).astype(jnp.bfloat16)


def stacked(value, order, axis):
    high, low = halves(value)
    return jnp.concatenate([{"h": high, "l": low}[letter] for letter in order], axis=axis)


def lists_kernel(list_ref, count_ref, out_ref):
    rank = lax.axis_index("rep")
    for slot in range(out_ref.shape[0]):
        listed = jnp.where(slot < count_ref[rank], list_ref[rank, slot], -1)
        out_ref[slot : slot + 1, :] = jnp.full((1, out_ref.shape[1]), listed.astype(jnp.float32))


def near_kernel(coords_ref, vecs_ref, out_ref):
    piece_feats, group_cols = coords_ref.shape
    eig_count, width = vecs_ref.shape
    rows = eig_count * width // group_cols
    out_ref[:piece_feats, :] = coords_ref[...]
    for part in range(group_cols // width):
        out_ref[piece_feats:, part * width : (part + 1) * width] = vecs_ref[part * rows : (part + 1) * rows, :]


def pair_kernel(piece_feats, vecs_ref, near_ref, out_ref):
    eig_count, width = vecs_ref.shape
    rows = near_ref.shape[0] - piece_feats
    out_ref[:eig_count, :] = vecs_ref[...]
    for part in range(eig_count // rows):
        near = near_ref[piece_feats:, part * width : (part + 1) * width]
        out_ref[eig_count + part * rows : eig_count + (part + 1) * rows, :] = near


def group_kernel(piece_count, *refs):
    piece_refs, vec_refs, out_ref = refs[:piece_count], refs[piece_count:-1], refs[-1]
    piece_feats = piece_refs[0].shape[0]
    width = vec_refs[0].shape[1]
    feat_count = piece_count * piece_feats
    eig_count = out_ref.shape[0] - feat_count
    rank = lax.axis_index("rep")
    for piece, ref in enumerate(piece_refs):
        out_ref[piece * piece_feats : (piece + 1) * piece_feats, :] = ref[:piece_feats, :]
    spot = 0
    for ref in vec_refs:
        for start in range(0, ref.shape[0], eig_count):
            span = pl.ds(pl.multiple_of((rank ^ spot) * width, width), width)
            out_ref[feat_count:, span] = ref[start : start + eig_count, :]
            spot += 1


def columns_kernel(feat_count, group_ref, col_ref, vec_ref):
    chunk = 2 * vec_ref.shape[0]
    cols = group_ref[:feat_count, :]
    col_ref[...] = stacked(cols.T, "hhl", 1)
    vecs = group_ref[feat_count:, :] * jnp.exp(jnp.sum(cols * cols, axis=0, keepdims=True) * (-1.0 / feat_count))
    for start in range(0, cols.shape[1], chunk):
        vec_ref[:, 3 * start : 3 * (start + chunk)] = stacked(vecs[:, start : start + chunk], "hhl", 1)


def rows_kernel(feat_count, *refs):
    panel_refs, (row_ref, scale_ref, mask_ref) = refs[:-3], refs[-3:]
    width = panel_refs[0].shape[1]
    group_blocks = mask_ref.shape[0] // 2
    blk_index = lax.axis_index("blk")
    for place, ref in enumerate(panel_refs):
        span = slice(place * width, (place + 1) * width)
        rows = ref[:feat_count, :]
        scale_ref[:, span] = jnp.exp(jnp.sum(rows * rows, axis=0, keepdims=True) * (-1.0 / feat_count))
        row_ref[:, span] = stacked(rows * (2.0 / feat_count), "hlh", 0)
        lists = ref[feat_count:, :]
        for spot in range(2 * group_blocks):
            column = (blk_index ^ (spot // group_blocks)) * group_blocks + spot % group_blocks
            hits = jnp.where(lists == column.astype(jnp.float32), 1.0, 0.0)
            mask_ref[spot : spot + 1, span] = jnp.max(hits, axis=0, keepdims=True)


def apply_kernel(row_ref, scale_ref, mask_ref, *refs):
    own_cols, own_vecs, sibling_cols, sibling_vecs, *out_refs = refs
    eig_count, width = out_refs[0].shape
    group_cols = own_cols.shape[0]
    chunk = 2 * width
    rows = row_ref[...]
    total = None
    for group, (col_ref, vec_ref) in enumerate(((own_cols, own_vecs), (sibling_cols, sibling_vecs))):
        for start in range(0, group_cols, chunk):
            inner = jnp.dot(col_ref[start : start + chunk, :], rows, preferred_element_type=jnp.float32)
            at = (group * group_cols + start) // width
            both = [jnp.broadcast_to(mask_ref[spot : spot + 1, :], (width, rows.shape[1])) for spot in (at, at + 1)]
            weight = stacked(jnp.exp(inner) * jnp.concatenate(both, axis=0), "hlh", 0)
            vecs = vec_ref[:, 3 * start : 3 * (start + chunk)]
            added = jnp.dot(vecs, weight, preferred_element_type=jnp.float32)
            total = added if total is None else total + added
    total = total * scale_ref[...]
    for spot, out_ref in enumerate(out_refs):
        out_ref[...] = total[:, spot * width : (spot + 1) * width]


def swapped(value, axis, step):
    count = lax.axis_size(axis)
    return lax.ppermute(value, axis, [(source, source ^ step) for source in range(count)])


def shards(coords, eigvecs, nbr_list, nbr_count):
    cycle_size = lax.axis_size("blk")
    rep_size = lax.axis_size("rep")
    rep_index = lax.axis_index("rep")
    group_blocks, slot_count = nbr_list.shape
    eig_count, width = eigvecs.shape
    piece_feats, group_cols = coords.shape
    feat_count = rep_size * piece_feats
    f32, bf16 = jnp.float32, jnp.bfloat16
    shape = jax.ShapeDtypeStruct
    smem = pl.BlockSpec(memory_space=pltpu.SMEM)
    params = pltpu.CompilerParams(vmem_limit_bytes=(8 + group_blocks) * 1024 * 1024)
    hint = pl.CostEstimate(flops=TRANSFER_FLOPS, bytes_accessed=1024 * 1024, transcendentals=0)

    far = range(2, rep_size)
    far_coords = [swapped(coords, "rep", step) for step in far]
    near = pl.pallas_call(
        near_kernel,
        out_shape=shape((piece_feats + eig_count * width // group_cols, group_cols), f32),
        compiler_params=params,
    )(coords, eigvecs)
    near = swapped(near, "rep", 1)
    vecs = [
        pl.pallas_call(
            functools.partial(pair_kernel, piece_feats),
            out_shape=shape((2 * eig_count, width), f32),
            compiler_params=params,
        )(eigvecs, near)
    ]
    bit = 2
    while bit < rep_size:
        vecs.append(swapped(jnp.concatenate(vecs, axis=0), "rep", bit))
        bit *= 2
    lists = pl.pallas_call(
        lists_kernel,
        in_specs=[smem, smem],
        out_shape=shape((slot_count, width), f32),
        compiler_params=params,
    )(nbr_list, nbr_count)

    pieces = [coords, near[:piece_feats], *far_coords]
    own_block = [lax.dynamic_slice_in_dim(piece, rep_index * width, width, 1) for piece in pieces]
    panel = jnp.concatenate([*own_block, lists], axis=0)
    steps = list(range(0, cycle_size, 2))
    panels = [panel] + [swapped(panel, "blk", step) for step in steps[1:]]

    own_group = pl.pallas_call(
        functools.partial(group_kernel, rep_size),
        out_shape=shape((feat_count + eig_count, group_cols), f32),
        compiler_params=params,
    )(coords, near, *far_coords, *vecs)
    sibling_group = swapped(own_group, "blk", 1)

    def columns_of(group):
        return pl.pallas_call(
            functools.partial(columns_kernel, feat_count),
            out_shape=[shape((group_cols, 3 * feat_count), bf16), shape((eig_count, 3 * group_cols), bf16)],
            compiler_params=params,
        )(group)

    row_count = len(panels) * width
    rows = pl.pallas_call(
        functools.partial(rows_kernel, feat_count),
        out_shape=[
            shape((3 * feat_count, row_count), bf16),
            shape((1, row_count), f32),
            shape((2 * group_blocks, row_count), f32),
        ],
        compiler_params=params,
        cost_estimate=hint,
    )(*panels)
    tiles = pl.pallas_call(
        apply_kernel,
        out_shape=[shape((eig_count, width), f32)] * len(panels),
        compiler_params=params,
    )(*rows, *columns_of(own_group), *columns_of(sibling_group))

    total = tiles[0]
    for tile, step in zip(tiles[1:], steps[1:]):
        total = total + swapped(tile, "blk", step)
    return total


def solution(mesh):
    return jax.shard_map(
        shards,
        mesh=mesh,
        in_specs=(P("rep", "blk"), P(None, ("blk", "rep")), P("blk", None), P("blk")),
        out_specs=P(None, ("blk", "rep")),
        check_vma=False,
    )
```

time: 45.4 us -> 37.3 us (0.82)
  blocking collectives: 30.2 us -> 0 us
  starting transfers between devices: 4.07 us -> 15.4 us
  waiting for transfers between devices: 4.69 us -> 14.1 us
  Pallas kernels: 3.04 us -> 5.16 us
  local copies, waits for them, and re-layouts: 2.18 us -> 1.64 us
    all_gather x1 -> x0, blocking collectives: 16.4 us -> none  [shards(): gathered = lax.all_gather(coords, 'rep', axis=0, tiled=True)]
    all_to_all x1 -> x0, blocking collectives: 13.8 us -> none  [shards(): arrived = lax.all_to_all(pieces, 'rep', 0, 0)]
    ppermute x7 -> x11, starting transfers between devices: 4.07 us -> 15.4 us  [swapped(): lax.ppermute(value, axis, [(source, source ^ step) for source in range(co...]
    ppermute x7 -> x11, waiting for transfers between devices: 4.69 us -> 14.1 us  [swapped(): lax.ppermute(value, axis, [(source, source ^ step) for source in range(co...]
    pallas_call x1 -> x8, Pallas kernels: 3.04 us -> 5.16 us  [the longest x1 1.91 us: shards(): pl.pallas_call(apply_kernel, out_shape=[shape((eig_count, width), f32)] *...]
    add x1, other arithmetic: 0.01 us -> 0.65 us  [shards(): total = total + swapped(tile, 'blk', step)]
    reduce_sum x1 -> x0, other arithmetic: 0.64 us -> none  [shards(): return jnp.sum(arrived, axis=0)]
    unnamed x6 -> x12, local copies, waits for them, and re-layouts: 2.08 us -> 1.63 us
  transfers between devices with their start and end apart: 7 -> 11, of which waited for: 4 -> 9; matrix products, arithmetic and copies ran while one was open for 1% -> 2% of each run, Pallas kernels for 0% -> 5%
where the time goes in v3:
time: 37.3 us; the launch traced here: 37 us
  starting transfers between devices  15.4 us (41%)
  waiting for transfers between devices  14.1 us (38%)
  Pallas kernels  5.16 us (14%)
  local copies, waits for them, and re-layouts  1.64 us (4%)
  other arithmetic  0.65 us (2%)
    ppermute x11, starting transfers between devices, swapped(): lax.ppermute(value, axis, [(source, source ^ step) for source in range(co...  15.4 us
    ppermute x11, waiting for transfers between devices, swapped(): lax.ppermute(value, axis, [(source, source ^ step) for source in range(co...  14.1 us
    pallas_call x1, Pallas kernels, shards(): pl.pallas_call(apply_kernel, out_shape=[shape((eig_count, width), f32)] *...  1.91 us
    unnamed x12, local copies, waits for them, and re-layouts  1.63 us
    pallas_call x1, Pallas kernels, shards(): pl.pallas_call(functools.partial(group_kernel, rep_size), out_shape=shape...  0.95 us
    pallas_call x1, Pallas kernels, shards(): pl.pallas_call(near_kernel, out_shape=shape((piece_feats + eig_count * wi...  0.93 us
  transfers between devices with their start and end apart: 11, of which 9 were waited for; matrix products, arithmetic and copies ran while one was open for 2% of the time, Pallas kernels for 5%

profile of v3, /device:TPU:0, one launch (start us, length us, event | category | flops | bytes accessed | tf_op | source)
XLA Modules:
  0.0 37.0 jit_solution(9250252894854589660)
XLA Ops:
  0.0 0.0 copy-start
  0.0 0.8 %copy-done = f32[128,128]{1,0:T(8,128)S(1)} copy-done((f32[128,128]{1,0:T(8,128)S(1)}, f32[128,128]{1,0:T(8,128)}, u32[]{:S(2)}) %copy-start) | copy-done | bytes 65560
  0.8 0.0 copy-start.2
  0.8 0.0 copy-start.3
  0.8 0.9 %shard_map.46 = f32[80,512]{1,0:T(8,128)S(1)} custom-call(f32[48,512]{1,0:T(8,128)} %refs_0_.1, f32[128,128]{1,0:T(8,128)S(1)} %copy-done), custom_call_target="tpu_custom_call" | custom-call | tf_op jit(solution)/shard_map/pallas_call | solution.py:134
  1.8 0.0 copy-start.1
  1.8 3.1 %collective-permute-start = (f32[80,512]{1,0:T(8,128)S(1)}, f32[80,512]{1,0:T(8,128)S(1)}, u32[]{:S(2)}, u32[]{:S(2)}) collective-permute-start(f32[80,512]{1,0:T(8,128)S(1)} %shard_map.46), channel_id=1, source_target_pairs={{0,1},{1,0},{2,3},{3,2},{4,5},{5,4},{6,7},{7,6},{8,9},{9,8},{10,11... | collective-permute-start | bytes 491528 | tf_op jit(solution)/shard_map/ppermute | solution.py:115
  4.9 2.6 %collective-permute-start.1 = (f32[48,512]{1,0:T(8,128)}, f32[48,512]{1,0:T(8,128)S(1)}, u32[]{:S(2)}, u32[]{:S(2)}) collective-permute-start(f32[48,512]{1,0:T(8,128)} %refs_0_.1), channel_id=1, source_target_pairs={{0,2},{1,3},{2,0},{3,1},{4,6},{5,7},{6,4},{7,5},{8,10},{9,11},{10,... | collective-permute-start | bytes 294920 | tf_op jit(solution)/shard_map/ppermute | solution.py:115
  7.5 0.0 collective-permute-start.2
  7.5 0.0 copy-done.2
  7.5 0.0 copy-done.3
  7.5 0.6 %shard_map.47 = f32[8,128]{1,0:T(8,128)S(1)} custom-call(s32[4,8]{1,0:T(4,128)S(1)} %copy-done.2, s32[4]{0:T(128)S(1)} %copy-done.3), custom_call_target="tpu_custom_call" | custom-call | tf_op jit(solution)/shard_map/pallas_call | solution.py:151
  8.1 0.7 %dynamic-slice_dynamic-update-slice_fusion.3 = f32[200,128]{1,0:T(8,128)S(1)} fusion(f32[48,512]{1,0:T(8,128)} %refs_0_.1, s32[]{:T(128)S(6)} %select_n.2), kind=kLoop, calls=%fused_computation.4 | loop fusion | bytes 49156
  8.8 1.7 %collective-permute-done.near_ref.refs_1_ = f32[80,512]{1,0:T(8,128)S(1)} collective-permute-done((f32[80,512]{1,0:T(8,128)S(1)}, f32[80,512]{1,0:T(8,128)S(1)}, u32[]{:S(2)}, u32[]{:S(2)}) %collective-permute-start) | collective-permute-done | bytes 163872 | tf_op jit(solution)/shard_map/ppermute | solution.py:115
  10.5 0.0 copy-done.1
  10.5 2.5 %collective-permute-start.6 = (f32[256,128]{1,0:T(8,128)S(1)}, f32[256,128]{1,0:T(8,128)S(1)}, u32[]{:S(2)}, u32[]{:S(2)}) collective-permute-start(f32[256,128]{1,0:T(8,128)S(1)} %shard_map.49.refs_4_), channel_id=1, source_target_pairs={{0,2},{1,3},{2,0},{3,1},{4,6},{5,7},{6,4},{7,5},{8,10},{9,11},{10,... | collective-permute-start | bytes 393224 | tf_op jit(solution)/shard_map/ppermute | solution.py:115
  13.1 5.6 %collective-permute-done.1.refs_2_ = f32[48,512]{1,0:T(8,128)S(1)} collective-permute-done((f32[48,512]{1,0:T(8,128)}, f32[48,512]{1,0:T(8,128)S(1)}, u32[]{:S(2)}, u32[]{:S(2)}) %collective-permute-start.1) | collective-permute-done | bytes 98336 | tf_op jit(solution)/shard_map/ppermute | solution.py:115
  18.7 0.0 collective-permute-done.2.refs_3_
  18.7 2.5 %collective-permute-start.5 = (f32[200,128]{1,0:T(8,128)S(1)}, f32[200,128]{1,0:T(8,128)S(1)}, u32[]{:S(2)}, u32[]{:S(2)}) collective-permute-start(f32[200,128]{1,0:T(8,128)S(1)} %constant_dynamic-update-slice_fusion.refs_0_), channel_id=1, source_target_pairs={{0,24},{4,28},{8,16},{12,20},{16,8},{20,12},{24,0},{28,4},{1,25},{... | collective-permute-start | bytes 307208 | tf_op jit(solution)/shard_map/ppermute | solution.py:115
  21.2 0.5 %collective-permute-start.4 = (f32[200,128]{1,0:T(8,128)S(1)}, f32[200,128]{1,0:T(8,128)S(1)}, u32[]{:S(2)}, u32[]{:S(2)}) collective-permute-start(f32[200,128]{1,0:T(8,128)S(1)} %constant_dynamic-update-slice_fusion.refs_0_), channel_id=1, source_target_pairs={{0,16},{4,20},{8,24},{12,28},{16,0},{20,4},{24,8},{28,12},{1,17},{... | collective-permute-start | bytes 307208 | tf_op jit(solution)/shard_map/ppermute | solution.py:115
  21.7 0.5 %collective-permute-start.3 = (f32[200,128]{1,0:T(8,128)S(1)}, f32[200,128]{1,0:T(8,128)S(1)}, u32[]{:S(2)}, u32[]{:S(2)}) collective-permute-start(f32[200,128]{1,0:T(8,128)S(1)} %constant_dynamic-update-slice_fusion.refs_0_), channel_id=1, source_target_pairs={{0,8},{4,12},{8,0},{12,4},{16,24},{20,28},{24,16},{28,20},{1,9},{5... | collective-permute-start | bytes 307208 | tf_op jit(solution)/shard_map/ppermute | solution.py:115
  22.3 0.1 collective-permute-done.6.refs_5_
  22.4 0.9 %shard_map.50.group_ref = f32[320,512]{1,0:T(8,128)S(1)} custom-call(f32[48,512]{1,0:T(8,128)} %refs_0_.1, f32[80,512]{1,0:T(8,128)S(1)} %collective-permute-done.near_ref.refs_1_, f32[48,512]{1,0:T(8,128)S(1)} %collective-permute-done.1.refs_2_, f32[48,512]{1,0:T(8,128)S(1)} %collective-permute-done.2.refs_3_, f32[256,128]{1,0:T(8,128)S(1)} %shard_map.49.refs_4_, ...), custom_call_target="tpu_custom_call" | custom-call | tf_op jit(solution)/shard_map/pallas_call | solution.py:164
  23.4 0.1 collective-permute-start.7
  23.5 0.9 %collective-permute-done.5.refs_3_ = f32[200,128]{1,0:T(8,128)S(1)} collective-permute-done((f32[200,128]{1,0:T(8,128)S(1)}, f32[200,128]{1,0:T(8,128)S(1)}, u32[]{:S(2)}, u32[]{:S(2)}) %collective-permute-start.5) | collective-permute-done | bytes 102432 | tf_op jit(solution)/shard_map/ppermute | solution.py:115
  24.3 1.5 %collective-permute-done.4.refs_2_ = f32[200,128]{1,0:T(8,128)S(1)} collective-permute-done((f32[200,128]{1,0:T(8,128)S(1)}, f32[200,128]{1,0:T(8,128)S(1)}, u32[]{:S(2)}, u32[]{:S(2)}) %collective-permute-start.4) | collective-permute-done | bytes 102432 | tf_op jit(solution)/shard_map/ppermute | solution.py:115
  25.9 0.5 %collective-permute-done.3.refs_1_ = f32[200,128]{1,0:T(8,128)S(1)} collective-permute-done((f32[200,128]{1,0:T(8,128)S(1)}, f32[200,128]{1,0:T(8,128)S(1)}, u32[]{:S(2)}, u32[]{:S(2)}) %collective-permute-start.3) | collective-permute-done | bytes 102432 | tf_op jit(solution)/shard_map/ppermute | solution.py:115
  26.4 0.2 shard_map.48
  26.6 0.3 shard_map.51
  26.9 0.0 collective-permute-done.7.group_ref
  26.9 0.3 shard_map.52
  27.2 1.9 %shard_map.53 = (f32[128,128]{1,0:T(8,128)S(1)}, f32[128,128]{1,0:T(8,128)S(1)}, f32[128,128]{1,0:T(8,128)S(1)}, f32[128,128]{1,0:T(8,128)S(1)}) custom-call(bf16[576,512]{1,0:T(8,128)(2,1)S(1)} %get-tuple-element.16.row_ref, f32[1,512]{1,0:T(1,128)S(1)} %get-tuple-element.17.scale_ref, f32[8,512]{1,0:T(8,128)S(1)} %get-tuple-element.18.mask_ref, ...), custom_call_target="tpu_custom_call" | custom-call | tf_op jit(solution)/shard_map/pallas_call | solution.py:189
  29.1 0.7 %collective-permute-start.8 = (f32[128,128]{1,0:T(8,128)S(1)}, f32[128,128]{1,0:T(8,128)S(1)}, u32[]{:S(2)}, u32[]{:S(2)}) collective-permute-start(f32[128,128]{1,0:T(8,128)S(1)} %get-tuple-element.24), channel_id=1, source_target_pairs={{0,8},{4,12},{8,0},{12,4},{16,24},{20,28},{24,16},{28,20},{1,9},{5... | collective-permute-start | bytes 196616 | tf_op jit(solution)/shard_map/ppermute | solution.py:115
  29.8 1.4 %collective-permute-start.9 = (f32[128,128]{1,0:T(8,128)S(1)}, f32[128,128]{1,0:T(8,128)S(1)}, u32[]{:S(2)}, u32[]{:S(2)}) collective-permute-start(f32[128,128]{1,0:T(8,128)S(1)} %get-tuple-element.25), channel_id=1, source_target_pairs={{0,16},{4,20},{8,24},{12,28},{16,0},{20,4},{24,8},{28,12},{1,17},{... | collective-permute-start | bytes 196616 | tf_op jit(solution)/shard_map/ppermute | solution.py:115
  31.2 1.4 %collective-permute-start.10 = (f32[128,128]{1,0:T(8,128)S(1)}, f32[128,128]{1,0:T(8,128)S(1)}, u32[]{:S(2)}, u32[]{:S(2)}) collective-permute-start(f32[128,128]{1,0:T(8,128)S(1)} %get-tuple-element.26), channel_id=1, source_target_pairs={{0,24},{4,28},{8,16},{12,20},{16,8},{20,12},{24,0},{28,4},{1,25},{... | collective-permute-start | bytes 196616 | tf_op jit(solution)/shard_map/ppermute | solution.py:115
  32.7 1.3 %collective-permute-done.8 = f32[128,128]{1,0:T(8,128)S(1)} collective-permute-done((f32[128,128]{1,0:T(8,128)S(1)}, f32[128,128]{1,0:T(8,128)S(1)}, u32[]{:S(2)}, u32[]{:S(2)}) %collective-permute-start.8) | collective-permute-done | bytes 65568 | tf_op jit(solution)/shard_map/ppermute | solution.py:115
  34.0 0.3 collective-permute-done.9
  34.2 2.2 %collective-permute-done.10 = f32[128,128]{1,0:T(8,128)S(1)} collective-permute-done((f32[128,128]{1,0:T(8,128)S(1)}, f32[128,128]{1,0:T(8,128)S(1)}, u32[]{:S(2)}, u32[]{:S(2)}) %collective-permute-start.10) | collective-permute-done | bytes 65568 | tf_op jit(solution)/shard_map/ppermute | solution.py:115
  36.4 0.6 %add_add_fusion = f32[128,128]{1,0:T(8,128)} fusion(f32[128,128]{1,0:T(8,128)S(1)} %collective-permute-done.10, f32[128,128]{1,0:T(8,128)S(1)} %collective-permute-done.9, f32[128,128]{1,0:T(8,128)S(1)} %get-tuple-element.23, f32[128,128]{1,0:T(8,128)S(1)} %collective-permute-done.8), kind=kLoop, calls=%fused_computation | loop fusion | flops 49152 | bytes 327680 | tf_op jit(solution)/shard_map/add | solution.py:197
  (6 shorter events, 0.0 us)
Async XLA Ops:
  0.0 0.8 %copy-start = (f32[128,128]{1,0:T(8,128)S(1)}, f32[128,128]{1,0:T(8,128)}, u32[]{:S(2)}) copy-start(f32[128,128]{1,0:T(8,128)} %vecs_ref.3) | copy-start | bytes 196612
  0.8 6.6 %copy-start.2 = (s32[4,8]{1,0:T(4,128)S(1)}, s32[4,8]{1,0:T(4,128)}, u32[]{:S(2)}) copy-start(s32[4,8]{1,0:T(4,128)} %list_ref.1) | copy-start | bytes 388
  0.8 6.6 %copy-start.3 = (s32[4]{0:T(128)S(1)}, s32[4]{0:T(128)}, u32[]{:S(2)}) copy-start(s32[4]{0:T(128)} %count_ref.1) | copy-start | bytes 52
  1.8 8.7 %copy-start.1 = (f32[128,128]{1,0:T(8,128)S(1)}, f32[128,128]{1,0:T(8,128)}, u32[]{:S(2)}) copy-start(f32[128,128]{1,0:T(8,128)} %vecs_ref.3) | copy-start | bytes 196612
  1.8 8.7 %collective-permute-start = (f32[80,512]{1,0:T(8,128)S(1)}, f32[80,512]{1,0:T(8,128)S(1)}, u32[]{:S(2)}, u32[]{:S(2)}) collective-permute-start(f32[80,512]{1,0:T(8,128)S(1)} %shard_map.46), channel_id=1, source_target_pairs={{0,1},{1,0},{2,3},{3,2},{4,5},{5,4},{6,7},{7,6},{8,9},{9,8},{10,11... | collective-permute-start | bytes 491528 | tf_op jit(solution)/shard_map/ppermute | solution.py:115
  4.9 13.8 %collective-permute-start.1 = (f32[48,512]{1,0:T(8,128)}, f32[48,512]{1,0:T(8,128)S(1)}, u32[]{:S(2)}, u32[]{:S(2)}) collective-permute-start(f32[48,512]{1,0:T(8,128)} %refs_0_.1), channel_id=1, source_target_pairs={{0,2},{1,3},{2,0},{3,1},{4,6},{5,7},{6,4},{7,5},{8,10},{9,11},{10,... | collective-permute-start | bytes 294920 | tf_op jit(solution)/shard_map/ppermute | solution.py:115
  7.5 11.2 %collective-permute-start.2 = (f32[48,512]{1,0:T(8,128)}, f32[48,512]{1,0:T(8,128)S(1)}, u32[]{:S(2)}, u32[]{:S(2)}) collective-permute-start(f32[48,512]{1,0:T(8,128)} %refs_0_.1), channel_id=1, source_target_pairs={{0,3},{1,2},{2,1},{3,0},{4,7},{5,6},{6,5},{7,4},{8,11},{9,10},{10,... | collective-permute-start | bytes 294920 | tf_op jit(solution)/shard_map/ppermute | solution.py:115
  10.5 11.9 %collective-permute-start.6 = (f32[256,128]{1,0:T(8,128)S(1)}, f32[256,128]{1,0:T(8,128)S(1)}, u32[]{:S(2)}, u32[]{:S(2)}) collective-permute-start(f32[256,128]{1,0:T(8,128)S(1)} %shard_map.49.refs_4_), channel_id=1, source_target_pairs={{0,2},{1,3},{2,0},{3,1},{4,6},{5,7},{6,4},{7,5},{8,10},{9,11},{10,... | collective-permute-start | bytes 393224 | tf_op jit(solution)/shard_map/ppermute | solution.py:115
  18.7 5.6 %collective-permute-start.5 = (f32[200,128]{1,0:T(8,128)S(1)}, f32[200,128]{1,0:T(8,128)S(1)}, u32[]{:S(2)}, u32[]{:S(2)}) collective-permute-start(f32[200,128]{1,0:T(8,128)S(1)} %constant_dynamic-update-slice_fusion.refs_0_), channel_id=1, source_target_pairs={{0,24},{4,28},{8,16},{12,20},{16,8},{20,12},{24,0},{28,4},{1,25},{... | collective-permute-start | bytes 307208 | tf_op jit(solution)/shard_map/ppermute | solution.py:115
  21.2 4.7 %collective-permute-start.4 = (f32[200,128]{1,0:T(8,128)S(1)}, f32[200,128]{1,0:T(8,128)S(1)}, u32[]{:S(2)}, u32[]{:S(2)}) collective-permute-start(f32[200,128]{1,0:T(8,128)S(1)} %constant_dynamic-update-slice_fusion.refs_0_), channel_id=1, source_target_pairs={{0,16},{4,20},{8,24},{12,28},{16,0},{20,4},{24,8},{28,12},{1,17},{... | collective-permute-start | bytes 307208 | tf_op jit(solution)/shard_map/ppermute | solution.py:115
  21.7 4.7 %collective-permute-start.3 = (f32[200,128]{1,0:T(8,128)S(1)}, f32[200,128]{1,0:T(8,128)S(1)}, u32[]{:S(2)}, u32[]{:S(2)}) collective-permute-start(f32[200,128]{1,0:T(8,128)S(1)} %constant_dynamic-update-slice_fusion.refs_0_), channel_id=1, source_target_pairs={{0,8},{4,12},{8,0},{12,4},{16,24},{20,28},{24,16},{28,20},{1,9},{5... | collective-permute-start | bytes 307208 | tf_op jit(solution)/shard_map/ppermute | solution.py:115
  23.4 3.5 %collective-permute-start.7 = (f32[320,512]{1,0:T(8,128)S(1)}, f32[320,512]{1,0:T(8,128)S(1)}, u32[]{:S(2)}, u32[]{:S(2)}) collective-permute-start(f32[320,512]{1,0:T(8,128)S(1)} %shard_map.50.group_ref), channel_id=1, source_target_pairs={{0,4},{4,0},{8,12},{12,8},{16,20},{20,16},{24,28},{28,24},{1,5},{5... | collective-permute-start | bytes 1966088 | tf_op jit(solution)/shard_map/ppermute | solution.py:115
  29.1 4.8 %collective-permute-start.8 = (f32[128,128]{1,0:T(8,128)S(1)}, f32[128,128]{1,0:T(8,128)S(1)}, u32[]{:S(2)}, u32[]{:S(2)}) collective-permute-start(f32[128,128]{1,0:T(8,128)S(1)} %get-tuple-element.24), channel_id=1, source_target_pairs={{0,8},{4,12},{8,0},{12,4},{16,24},{20,28},{24,16},{28,20},{1,9},{5... | collective-permute-start | bytes 196616 | tf_op jit(solution)/shard_map/ppermute | solution.py:115
  29.8 4.4 %collective-permute-start.9 = (f32[128,128]{1,0:T(8,128)S(1)}, f32[128,128]{1,0:T(8,128)S(1)}, u32[]{:S(2)}, u32[]{:S(2)}) collective-permute-start(f32[128,128]{1,0:T(8,128)S(1)} %get-tuple-element.25), channel_id=1, source_target_pairs={{0,16},{4,20},{8,24},{12,28},{16,0},{20,4},{24,8},{28,12},{1,17},{... | collective-permute-start | bytes 196616 | tf_op jit(solution)/shard_map/ppermute | solution.py:115
  31.2 5.2 %collective-permute-start.10 = (f32[128,128]{1,0:T(8,128)S(1)}, f32[128,128]{1,0:T(8,128)S(1)}, u32[]{:S(2)}, u32[]{:S(2)}) collective-permute-start(f32[128,128]{1,0:T(8,128)S(1)} %get-tuple-element.26), channel_id=1, source_target_pairs={{0,24},{4,28},{8,16},{12,20},{16,8},{20,12},{24,0},{28,4},{1,25},{... | collective-permute-start | bytes 196616 | tf_op jit(solution)/shard_map/ppermute | solution.py:115

commit v4 on v3

--- a/solution.py
+++ b/solution.py
@@ -8,7 +8,7 @@
 from jax.sharding import PartitionSpec as P
 
 
-TRANSFER_FLOPS = 7 * 10**9
+TRANSFER_FLOPS = 62 * 10**8
 
 
 def halves(value):
@@ -28,22 +28,8 @@
         out_ref[slot : slot + 1, :] = jnp.full((1, out_ref.shape[1]), listed.astype(jnp.float32))
 
 
-def near_kernel(coords_ref, vecs_ref, out_ref):
-    piece_feats, group_cols = coords_ref.shape
-    eig_count, width = vecs_ref.shape
-    rows = eig_count * width // group_cols
-    out_ref[:piece_feats, :] = coords_ref[...]
-    for part in range(group_cols // width):
-        out_ref[piece_feats:, part * width : (part + 1) * width] = vecs_ref[part * rows : (part + 1) * rows, :]
-
-
-def pair_kernel(piece_feats, vecs_ref, near_ref, out_ref):
-    eig_count, width = vecs_ref.shape
-    rows = near_ref.shape[0] - piece_feats
-    out_ref[:eig_count, :] = vecs_ref[...]
-    for part in range(eig_count // rows):
-        near = near_ref[piece_feats:, part * width : (part + 1) * width]
-        out_ref[eig_count + part * rows : eig_count + (part + 1) * rows, :] = near
+def copy_kernel(before_ref, in_ref, out_ref):
+    out_ref[...] = in_ref[...]
 
 
 def group_kernel(piece_count, *refs):
@@ -51,16 +37,12 @@
     piece_feats = piece_refs[0].shape[0]
     width = vec_refs[0].shape[1]
     feat_count = piece_count * piece_feats
-    eig_count = out_ref.shape[0] - feat_count
     rank = lax.axis_index("rep")
     for piece, ref in enumerate(piece_refs):
-        out_ref[piece * piece_feats : (piece + 1) * piece_feats, :] = ref[:piece_feats, :]
-    spot = 0
-    for ref in vec_refs:
-        for start in range(0, ref.shape[0], eig_count):
-            span = pl.ds(pl.multiple_of((rank ^ spot) * width, width), width)
-            out_ref[feat_count:, span] = ref[start : start + eig_count, :]
-            spot += 1
+        out_ref[piece * piece_feats : (piece + 1) * piece_feats, :] = ref[...]
+    for spot, ref in enumerate(vec_refs[::-1]):
+        span = pl.ds(pl.multiple_of((rank ^ spot) * width, width), width)
+        out_ref[feat_count:, span] = ref[...]
 
 
 def columns_kernel(feat_count, group_ref, col_ref, vec_ref):
@@ -89,25 +71,33 @@
             mask_ref[spot : spot + 1, span] = jnp.max(hits, axis=0, keepdims=True)
 
 
-def apply_kernel(row_ref, scale_ref, mask_ref, *refs):
+def apply_kernel(first, count, before_ref, row_ref, scale_ref, mask_ref, *refs):
     own_cols, own_vecs, sibling_cols, sibling_vecs, *out_refs = refs
-    eig_count, width = out_refs[0].shape
+    width = out_refs[0].shape[1]
     group_cols = own_cols.shape[0]
     chunk = 2 * width
-    rows = row_ref[...]
+    span = slice(first * width, (first + count) * width)
+    rows = row_ref[:, span]
     total = None
     for group, (col_ref, vec_ref) in enumerate(((own_cols, own_vecs), (sibling_cols, sibling_vecs))):
         for start in range(0, group_cols, chunk):
             inner = jnp.dot(col_ref[start : start + chunk, :], rows, preferred_element_type=jnp.float32)
             at = (group * group_cols + start) // width
-            both = [jnp.broadcast_to(mask_ref[spot : spot + 1, :], (width, rows.shape[1])) for spot in (at, at + 1)]
+            both = [jnp.broadcast_to(mask_ref[spot : spot + 1, span], (width, count * width)) for spot in (at, at + 1)]
             weight = stacked(jnp.exp(inner) * jnp.concatenate(both, axis=0), "hlh", 0)
             vecs = vec_ref[:, 3 * start : 3 * (start + chunk)]
             added = jnp.dot(vecs, weight, preferred_element_type=jnp.float32)
             total = added if total is None else total + added
-    total = total * scale_ref[...]
+    total = total * scale_ref[:, span]
     for spot, out_ref in enumerate(out_refs):
         out_ref[...] = total[:, spot * width : (spot + 1) * width]
+
+
+def add_kernel(*refs):
+    total = refs[0][...]
+    for ref in refs[1:-1]:
+        total = total + ref[...]
+    refs[-1][...] = total
 
 
 def swapped(value, axis, step):
@@ -126,28 +116,19 @@
     f32, bf16 = jnp.float32, jnp.bfloat16
     shape = jax.ShapeDtypeStruct
     smem = pl.BlockSpec(memory_space=pltpu.SMEM)
+    vmem = pl.BlockSpec(memory_space=pltpu.VMEM)
+    anywhere = pl.BlockSpec(memory_space=pl.ANY)
     params = pltpu.CompilerParams(vmem_limit_bytes=(8 + group_blocks) * 1024 * 1024)
     hint = pl.CostEstimate(flops=TRANSFER_FLOPS, bytes_accessed=1024 * 1024, transcendentals=0)
 
-    far = range(2, rep_size)
-    far_coords = [swapped(coords, "rep", step) for step in far]
-    near = pl.pallas_call(
-        near_kernel,
-        out_shape=shape((piece_feats + eig_count * width // group_cols, group_cols), f32),
-        compiler_params=params,
-    )(coords, eigvecs)
-    near = swapped(near, "rep", 1)
-    vecs = [
-        pl.pallas_call(
-            functools.partial(pair_kernel, piece_feats),
-            out_shape=shape((2 * eig_count, width), f32),
-            compiler_params=params,
-        )(eigvecs, near)
-    ]
-    bit = 2
-    while bit < rep_size:
-        vecs.append(swapped(jnp.concatenate(vecs, axis=0), "rep", bit))
-        bit *= 2
+    pieces = [coords] + [swapped(coords, "rep", step) for step in range(1, rep_size)]
+    late_vecs = pl.pallas_call(
+        copy_kernel,
+        in_specs=[anywhere, vmem],
+        out_shape=shape(eigvecs.shape, f32),
+        compiler_params=params,
+    )(pieces[1], eigvecs)
+    vecs = [swapped(late_vecs, "rep", step) for step in range(rep_size - 1, 0, -1)] + [late_vecs]
     lists = pl.pallas_call(
         lists_kernel,
         in_specs=[smem, smem],
@@ -155,7 +136,6 @@
         compiler_params=params,
     )(nbr_list, nbr_count)
 
-    pieces = [coords, near[:piece_feats], *far_coords]
     own_block = [lax.dynamic_slice_in_dim(piece, rep_index * width, width, 1) for piece in pieces]
     panel = jnp.concatenate([*own_block, lists], axis=0)
     steps = list(range(0, cycle_size, 2))
@@ -165,7 +145,7 @@
         functools.partial(group_kernel, rep_size),
         out_shape=shape((feat_count + eig_count, group_cols), f32),
         compiler_params=params,
-    )(coords, near, *far_coords, *vecs)
+    )(*pieces, *vecs)
     sibling_group = swapped(own_group, "blk", 1)
 
     def columns_of(group):
@@ -186,16 +166,32 @@
         compiler_params=params,
         cost_estimate=hint,
     )(*panels)
-    tiles = pl.pallas_call(
-        apply_kernel,
-        out_shape=[shape((eig_count, width), f32)] * len(panels),
-        compiler_params=params,
-    )(*rows, *columns_of(own_group), *columns_of(sibling_group))
-
+    columns = [*columns_of(own_group), *columns_of(sibling_group)]
+    half = len(steps) // 2
+    tiles = {}
+    before = rows[1]
+    for first in (half, 0):
+        done = pl.pallas_call(
+            functools.partial(apply_kernel, first, half),
+            in_specs=[anywhere] + [vmem] * 7,
+            out_shape=[shape((eig_count, width), f32)] * half,
+            compiler_params=params,
+        )(before, *rows, *columns)
+        before = done[0]
+        for spot in range(half):
+            tiles[first + spot] = done[spot]
+
+    arrived = [swapped(tiles[place], "blk", steps[place]) for place in range(1, len(steps))]
+    far = pl.pallas_call(
+        add_kernel,
+        out_shape=shape((eig_count, width), f32),
+        compiler_params=params,
+        cost_estimate=hint,
+    )(*arrived[half - 1 :])
     total = tiles[0]
-    for tile, step in zip(tiles[1:], steps[1:]):
-        total = total + swapped(tile, "blk", step)
-    return total
+    for tile in arrived[: half - 1]:
+        total = total + tile
+    return total + far
 
 
 def solution(mesh):

time: 37.3 us -> 32.2 us (0.86)
  waiting for transfers between devices: 14.1 us -> 7.73 us
  starting transfers between devices: 15.4 us -> 17.7 us
  Pallas kernels: 5.16 us -> 3.52 us
  local copies, waits for them, and re-layouts: 1.64 us -> 2.12 us
    ppermute x11 -> x13, waiting for transfers between devices: 14.1 us -> 7.73 us  [swapped(): lax.ppermute(value, axis, [(source, source ^ step) for source in range(co...]
    ppermute x11 -> x13, starting transfers between devices: 15.4 us -> 17.7 us  [swapped(): lax.ppermute(value, axis, [(source, source ^ step) for source in range(co...]
    pallas_call x1, Pallas kernels: 0.95 us -> 0.05 us  [shards(): pl.pallas_call(functools.partial(group_kernel, rep_size), out_shape=shape...]
    pallas_call x3 -> x4, Pallas kernels: 2.85 us -> 2.11 us  [the longest x2 2.1 us: shards(): pl.pallas_call(functools.partial(apply_kernel, first, half), in_specs=[an...]
    unnamed x12, local copies, waits for them, and re-layouts: 1.63 us -> 2.12 us
  transfers between devices with their start and end apart: 11 -> 13, of which waited for: 9 -> 8; matrix products, arithmetic and copies ran while one was open for 2% -> 2% of each run, Pallas kernels for 5% -> 7%
where the time goes in v4:
time: 32.2 us; the launch traced here: 31.9 us
  starting transfers between devices  17.7 us (55%)
  waiting for transfers between devices  7.73 us (24%)
  Pallas kernels  3.52 us (11%)
  local copies, waits for them, and re-layouts  2.12 us (7%)
  other arithmetic  0.64 us (2%)
    ppermute x13, starting transfers between devices, swapped(): lax.ppermute(value, axis, [(source, source ^ step) for source in range(co...  17.7 us
    ppermute x13, waiting for transfers between devices, swapped(): lax.ppermute(value, axis, [(source, source ^ step) for source in range(co...  7.73 us
    unnamed x12, local copies, waits for them, and re-layouts  2.12 us
    pallas_call x2, Pallas kernels, shards(): pl.pallas_call(functools.partial(apply_kernel, first, half), in_specs=[an...  2.1 us
  transfers between devices with their start and end apart: 13, of which 8 were waited for; matrix products, arithmetic and copies ran while one was open for 2% of the time, Pallas kernels for 7%

profile of v4, /device:TPU:0, one launch (start us, length us, event | category | flops | bytes accessed | tf_op | source)
XLA Modules:
  0.0 31.9 jit_solution(10954199043559735948)
XLA Ops:
  0.0 0.0 copy-start.1
  0.0 4.0 %collective-permute-start.1 = (f32[48,512]{1,0:T(8,128)}, f32[48,512]{1,0:T(8,128)S(1)}, u32[]{:S(2)}, u32[]{:S(2)}) collective-permute-start(f32[48,512]{1,0:T(8,128)} %refs_0_.1), channel_id=1, source_target_pairs={{0,2},{1,3},{2,0},{3,1},{4,6},{5,7},{6,4},{7,5},{8,10},{9,11},{10,... | collective-permute-start | bytes 294920 | tf_op jit(solution)/shard_map/ppermute | solution.py:105
  4.0 1.6 %collective-permute-start = (f32[48,512]{1,0:T(8,128)}, f32[48,512]{1,0:T(8,128)S(1)}, u32[]{:S(2)}, u32[]{:S(2)}) collective-permute-start(f32[48,512]{1,0:T(8,128)} %refs_0_.1), channel_id=1, source_target_pairs={{0,1},{1,0},{2,3},{3,2},{4,5},{5,4},{6,7},{7,6},{8,9},{9,8},{10,11... | collective-permute-start | bytes 294920 | tf_op jit(solution)/shard_map/ppermute | solution.py:105
  5.6 0.0 collective-permute-start.2
  5.6 0.0 copy-start.2
  5.6 0.7 %copy-done.2 = s32[4,8]{1,0:T(4,128)S(1)} copy-done((s32[4,8]{1,0:T(4,128)S(1)}, s32[4,8]{1,0:T(4,128)}, u32[]{:S(2)}) %copy-start.2) | copy-done | bytes 152
  6.3 0.0 copy-start.3
  6.3 0.7 %copy-done.3 = s32[4]{0:T(128)S(1)} copy-done((s32[4]{0:T(128)S(1)}, s32[4]{0:T(128)}, u32[]{:S(2)}) %copy-start.3) | copy-done | bytes 40
  7.0 0.6 %shard_map.46 = f32[8,128]{1,0:T(8,128)S(1)} custom-call(s32[4,8]{1,0:T(4,128)S(1)} %copy-done.2, s32[4]{0:T(128)S(1)} %copy-done.3), custom_call_target="tpu_custom_call" | custom-call | tf_op jit(solution)/shard_map/pallas_call | solution.py:132
  7.6 0.7 %dynamic-slice_dynamic-update-slice_fusion.3 = f32[200,128]{1,0:T(8,128)S(1)} fusion(f32[48,512]{1,0:T(8,128)} %refs_0_.1, s32[]{:T(128)S(6)} %select_n.2), kind=kLoop, calls=%fused_computation.4 | loop fusion | bytes 49156
  8.3 1.2 %collective-permute-done.before_ref.refs_1_ = f32[48,512]{1,0:T(8,128)S(1)} collective-permute-done((f32[48,512]{1,0:T(8,128)}, f32[48,512]{1,0:T(8,128)S(1)}, u32[]{:S(2)}, u32[]{:S(2)}) %collective-permute-start) | collective-permute-done | bytes 98336 | tf_op jit(solution)/shard_map/ppermute | solution.py:105
  9.5 0.0 copy-done.1
  9.5 0.0 copy-start
  9.5 2.4 %collective-permute-start.8 = (f32[128,128]{1,0:T(8,128)S(1)}, f32[128,128]{1,0:T(8,128)S(1)}, u32[]{:S(2)}, u32[]{:S(2)}) collective-permute-start(f32[128,128]{1,0:T(8,128)S(1)} %shard_map.48.refs_7_), channel_id=1, source_target_pairs={{0,1},{1,0},{2,3},{3,2},{4,5},{5,4},{6,7},{7,6},{8,9},{9,8},{10,11... | collective-permute-start | bytes 196616 | tf_op jit(solution)/shard_map/ppermute | solution.py:105
  12.0 0.8 %collective-permute-start.7 = (f32[128,128]{1,0:T(8,128)S(1)}, f32[128,128]{1,0:T(8,128)S(1)}, u32[]{:S(2)}, u32[]{:S(2)}) collective-permute-start(f32[128,128]{1,0:T(8,128)S(1)} %shard_map.48.refs_7_), channel_id=1, source_target_pairs={{0,2},{1,3},{2,0},{3,1},{4,6},{5,7},{6,4},{7,5},{8,10},{9,11},{10,... | collective-permute-start | bytes 196616 | tf_op jit(solution)/shard_map/ppermute | solution.py:105
  12.8 1.6 %collective-permute-start.6 = (f32[128,128]{1,0:T(8,128)S(1)}, f32[128,128]{1,0:T(8,128)S(1)}, u32[]{:S(2)}, u32[]{:S(2)}) collective-permute-start(f32[128,128]{1,0:T(8,128)S(1)} %shard_map.48.refs_7_), channel_id=1, source_target_pairs={{0,3},{1,2},{2,1},{3,0},{4,7},{5,6},{6,5},{7,4},{8,11},{9,10},{10,... | collective-permute-start | bytes 196616 | tf_op jit(solution)/shard_map/ppermute | solution.py:105
  14.4 0.0 collective-permute-done.1.refs_2_
  14.4 0.0 collective-permute-done.2.refs_3_
  14.5 2.5 %collective-permute-start.5 = (f32[200,128]{1,0:T(8,128)S(1)}, f32[200,128]{1,0:T(8,128)S(1)}, u32[]{:S(2)}, u32[]{:S(2)}) collective-permute-start(f32[200,128]{1,0:T(8,128)S(1)} %constant_dynamic-update-slice_fusion.refs_0_), channel_id=1, source_target_pairs={{0,24},{4,28},{8,16},{12,20},{16,8},{20,12},{24,0},{28,4},{1,25},{... | collective-permute-start | bytes 307208 | tf_op jit(solution)/shard_map/ppermute | solution.py:105
  17.0 0.5 %collective-permute-start.4 = (f32[200,128]{1,0:T(8,128)S(1)}, f32[200,128]{1,0:T(8,128)S(1)}, u32[]{:S(2)}, u32[]{:S(2)}) collective-permute-start(f32[200,128]{1,0:T(8,128)S(1)} %constant_dynamic-update-slice_fusion.refs_0_), channel_id=1, source_target_pairs={{0,16},{4,20},{8,24},{12,28},{16,0},{20,4},{24,8},{28,12},{1,17},{... | collective-permute-start | bytes 307208 | tf_op jit(solution)/shard_map/ppermute | solution.py:105
  17.5 0.0 collective-permute-done.8.refs_6_
  17.5 0.5 %collective-permute-start.3 = (f32[200,128]{1,0:T(8,128)S(1)}, f32[200,128]{1,0:T(8,128)S(1)}, u32[]{:S(2)}, u32[]{:S(2)}) collective-permute-start(f32[200,128]{1,0:T(8,128)S(1)} %constant_dynamic-update-slice_fusion.refs_0_), channel_id=1, source_target_pairs={{0,8},{4,12},{8,0},{12,4},{16,24},{20,28},{24,16},{28,20},{1,9},{5... | collective-permute-start | bytes 307208 | tf_op jit(solution)/shard_map/ppermute | solution.py:105
  18.0 0.0 collective-permute-done.7.refs_5_
  18.0 0.9 %collective-permute-done.6.refs_4_ = f32[128,128]{1,0:T(8,128)S(1)} collective-permute-done((f32[128,128]{1,0:T(8,128)S(1)}, f32[128,128]{1,0:T(8,128)S(1)}, u32[]{:S(2)}, u32[]{:S(2)}) %collective-permute-start.6) | collective-permute-done | bytes 65568 | tf_op jit(solution)/shard_map/ppermute | solution.py:105
  19.0 0.0 copy-done
  19.0 0.1 shard_map.49.group_ref
  19.0 0.1 collective-permute-start.9
  19.1 0.3 shard_map.50
  19.4 1.0 %collective-permute-done.5.refs_3_ = f32[200,128]{1,0:T(8,128)S(1)} collective-permute-done((f32[200,128]{1,0:T(8,128)S(1)}, f32[200,128]{1,0:T(8,128)S(1)}, u32[]{:S(2)}, u32[]{:S(2)}) %collective-permute-start.5) | collective-permute-done | bytes 102432 | tf_op jit(solution)/shard_map/ppermute | solution.py:105
  20.4 1.2 %collective-permute-done.4.refs_2_ = f32[200,128]{1,0:T(8,128)S(1)} collective-permute-done((f32[200,128]{1,0:T(8,128)S(1)}, f32[200,128]{1,0:T(8,128)S(1)}, u32[]{:S(2)}, u32[]{:S(2)}) %collective-permute-start.4) | collective-permute-done | bytes 102432 | tf_op jit(solution)/shard_map/ppermute | solution.py:105
  21.6 0.5 %collective-permute-done.3.refs_1_ = f32[200,128]{1,0:T(8,128)S(1)} collective-permute-done((f32[200,128]{1,0:T(8,128)S(1)}, f32[200,128]{1,0:T(8,128)S(1)}, u32[]{:S(2)}, u32[]{:S(2)}) %collective-permute-start.3) | collective-permute-done | bytes 102432 | tf_op jit(solution)/shard_map/ppermute | solution.py:105
  22.1 0.2 shard_map.47
  22.3 0.0 collective-permute-done.9.group_ref
  22.3 0.3 shard_map.51
  22.6 1.1 %shard_map.52 = (f32[128,128]{1,0:T(8,128)S(1)}, f32[128,128]{1,0:T(8,128)S(1)}) custom-call(f32[1,512]{1,0:T(1,128)S(1)} %get-tuple-element.16.before_ref.scale_ref, bf16[576,512]{1,0:T(8,128)(2,1)S(1)} %get-tuple-element.17.row_ref, f32[1,512]{1,0:T(1,128)S(1)} %get-tuple-element.16.before_ref.scale_ref, f32[8,512]{1,0:T(8,128)S(1)} %get-tuple-element.18.mask_ref, ...), custom_call_target="tpu_custom_call" | custom-call | tf_op jit(solution)/shard_map/pallas_call | solution.py:174
  23.7 1.6 %collective-permute-start.12 = (f32[128,128]{1,0:T(8,128)S(1)}, f32[128,128]{1,0:T(8,128)S(1)}, u32[]{:S(2)}, u32[]{:S(2)}) collective-permute-start(f32[128,128]{1,0:T(8,128)S(1)} %get-tuple-element.26), channel_id=1, source_target_pairs={{0,24},{4,28},{8,16},{12,20},{16,8},{20,12},{24,0},{28,4},{1,25},{... | collective-permute-start | bytes 196616 | tf_op jit(solution)/shard_map/ppermute | solution.py:105
  25.2 0.6 %collective-permute-start.11 = (f32[128,128]{1,0:T(8,128)S(1)}, f32[128,128]{1,0:T(8,128)S(1)}, u32[]{:S(2)}, u32[]{:S(2)}) collective-permute-start(f32[128,128]{1,0:T(8,128)S(1)} %get-tuple-element.23.before_ref), channel_id=1, source_target_pairs={{0,16},{4,20},{8,24},{12,28},{16,0},{20,4},{24,8},{28,12},{1,17},{... | collective-permute-start | bytes 196616 | tf_op jit(solution)/shard_map/ppermute | solution.py:105
  25.9 1.0 %shard_map.53 = (f32[128,128]{1,0:T(8,128)S(1)}, f32[128,128]{1,0:T(8,128)S(1)}) custom-call(f32[128,128]{1,0:T(8,128)S(1)} %get-tuple-element.23.before_ref, bf16[576,512]{1,0:T(8,128)(2,1)S(1)} %get-tuple-element.17.row_ref, f32[1,512]{1,0:T(1,128)S(1)} %get-tuple-element.16.before_ref.scale_ref, f32[8,512]{1,0:T(8,128)S(1)} %get-tuple-element.18.mask_ref, ...), custom_call_target="tpu_custom_call" | custom-call | tf_op jit(solution)/shard_map/pallas_call | solution.py:174
  26.9 1.5 %collective-permute-start.10 = (f32[128,128]{1,0:T(8,128)S(1)}, f32[128,128]{1,0:T(8,128)S(1)}, u32[]{:S(2)}, u32[]{:S(2)}) collective-permute-start(f32[128,128]{1,0:T(8,128)S(1)} %get-tuple-element.25), channel_id=1, source_target_pairs={{0,8},{4,12},{8,0},{12,4},{16,24},{20,28},{24,16},{28,20},{1,9},{5... | collective-permute-start | bytes 196616 | tf_op jit(solution)/shard_map/ppermute | solution.py:105
  28.4 0.6 %collective-permute-done.12.refs_1_ = f32[128,128]{1,0:T(8,128)S(1)} collective-permute-done((f32[128,128]{1,0:T(8,128)S(1)}, f32[128,128]{1,0:T(8,128)S(1)}, u32[]{:S(2)}, u32[]{:S(2)}) %collective-permute-start.12) | collective-permute-done | bytes 65568 | tf_op jit(solution)/shard_map/ppermute | solution.py:105
  28.9 0.7 %collective-permute-done.11.refs_0_ = f32[128,128]{1,0:T(8,128)S(1)} collective-permute-done((f32[128,128]{1,0:T(8,128)S(1)}, f32[128,128]{1,0:T(8,128)S(1)}, u32[]{:S(2)}, u32[]{:S(2)}) %collective-permute-start.11) | collective-permute-done | bytes 65568 | tf_op jit(solution)/shard_map/ppermute | solution.py:105
  29.6 1.6 %collective-permute-done.10 = f32[128,128]{1,0:T(8,128)S(1)} collective-permute-done((f32[128,128]{1,0:T(8,128)S(1)}, f32[128,128]{1,0:T(8,128)S(1)}, u32[]{:S(2)}, u32[]{:S(2)}) %collective-permute-start.10) | collective-permute-done | bytes 65568 | tf_op jit(solution)/shard_map/ppermute | solution.py:105
  31.2 0.6 %add_add_fusion = f32[128,128]{1,0:T(8,128)} fusion(f32[128,128]{1,0:T(8,128)S(1)} %shard_map.54, f32[128,128]{1,0:T(8,128)S(1)} %get-tuple-element.24, f32[128,128]{1,0:T(8,128)S(1)} %collective-permute-done.10), kind=kLoop, calls=%fused_computation | loop fusion | flops 32768 | bytes 262144 | tf_op jit(solution)/shard_map/add | solution.py:194
  (6 shorter events, 0.0 us)
Async XLA Ops:
  0.0 9.5 %copy-start.1 = (f32[128,128]{1,0:T(8,128)S(1)}, f32[128,128]{1,0:T(8,128)}, u32[]{:S(2)}) copy-start(f32[128,128]{1,0:T(8,128)} %in_ref.1) | copy-start | bytes 196612
  0.0 14.4 %collective-permute-start.1 = (f32[48,512]{1,0:T(8,128)}, f32[48,512]{1,0:T(8,128)S(1)}, u32[]{:S(2)}, u32[]{:S(2)}) collective-permute-start(f32[48,512]{1,0:T(8,128)} %refs_0_.1), channel_id=1, source_target_pairs={{0,2},{1,3},{2,0},{3,1},{4,6},{5,7},{6,4},{7,5},{8,10},{9,11},{10,... | collective-permute-start | bytes 294920 | tf_op jit(solution)/shard_map/ppermute | solution.py:105
  4.0 5.4 %collective-permute-start = (f32[48,512]{1,0:T(8,128)}, f32[48,512]{1,0:T(8,128)S(1)}, u32[]{:S(2)}, u32[]{:S(2)}) collective-permute-start(f32[48,512]{1,0:T(8,128)} %refs_0_.1), channel_id=1, source_target_pairs={{0,1},{1,0},{2,3},{3,2},{4,5},{5,4},{6,7},{7,6},{8,9},{9,8},{10,11... | collective-permute-start | bytes 294920 | tf_op jit(solution)/shard_map/ppermute | solution.py:105
  5.6 8.8 %collective-permute-start.2 = (f32[48,512]{1,0:T(8,128)}, f32[48,512]{1,0:T(8,128)S(1)}, u32[]{:S(2)}, u32[]{:S(2)}) collective-permute-start(f32[48,512]{1,0:T(8,128)} %refs_0_.1), channel_id=1, source_target_pairs={{0,3},{1,2},{2,1},{3,0},{4,7},{5,6},{6,5},{7,4},{8,11},{9,10},{10,... | collective-permute-start | bytes 294920 | tf_op jit(solution)/shard_map/ppermute | solution.py:105
  5.6 0.7 %copy-start.2 = (s32[4,8]{1,0:T(4,128)S(1)}, s32[4,8]{1,0:T(4,128)}, u32[]{:S(2)}) copy-start(s32[4,8]{1,0:T(4,128)} %list_ref.1) | copy-start | bytes 388
  6.3 0.7 %copy-start.3 = (s32[4]{0:T(128)S(1)}, s32[4]{0:T(128)}, u32[]{:S(2)}) copy-start(s32[4]{0:T(128)} %count_ref.1) | copy-start | bytes 52
  9.5 9.5 %copy-start = (f32[48,512]{1,0:T(8,128)S(1)}, f32[48,512]{1,0:T(8,128)}, u32[]{:S(2)}) copy-start(f32[48,512]{1,0:T(8,128)} %refs_0_.1) | copy-start | bytes 294916
  9.5 8.0 %collective-permute-start.8 = (f32[128,128]{1,0:T(8,128)S(1)}, f32[128,128]{1,0:T(8,128)S(1)}, u32[]{:S(2)}, u32[]{:S(2)}) collective-permute-start(f32[128,128]{1,0:T(8,128)S(1)} %shard_map.48.refs_7_), channel_id=1, source_target_pairs={{0,1},{1,0},{2,3},{3,2},{4,5},{5,4},{6,7},{7,6},{8,9},{9,8},{10,11... | collective-permute-start | bytes 196616 | tf_op jit(solution)/shard_map/ppermute | solution.py:105
  12.0 6.1 %collective-permute-start.7 = (f32[128,128]{1,0:T(8,128)S(1)}, f32[128,128]{1,0:T(8,128)S(1)}, u32[]{:S(2)}, u32[]{:S(2)}) collective-permute-start(f32[128,128]{1,0:T(8,128)S(1)} %shard_map.48.refs_7_), channel_id=1, source_target_pairs={{0,2},{1,3},{2,0},{3,1},{4,6},{5,7},{6,4},{7,5},{8,10},{9,11},{10,... | collective-permute-start | bytes 196616 | tf_op jit(solution)/shard_map/ppermute | solution.py:105
  12.8 6.2 %collective-permute-start.6 = (f32[128,128]{1,0:T(8,128)S(1)}, f32[128,128]{1,0:T(8,128)S(1)}, u32[]{:S(2)}, u32[]{:S(2)}) collective-permute-start(f32[128,128]{1,0:T(8,128)S(1)} %shard_map.48.refs_7_), channel_id=1, source_target_pairs={{0,3},{1,2},{2,1},{3,0},{4,7},{5,6},{6,5},{7,4},{8,11},{9,10},{10,... | collective-permute-start | bytes 196616 | tf_op jit(solution)/shard_map/ppermute | solution.py:105
  14.5 6.0 %collective-permute-start.5 = (f32[200,128]{1,0:T(8,128)S(1)}, f32[200,128]{1,0:T(8,128)S(1)}, u32[]{:S(2)}, u32[]{:S(2)}) collective-permute-start(f32[200,128]{1,0:T(8,128)S(1)} %constant_dynamic-update-slice_fusion.refs_0_), channel_id=1, source_target_pairs={{0,24},{4,28},{8,16},{12,20},{16,8},{20,12},{24,0},{28,4},{1,25},{... | collective-permute-start | bytes 307208 | tf_op jit(solution)/shard_map/ppermute | solution.py:105
  17.0 4.7 %collective-permute-start.4 = (f32[200,128]{1,0:T(8,128)S(1)}, f32[200,128]{1,0:T(8,128)S(1)}, u32[]{:S(2)}, u32[]{:S(2)}) collective-permute-start(f32[200,128]{1,0:T(8,128)S(1)} %constant_dynamic-update-slice_fusion.refs_0_), channel_id=1, source_target_pairs={{0,16},{4,20},{8,24},{12,28},{16,0},{20,4},{24,8},{28,12},{1,17},{... | collective-permute-start | bytes 307208 | tf_op jit(solution)/shard_map/ppermute | solution.py:105
  17.5 4.7 %collective-permute-start.3 = (f32[200,128]{1,0:T(8,128)S(1)}, f32[200,128]{1,0:T(8,128)S(1)}, u32[]{:S(2)}, u32[]{:S(2)}) collective-permute-start(f32[200,128]{1,0:T(8,128)S(1)} %constant_dynamic-update-slice_fusion.refs_0_), channel_id=1, source_target_pairs={{0,8},{4,12},{8,0},{12,4},{16,24},{20,28},{24,16},{28,20},{1,9},{5... | collective-permute-start | bytes 307208 | tf_op jit(solution)/shard_map/ppermute | solution.py:105
  19.0 3.3 %collective-permute-start.9 = (f32[320,512]{1,0:T(8,128)S(1)}, f32[320,512]{1,0:T(8,128)S(1)}, u32[]{:S(2)}, u32[]{:S(2)}) collective-permute-start(f32[320,512]{1,0:T(8,128)S(1)} %shard_map.49.group_ref), channel_id=1, source_target_pairs={{0,4},{4,0},{8,12},{12,8},{16,20},{20,16},{24,28},{28,24},{1,5},{5... | collective-permute-start | bytes 1966088 | tf_op jit(solution)/shard_map/ppermute | solution.py:105
  23.7 5.2 %collective-permute-start.12 = (f32[128,128]{1,0:T(8,128)S(1)}, f32[128,128]{1,0:T(8,128)S(1)}, u32[]{:S(2)}, u32[]{:S(2)}) collective-permute-start(f32[128,128]{1,0:T(8,128)S(1)} %get-tuple-element.26), channel_id=1, source_target_pairs={{0,24},{4,28},{8,16},{12,20},{16,8},{20,12},{24,0},{28,4},{1,25},{... | collective-permute-start | bytes 196616 | tf_op jit(solution)/shard_map/ppermute | solution.py:105
  25.2 4.4 %collective-permute-start.11 = (f32[128,128]{1,0:T(8,128)S(1)}, f32[128,128]{1,0:T(8,128)S(1)}, u32[]{:S(2)}, u32[]{:S(2)}) collective-permute-start(f32[128,128]{1,0:T(8,128)S(1)} %get-tuple-element.23.before_ref), channel_id=1, source_target_pairs={{0,16},{4,20},{8,24},{12,28},{16,0},{20,4},{24,8},{28,12},{1,17},{... | collective-permute-start | bytes 196616 | tf_op jit(solution)/shard_map/ppermute | solution.py:105
  26.9 4.3 %collective-permute-start.10 = (f32[128,128]{1,0:T(8,128)S(1)}, f32[128,128]{1,0:T(8,128)S(1)}, u32[]{:S(2)}, u32[]{:S(2)}) collective-permute-start(f32[128,128]{1,0:T(8,128)S(1)} %get-tuple-element.25), channel_id=1, source_target_pairs={{0,8},{4,12},{8,0},{12,4},{16,24},{20,28},{24,16},{28,20},{1,9},{5... | collective-permute-start | bytes 196616 | tf_op jit(solution)/shard_map/ppermute | solution.py:105

commit v5 on v4

v5 whole, which is shorter than its diff:
```python
import functools

import jax
import jax.numpy as jnp
from jax import lax
from jax.experimental import pallas as pl
from jax.experimental.pallas import tpu as pltpu
from jax.sharding import PartitionSpec as P


ROWS_FLOPS = 350 * 10**7
VECTORS_FLOPS = 200 * 10**7
ADD_FLOPS = 620 * 10**7


def halves(value):
    high = value.astype(jnp.bfloat16)
    return high, (value - high.astype(jnp.float32)).astype(jnp.bfloat16)


def stacked(value, order, axis):
    high, low = halves(value)
    return jnp.concatenate([{"h": high, "l": low}[letter] for letter in order], axis=axis)


def lists_kernel(list_ref, count_ref, out_ref):
    rank = lax.axis_index("rep")
    for slot in range(out_ref.shape[0]):
        listed = jnp.where(slot < count_ref[rank], list_ref[rank, slot], -1)
        out_ref[slot : slot + 1, :] = jnp.full((1, out_ref.shape[1]), listed.astype(jnp.float32))


def below_kernel(before_ref, *refs):
    start = 0
    for ref in refs[:-1]:
        refs[-1][start : start + ref.shape[0], :] = ref[...]
        start += ref.shape[0]


def columns_kernel(order, before_ref, *refs):
    piece_refs, (col_ref, bias_ref) = refs[:-2], refs[-2:]
    width = bias_ref.shape[1]
    rank = lax.axis_index("rep")
    for place, spot in enumerate(order):
        here = pl.ds(pl.multiple_of((rank ^ spot) * width, width), width)
        cols = jnp.concatenate([ref[:, here] for ref in piece_refs], axis=0).T
        there = slice(place * width, (place + 1) * width)
        bias = jnp.sum(cols * cols, axis=1, keepdims=True) * (-1.0 / cols.shape[1])
        bias_ref[there, :] = jnp.broadcast_to(bias, (width, width))
        col_ref[there, :] = stacked(cols, "hhl", 1)


def vectors_kernel(before_ref, own_ref, sibling_ref, out_ref):
    eig_count, width = out_ref.shape[0], own_ref.shape[1]
    place = 0
    for ref in (own_ref, sibling_ref):
        blocks = [ref[top : top + eig_count, :] for top in range(0, ref.shape[0], eig_count)]
        for pair in range(len(blocks) // 2):
            vecs = jnp.concatenate(blocks[2 * pair : 2 * pair + 2], axis=1)
            out_ref[:, place : place + 6 * width] = stacked(vecs, "hhl", 1)
            place += 6 * width


def rows_kernel(feat_count, *refs):
    panel_refs, (row_ref, scale_ref, mask_ref) = refs[:-3], refs[-3:]
    width = panel_refs[0].shape[1]
    group_blocks = mask_ref.shape[0] // 2
    blk_index, rank = lax.axis_index("blk"), lax.axis_index("rep")
    for place, ref in enumerate(panel_refs):
        span = slice(place * width, (place + 1) * width)
        rows = ref[:feat_count, :]
        scale_ref[:, span] = jnp.exp(jnp.sum(rows * rows, axis=0, keepdims=True) * (-1.0 / feat_count))
        row_ref[:, span] = stacked(rows * (2.0 / feat_count), "hlh", 0)
        lists = ref[feat_count:, :]
        for spot in range(2 * group_blocks):
            column = (blk_index ^ (spot // group_blocks)) * group_blocks + (rank ^ (spot % group_blocks))
            hits = jnp.where(lists == column.astype(jnp.float32), 1.0, 0.0)
            mask_ref[spot : spot + 1, span] = jnp.max(hits, axis=0, keepdims=True)


def apply_kernel(before_ref, row_ref, scale_ref, mask_ref, *refs):
    own_cols, own_bias, sibling_cols, sibling_bias, vec_ref, *out_refs = refs
    width = out_refs[0].shape[1]
    group_cols = own_cols.shape[0]
    chunk = 2 * width
    rows = row_ref[...]
    total = None
    for group, (col_ref, bias_ref) in enumerate(((own_cols, own_bias), (sibling_cols, sibling_bias))):
        for start in range(0, group_cols, chunk):
            inner = jnp.dot(col_ref[start : start + chunk, :], rows, preferred_element_type=jnp.float32)
            bias = jnp.concatenate([bias_ref[start : start + chunk, :]] * len(out_refs), axis=1)
            at = (group * group_cols + start) // width
            both = [jnp.broadcast_to(mask_ref[spot : spot + 1, :], (width, rows.shape[1])) for spot in (at, at + 1)]
            weight = stacked(jnp.exp(inner + bias) * jnp.concatenate(both, axis=0), "hlh", 0)
            there = 3 * (group * group_cols + start)
            added = jnp.dot(vec_ref[:, there : there + 3 * chunk], weight, preferred_element_type=jnp.float32)
            total = added if total is None else total + added
    total = total * scale_ref[...]
    for spot, out_ref in enumerate(out_refs):
        out_ref[...] = total[:, spot * width : (spot + 1) * width]


def add_kernel(*refs):
    total = refs[0][...]
    for ref in refs[1:-1]:
        total = total + ref[...]
    refs[-1][...] = total


def swapped(value, axis, step):
    count = lax.axis_size(axis)
    return lax.ppermute(value, axis, [(source, source ^ step) for source in range(count)])


def shards(coords, eigvecs, nbr_list, nbr_count):
    cycle_size = lax.axis_size("blk")
    rep_size = lax.axis_size("rep")
    rep_index = lax.axis_index("rep")
    group_blocks, slot_count = nbr_list.shape
    eig_count, width = eigvecs.shape
    piece_feats, group_cols = coords.shape
    feat_count = rep_size * piece_feats
    f32, bf16 = jnp.float32, jnp.bfloat16
    shape = jax.ShapeDtypeStruct
    smem = pl.BlockSpec(memory_space=pltpu.SMEM)
    vmem = pl.BlockSpec(memory_space=pltpu.VMEM)
    anywhere = pl.BlockSpec(memory_space=pl.ANY)
    params = pltpu.CompilerParams(vmem_limit_bytes=(8 + group_blocks) * 1024 * 1024)

    def hint(flops):
        return pl.CostEstimate(flops=flops, bytes_accessed=1024 * 1024, transcendentals=0)

    def block_of(piece, block):
        return lax.dynamic_slice_in_dim(piece, block * width, width, 1)

    pieces = [coords] + [swapped(coords, "rep", step) for step in range(1, rep_size)]
    own_block = [block_of(piece, rep_index) for piece in pieces]

    def below(before, values, **estimate):
        return pl.pallas_call(
            below_kernel,
            in_specs=[anywhere] + [vmem] * len(values),
            out_shape=shape((sum(value.shape[0] for value in values), values[0].shape[1]), f32),
            compiler_params=params,
            **estimate,
        )(before, *values)

    late_vecs = below(pieces[1], [eigvecs])
    far_vecs = [swapped(late_vecs, "rep", step) for step in range(1, rep_size)]
    vecs = below(pieces[1], [late_vecs, *far_vecs], cost_estimate=hint(VECTORS_FLOPS))
    order = list(range(rep_size))

    lists = pl.pallas_call(
        lists_kernel,
        in_specs=[smem, smem],
        out_shape=shape((slot_count, width), f32),
        compiler_params=params,
    )(nbr_list, nbr_count)
    panel = jnp.concatenate([*own_block, lists], axis=0)
    steps = list(range(0, cycle_size, 2))
    panels = [panel] + [swapped(panel, "blk", step) for step in steps[1:]]

    def columns_of(before, group_pieces):
        return pl.pallas_call(
            functools.partial(columns_kernel, order),
            in_specs=[anywhere] + [vmem] * len(group_pieces),
            out_shape=[shape((group_cols, 3 * feat_count), bf16), shape((group_cols, width), f32)],
            compiler_params=params,
        )(before, *group_pieces)

    sibling_cols = swapped(below(far_vecs[0], pieces), "blk", 1)
    sibling_vecs = swapped(vecs, "blk", 1)
    columns = [*columns_of(far_vecs[0], pieces), *columns_of(far_vecs[0], [sibling_cols])]

    half = len(steps) // 2
    rows = {}
    for first in (half, 0):
        rows[first] = pl.pallas_call(
            functools.partial(rows_kernel, feat_count),
            out_shape=[
                shape((3 * feat_count, half * width), bf16),
                shape((1, half * width), f32),
                shape((2 * group_blocks, half * width), f32),
            ],
            compiler_params=params,
            **(dict(cost_estimate=hint(ROWS_FLOPS)) if first else {}),
        )(*panels[first : first + half])
    vectors = pl.pallas_call(
        vectors_kernel,
        in_specs=[anywhere] + [vmem] * 2,
        out_shape=shape((eig_count, 6 * group_cols), bf16),
        compiler_params=params,
    )(columns[3], vecs, sibling_vecs)
    tiles = {}
    before = rows[half][1]
    for first in (half, 0):
        done = pl.pallas_call(
            apply_kernel,
            in_specs=[anywhere] + [vmem] * 8,
            out_shape=[shape((eig_count, width), f32)] * half,
            compiler_params=params,
        )(before, *rows[first], *columns, vectors)
        before = done[0]
        for spot in range(half):
            tiles[first + spot] = done[spot]

    arrived = [swapped(tiles[place], "blk", steps[place]) for place in range(1, len(steps))]
    far = pl.pallas_call(
        add_kernel,
        out_shape=shape((eig_count, width), f32),
        compiler_params=params,
        cost_estimate=hint(ADD_FLOPS),
    )(*arrived[half - 1 :])
    total = tiles[0]
    for tile in arrived[: half - 1]:
        total = total + tile
    return total + far


def solution(mesh):
    return jax.shard_map(
        shards,
        mesh=mesh,
        in_specs=(P("rep", "blk"), P(None, ("blk", "rep")), P("blk", None), P("blk")),
        out_specs=P(None, ("blk", "rep")),
        check_vma=False,
    )
```

time: 32.2 us -> 34.4 us (1.068)
  the two profiles are of different devices: /device:TPU:0 before, /device:TPU:16 now
where the time goes in v5:
time: 34.4 us; the launch traced here: 34.2 us
  starting transfers between devices  15.3 us (44%)
  waiting for transfers between devices  12.1 us (35%)
  Pallas kernels  3.9 us (11%)
  local copies, waits for them, and re-layouts  2.11 us (6%)
  other arithmetic  0.64 us (2%)
    ppermute x14, starting transfers between devices, swapped(): lax.ppermute(value, axis, [(source, source ^ step) for source in range(co...  15.3 us
    ppermute x14, waiting for transfers between devices, swapped(): lax.ppermute(value, axis, [(source, source ^ step) for source in range(co...  12.1 us
    pallas_call x2, Pallas kernels, shards(): pl.pallas_call(apply_kernel, in_specs=[anywhere] + [vmem] * 8, out_shape=...  2.11 us
    unnamed x12, local copies, waits for them, and re-layouts  2.11 us
    pallas_call x2, Pallas kernels, columns_of(): pl.pallas_call(functools.partial(columns_kernel, order), in_specs=[anywhe...  0.88 us
  transfers between devices with their start and end apart: 14, of which 4 were waited for; matrix products, arithmetic and copies ran while one was open for 2% of the time, Pallas kernels for 11%

profile of v5, /device:TPU:16, one launch (start us, length us, event | category | flops | bytes accessed | tf_op | source)
XLA Modules:
  0.0 34.2 jit_solution(1082369351305669497)
XLA Ops:
  0.0 0.0 copy-start.1
  0.0 1.6 %collective-permute-start = (f32[48,512]{1,0:T(8,128)}, f32[48,512]{1,0:T(8,128)S(1)}, u32[]{:S(2)}, u32[]{:S(2)}) collective-permute-start(f32[48,512]{1,0:T(8,128)} %refs_0_.5), channel_id=1, source_target_pairs={{0,1},{1,0},{2,3},{3,2},{4,5},{5,4},{6,7},{7,6},{8,9},{9,8},{10,11... | collective-permute-start | bytes 294920 | tf_op jit(solution)/shard_map/ppermute | solution.py:112
  1.6 0.3 collective-permute-start.1
  1.9 1.6 %collective-permute-start.2 = (f32[48,512]{1,0:T(8,128)}, f32[48,512]{1,0:T(8,128)S(1)}, u32[]{:S(2)}, u32[]{:S(2)}) collective-permute-start(f32[48,512]{1,0:T(8,128)} %refs_0_.5), channel_id=1, source_target_pairs={{0,3},{1,2},{2,1},{3,0},{4,7},{5,6},{6,5},{7,4},{8,11},{9,10},{10,... | collective-permute-start | bytes 294920 | tf_op jit(solution)/shard_map/ppermute | solution.py:112
  3.5 0.0 copy-start.2
  3.5 0.7 %copy-done.2 = s32[4,8]{1,0:T(4,128)S(1)} copy-done((s32[4,8]{1,0:T(4,128)S(1)}, s32[4,8]{1,0:T(4,128)}, u32[]{:S(2)}) %copy-start.2) | copy-done | bytes 152
  4.2 0.0 copy-start.3
  4.2 0.7 %copy-done.3 = s32[4]{0:T(128)S(1)} copy-done((s32[4]{0:T(128)S(1)}, s32[4]{0:T(128)}, u32[]{:S(2)}) %copy-start.3) | copy-done | bytes 40
  4.8 0.6 %shard_map.46 = f32[8,128]{1,0:T(8,128)S(1)} custom-call(s32[4,8]{1,0:T(4,128)S(1)} %copy-done.2, s32[4]{0:T(128)S(1)} %copy-done.3), custom_call_target="tpu_custom_call" | custom-call | tf_op jit(solution)/shard_map/pallas_call | solution.py:153
  5.4 0.7 %dynamic-slice_dynamic-update-slice_fusion.3 = f32[200,128]{1,0:T(8,128)S(1)} fusion(f32[48,512]{1,0:T(8,128)} %refs_0_.5, s32[]{:T(128)S(6)} %select_n.2), kind=kLoop, calls=%fused_computation.4 | loop fusion | bytes 49156
  6.2 0.0 collective-permute-done.before_ref.refs_1_
  6.2 0.0 copy-done.1
  6.2 0.0 copy-start
  6.2 2.5 %collective-permute-start.5 = (f32[128,128]{1,0:T(8,128)S(1)}, f32[128,128]{1,0:T(8,128)S(1)}, u32[]{:S(2)}, u32[]{:S(2)}) collective-permute-start(f32[128,128]{1,0:T(8,128)S(1)} %shard_map.48.refs_0_), channel_id=1, source_target_pairs={{0,1},{1,0},{2,3},{3,2},{4,5},{5,4},{6,7},{7,6},{8,9},{9,8},{10,11... | collective-permute-start | bytes 196616 | tf_op jit(solution)/shard_map/ppermute | solution.py:112
  8.7 0.0 collective-permute-start.7
  8.7 1.5 %collective-permute-start.8 = (f32[128,128]{1,0:T(8,128)S(1)}, f32[128,128]{1,0:T(8,128)S(1)}, u32[]{:S(2)}, u32[]{:S(2)}) collective-permute-start(f32[128,128]{1,0:T(8,128)S(1)} %shard_map.48.refs_0_), channel_id=1, source_target_pairs={{0,3},{1,2},{2,1},{3,0},{4,7},{5,6},{6,5},{7,4},{8,11},{9,10},{10,... | collective-permute-start | bytes 196616 | tf_op jit(solution)/shard_map/ppermute | solution.py:112
  10.3 0.0 collective-permute-done.1.refs_2_
  10.3 5.9 %collective-permute-done.2.refs_3_ = f32[48,512]{1,0:T(8,128)S(1)} collective-permute-done((f32[48,512]{1,0:T(8,128)}, f32[48,512]{1,0:T(8,128)S(1)}, u32[]{:S(2)}, u32[]{:S(2)}) %collective-permute-start.2) | collective-permute-done | bytes 98336 | tf_op jit(solution)/shard_map/ppermute | solution.py:112
  16.2 1.5 %collective-permute-start.3 = (f32[200,128]{1,0:T(8,128)S(1)}, f32[200,128]{1,0:T(8,128)S(1)}, u32[]{:S(2)}, u32[]{:S(2)}) collective-permute-start(f32[200,128]{1,0:T(8,128)S(1)} %constant_dynamic-update-slice_fusion.refs_0_), channel_id=1, source_target_pairs={{0,16},{4,20},{8,24},{12,28},{16,0},{20,4},{24,8},{28,12},{1,17},{... | collective-permute-start | bytes 307208 | tf_op jit(solution)/shard_map/ppermute | solution.py:112
  17.8 1.4 %collective-permute-start.4 = (f32[200,128]{1,0:T(8,128)S(1)}, f32[200,128]{1,0:T(8,128)S(1)}, u32[]{:S(2)}, u32[]{:S(2)}) collective-permute-start(f32[200,128]{1,0:T(8,128)S(1)} %constant_dynamic-update-slice_fusion.refs_0_), channel_id=1, source_target_pairs={{0,24},{4,28},{8,16},{12,20},{16,8},{20,12},{24,0},{28,4},{1,25},{... | collective-permute-start | bytes 307208 | tf_op jit(solution)/shard_map/ppermute | solution.py:112
  19.2 0.0 collective-permute-done.5.before_ref.refs_1_
  19.2 0.5 %collective-permute-start.10 = (f32[200,128]{1,0:T(8,128)S(1)}, f32[200,128]{1,0:T(8,128)S(1)}, u32[]{:S(2)}, u32[]{:S(2)}) collective-permute-start(f32[200,128]{1,0:T(8,128)S(1)} %constant_dynamic-update-slice_fusion.refs_0_), channel_id=1, source_target_pairs={{0,8},{4,12},{8,0},{12,4},{16,24},{20,28},{24,16},{28,20},{1,9},{5... | collective-permute-start | bytes 307208 | tf_op jit(solution)/shard_map/ppermute | solution.py:112
  19.7 0.0 copy-done
  19.8 0.0 collective-permute-done.7.refs_2_
  19.8 0.1 collective-permute-start.6
  19.8 0.0 collective-permute-done.8.refs_3_
  19.9 0.5 %collective-permute-start.9 = (f32[512,128]{1,0:T(8,128)S(1)}, f32[512,128]{1,0:T(8,128)S(1)}, u32[]{:S(2)}, u32[]{:S(2)}) collective-permute-start(f32[512,128]{1,0:T(8,128)S(1)} %shard_map.52.own_ref), channel_id=1, source_target_pairs={{0,4},{4,0},{8,12},{12,8},{16,20},{20,16},{24,28},{28,24},{1,5},{5... | collective-permute-start | bytes 786440 | tf_op jit(solution)/shard_map/ppermute | solution.py:112
  20.4 0.4 %shard_map.49 = (bf16[512,576]{1,0:T(8,128)(2,1)S(1)}, f32[512,128]{1,0:T(8,128)S(1)}) custom-call(f32[128,128]{1,0:T(8,128)S(1)} %collective-permute-done.5.before_ref.refs_1_, f32[48,512]{1,0:T(8,128)S(1)} %copy-done, f32[48,512]{1,0:T(8,128)S(1)} %collective-permute-done.before_ref.refs_1_, f32[48,512]{1,0:T(8,128)S(1)} %collective-permute-done.1.refs_2_, ...), custom_call_target="tpu_custom_call" | custom-call | tf_op jit(solution)/shard_map/pallas_call | solution.py:164
  20.9 0.0 collective-permute-done.3.refs_0_
  20.9 2.4 %collective-permute-done.4.refs_1_ = f32[200,128]{1,0:T(8,128)S(1)} collective-permute-done((f32[200,128]{1,0:T(8,128)S(1)}, f32[200,128]{1,0:T(8,128)S(1)}, u32[]{:S(2)}, u32[]{:S(2)}) %collective-permute-start.4) | collective-permute-done | bytes 102432 | tf_op jit(solution)/shard_map/ppermute | solution.py:112
  23.3 0.1 shard_map.47
  23.4 0.0 collective-permute-done.6.refs_0_
  23.4 0.4 %shard_map.51 = (bf16[512,576]{1,0:T(8,128)(2,1)S(1)}, f32[512,128]{1,0:T(8,128)S(1)}) custom-call(f32[128,128]{1,0:T(8,128)S(1)} %collective-permute-done.5.before_ref.refs_1_, f32[192,512]{1,0:T(8,128)S(1)} %collective-permute-done.6.refs_0_), custom_call_target="tpu_custom_call" | custom-call | tf_op jit(solution)/shard_map/pallas_call | solution.py:164
  23.9 0.0 collective-permute-done.9.sibling_ref
  23.9 0.1 shard_map.53.refs_4_
  24.0 1.0 %shard_map.54 = (f32[128,128]{1,0:T(8,128)S(1)}, f32[128,128]{1,0:T(8,128)S(1)}) custom-call(f32[1,256]{1,0:T(1,128)S(1)} %get-tuple-element.19.before_ref.scale_ref, bf16[576,256]{1,0:T(8,128)(2,1)S(1)} %get-tuple-element.20.row_ref, f32[1,256]{1,0:T(1,128)S(1)} %get-tuple-element.19.before_ref.scale_ref, f32[8,256]{1,0:T(8,128)S(1)} %get-tuple-element.21.mask_ref, ...), custom_call_target="tpu_custom_call" | custom-call | tf_op jit(solution)/shard_map/pallas_call | solution.py:197
  25.0 0.6 %collective-permute-start.12 = (f32[128,128]{1,0:T(8,128)S(1)}, f32[128,128]{1,0:T(8,128)S(1)}, u32[]{:S(2)}, u32[]{:S(2)}) collective-permute-start(f32[128,128]{1,0:T(8,128)S(1)} %get-tuple-element.26.before_ref), channel_id=1, source_target_pairs={{0,16},{4,20},{8,24},{12,28},{16,0},{20,4},{24,8},{28,12},{1,17},{... | collective-permute-start | bytes 196616 | tf_op jit(solution)/shard_map/ppermute | solution.py:112
  25.6 2.4 %collective-permute-start.13 = (f32[128,128]{1,0:T(8,128)S(1)}, f32[128,128]{1,0:T(8,128)S(1)}, u32[]{:S(2)}, u32[]{:S(2)}) collective-permute-start(f32[128,128]{1,0:T(8,128)S(1)} %get-tuple-element.32), channel_id=1, source_target_pairs={{0,24},{4,28},{8,16},{12,20},{16,8},{20,12},{24,0},{28,4},{1,25},{... | collective-permute-start | bytes 196616 | tf_op jit(solution)/shard_map/ppermute | solution.py:112
  28.0 0.0 collective-permute-done.10.refs_1_
  28.0 0.1 shard_map.55
  28.1 1.1 %shard_map.56 = (f32[128,128]{1,0:T(8,128)S(1)}, f32[128,128]{1,0:T(8,128)S(1)}) custom-call(f32[128,128]{1,0:T(8,128)S(1)} %get-tuple-element.26.before_ref, bf16[576,256]{1,0:T(8,128)(2,1)S(1)} %get-tuple-element.27.row_ref, f32[1,256]{1,0:T(1,128)S(1)} %get-tuple-element.28.scale_ref, f32[8,256]{1,0:T(8,128)S(1)} %get-tuple-element.29.mask_ref, ...), custom_call_target="tpu_custom_call" | custom-call | tf_op jit(solution)/shard_map/pallas_call | solution.py:197
  29.2 0.6 %collective-permute-start.11 = (f32[128,128]{1,0:T(8,128)S(1)}, f32[128,128]{1,0:T(8,128)S(1)}, u32[]{:S(2)}, u32[]{:S(2)}) collective-permute-start(f32[128,128]{1,0:T(8,128)S(1)} %get-tuple-element.31), channel_id=1, source_target_pairs={{0,8},{4,12},{8,0},{12,4},{16,24},{20,28},{24,16},{28,20},{1,9},{5... | collective-permute-start | bytes 196616 | tf_op jit(solution)/shard_map/ppermute | solution.py:112
  29.8 0.0 collective-permute-done.12.refs_0_
  29.8 1.2 %collective-permute-done.13.refs_1_ = f32[128,128]{1,0:T(8,128)S(1)} collective-permute-done((f32[128,128]{1,0:T(8,128)S(1)}, f32[128,128]{1,0:T(8,128)S(1)}, u32[]{:S(2)}, u32[]{:S(2)}) %collective-permute-start.13) | collective-permute-done | bytes 65568 | tf_op jit(solution)/shard_map/ppermute | solution.py:112
  31.1 2.5 %collective-permute-done.11 = f32[128,128]{1,0:T(8,128)S(1)} collective-permute-done((f32[128,128]{1,0:T(8,128)S(1)}, f32[128,128]{1,0:T(8,128)S(1)}, u32[]{:S(2)}, u32[]{:S(2)}) %collective-permute-start.11) | collective-permute-done | bytes 65568 | tf_op jit(solution)/shard_map/ppermute | solution.py:112
  33.5 0.6 %add_add_fusion = f32[128,128]{1,0:T(8,128)} fusion(f32[128,128]{1,0:T(8,128)S(1)} %shard_map.57, f32[128,128]{1,0:T(8,128)S(1)} %get-tuple-element.30, f32[128,128]{1,0:T(8,128)S(1)} %collective-permute-done.11), kind=kLoop, calls=%fused_computation | loop fusion | flops 32768 | bytes 262144 | tf_op jit(solution)/shard_map/add | solution.py:217
  (8 shorter events, 0.1 us)
Async XLA Ops:
  0.0 6.2 %copy-start.1 = (f32[128,128]{1,0:T(8,128)S(1)}, f32[128,128]{1,0:T(8,128)}, u32[]{:S(2)}) copy-start(f32[128,128]{1,0:T(8,128)} %refs_0_.3) | copy-start | bytes 196612
  0.0 6.2 %collective-permute-start = (f32[48,512]{1,0:T(8,128)}, f32[48,512]{1,0:T(8,128)S(1)}, u32[]{:S(2)}, u32[]{:S(2)}) collective-permute-start(f32[48,512]{1,0:T(8,128)} %refs_0_.5), channel_id=1, source_target_pairs={{0,1},{1,0},{2,3},{3,2},{4,5},{5,4},{6,7},{7,6},{8,9},{9,8},{10,11... | collective-permute-start | bytes 294920 | tf_op jit(solution)/shard_map/ppermute | solution.py:112
  1.6 8.7 %collective-permute-start.1 = (f32[48,512]{1,0:T(8,128)}, f32[48,512]{1,0:T(8,128)S(1)}, u32[]{:S(2)}, u32[]{:S(2)}) collective-permute-start(f32[48,512]{1,0:T(8,128)} %refs_0_.5), channel_id=1, source_target_pairs={{0,2},{1,3},{2,0},{3,1},{4,6},{5,7},{6,4},{7,5},{8,10},{9,11},{10,... | collective-permute-start | bytes 294920 | tf_op jit(solution)/shard_map/ppermute | solution.py:112
  1.9 14.3 %collective-permute-start.2 = (f32[48,512]{1,0:T(8,128)}, f32[48,512]{1,0:T(8,128)S(1)}, u32[]{:S(2)}, u32[]{:S(2)}) collective-permute-start(f32[48,512]{1,0:T(8,128)} %refs_0_.5), channel_id=1, source_target_pairs={{0,3},{1,2},{2,1},{3,0},{4,7},{5,6},{6,5},{7,4},{8,11},{9,10},{10,... | collective-permute-start | bytes 294920 | tf_op jit(solution)/shard_map/ppermute | solution.py:112
  3.5 0.7 %copy-start.2 = (s32[4,8]{1,0:T(4,128)S(1)}, s32[4,8]{1,0:T(4,128)}, u32[]{:S(2)}) copy-start(s32[4,8]{1,0:T(4,128)} %list_ref.1) | copy-start | bytes 388
  4.2 0.7 %copy-start.3 = (s32[4]{0:T(128)S(1)}, s32[4]{0:T(128)}, u32[]{:S(2)}) copy-start(s32[4]{0:T(128)} %count_ref.1) | copy-start | bytes 52
  6.2 13.5 %copy-start = (f32[48,512]{1,0:T(8,128)S(1)}, f32[48,512]{1,0:T(8,128)}, u32[]{:S(2)}) copy-start(f32[48,512]{1,0:T(8,128)} %refs_0_.5) | copy-start | bytes 294916
  6.2 13.0 %collective-permute-start.5 = (f32[128,128]{1,0:T(8,128)S(1)}, f32[128,128]{1,0:T(8,128)S(1)}, u32[]{:S(2)}, u32[]{:S(2)}) collective-permute-start(f32[128,128]{1,0:T(8,128)S(1)} %shard_map.48.refs_0_), channel_id=1, source_target_pairs={{0,1},{1,0},{2,3},{3,2},{4,5},{5,4},{6,7},{7,6},{8,9},{9,8},{10,11... | collective-permute-start | bytes 196616 | tf_op jit(solution)/shard_map/ppermute | solution.py:112
  8.7 11.0 %collective-permute-start.7 = (f32[128,128]{1,0:T(8,128)S(1)}, f32[128,128]{1,0:T(8,128)S(1)}, u32[]{:S(2)}, u32[]{:S(2)}) collective-permute-start(f32[128,128]{1,0:T(8,128)S(1)} %shard_map.48.refs_0_), channel_id=1, source_target_pairs={{0,2},{1,3},{2,0},{3,1},{4,6},{5,7},{6,4},{7,5},{8,10},{9,11},{10,... | collective-permute-start | bytes 196616 | tf_op jit(solution)/shard_map/ppermute | solution.py:112
  8.7 11.1 %collective-permute-start.8 = (f32[128,128]{1,0:T(8,128)S(1)}, f32[128,128]{1,0:T(8,128)S(1)}, u32[]{:S(2)}, u32[]{:S(2)}) collective-permute-start(f32[128,128]{1,0:T(8,128)S(1)} %shard_map.48.refs_0_), channel_id=1, source_target_pairs={{0,3},{1,2},{2,1},{3,0},{4,7},{5,6},{6,5},{7,4},{8,11},{9,10},{10,... | collective-permute-start | bytes 196616 | tf_op jit(solution)/shard_map/ppermute | solution.py:112
  16.2 4.7 %collective-permute-start.3 = (f32[200,128]{1,0:T(8,128)S(1)}, f32[200,128]{1,0:T(8,128)S(1)}, u32[]{:S(2)}, u32[]{:S(2)}) collective-permute-start(f32[200,128]{1,0:T(8,128)S(1)} %constant_dynamic-update-slice_fusion.refs_0_), channel_id=1, source_target_pairs={{0,16},{4,20},{8,24},{12,28},{16,0},{20,4},{24,8},{28,12},{1,17},{... | collective-permute-start | bytes 307208 | tf_op jit(solution)/shard_map/ppermute | solution.py:112
  17.8 5.6 %collective-permute-start.4 = (f32[200,128]{1,0:T(8,128)S(1)}, f32[200,128]{1,0:T(8,128)S(1)}, u32[]{:S(2)}, u32[]{:S(2)}) collective-permute-start(f32[200,128]{1,0:T(8,128)S(1)} %constant_dynamic-update-slice_fusion.refs_0_), channel_id=1, source_target_pairs={{0,24},{4,28},{8,16},{12,20},{16,8},{20,12},{24,0},{28,4},{1,25},{... | collective-permute-start | bytes 307208 | tf_op jit(solution)/shard_map/ppermute | solution.py:112
  19.2 8.8 %collective-permute-start.10 = (f32[200,128]{1,0:T(8,128)S(1)}, f32[200,128]{1,0:T(8,128)S(1)}, u32[]{:S(2)}, u32[]{:S(2)}) collective-permute-start(f32[200,128]{1,0:T(8,128)S(1)} %constant_dynamic-update-slice_fusion.refs_0_), channel_id=1, source_target_pairs={{0,8},{4,12},{8,0},{12,4},{16,24},{20,28},{24,16},{28,20},{1,9},{5... | collective-permute-start | bytes 307208 | tf_op jit(solution)/shard_map/ppermute | solution.py:112
  19.8 3.6 %collective-permute-start.6 = (f32[192,512]{1,0:T(8,128)S(1)}, f32[192,512]{1,0:T(8,128)S(1)}, u32[]{:S(2)}, u32[]{:S(2)}) collective-permute-start(f32[192,512]{1,0:T(8,128)S(1)} %shard_map.50), channel_id=1, source_target_pairs={{0,4},{4,0},{8,12},{12,8},{16,20},{20,16},{24,28},{28,24},{1,5},{5... | collective-permute-start | bytes 1179656 | tf_op jit(solution)/shard_map/ppermute | solution.py:112
  19.9 4.0 %collective-permute-start.9 = (f32[512,128]{1,0:T(8,128)S(1)}, f32[512,128]{1,0:T(8,128)S(1)}, u32[]{:S(2)}, u32[]{:S(2)}) collective-permute-start(f32[512,128]{1,0:T(8,128)S(1)} %shard_map.52.own_ref), channel_id=1, source_target_pairs={{0,4},{4,0},{8,12},{12,8},{16,20},{20,16},{24,28},{28,24},{1,5},{5... | collective-permute-start | bytes 786440 | tf_op jit(solution)/shard_map/ppermute | solution.py:112
  25.0 4.8 %collective-permute-start.12 = (f32[128,128]{1,0:T(8,128)S(1)}, f32[128,128]{1,0:T(8,128)S(1)}, u32[]{:S(2)}, u32[]{:S(2)}) collective-permute-start(f32[128,128]{1,0:T(8,128)S(1)} %get-tuple-element.26.before_ref), channel_id=1, source_target_pairs={{0,16},{4,20},{8,24},{12,28},{16,0},{20,4},{24,8},{28,12},{1,17},{... | collective-permute-start | bytes 196616 | tf_op jit(solution)/shard_map/ppermute | solution.py:112
  25.6 5.5 %collective-permute-start.13 = (f32[128,128]{1,0:T(8,128)S(1)}, f32[128,128]{1,0:T(8,128)S(1)}, u32[]{:S(2)}, u32[]{:S(2)}) collective-permute-start(f32[128,128]{1,0:T(8,128)S(1)} %get-tuple-element.32), channel_id=1, source_target_pairs={{0,24},{4,28},{8,16},{12,20},{16,8},{20,12},{24,0},{28,4},{1,25},{... | collective-permute-start | bytes 196616 | tf_op jit(solution)/shard_map/ppermute | solution.py:112
  29.2 4.3 %collective-permute-start.11 = (f32[128,128]{1,0:T(8,128)S(1)}, f32[128,128]{1,0:T(8,128)S(1)}, u32[]{:S(2)}, u32[]{:S(2)}) collective-permute-start(f32[128,128]{1,0:T(8,128)S(1)} %get-tuple-element.31), channel_id=1, source_target_pairs={{0,8},{4,12},{8,0},{12,4},{16,24},{20,28},{24,16},{28,20},{1,9},{5... | collective-permute-start | bytes 196616 | tf_op jit(solution)/shard_map/ppermute | solution.py:112

commit v6 on v4

--- a/solution.py
+++ b/solution.py
@@ -40,7 +40,7 @@
     rank = lax.axis_index("rep")
     for piece, ref in enumerate(piece_refs):
         out_ref[piece * piece_feats : (piece + 1) * piece_feats, :] = ref[...]
-    for spot, ref in enumerate(vec_refs[::-1]):
+    for spot, ref in enumerate(vec_refs):
         span = pl.ds(pl.multiple_of((rank ^ spot) * width, width), width)
         out_ref[feat_count:, span] = ref[...]
 
@@ -71,26 +71,29 @@
             mask_ref[spot : spot + 1, span] = jnp.max(hits, axis=0, keepdims=True)
 
 
-def apply_kernel(first, count, before_ref, row_ref, scale_ref, mask_ref, *refs):
-    own_cols, own_vecs, sibling_cols, sibling_vecs, *out_refs = refs
+def apply_kernel(groups, before_ref, row_ref, scale_ref, mask_ref, *refs):
+    column_refs, refs = refs[: 2 * len(groups)], refs[2 * len(groups) :]
+    out_refs = refs[-(row_ref.shape[1] // column_refs[1].shape[0]) :]
+    so_far = refs[: len(refs) - len(out_refs)]
     width = out_refs[0].shape[1]
-    group_cols = own_cols.shape[0]
     chunk = 2 * width
-    span = slice(first * width, (first + count) * width)
-    rows = row_ref[:, span]
+    rows = row_ref[...]
     total = None
-    for group, (col_ref, vec_ref) in enumerate(((own_cols, own_vecs), (sibling_cols, sibling_vecs))):
+    for place, group in enumerate(groups):
+        col_ref, vec_ref = column_refs[2 * place : 2 * place + 2]
+        group_cols = col_ref.shape[0]
         for start in range(0, group_cols, chunk):
             inner = jnp.dot(col_ref[start : start + chunk, :], rows, preferred_element_type=jnp.float32)
             at = (group * group_cols + start) // width
-            both = [jnp.broadcast_to(mask_ref[spot : spot + 1, span], (width, count * width)) for spot in (at, at + 1)]
+            both = [jnp.broadcast_to(mask_ref[spot : spot + 1, :], (width, rows.shape[1])) for spot in (at, at + 1)]
             weight = stacked(jnp.exp(inner) * jnp.concatenate(both, axis=0), "hlh", 0)
             vecs = vec_ref[:, 3 * start : 3 * (start + chunk)]
             added = jnp.dot(vecs, weight, preferred_element_type=jnp.float32)
             total = added if total is None else total + added
-    total = total * scale_ref[:, span]
+    total = total * scale_ref[...]
     for spot, out_ref in enumerate(out_refs):
-        out_ref[...] = total[:, spot * width : (spot + 1) * width]
+        tile = total[:, spot * width : (spot + 1) * width]
+        out_ref[...] = tile + so_far[spot][...] if so_far else tile
 
 
 def add_kernel(*refs):
@@ -121,14 +124,16 @@
     params = pltpu.CompilerParams(vmem_limit_bytes=(8 + group_blocks) * 1024 * 1024)
     hint = pl.CostEstimate(flops=TRANSFER_FLOPS, bytes_accessed=1024 * 1024, transcendentals=0)
 
-    pieces = [coords] + [swapped(coords, "rep", step) for step in range(1, rep_size)]
+    near = swapped(coords, "rep", 1)
+    pieces = [swapped(coords, "rep", step) for step in range(2, rep_size)]
+    pieces = [coords, pieces[0], near, *pieces[1:]]
     late_vecs = pl.pallas_call(
         copy_kernel,
         in_specs=[anywhere, vmem],
         out_shape=shape(eigvecs.shape, f32),
         compiler_params=params,
-    )(pieces[1], eigvecs)
-    vecs = [swapped(late_vecs, "rep", step) for step in range(rep_size - 1, 0, -1)] + [late_vecs]
+    )(near, eigvecs)
+    vecs = [late_vecs] + [swapped(late_vecs, "rep", step) for step in range(1, rep_size)]
     lists = pl.pallas_call(
         lists_kernel,
         in_specs=[smem, smem],
@@ -155,31 +160,34 @@
             compiler_params=params,
         )(group)
 
-    row_count = len(panels) * width
-    rows = pl.pallas_call(
-        functools.partial(rows_kernel, feat_count),
-        out_shape=[
-            shape((3 * feat_count, row_count), bf16),
-            shape((1, row_count), f32),
-            shape((2 * group_blocks, row_count), f32),
-        ],
-        compiler_params=params,
-        cost_estimate=hint,
-    )(*panels)
-    columns = [*columns_of(own_group), *columns_of(sibling_group)]
     half = len(steps) // 2
-    tiles = {}
-    before = rows[1]
-    for first in (half, 0):
-        done = pl.pallas_call(
-            functools.partial(apply_kernel, first, half),
-            in_specs=[anywhere] + [vmem] * 7,
+
+    def rows_of(first, **estimate):
+        return pl.pallas_call(
+            functools.partial(rows_kernel, feat_count),
+            out_shape=[
+                shape((3 * feat_count, half * width), bf16),
+                shape((1, half * width), f32),
+                shape((2 * group_blocks, half * width), f32),
+            ],
+            compiler_params=params,
+            **estimate,
+        )(*panels[first : first + half])
+
+    def tiles_of(before, groups, rows, columns, so_far=()):
+        return pl.pallas_call(
+            functools.partial(apply_kernel, groups),
+            in_specs=[anywhere] + [vmem] * (3 + len(columns) + len(so_far)),
             out_shape=[shape((eig_count, width), f32)] * half,
             compiler_params=params,
-        )(before, *rows, *columns)
-        before = done[0]
-        for spot in range(half):
-            tiles[first + spot] = done[spot]
+        )(before, *rows, *columns, *so_far)
+
+    far_rows, near_rows = rows_of(half, cost_estimate=hint), rows_of(0)
+    own, sibling = columns_of(own_group), columns_of(sibling_group)
+    far_tiles = tiles_of(far_rows[1], (0,), far_rows, own)
+    far_tiles = tiles_of(far_tiles[0], (1,), far_rows, sibling, far_tiles)
+    near_tiles = tiles_of(far_tiles[0], (0, 1), near_rows, [*own, *sibling])
+    tiles = [*near_tiles, *far_tiles]
 
     arrived = [swapped(tiles[place], "blk", steps[place]) for place in range(1, len(steps))]
     far = pl.pallas_call(

time: 32.2 us -> 33 us (1.025)
  starting transfers between devices: 17.7 us -> 18.8 us
  waiting for transfers between devices: 7.73 us -> 7.04 us
  Pallas kernels: 3.52 us -> 4.09 us
    ppermute x13, starting transfers between devices: 17.7 us -> 18.8 us  [swapped(): lax.ppermute(value, axis, [(source, source ^ step) for source in range(co...]
    ppermute x13, waiting for transfers between devices: 7.73 us -> 7.04 us  [swapped(): lax.ppermute(value, axis, [(source, source ^ step) for source in range(co...]
    pallas_call x3 -> x5, Pallas kernels: 2.27 us -> 2.85 us  [the longest x3 2.67 us: tiles_of(): pl.pallas_call(functools.partial(apply_kernel, groups), in_specs=[anywher...]
  transfers between devices with their start and end apart: 13 -> 13, of which waited for: 8 -> 6; matrix products, arithmetic and copies ran while one was open for 2% -> 2% of each run, Pallas kernels for 7% -> 12%
where the time goes in v6:
time: 33 us; the launch traced here: 32.8 us
  starting transfers between devices  18.8 us (57%)
  waiting for transfers between devices  7.04 us (21%)
  Pallas kernels  4.09 us (12%)
  local copies, waits for them, and re-layouts  2.12 us (6%)
  other arithmetic  0.64 us (2%)
    ppermute x13, starting transfers between devices, swapped(): lax.ppermute(value, axis, [(source, source ^ step) for source in range(co...  18.8 us
    ppermute x13, waiting for transfers between devices, swapped(): lax.ppermute(value, axis, [(source, source ^ step) for source in range(co...  7.04 us
    pallas_call x3, Pallas kernels, tiles_of(): pl.pallas_call(functools.partial(apply_kernel, groups), in_specs=[anywher...  2.67 us
    unnamed x12, local copies, waits for them, and re-layouts  2.12 us
  transfers between devices with their start and end apart: 13, of which 6 were waited for; matrix products, arithmetic and copies ran while one was open for 2% of the time, Pallas kernels for 12%

profile of v6, /device:TPU:0, one launch (start us, length us, event | category | flops | bytes accessed | tf_op | source)
XLA Modules:
  0.0 32.8 jit_solution(13013359538508895799)
XLA Ops:
  0.0 0.0 copy-start.1
  0.0 4.0 %collective-permute-start = (f32[48,512]{1,0:T(8,128)}, f32[48,512]{1,0:T(8,128)S(1)}, u32[]{:S(2)}, u32[]{:S(2)}) collective-permute-start(f32[48,512]{1,0:T(8,128)} %refs_0_.1), channel_id=1, source_target_pairs={{0,2},{1,3},{2,0},{3,1},{4,6},{5,7},{6,4},{7,5},{8,10},{9,11},{10,... | collective-permute-start | bytes 294920 | tf_op jit(solution)/shard_map/ppermute | solution.py:108
  4.0 1.6 %collective-permute-start.1 = (f32[48,512]{1,0:T(8,128)}, f32[48,512]{1,0:T(8,128)S(1)}, u32[]{:S(2)}, u32[]{:S(2)}) collective-permute-start(f32[48,512]{1,0:T(8,128)} %refs_0_.1), channel_id=1, source_target_pairs={{0,1},{1,0},{2,3},{3,2},{4,5},{5,4},{6,7},{7,6},{8,9},{9,8},{10,11... | collective-permute-start | bytes 294920 | tf_op jit(solution)/shard_map/ppermute | solution.py:108
  5.6 0.0 collective-permute-start.2
  5.6 0.0 copy-start.2
  5.6 0.7 %copy-done.2 = s32[4,8]{1,0:T(4,128)S(1)} copy-done((s32[4,8]{1,0:T(4,128)S(1)}, s32[4,8]{1,0:T(4,128)}, u32[]{:S(2)}) %copy-start.2) | copy-done | bytes 152
  6.3 0.0 copy-start.3
  6.3 0.7 %copy-done.3 = s32[4]{0:T(128)S(1)} copy-done((s32[4]{0:T(128)S(1)}, s32[4]{0:T(128)}, u32[]{:S(2)}) %copy-start.3) | copy-done | bytes 40
  7.0 0.6 %shard_map.46 = f32[8,128]{1,0:T(8,128)S(1)} custom-call(s32[4,8]{1,0:T(4,128)S(1)} %copy-done.2, s32[4]{0:T(128)S(1)} %copy-done.3), custom_call_target="tpu_custom_call" | custom-call | tf_op jit(solution)/shard_map/pallas_call | solution.py:137
  7.6 0.7 %dynamic-slice_dynamic-update-slice_fusion.3 = f32[200,128]{1,0:T(8,128)S(1)} fusion(f32[48,512]{1,0:T(8,128)} %refs_0_.1, s32[]{:T(128)S(6)} %select_n.2), kind=kLoop, calls=%fused_computation.4 | loop fusion | bytes 49156
  8.3 1.2 %collective-permute-done.1.before_ref.refs_2_ = f32[48,512]{1,0:T(8,128)S(1)} collective-permute-done((f32[48,512]{1,0:T(8,128)}, f32[48,512]{1,0:T(8,128)S(1)}, u32[]{:S(2)}, u32[]{:S(2)}) %collective-permute-start.1) | collective-permute-done | bytes 98336 | tf_op jit(solution)/shard_map/ppermute | solution.py:108
  9.5 0.0 copy-done.1
  9.5 0.0 copy-start
  9.5 2.4 %collective-permute-start.5 = (f32[128,128]{1,0:T(8,128)S(1)}, f32[128,128]{1,0:T(8,128)S(1)}, u32[]{:S(2)}, u32[]{:S(2)}) collective-permute-start(f32[128,128]{1,0:T(8,128)S(1)} %shard_map.48.refs_4_), channel_id=1, source_target_pairs={{0,1},{1,0},{2,3},{3,2},{4,5},{5,4},{6,7},{7,6},{8,9},{9,8},{10,11... | collective-permute-start | bytes 196616 | tf_op jit(solution)/shard_map/ppermute | solution.py:108
  12.0 0.8 %collective-permute-start.6 = (f32[128,128]{1,0:T(8,128)S(1)}, f32[128,128]{1,0:T(8,128)S(1)}, u32[]{:S(2)}, u32[]{:S(2)}) collective-permute-start(f32[128,128]{1,0:T(8,128)S(1)} %shard_map.48.refs_4_), channel_id=1, source_target_pairs={{0,2},{1,3},{2,0},{3,1},{4,6},{5,7},{6,4},{7,5},{8,10},{9,11},{10,... | collective-permute-start | bytes 196616 | tf_op jit(solution)/shard_map/ppermute | solution.py:108
  12.8 1.6 %collective-permute-start.7 = (f32[128,128]{1,0:T(8,128)S(1)}, f32[128,128]{1,0:T(8,128)S(1)}, u32[]{:S(2)}, u32[]{:S(2)}) collective-permute-start(f32[128,128]{1,0:T(8,128)S(1)} %shard_map.48.refs_4_), channel_id=1, source_target_pairs={{0,3},{1,2},{2,1},{3,0},{4,7},{5,6},{6,5},{7,4},{8,11},{9,10},{10,... | collective-permute-start | bytes 196616 | tf_op jit(solution)/shard_map/ppermute | solution.py:108
  14.4 0.0 collective-permute-done.refs_1_
  14.4 0.0 collective-permute-done.2.refs_3_
  14.5 1.6 %collective-permute-start.3 = (f32[200,128]{1,0:T(8,128)S(1)}, f32[200,128]{1,0:T(8,128)S(1)}, u32[]{:S(2)}, u32[]{:S(2)}) collective-permute-start(f32[200,128]{1,0:T(8,128)S(1)} %constant_dynamic-update-slice_fusion.refs_0_), channel_id=1, source_target_pairs={{0,16},{4,20},{8,24},{12,28},{16,0},{20,4},{24,8},{28,12},{1,17},{... | collective-permute-start | bytes 307208 | tf_op jit(solution)/shard_map/ppermute | solution.py:108
  16.0 1.4 %collective-permute-start.4 = (f32[200,128]{1,0:T(8,128)S(1)}, f32[200,128]{1,0:T(8,128)S(1)}, u32[]{:S(2)}, u32[]{:S(2)}) collective-permute-start(f32[200,128]{1,0:T(8,128)S(1)} %constant_dynamic-update-slice_fusion.refs_0_), channel_id=1, source_target_pairs={{0,24},{4,28},{8,16},{12,20},{16,8},{20,12},{24,0},{28,4},{1,25},{... | collective-permute-start | bytes 307208 | tf_op jit(solution)/shard_map/ppermute | solution.py:108
  17.5 0.0 collective-permute-done.5.refs_5_
  17.5 0.2 collective-permute-done.6.refs_6_
  17.7 1.2 %collective-permute-done.7.refs_7_ = f32[128,128]{1,0:T(8,128)S(1)} collective-permute-done((f32[128,128]{1,0:T(8,128)S(1)}, f32[128,128]{1,0:T(8,128)S(1)}, u32[]{:S(2)}, u32[]{:S(2)}) %collective-permute-start.7) | collective-permute-done | bytes 65568 | tf_op jit(solution)/shard_map/ppermute | solution.py:108
  19.0 0.0 copy-done
  19.0 0.1 shard_map.49.group_ref
  19.0 0.1 collective-permute-start.8
  19.1 1.6 %collective-permute-start.9 = (f32[200,128]{1,0:T(8,128)S(1)}, f32[200,128]{1,0:T(8,128)S(1)}, u32[]{:S(2)}, u32[]{:S(2)}) collective-permute-start(f32[200,128]{1,0:T(8,128)S(1)} %constant_dynamic-update-slice_fusion.refs_0_), channel_id=1, source_target_pairs={{0,8},{4,12},{8,0},{12,4},{16,24},{20,28},{24,16},{28,20},{1,9},{5... | collective-permute-start | bytes 307208 | tf_op jit(solution)/shard_map/ppermute | solution.py:108
  20.6 0.3 shard_map.50
  20.9 0.0 collective-permute-done.3.refs_0_
  21.0 0.6 %collective-permute-done.4.refs_1_ = f32[200,128]{1,0:T(8,128)S(1)} collective-permute-done((f32[200,128]{1,0:T(8,128)S(1)}, f32[200,128]{1,0:T(8,128)S(1)}, u32[]{:S(2)}, u32[]{:S(2)}) %collective-permute-start.4) | collective-permute-done | bytes 102432 | tf_op jit(solution)/shard_map/ppermute | solution.py:108
  21.6 0.1 shard_map.47
  21.7 0.8 %shard_map.51 = (f32[128,128]{1,0:T(8,128)S(1)}, f32[128,128]{1,0:T(8,128)S(1)}) custom-call(f32[1,256]{1,0:T(1,128)S(1)} %get-tuple-element.21.before_ref.scale_ref, bf16[576,256]{1,0:T(8,128)(2,1)S(1)} %get-tuple-element.22.row_ref, f32[1,256]{1,0:T(1,128)S(1)} %get-tuple-element.21.before_ref.scale_ref, f32[8,256]{1,0:T(8,128)S(1)} %get-tuple-element.23.mask_ref, ...), custom_call_target="tpu_custom_call" | custom-call | tf_op jit(solution)/shard_map/pallas_call | solution.py:178
  22.5 0.0 collective-permute-done.8.group_ref
  22.5 0.3 shard_map.52
  22.8 0.8 %shard_map.53 = (f32[128,128]{1,0:T(8,128)S(1)}, f32[128,128]{1,0:T(8,128)S(1)}) custom-call(f32[128,128]{1,0:T(8,128)S(1)} %get-tuple-element.26.before_ref.refs_2_, bf16[576,256]{1,0:T(8,128)(2,1)S(1)} %get-tuple-element.22.row_ref, f32[1,256]{1,0:T(1,128)S(1)} %get-tuple-element.21.before_ref.scale_ref, f32[8,256]{1,0:T(8,128)S(1)} %get-tuple-element.23.mask_ref, ...), custom_call_target="tpu_custom_call" | custom-call | tf_op jit(solution)/shard_map/pallas_call | solution.py:178
  23.6 1.0 %collective-permute-start.11 = (f32[128,128]{1,0:T(8,128)S(1)}, f32[128,128]{1,0:T(8,128)S(1)}, u32[]{:S(2)}, u32[]{:S(2)}) collective-permute-start(f32[128,128]{1,0:T(8,128)S(1)} %get-tuple-element.30.before_ref), channel_id=1, source_target_pairs={{0,16},{4,20},{8,24},{12,28},{16,0},{20,4},{24,8},{28,12},{1,17},{... | collective-permute-start | bytes 196616 | tf_op jit(solution)/shard_map/ppermute | solution.py:108
  24.6 2.1 %collective-permute-start.12 = (f32[128,128]{1,0:T(8,128)S(1)}, f32[128,128]{1,0:T(8,128)S(1)}, u32[]{:S(2)}, u32[]{:S(2)}) collective-permute-start(f32[128,128]{1,0:T(8,128)S(1)} %get-tuple-element.36), channel_id=1, source_target_pairs={{0,24},{4,28},{8,16},{12,20},{16,8},{20,12},{24,0},{28,4},{1,25},{... | collective-permute-start | bytes 196616 | tf_op jit(solution)/shard_map/ppermute | solution.py:108
  26.7 0.0 collective-permute-done.9.refs_1_
  26.7 0.1 shard_map.54
  26.7 1.1 %shard_map.55 = (f32[128,128]{1,0:T(8,128)S(1)}, f32[128,128]{1,0:T(8,128)S(1)}) custom-call(f32[128,128]{1,0:T(8,128)S(1)} %get-tuple-element.30.before_ref, bf16[576,256]{1,0:T(8,128)(2,1)S(1)} %get-tuple-element.31.row_ref, f32[1,256]{1,0:T(1,128)S(1)} %get-tuple-element.32.scale_ref, f32[8,256]{1,0:T(8,128)S(1)} %get-tuple-element.33.mask_ref, ...), custom_call_target="tpu_custom_call" | custom-call | tf_op jit(solution)/shard_map/pallas_call | solution.py:178
  27.8 0.6 %collective-permute-start.10 = (f32[128,128]{1,0:T(8,128)S(1)}, f32[128,128]{1,0:T(8,128)S(1)}, u32[]{:S(2)}, u32[]{:S(2)}) collective-permute-start(f32[128,128]{1,0:T(8,128)S(1)} %get-tuple-element.35), channel_id=1, source_target_pairs={{0,8},{4,12},{8,0},{12,4},{16,24},{20,28},{24,16},{28,20},{1,9},{5... | collective-permute-start | bytes 196616 | tf_op jit(solution)/shard_map/ppermute | solution.py:108
  28.4 0.0 collective-permute-done.11.refs_0_
  28.4 1.5 %collective-permute-done.12.refs_1_ = f32[128,128]{1,0:T(8,128)S(1)} collective-permute-done((f32[128,128]{1,0:T(8,128)S(1)}, f32[128,128]{1,0:T(8,128)S(1)}, u32[]{:S(2)}, u32[]{:S(2)}) %collective-permute-start.12) | collective-permute-done | bytes 65568 | tf_op jit(solution)/shard_map/ppermute | solution.py:108
  29.9 2.2 %collective-permute-done.10 = f32[128,128]{1,0:T(8,128)S(1)} collective-permute-done((f32[128,128]{1,0:T(8,128)S(1)}, f32[128,128]{1,0:T(8,128)S(1)}, u32[]{:S(2)}, u32[]{:S(2)}) %collective-permute-start.10) | collective-permute-done | bytes 65568 | tf_op jit(solution)/shard_map/ppermute | solution.py:108
  32.2 0.6 %add_add_fusion = f32[128,128]{1,0:T(8,128)} fusion(f32[128,128]{1,0:T(8,128)S(1)} %shard_map.56, f32[128,128]{1,0:T(8,128)S(1)} %get-tuple-element.34, f32[128,128]{1,0:T(8,128)S(1)} %collective-permute-done.10), kind=kLoop, calls=%fused_computation | loop fusion | flops 32768 | bytes 262144 | tf_op jit(solution)/shard_map/add | solution.py:202
  (6 shorter events, 0.0 us)
Async XLA Ops:
  0.0 9.5 %copy-start.1 = (f32[128,128]{1,0:T(8,128)S(1)}, f32[128,128]{1,0:T(8,128)}, u32[]{:S(2)}) copy-start(f32[128,128]{1,0:T(8,128)} %in_ref.1) | copy-start | bytes 196612
  0.0 14.4 %collective-permute-start = (f32[48,512]{1,0:T(8,128)}, f32[48,512]{1,0:T(8,128)S(1)}, u32[]{:S(2)}, u32[]{:S(2)}) collective-permute-start(f32[48,512]{1,0:T(8,128)} %refs_0_.1), channel_id=1, source_target_pairs={{0,2},{1,3},{2,0},{3,1},{4,6},{5,7},{6,4},{7,5},{8,10},{9,11},{10,... | collective-permute-start | bytes 294920 | tf_op jit(solution)/shard_map/ppermute | solution.py:108
  4.0 5.4 %collective-permute-start.1 = (f32[48,512]{1,0:T(8,128)}, f32[48,512]{1,0:T(8,128)S(1)}, u32[]{:S(2)}, u32[]{:S(2)}) collective-permute-start(f32[48,512]{1,0:T(8,128)} %refs_0_.1), channel_id=1, source_target_pairs={{0,1},{1,0},{2,3},{3,2},{4,5},{5,4},{6,7},{7,6},{8,9},{9,8},{10,11... | collective-permute-start | bytes 294920 | tf_op jit(solution)/shard_map/ppermute | solution.py:108
  5.6 8.8 %collective-permute-start.2 = (f32[48,512]{1,0:T(8,128)}, f32[48,512]{1,0:T(8,128)S(1)}, u32[]{:S(2)}, u32[]{:S(2)}) collective-permute-start(f32[48,512]{1,0:T(8,128)} %refs_0_.1), channel_id=1, source_target_pairs={{0,3},{1,2},{2,1},{3,0},{4,7},{5,6},{6,5},{7,4},{8,11},{9,10},{10,... | collective-permute-start | bytes 294920 | tf_op jit(solution)/shard_map/ppermute | solution.py:108
  5.6 0.7 %copy-start.2 = (s32[4,8]{1,0:T(4,128)S(1)}, s32[4,8]{1,0:T(4,128)}, u32[]{:S(2)}) copy-start(s32[4,8]{1,0:T(4,128)} %list_ref.1) | copy-start | bytes 388
  6.3 0.7 %copy-start.3 = (s32[4]{0:T(128)S(1)}, s32[4]{0:T(128)}, u32[]{:S(2)}) copy-start(s32[4]{0:T(128)} %count_ref.1) | copy-start | bytes 52
  9.5 9.5 %copy-start = (f32[48,512]{1,0:T(8,128)S(1)}, f32[48,512]{1,0:T(8,128)}, u32[]{:S(2)}) copy-start(f32[48,512]{1,0:T(8,128)} %refs_0_.1) | copy-start | bytes 294916
  9.5 8.0 %collective-permute-start.5 = (f32[128,128]{1,0:T(8,128)S(1)}, f32[128,128]{1,0:T(8,128)S(1)}, u32[]{:S(2)}, u32[]{:S(2)}) collective-permute-start(f32[128,128]{1,0:T(8,128)S(1)} %shard_map.48.refs_4_), channel_id=1, source_target_pairs={{0,1},{1,0},{2,3},{3,2},{4,5},{5,4},{6,7},{7,6},{8,9},{9,8},{10,11... | collective-permute-start | bytes 196616 | tf_op jit(solution)/shard_map/ppermute | solution.py:108
  12.0 5.8 %collective-permute-start.6 = (f32[128,128]{1,0:T(8,128)S(1)}, f32[128,128]{1,0:T(8,128)S(1)}, u32[]{:S(2)}, u32[]{:S(2)}) collective-permute-start(f32[128,128]{1,0:T(8,128)S(1)} %shard_map.48.refs_4_), channel_id=1, source_target_pairs={{0,2},{1,3},{2,0},{3,1},{4,6},{5,7},{6,4},{7,5},{8,10},{9,11},{10,... | collective-permute-start | bytes 196616 | tf_op jit(solution)/shard_map/ppermute | solution.py:108
  12.8 6.2 %collective-permute-start.7 = (f32[128,128]{1,0:T(8,128)S(1)}, f32[128,128]{1,0:T(8,128)S(1)}, u32[]{:S(2)}, u32[]{:S(2)}) collective-permute-start(f32[128,128]{1,0:T(8,128)S(1)} %shard_map.48.refs_4_), channel_id=1, source_target_pairs={{0,3},{1,2},{2,1},{3,0},{4,7},{5,6},{6,5},{7,4},{8,11},{9,10},{10,... | collective-permute-start | bytes 196616 | tf_op jit(solution)/shard_map/ppermute | solution.py:108
  14.5 6.5 %collective-permute-start.3 = (f32[200,128]{1,0:T(8,128)S(1)}, f32[200,128]{1,0:T(8,128)S(1)}, u32[]{:S(2)}, u32[]{:S(2)}) collective-permute-start(f32[200,128]{1,0:T(8,128)S(1)} %constant_dynamic-update-slice_fusion.refs_0_), channel_id=1, source_target_pairs={{0,16},{4,20},{8,24},{12,28},{16,0},{20,4},{24,8},{28,12},{1,17},{... | collective-permute-start | bytes 307208 | tf_op jit(solution)/shard_map/ppermute | solution.py:108
  16.0 5.6 %collective-permute-start.4 = (f32[200,128]{1,0:T(8,128)S(1)}, f32[200,128]{1,0:T(8,128)S(1)}, u32[]{:S(2)}, u32[]{:S(2)}) collective-permute-start(f32[200,128]{1,0:T(8,128)S(1)} %constant_dynamic-update-slice_fusion.refs_0_), channel_id=1, source_target_pairs={{0,24},{4,28},{8,16},{12,20},{16,8},{20,12},{24,0},{28,4},{1,25},{... | collective-permute-start | bytes 307208 | tf_op jit(solution)/shard_map/ppermute | solution.py:108
  19.0 3.5 %collective-permute-start.8 = (f32[320,512]{1,0:T(8,128)S(1)}, f32[320,512]{1,0:T(8,128)S(1)}, u32[]{:S(2)}, u32[]{:S(2)}) collective-permute-start(f32[320,512]{1,0:T(8,128)S(1)} %shard_map.49.group_ref), channel_id=1, source_target_pairs={{0,4},{4,0},{8,12},{12,8},{16,20},{20,16},{24,28},{28,24},{1,5},{5... | collective-permute-start | bytes 1966088 | tf_op jit(solution)/shard_map/ppermute | solution.py:108
  19.1 7.6 %collective-permute-start.9 = (f32[200,128]{1,0:T(8,128)S(1)}, f32[200,128]{1,0:T(8,128)S(1)}, u32[]{:S(2)}, u32[]{:S(2)}) collective-permute-start(f32[200,128]{1,0:T(8,128)S(1)} %constant_dynamic-update-slice_fusion.refs_0_), channel_id=1, source_target_pairs={{0,8},{4,12},{8,0},{12,4},{16,24},{20,28},{24,16},{28,20},{1,9},{5... | collective-permute-start | bytes 307208 | tf_op jit(solution)/shard_map/ppermute | solution.py:108
  23.6 4.8 %collective-permute-start.11 = (f32[128,128]{1,0:T(8,128)S(1)}, f32[128,128]{1,0:T(8,128)S(1)}, u32[]{:S(2)}, u32[]{:S(2)}) collective-permute-start(f32[128,128]{1,0:T(8,128)S(1)} %get-tuple-element.30.before_ref), channel_id=1, source_target_pairs={{0,16},{4,20},{8,24},{12,28},{16,0},{20,4},{24,8},{28,12},{1,17},{... | collective-permute-start | bytes 196616 | tf_op jit(solution)/shard_map/ppermute | solution.py:108
  24.6 5.3 %collective-permute-start.12 = (f32[128,128]{1,0:T(8,128)S(1)}, f32[128,128]{1,0:T(8,128)S(1)}, u32[]{:S(2)}, u32[]{:S(2)}) collective-permute-start(f32[128,128]{1,0:T(8,128)S(1)} %get-tuple-element.36), channel_id=1, source_target_pairs={{0,24},{4,28},{8,16},{12,20},{16,8},{20,12},{24,0},{28,4},{1,25},{... | collective-permute-start | bytes 196616 | tf_op jit(solution)/shard_map/ppermute | solution.py:108
  27.8 4.3 %collective-permute-start.10 = (f32[128,128]{1,0:T(8,128)S(1)}, f32[128,128]{1,0:T(8,128)S(1)}, u32[]{:S(2)}, u32[]{:S(2)}) collective-permute-start(f32[128,128]{1,0:T(8,128)S(1)} %get-tuple-element.35), channel_id=1, source_target_pairs={{0,8},{4,12},{8,0},{12,4},{16,24},{20,28},{24,16},{28,20},{1,9},{5... | collective-permute-start | bytes 196616 | tf_op jit(solution)/shard_map/ppermute | solution.py:108

commit v7 on v5

--- a/solution.py
+++ b/solution.py
@@ -8,7 +8,7 @@
 from jax.sharding import PartitionSpec as P
 
 
-ROWS_FLOPS = 350 * 10**7
+ROWS_FLOPS = 400 * 10**7
 VECTORS_FLOPS = 200 * 10**7
 ADD_FLOPS = 620 * 10**7
 
@@ -38,23 +38,25 @@
 
 
 def columns_kernel(order, before_ref, *refs):
-    piece_refs, (col_ref, bias_ref) = refs[:-2], refs[-2:]
-    width = bias_ref.shape[1]
+    piece_refs, (col_ref, scale_ref) = refs[:-2], refs[-2:]
+    width = scale_ref.shape[1] // len(order)
     rank = lax.axis_index("rep")
     for place, spot in enumerate(order):
         here = pl.ds(pl.multiple_of((rank ^ spot) * width, width), width)
-        cols = jnp.concatenate([ref[:, here] for ref in piece_refs], axis=0).T
         there = slice(place * width, (place + 1) * width)
-        bias = jnp.sum(cols * cols, axis=1, keepdims=True) * (-1.0 / cols.shape[1])
-        bias_ref[there, :] = jnp.broadcast_to(bias, (width, width))
-        col_ref[there, :] = stacked(cols, "hhl", 1)
-
-
-def vectors_kernel(before_ref, own_ref, sibling_ref, out_ref):
+        cols = jnp.concatenate([ref[:, here] for ref in piece_refs], axis=0)
+        scale_ref[:, there] = jnp.exp(jnp.sum(cols * cols, axis=0, keepdims=True) * (-1.0 / cols.shape[0]))
+        col_ref[there, :] = stacked(cols.T, "hhl", 1)
+
+
+def vectors_kernel(own_ref, sibling_ref, own_scale, sibling_scale, out_ref):
     eig_count, width = out_ref.shape[0], own_ref.shape[1]
     place = 0
-    for ref in (own_ref, sibling_ref):
-        blocks = [ref[top : top + eig_count, :] for top in range(0, ref.shape[0], eig_count)]
+    for ref, scale_ref in ((own_ref, own_scale), (sibling_ref, sibling_scale)):
+        tops = range(0, ref.shape[0], eig_count)
+        blocks = [
+            ref[top : top + eig_count, :] * scale_ref[:, at * width : (at + 1) * width] for at, top in enumerate(tops)
+        ]
         for pair in range(len(blocks) // 2):
             vecs = jnp.concatenate(blocks[2 * pair : 2 * pair + 2], axis=1)
             out_ref[:, place : place + 6 * width] = stacked(vecs, "hhl", 1)
@@ -79,19 +81,18 @@
 
 
 def apply_kernel(before_ref, row_ref, scale_ref, mask_ref, *refs):
-    own_cols, own_bias, sibling_cols, sibling_bias, vec_ref, *out_refs = refs
+    own_cols, sibling_cols, vec_ref, *out_refs = refs
     width = out_refs[0].shape[1]
     group_cols = own_cols.shape[0]
     chunk = 2 * width
     rows = row_ref[...]
     total = None
-    for group, (col_ref, bias_ref) in enumerate(((own_cols, own_bias), (sibling_cols, sibling_bias))):
+    for group, col_ref in enumerate((own_cols, sibling_cols)):
         for start in range(0, group_cols, chunk):
             inner = jnp.dot(col_ref[start : start + chunk, :], rows, preferred_element_type=jnp.float32)
-            bias = jnp.concatenate([bias_ref[start : start + chunk, :]] * len(out_refs), axis=1)
             at = (group * group_cols + start) // width
             both = [jnp.broadcast_to(mask_ref[spot : spot + 1, :], (width, rows.shape[1])) for spot in (at, at + 1)]
-            weight = stacked(jnp.exp(inner + bias) * jnp.concatenate(both, axis=0), "hlh", 0)
+            weight = stacked(jnp.exp(inner) * jnp.concatenate(both, axis=0), "hlh", 0)
             there = 3 * (group * group_cols + start)
             added = jnp.dot(vec_ref[:, there : there + 3 * chunk], weight, preferred_element_type=jnp.float32)
             total = added if total is None else total + added
@@ -133,7 +134,7 @@
     def block_of(piece, block):
         return lax.dynamic_slice_in_dim(piece, block * width, width, 1)
 
-    pieces = [coords] + [swapped(coords, "rep", step) for step in range(1, rep_size)]
+    pieces = [coords] + [swapped(coords, "rep", step) for step in [2, 1, *range(3, rep_size)]]
     own_block = [block_of(piece, rep_index) for piece in pieces]
 
     def below(before, values, **estimate):
@@ -158,13 +159,15 @@
     )(nbr_list, nbr_count)
     panel = jnp.concatenate([*own_block, lists], axis=0)
     steps = list(range(0, cycle_size, 2))
+    half = len(steps) // 2
+    steps[half:] = steps[:half - 1:-1]
     panels = [panel] + [swapped(panel, "blk", step) for step in steps[1:]]
 
     def columns_of(before, group_pieces):
         return pl.pallas_call(
             functools.partial(columns_kernel, order),
             in_specs=[anywhere] + [vmem] * len(group_pieces),
-            out_shape=[shape((group_cols, 3 * feat_count), bf16), shape((group_cols, width), f32)],
+            out_shape=[shape((group_cols, 3 * feat_count), bf16), shape((1, group_cols), f32)],
             compiler_params=params,
         )(before, *group_pieces)
 
@@ -172,7 +175,6 @@
     sibling_vecs = swapped(vecs, "blk", 1)
     columns = [*columns_of(far_vecs[0], pieces), *columns_of(far_vecs[0], [sibling_cols])]
 
-    half = len(steps) // 2
     rows = {}
     for first in (half, 0):
         rows[first] = pl.pallas_call(
@@ -187,19 +189,18 @@
         )(*panels[first : first + half])
     vectors = pl.pallas_call(
         vectors_kernel,
-        in_specs=[anywhere] + [vmem] * 2,
         out_shape=shape((eig_count, 6 * group_cols), bf16),
         compiler_params=params,
-    )(columns[3], vecs, sibling_vecs)
+    )(vecs, sibling_vecs, columns[1], columns[3])
     tiles = {}
     before = rows[half][1]
     for first in (half, 0):
         done = pl.pallas_call(
             apply_kernel,
-            in_specs=[anywhere] + [vmem] * 8,
+            in_specs=[anywhere] + [vmem] * 6,
             out_shape=[shape((eig_count, width), f32)] * half,
             compiler_params=params,
-        )(before, *rows[first], *columns, vectors)
+        )(before, *rows[first], columns[0], columns[2], vectors)
         before = done[0]
         for spot in range(half):
             tiles[first + spot] = done[spot]

time: 34.4 us -> 33.6 us (0.977)
  the two profiles are of different devices: /device:TPU:16 before, /device:TPU:0 now
where the time goes in v7:
time: 33.6 us; the launch traced here: 33.4 us
  starting transfers between devices  18.2 us (54%)
  waiting for transfers between devices  8.69 us (26%)
  Pallas kernels  3.62 us (11%)
  local copies, waits for them, and re-layouts  2.13 us (6%)
  other arithmetic  0.64 us (2%)
    ppermute x14, starting transfers between devices, swapped(): lax.ppermute(value, axis, [(source, source ^ step) for source in range(co...  18.2 us
    ppermute x14, waiting for transfers between devices, swapped(): lax.ppermute(value, axis, [(source, source ^ step) for source in range(co...  8.69 us
    unnamed x12, local copies, waits for them, and re-layouts  2.12 us
    pallas_call x2, Pallas kernels, shards(): pl.pallas_call(apply_kernel, in_specs=[anywhere] + [vmem] * 6, out_shape=...  2.1 us
  transfers between devices with their start and end apart: 14, of which 6 were waited for; matrix products, arithmetic and copies ran while one was open for 2% of the time, Pallas kernels for 11%

profile of v7, /device:TPU:0, one launch (start us, length us, event | category | flops | bytes accessed | tf_op | source)
XLA Modules:
  0.0 33.4 jit_solution(1479243645134758152)
XLA Ops:
  0.0 0.0 copy-start.1
  0.0 4.0 %collective-permute-start = (f32[48,512]{1,0:T(8,128)}, f32[48,512]{1,0:T(8,128)S(1)}, u32[]{:S(2)}, u32[]{:S(2)}) collective-permute-start(f32[48,512]{1,0:T(8,128)} %refs_0_.5), channel_id=1, source_target_pairs={{0,2},{1,3},{2,0},{3,1},{4,6},{5,7},{6,4},{7,5},{8,10},{9,11},{10,... | collective-permute-start | bytes 294920 | tf_op jit(solution)/shard_map/ppermute | solution.py:113
  4.0 1.6 %collective-permute-start.1 = (f32[48,512]{1,0:T(8,128)}, f32[48,512]{1,0:T(8,128)S(1)}, u32[]{:S(2)}, u32[]{:S(2)}) collective-permute-start(f32[48,512]{1,0:T(8,128)} %refs_0_.5), channel_id=1, source_target_pairs={{0,1},{1,0},{2,3},{3,2},{4,5},{5,4},{6,7},{7,6},{8,9},{9,8},{10,11... | collective-permute-start | bytes 294920 | tf_op jit(solution)/shard_map/ppermute | solution.py:113
  5.6 0.0 collective-permute-start.2
  5.6 0.0 copy-start.2
  5.6 0.7 %copy-done.2 = s32[4,8]{1,0:T(4,128)S(1)} copy-done((s32[4,8]{1,0:T(4,128)S(1)}, s32[4,8]{1,0:T(4,128)}, u32[]{:S(2)}) %copy-start.2) | copy-done | bytes 152
  6.3 0.0 copy-start.3
  6.3 0.7 %copy-done.3 = s32[4]{0:T(128)S(1)} copy-done((s32[4]{0:T(128)S(1)}, s32[4]{0:T(128)}, u32[]{:S(2)}) %copy-start.3) | copy-done | bytes 40
  7.0 0.6 %shard_map.46 = f32[8,128]{1,0:T(8,128)S(1)} custom-call(s32[4,8]{1,0:T(4,128)S(1)} %copy-done.2, s32[4]{0:T(128)S(1)} %copy-done.3), custom_call_target="tpu_custom_call" | custom-call | tf_op jit(solution)/shard_map/pallas_call | solution.py:154
  7.6 0.7 %dynamic-slice_dynamic-update-slice_fusion.3 = f32[200,128]{1,0:T(8,128)S(1)} fusion(f32[48,512]{1,0:T(8,128)} %refs_0_.5, s32[]{:T(128)S(6)} %select_n.2), kind=kLoop, calls=%fused_computation.4 | loop fusion | bytes 49156
  8.3 1.9 %collective-permute-done.before_ref.refs_1_ = f32[48,512]{1,0:T(8,128)S(1)} collective-permute-done((f32[48,512]{1,0:T(8,128)}, f32[48,512]{1,0:T(8,128)S(1)}, u32[]{:S(2)}, u32[]{:S(2)}) %collective-permute-start) | collective-permute-done | bytes 98336 | tf_op jit(solution)/shard_map/ppermute | solution.py:113
  10.2 0.0 copy-done.1
  10.2 0.0 copy-start
  10.2 0.5 %collective-permute-start.5 = (f32[128,128]{1,0:T(8,128)S(1)}, f32[128,128]{1,0:T(8,128)S(1)}, u32[]{:S(2)}, u32[]{:S(2)}) collective-permute-start(f32[128,128]{1,0:T(8,128)S(1)} %shard_map.48.refs_0_), channel_id=1, source_target_pairs={{0,1},{1,0},{2,3},{3,2},{4,5},{5,4},{6,7},{7,6},{8,9},{9,8},{10,11... | collective-permute-start | bytes 196616 | tf_op jit(solution)/shard_map/ppermute | solution.py:113
  10.7 4.7 %collective-permute-start.7 = (f32[128,128]{1,0:T(8,128)S(1)}, f32[128,128]{1,0:T(8,128)S(1)}, u32[]{:S(2)}, u32[]{:S(2)}) collective-permute-start(f32[128,128]{1,0:T(8,128)S(1)} %shard_map.48.refs_0_), channel_id=1, source_target_pairs={{0,2},{1,3},{2,0},{3,1},{4,6},{5,7},{6,4},{7,5},{8,10},{9,11},{10,... | collective-permute-start | bytes 196616 | tf_op jit(solution)/shard_map/ppermute | solution.py:113
  15.4 0.0 collective-permute-start.8
  15.4 0.0 collective-permute-done.1.refs_2_
  15.5 0.0 collective-permute-done.2.refs_3_
  15.5 2.5 %collective-permute-start.3 = (f32[200,128]{1,0:T(8,128)S(1)}, f32[200,128]{1,0:T(8,128)S(1)}, u32[]{:S(2)}, u32[]{:S(2)}) collective-permute-start(f32[200,128]{1,0:T(8,128)S(1)} %constant_dynamic-update-slice_fusion.refs_0_), channel_id=1, source_target_pairs={{0,24},{4,28},{8,16},{12,20},{16,8},{20,12},{24,0},{28,4},{1,25},{... | collective-permute-start | bytes 307208 | tf_op jit(solution)/shard_map/ppermute | solution.py:113
  18.0 0.5 %collective-permute-start.4 = (f32[200,128]{1,0:T(8,128)S(1)}, f32[200,128]{1,0:T(8,128)S(1)}, u32[]{:S(2)}, u32[]{:S(2)}) collective-permute-start(f32[200,128]{1,0:T(8,128)S(1)} %constant_dynamic-update-slice_fusion.refs_0_), channel_id=1, source_target_pairs={{0,16},{4,20},{8,24},{12,28},{16,0},{20,4},{24,8},{28,12},{1,17},{... | collective-permute-start | bytes 307208 | tf_op jit(solution)/shard_map/ppermute | solution.py:113
  18.5 0.0 collective-permute-done.5.before_ref.refs_1_
  18.5 0.5 %collective-permute-start.10 = (f32[200,128]{1,0:T(8,128)S(1)}, f32[200,128]{1,0:T(8,128)S(1)}, u32[]{:S(2)}, u32[]{:S(2)}) collective-permute-start(f32[200,128]{1,0:T(8,128)S(1)} %constant_dynamic-update-slice_fusion.refs_0_), channel_id=1, source_target_pairs={{0,8},{4,12},{8,0},{12,4},{16,24},{20,28},{24,16},{28,20},{1,9},{5... | collective-permute-start | bytes 307208 | tf_op jit(solution)/shard_map/ppermute | solution.py:113
  19.1 0.0 copy-done
  19.1 0.0 collective-permute-done.7.refs_2_
  19.1 0.1 collective-permute-start.6
  19.2 2.3 %collective-permute-done.8.refs_3_ = f32[128,128]{1,0:T(8,128)S(1)} collective-permute-done((f32[128,128]{1,0:T(8,128)S(1)}, f32[128,128]{1,0:T(8,128)S(1)}, u32[]{:S(2)}, u32[]{:S(2)}) %collective-permute-start.8) | collective-permute-done | bytes 65568 | tf_op jit(solution)/shard_map/ppermute | solution.py:113
  21.5 0.1 collective-permute-start.9
  21.6 0.3 shard_map.49
  21.9 0.0 collective-permute-done.3.refs_0_
  21.9 1.0 %collective-permute-done.4.refs_1_ = f32[200,128]{1,0:T(8,128)S(1)} collective-permute-done((f32[200,128]{1,0:T(8,128)S(1)}, f32[200,128]{1,0:T(8,128)S(1)}, u32[]{:S(2)}, u32[]{:S(2)}) %collective-permute-start.4) | collective-permute-done | bytes 102432 | tf_op jit(solution)/shard_map/ppermute | solution.py:113
  22.9 0.1 shard_map.47
  23.0 0.0 collective-permute-done.6.refs_0_
  23.0 0.3 shard_map.51
  23.3 0.0 collective-permute-done.9.sibling_ref
  23.3 0.1 shard_map.53.refs_2_
  23.4 1.0 %shard_map.54 = (f32[128,128]{1,0:T(8,128)S(1)}, f32[128,128]{1,0:T(8,128)S(1)}) custom-call(f32[1,256]{1,0:T(1,128)S(1)} %get-tuple-element.19.before_ref.scale_ref, bf16[576,256]{1,0:T(8,128)(2,1)S(1)} %get-tuple-element.20.row_ref, f32[1,256]{1,0:T(1,128)S(1)} %get-tuple-element.19.before_ref.scale_ref, f32[8,256]{1,0:T(8,128)S(1)} %get-tuple-element.21.mask_ref, ...), custom_call_target="tpu_custom_call" | custom-call | tf_op jit(solution)/shard_map/pallas_call | solution.py:198
  24.5 2.3 %collective-permute-start.12 = (f32[128,128]{1,0:T(8,128)S(1)}, f32[128,128]{1,0:T(8,128)S(1)}, u32[]{:S(2)}, u32[]{:S(2)}) collective-permute-start(f32[128,128]{1,0:T(8,128)S(1)} %get-tuple-element.26.before_ref), channel_id=1, source_target_pairs={{0,24},{4,28},{8,16},{12,20},{16,8},{20,12},{24,0},{28,4},{1,25},{... | collective-permute-start | bytes 196616 | tf_op jit(solution)/shard_map/ppermute | solution.py:113
  26.8 0.5 %collective-permute-start.13 = (f32[128,128]{1,0:T(8,128)S(1)}, f32[128,128]{1,0:T(8,128)S(1)}, u32[]{:S(2)}, u32[]{:S(2)}) collective-permute-start(f32[128,128]{1,0:T(8,128)S(1)} %get-tuple-element.32), channel_id=1, source_target_pairs={{0,16},{4,20},{8,24},{12,28},{16,0},{20,4},{24,8},{28,12},{1,17},{... | collective-permute-start | bytes 196616 | tf_op jit(solution)/shard_map/ppermute | solution.py:113
  27.3 0.0 collective-permute-done.10.refs_1_
  27.3 0.1 shard_map.55
  27.4 1.1 %shard_map.56 = (f32[128,128]{1,0:T(8,128)S(1)}, f32[128,128]{1,0:T(8,128)S(1)}) custom-call(f32[128,128]{1,0:T(8,128)S(1)} %get-tuple-element.26.before_ref, bf16[576,256]{1,0:T(8,128)(2,1)S(1)} %get-tuple-element.27.row_ref, f32[1,256]{1,0:T(1,128)S(1)} %get-tuple-element.28.scale_ref, f32[8,256]{1,0:T(8,128)S(1)} %get-tuple-element.29.mask_ref, ...), custom_call_target="tpu_custom_call" | custom-call | tf_op jit(solution)/shard_map/pallas_call | solution.py:198
  28.4 0.8 %collective-permute-start.11 = (f32[128,128]{1,0:T(8,128)S(1)}, f32[128,128]{1,0:T(8,128)S(1)}, u32[]{:S(2)}, u32[]{:S(2)}) collective-permute-start(f32[128,128]{1,0:T(8,128)S(1)} %get-tuple-element.31), channel_id=1, source_target_pairs={{0,8},{4,12},{8,0},{12,4},{16,24},{20,28},{24,16},{28,20},{1,9},{5... | collective-permute-start | bytes 196616 | tf_op jit(solution)/shard_map/ppermute | solution.py:113
  29.2 0.5 %collective-permute-done.12.refs_0_ = f32[128,128]{1,0:T(8,128)S(1)} collective-permute-done((f32[128,128]{1,0:T(8,128)S(1)}, f32[128,128]{1,0:T(8,128)S(1)}, u32[]{:S(2)}, u32[]{:S(2)}) %collective-permute-start.12) | collective-permute-done | bytes 65568 | tf_op jit(solution)/shard_map/ppermute | solution.py:113
  29.7 1.4 %collective-permute-done.13.refs_1_ = f32[128,128]{1,0:T(8,128)S(1)} collective-permute-done((f32[128,128]{1,0:T(8,128)S(1)}, f32[128,128]{1,0:T(8,128)S(1)}, u32[]{:S(2)}, u32[]{:S(2)}) %collective-permute-start.13) | collective-permute-done | bytes 65568 | tf_op jit(solution)/shard_map/ppermute | solution.py:113
  31.1 1.7 %collective-permute-done.11 = f32[128,128]{1,0:T(8,128)S(1)} collective-permute-done((f32[128,128]{1,0:T(8,128)S(1)}, f32[128,128]{1,0:T(8,128)S(1)}, u32[]{:S(2)}, u32[]{:S(2)}) %collective-permute-start.11) | collective-permute-done | bytes 65568 | tf_op jit(solution)/shard_map/ppermute | solution.py:113
  32.8 0.6 %add_add_fusion = f32[128,128]{1,0:T(8,128)} fusion(f32[128,128]{1,0:T(8,128)S(1)} %shard_map.57, f32[128,128]{1,0:T(8,128)S(1)} %get-tuple-element.30, f32[128,128]{1,0:T(8,128)S(1)} %collective-permute-done.11), kind=kLoop, calls=%fused_computation | loop fusion | flops 32768 | bytes 262144 | tf_op jit(solution)/shard_map/add | solution.py:218
  (8 shorter events, 0.1 us)
Async XLA Ops:
  0.0 10.2 %copy-start.1 = (f32[128,128]{1,0:T(8,128)S(1)}, f32[128,128]{1,0:T(8,128)}, u32[]{:S(2)}) copy-start(f32[128,128]{1,0:T(8,128)} %refs_0_.3) | copy-start | bytes 196612
  0.0 10.2 %collective-permute-start = (f32[48,512]{1,0:T(8,128)}, f32[48,512]{1,0:T(8,128)S(1)}, u32[]{:S(2)}, u32[]{:S(2)}) collective-permute-start(f32[48,512]{1,0:T(8,128)} %refs_0_.5), channel_id=1, source_target_pairs={{0,2},{1,3},{2,0},{3,1},{4,6},{5,7},{6,4},{7,5},{8,10},{9,11},{10,... | collective-permute-start | bytes 294920 | tf_op jit(solution)/shard_map/ppermute | solution.py:113
  4.0 11.4 %collective-permute-start.1 = (f32[48,512]{1,0:T(8,128)}, f32[48,512]{1,0:T(8,128)S(1)}, u32[]{:S(2)}, u32[]{:S(2)}) collective-permute-start(f32[48,512]{1,0:T(8,128)} %refs_0_.5), channel_id=1, source_target_pairs={{0,1},{1,0},{2,3},{3,2},{4,5},{5,4},{6,7},{7,6},{8,9},{9,8},{10,11... | collective-permute-start | bytes 294920 | tf_op jit(solution)/shard_map/ppermute | solution.py:113
  5.6 9.8 %collective-permute-start.2 = (f32[48,512]{1,0:T(8,128)}, f32[48,512]{1,0:T(8,128)S(1)}, u32[]{:S(2)}, u32[]{:S(2)}) collective-permute-start(f32[48,512]{1,0:T(8,128)} %refs_0_.5), channel_id=1, source_target_pairs={{0,3},{1,2},{2,1},{3,0},{4,7},{5,6},{6,5},{7,4},{8,11},{9,10},{10,... | collective-permute-start | bytes 294920 | tf_op jit(solution)/shard_map/ppermute | solution.py:113
  5.6 0.7 %copy-start.2 = (s32[4,8]{1,0:T(4,128)S(1)}, s32[4,8]{1,0:T(4,128)}, u32[]{:S(2)}) copy-start(s32[4,8]{1,0:T(4,128)} %list_ref.1) | copy-start | bytes 388
  6.3 0.7 %copy-start.3 = (s32[4]{0:T(128)S(1)}, s32[4]{0:T(128)}, u32[]{:S(2)}) copy-start(s32[4]{0:T(128)} %count_ref.1) | copy-start | bytes 52
  10.2 8.9 %copy-start = (f32[48,512]{1,0:T(8,128)S(1)}, f32[48,512]{1,0:T(8,128)}, u32[]{:S(2)}) copy-start(f32[48,512]{1,0:T(8,128)} %refs_0_.5) | copy-start | bytes 294916
  10.2 8.3 %collective-permute-start.5 = (f32[128,128]{1,0:T(8,128)S(1)}, f32[128,128]{1,0:T(8,128)S(1)}, u32[]{:S(2)}, u32[]{:S(2)}) collective-permute-start(f32[128,128]{1,0:T(8,128)S(1)} %shard_map.48.refs_0_), channel_id=1, source_target_pairs={{0,1},{1,0},{2,3},{3,2},{4,5},{5,4},{6,7},{7,6},{8,9},{9,8},{10,11... | collective-permute-start | bytes 196616 | tf_op jit(solution)/shard_map/ppermute | solution.py:113
  10.7 8.4 %collective-permute-start.7 = (f32[128,128]{1,0:T(8,128)S(1)}, f32[128,128]{1,0:T(8,128)S(1)}, u32[]{:S(2)}, u32[]{:S(2)}) collective-permute-start(f32[128,128]{1,0:T(8,128)S(1)} %shard_map.48.refs_0_), channel_id=1, source_target_pairs={{0,2},{1,3},{2,0},{3,1},{4,6},{5,7},{6,4},{7,5},{8,10},{9,11},{10,... | collective-permute-start | bytes 196616 | tf_op jit(solution)/shard_map/ppermute | solution.py:113
  15.4 6.1 %collective-permute-start.8 = (f32[128,128]{1,0:T(8,128)S(1)}, f32[128,128]{1,0:T(8,128)S(1)}, u32[]{:S(2)}, u32[]{:S(2)}) collective-permute-start(f32[128,128]{1,0:T(8,128)S(1)} %shard_map.48.refs_0_), channel_id=1, source_target_pairs={{0,3},{1,2},{2,1},{3,0},{4,7},{5,6},{6,5},{7,4},{8,11},{9,10},{10,... | collective-permute-start | bytes 196616 | tf_op jit(solution)/shard_map/ppermute | solution.py:113
  15.5 6.4 %collective-permute-start.3 = (f32[200,128]{1,0:T(8,128)S(1)}, f32[200,128]{1,0:T(8,128)S(1)}, u32[]{:S(2)}, u32[]{:S(2)}) collective-permute-start(f32[200,128]{1,0:T(8,128)S(1)} %constant_dynamic-update-slice_fusion.refs_0_), channel_id=1, source_target_pairs={{0,24},{4,28},{8,16},{12,20},{16,8},{20,12},{24,0},{28,4},{1,25},{... | collective-permute-start | bytes 307208 | tf_op jit(solution)/shard_map/ppermute | solution.py:113
  18.0 4.9 %collective-permute-start.4 = (f32[200,128]{1,0:T(8,128)S(1)}, f32[200,128]{1,0:T(8,128)S(1)}, u32[]{:S(2)}, u32[]{:S(2)}) collective-permute-start(f32[200,128]{1,0:T(8,128)S(1)} %constant_dynamic-update-slice_fusion.refs_0_), channel_id=1, source_target_pairs={{0,16},{4,20},{8,24},{12,28},{16,0},{20,4},{24,8},{28,12},{1,17},{... | collective-permute-start | bytes 307208 | tf_op jit(solution)/shard_map/ppermute | solution.py:113
  18.5 8.8 %collective-permute-start.10 = (f32[200,128]{1,0:T(8,128)S(1)}, f32[200,128]{1,0:T(8,128)S(1)}, u32[]{:S(2)}, u32[]{:S(2)}) collective-permute-start(f32[200,128]{1,0:T(8,128)S(1)} %constant_dynamic-update-slice_fusion.refs_0_), channel_id=1, source_target_pairs={{0,8},{4,12},{8,0},{12,4},{16,24},{20,28},{24,16},{28,20},{1,9},{5... | collective-permute-start | bytes 307208 | tf_op jit(solution)/shard_map/ppermute | solution.py:113
  19.1 3.9 %collective-permute-start.6 = (f32[192,512]{1,0:T(8,128)S(1)}, f32[192,512]{1,0:T(8,128)S(1)}, u32[]{:S(2)}, u32[]{:S(2)}) collective-permute-start(f32[192,512]{1,0:T(8,128)S(1)} %shard_map.50), channel_id=1, source_target_pairs={{0,4},{4,0},{8,12},{12,8},{16,20},{20,16},{24,28},{28,24},{1,5},{5... | collective-permute-start | bytes 1179656 | tf_op jit(solution)/shard_map/ppermute | solution.py:113
  21.5 1.8 %collective-permute-start.9 = (f32[512,128]{1,0:T(8,128)S(1)}, f32[512,128]{1,0:T(8,128)S(1)}, u32[]{:S(2)}, u32[]{:S(2)}) collective-permute-start(f32[512,128]{1,0:T(8,128)S(1)} %shard_map.52.own_ref), channel_id=1, source_target_pairs={{0,4},{4,0},{8,12},{12,8},{16,20},{20,16},{24,28},{28,24},{1,5},{5... | collective-permute-start | bytes 786440 | tf_op jit(solution)/shard_map/ppermute | solution.py:113
  24.5 5.3 %collective-permute-start.12 = (f32[128,128]{1,0:T(8,128)S(1)}, f32[128,128]{1,0:T(8,128)S(1)}, u32[]{:S(2)}, u32[]{:S(2)}) collective-permute-start(f32[128,128]{1,0:T(8,128)S(1)} %get-tuple-element.26.before_ref), channel_id=1, source_target_pairs={{0,24},{4,28},{8,16},{12,20},{16,8},{20,12},{24,0},{28,4},{1,25},{... | collective-permute-start | bytes 196616 | tf_op jit(solution)/shard_map/ppermute | solution.py:113
  26.8 4.3 %collective-permute-start.13 = (f32[128,128]{1,0:T(8,128)S(1)}, f32[128,128]{1,0:T(8,128)S(1)}, u32[]{:S(2)}, u32[]{:S(2)}) collective-permute-start(f32[128,128]{1,0:T(8,128)S(1)} %get-tuple-element.32), channel_id=1, source_target_pairs={{0,16},{4,20},{8,24},{12,28},{16,0},{20,4},{24,8},{28,12},{1,17},{... | collective-permute-start | bytes 196616 | tf_op jit(solution)/shard_map/ppermute | solution.py:113
  28.4 4.3 %collective-permute-start.11 = (f32[128,128]{1,0:T(8,128)S(1)}, f32[128,128]{1,0:T(8,128)S(1)}, u32[]{:S(2)}, u32[]{:S(2)}) collective-permute-start(f32[128,128]{1,0:T(8,128)S(1)} %get-tuple-element.31), channel_id=1, source_target_pairs={{0,8},{4,12},{8,0},{12,4},{16,24},{20,28},{24,16},{28,20},{1,9},{5... | collective-permute-start | bytes 196616 | tf_op jit(solution)/shard_map/ppermute | solution.py:113

commit v8 on v4

--- a/solution.py
+++ b/solution.py
@@ -71,33 +71,30 @@
             mask_ref[spot : spot + 1, span] = jnp.max(hits, axis=0, keepdims=True)
 
 
-def apply_kernel(first, count, before_ref, row_ref, scale_ref, mask_ref, *refs):
+def apply_kernel(row_ref, scale_ref, mask_ref, *refs):
     own_cols, own_vecs, sibling_cols, sibling_vecs, *out_refs = refs
     width = out_refs[0].shape[1]
     group_cols = own_cols.shape[0]
     chunk = 2 * width
-    span = slice(first * width, (first + count) * width)
-    rows = row_ref[:, span]
-    total = None
+    pairs = range(len(out_refs) // 2)
+    totals = [None for _ in pairs]
     for group, (col_ref, vec_ref) in enumerate(((own_cols, own_vecs), (sibling_cols, sibling_vecs))):
         for start in range(0, group_cols, chunk):
-            inner = jnp.dot(col_ref[start : start + chunk, :], rows, preferred_element_type=jnp.float32)
             at = (group * group_cols + start) // width
-            both = [jnp.broadcast_to(mask_ref[spot : spot + 1, span], (width, count * width)) for spot in (at, at + 1)]
-            weight = stacked(jnp.exp(inner) * jnp.concatenate(both, axis=0), "hlh", 0)
-            vecs = vec_ref[:, 3 * start : 3 * (start + chunk)]
-            added = jnp.dot(vecs, weight, preferred_element_type=jnp.float32)
-            total = added if total is None else total + added
-    total = total * scale_ref[:, span]
-    for spot, out_ref in enumerate(out_refs):
-        out_ref[...] = total[:, spot * width : (spot + 1) * width]
-
-
-def add_kernel(*refs):
-    total = refs[0][...]
-    for ref in refs[1:-1]:
-        total = total + ref[...]
-    refs[-1][...] = total
+            for pair in pairs:
+                span = slice(pair * chunk, (pair + 1) * chunk)
+                inner = jnp.dot(
+                    col_ref[start : start + chunk, :], row_ref[:, span], preferred_element_type=jnp.float32
+                )
+                both = [jnp.broadcast_to(mask_ref[spot : spot + 1, span], (width, chunk)) for spot in (at, at + 1)]
+                weight = stacked(jnp.exp(inner) * jnp.concatenate(both, axis=0), "hlh", 0)
+                vecs = vec_ref[:, 3 * start : 3 * (start + chunk)]
+                added = jnp.dot(vecs, weight, preferred_element_type=jnp.float32)
+                totals[pair] = added if totals[pair] is None else totals[pair] + added
+    for pair in pairs:
+        total = totals[pair] * scale_ref[:, pair * chunk : (pair + 1) * chunk]
+        out_refs[2 * pair][...] = total[:, :width]
+        out_refs[2 * pair + 1][...] = total[:, width:]
 
 
 def swapped(value, axis, step):
@@ -167,31 +164,15 @@
         cost_estimate=hint,
     )(*panels)
     columns = [*columns_of(own_group), *columns_of(sibling_group)]
-    half = len(steps) // 2
-    tiles = {}
-    before = rows[1]
-    for first in (half, 0):
-        done = pl.pallas_call(
-            functools.partial(apply_kernel, first, half),
-            in_specs=[anywhere] + [vmem] * 7,
-            out_shape=[shape((eig_count, width), f32)] * half,
-            compiler_params=params,
-        )(before, *rows, *columns)
-        before = done[0]
-        for spot in range(half):
-            tiles[first + spot] = done[spot]
-
-    arrived = [swapped(tiles[place], "blk", steps[place]) for place in range(1, len(steps))]
-    far = pl.pallas_call(
-        add_kernel,
-        out_shape=shape((eig_count, width), f32),
+    tiles = pl.pallas_call(
+        apply_kernel,
+        out_shape=[shape((eig_count, width), f32)] * len(panels),
         compiler_params=params,
-        cost_estimate=hint,
-    )(*arrived[half - 1 :])
+    )(*rows, *columns)
     total = tiles[0]
-    for tile in arrived[: half - 1]:
-        total = total + tile
-    return total + far
+    for place in range(len(steps) - 1, 0, -1):
+        total = total + swapped(tiles[place], "blk", steps[place])
+    return total
 
 
 def solution(mesh):

time: 32.2 us -> 31.9 us (level)
    pallas_call x3 -> x1, Pallas kernels: 2.11 us -> 1.86 us  [shards(): pl.pallas_call(apply_kernel, out_shape=[shape((eig_count, width), f32)] *...]
  transfers between devices with their start and end apart: 13 -> 13, of which waited for: 8 -> 8; matrix products, arithmetic and copies ran while one was open for 2% -> 2% of each run, Pallas kernels for 7% -> 4%
where the time goes in v8:
time: 31.9 us; the launch traced here: 31.6 us
  starting transfers between devices  17.7 us (55%)
  waiting for transfers between devices  7.75 us (24%)
  Pallas kernels  3.27 us (10%)
  local copies, waits for them, and re-layouts  2.12 us (7%)
  other arithmetic  0.65 us (2%)
    ppermute x13, starting transfers between devices, swapped(): lax.ppermute(value, axis, [(source, source ^ step) for source in range(co...  17.7 us
    ppermute x13, waiting for transfers between devices, swapped(): lax.ppermute(value, axis, [(source, source ^ step) for source in range(co...  7.75 us
    unnamed x12, local copies, waits for them, and re-layouts  2.12 us
    pallas_call x1, Pallas kernels, shards(): pl.pallas_call(apply_kernel, out_shape=[shape((eig_count, width), f32)] *...  1.86 us
    add x1, other arithmetic, shards(): total = total + swapped(tiles[place], 'blk', steps[place])  0.65 us
  transfers between devices with their start and end apart: 13, of which 8 were waited for; matrix products, arithmetic and copies ran while one was open for 2% of the time, Pallas kernels for 4%

profile of v8, /device:TPU:0, one launch (start us, length us, event | category | flops | bytes accessed | tf_op | source)
XLA Modules:
  0.0 31.6 jit_solution(14759417394391287704)
XLA Ops:
  0.0 0.0 copy-start.1
  0.0 4.0 %collective-permute-start.1 = (f32[48,512]{1,0:T(8,128)}, f32[48,512]{1,0:T(8,128)S(1)}, u32[]{:S(2)}, u32[]{:S(2)}) collective-permute-start(f32[48,512]{1,0:T(8,128)} %refs_0_.1), channel_id=1, source_target_pairs={{0,2},{1,3},{2,0},{3,1},{4,6},{5,7},{6,4},{7,5},{8,10},{9,11},{10,... | collective-permute-start | bytes 294920 | tf_op jit(solution)/shard_map/ppermute | solution.py:102
  4.0 1.6 %collective-permute-start = (f32[48,512]{1,0:T(8,128)}, f32[48,512]{1,0:T(8,128)S(1)}, u32[]{:S(2)}, u32[]{:S(2)}) collective-permute-start(f32[48,512]{1,0:T(8,128)} %refs_0_.1), channel_id=1, source_target_pairs={{0,1},{1,0},{2,3},{3,2},{4,5},{5,4},{6,7},{7,6},{8,9},{9,8},{10,11... | collective-permute-start | bytes 294920 | tf_op jit(solution)/shard_map/ppermute | solution.py:102
  5.6 0.0 collective-permute-start.2
  5.6 0.0 copy-start.2
  5.6 0.7 %copy-done.2 = s32[4,8]{1,0:T(4,128)S(1)} copy-done((s32[4,8]{1,0:T(4,128)S(1)}, s32[4,8]{1,0:T(4,128)}, u32[]{:S(2)}) %copy-start.2) | copy-done | bytes 152
  6.3 0.0 copy-start.3
  6.3 0.7 %copy-done.3 = s32[4]{0:T(128)S(1)} copy-done((s32[4]{0:T(128)S(1)}, s32[4]{0:T(128)}, u32[]{:S(2)}) %copy-start.3) | copy-done | bytes 40
  7.0 0.6 %shard_map.46 = f32[8,128]{1,0:T(8,128)S(1)} custom-call(s32[4,8]{1,0:T(4,128)S(1)} %copy-done.2, s32[4]{0:T(128)S(1)} %copy-done.3), custom_call_target="tpu_custom_call" | custom-call | tf_op jit(solution)/shard_map/pallas_call | solution.py:129
  7.6 0.7 %dynamic-slice_dynamic-update-slice_fusion.3 = f32[200,128]{1,0:T(8,128)S(1)} fusion(f32[48,512]{1,0:T(8,128)} %refs_0_.1, s32[]{:T(128)S(6)} %select_n.2), kind=kLoop, calls=%fused_computation.4 | loop fusion | bytes 49156
  8.3 1.2 %collective-permute-done.before_ref.refs_1_ = f32[48,512]{1,0:T(8,128)S(1)} collective-permute-done((f32[48,512]{1,0:T(8,128)}, f32[48,512]{1,0:T(8,128)S(1)}, u32[]{:S(2)}, u32[]{:S(2)}) %collective-permute-start) | collective-permute-done | bytes 98336 | tf_op jit(solution)/shard_map/ppermute | solution.py:102
  9.5 0.0 copy-done.1
  9.5 0.0 copy-start
  9.5 2.4 %collective-permute-start.8 = (f32[128,128]{1,0:T(8,128)S(1)}, f32[128,128]{1,0:T(8,128)S(1)}, u32[]{:S(2)}, u32[]{:S(2)}) collective-permute-start(f32[128,128]{1,0:T(8,128)S(1)} %shard_map.48.refs_7_), channel_id=1, source_target_pairs={{0,1},{1,0},{2,3},{3,2},{4,5},{5,4},{6,7},{7,6},{8,9},{9,8},{10,11... | collective-permute-start | bytes 196616 | tf_op jit(solution)/shard_map/ppermute | solution.py:102
  12.0 0.8 %collective-permute-start.7 = (f32[128,128]{1,0:T(8,128)S(1)}, f32[128,128]{1,0:T(8,128)S(1)}, u32[]{:S(2)}, u32[]{:S(2)}) collective-permute-start(f32[128,128]{1,0:T(8,128)S(1)} %shard_map.48.refs_7_), channel_id=1, source_target_pairs={{0,2},{1,3},{2,0},{3,1},{4,6},{5,7},{6,4},{7,5},{8,10},{9,11},{10,... | collective-permute-start | bytes 196616 | tf_op jit(solution)/shard_map/ppermute | solution.py:102
  12.8 1.6 %collective-permute-start.6 = (f32[128,128]{1,0:T(8,128)S(1)}, f32[128,128]{1,0:T(8,128)S(1)}, u32[]{:S(2)}, u32[]{:S(2)}) collective-permute-start(f32[128,128]{1,0:T(8,128)S(1)} %shard_map.48.refs_7_), channel_id=1, source_target_pairs={{0,3},{1,2},{2,1},{3,0},{4,7},{5,6},{6,5},{7,4},{8,11},{9,10},{10,... | collective-permute-start | bytes 196616 | tf_op jit(solution)/shard_map/ppermute | solution.py:102
  14.4 0.0 collective-permute-done.1.refs_2_
  14.4 0.0 collective-permute-done.2.refs_3_
  14.5 2.5 %collective-permute-start.5 = (f32[200,128]{1,0:T(8,128)S(1)}, f32[200,128]{1,0:T(8,128)S(1)}, u32[]{:S(2)}, u32[]{:S(2)}) collective-permute-start(f32[200,128]{1,0:T(8,128)S(1)} %constant_dynamic-update-slice_fusion.refs_0_), channel_id=1, source_target_pairs={{0,24},{4,28},{8,16},{12,20},{16,8},{20,12},{24,0},{28,4},{1,25},{... | collective-permute-start | bytes 307208 | tf_op jit(solution)/shard_map/ppermute | solution.py:102
  17.0 0.5 %collective-permute-start.4 = (f32[200,128]{1,0:T(8,128)S(1)}, f32[200,128]{1,0:T(8,128)S(1)}, u32[]{:S(2)}, u32[]{:S(2)}) collective-permute-start(f32[200,128]{1,0:T(8,128)S(1)} %constant_dynamic-update-slice_fusion.refs_0_), channel_id=1, source_target_pairs={{0,16},{4,20},{8,24},{12,28},{16,0},{20,4},{24,8},{28,12},{1,17},{... | collective-permute-start | bytes 307208 | tf_op jit(solution)/shard_map/ppermute | solution.py:102
  17.5 0.0 collective-permute-done.8.refs_6_
  17.5 0.5 %collective-permute-start.3 = (f32[200,128]{1,0:T(8,128)S(1)}, f32[200,128]{1,0:T(8,128)S(1)}, u32[]{:S(2)}, u32[]{:S(2)}) collective-permute-start(f32[200,128]{1,0:T(8,128)S(1)} %constant_dynamic-update-slice_fusion.refs_0_), channel_id=1, source_target_pairs={{0,8},{4,12},{8,0},{12,4},{16,24},{20,28},{24,16},{28,20},{1,9},{5... | collective-permute-start | bytes 307208 | tf_op jit(solution)/shard_map/ppermute | solution.py:102
  18.0 0.0 collective-permute-done.7.refs_5_
  18.0 0.9 %collective-permute-done.6.refs_4_ = f32[128,128]{1,0:T(8,128)S(1)} collective-permute-done((f32[128,128]{1,0:T(8,128)S(1)}, f32[128,128]{1,0:T(8,128)S(1)}, u32[]{:S(2)}, u32[]{:S(2)}) %collective-permute-start.6) | collective-permute-done | bytes 65568 | tf_op jit(solution)/shard_map/ppermute | solution.py:102
  19.0 0.0 copy-done
  19.0 0.1 shard_map.49.group_ref
  19.0 0.1 collective-permute-start.9
  19.1 0.3 shard_map.50
  19.4 1.0 %collective-permute-done.5.refs_3_ = f32[200,128]{1,0:T(8,128)S(1)} collective-permute-done((f32[200,128]{1,0:T(8,128)S(1)}, f32[200,128]{1,0:T(8,128)S(1)}, u32[]{:S(2)}, u32[]{:S(2)}) %collective-permute-start.5) | collective-permute-done | bytes 102432 | tf_op jit(solution)/shard_map/ppermute | solution.py:102
  20.4 1.2 %collective-permute-done.4.refs_2_ = f32[200,128]{1,0:T(8,128)S(1)} collective-permute-done((f32[200,128]{1,0:T(8,128)S(1)}, f32[200,128]{1,0:T(8,128)S(1)}, u32[]{:S(2)}, u32[]{:S(2)}) %collective-permute-start.4) | collective-permute-done | bytes 102432 | tf_op jit(solution)/shard_map/ppermute | solution.py:102
  21.6 0.5 %collective-permute-done.3.refs_1_ = f32[200,128]{1,0:T(8,128)S(1)} collective-permute-done((f32[200,128]{1,0:T(8,128)S(1)}, f32[200,128]{1,0:T(8,128)S(1)}, u32[]{:S(2)}, u32[]{:S(2)}) %collective-permute-start.3) | collective-permute-done | bytes 102432 | tf_op jit(solution)/shard_map/ppermute | solution.py:102
  22.1 0.2 shard_map.47
  22.3 0.0 collective-permute-done.9.group_ref
  22.3 0.3 shard_map.51
  22.6 1.9 %shard_map.52 = (f32[128,128]{1,0:T(8,128)S(1)}, f32[128,128]{1,0:T(8,128)S(1)}, f32[128,128]{1,0:T(8,128)S(1)}, f32[128,128]{1,0:T(8,128)S(1)}) custom-call(bf16[576,512]{1,0:T(8,128)(2,1)S(1)} %get-tuple-element.16.row_ref, f32[1,512]{1,0:T(1,128)S(1)} %get-tuple-element.17.scale_ref, f32[8,512]{1,0:T(8,128)S(1)} %get-tuple-element.18.mask_ref, ...), custom_call_target="tpu_custom_call" | custom-call | tf_op jit(solution)/shard_map/pallas_call | solution.py:167
  24.5 1.6 %collective-permute-start.10 = (f32[128,128]{1,0:T(8,128)S(1)}, f32[128,128]{1,0:T(8,128)S(1)}, u32[]{:S(2)}, u32[]{:S(2)}) collective-permute-start(f32[128,128]{1,0:T(8,128)S(1)} %get-tuple-element.24), channel_id=1, source_target_pairs={{0,24},{4,28},{8,16},{12,20},{16,8},{20,12},{24,0},{28,4},{1,25},{... | collective-permute-start | bytes 196616 | tf_op jit(solution)/shard_map/ppermute | solution.py:102
  26.1 0.6 %collective-permute-start.11 = (f32[128,128]{1,0:T(8,128)S(1)}, f32[128,128]{1,0:T(8,128)S(1)}, u32[]{:S(2)}, u32[]{:S(2)}) collective-permute-start(f32[128,128]{1,0:T(8,128)S(1)} %get-tuple-element.25), channel_id=1, source_target_pairs={{0,16},{4,20},{8,24},{12,28},{16,0},{20,4},{24,8},{28,12},{1,17},{... | collective-permute-start | bytes 196616 | tf_op jit(solution)/shard_map/ppermute | solution.py:102
  26.7 1.4 %collective-permute-start.12 = (f32[128,128]{1,0:T(8,128)S(1)}, f32[128,128]{1,0:T(8,128)S(1)}, u32[]{:S(2)}, u32[]{:S(2)}) collective-permute-start(f32[128,128]{1,0:T(8,128)S(1)} %get-tuple-element.26), channel_id=1, source_target_pairs={{0,8},{4,12},{8,0},{12,4},{16,24},{20,28},{24,16},{28,20},{1,9},{5... | collective-permute-start | bytes 196616 | tf_op jit(solution)/shard_map/ppermute | solution.py:102
  28.1 2.0 %collective-permute-done.10 = f32[128,128]{1,0:T(8,128)S(1)} collective-permute-done((f32[128,128]{1,0:T(8,128)S(1)}, f32[128,128]{1,0:T(8,128)S(1)}, u32[]{:S(2)}, u32[]{:S(2)}) %collective-permute-start.10) | collective-permute-done | bytes 65568 | tf_op jit(solution)/shard_map/ppermute | solution.py:102
  30.0 0.5 %collective-permute-done.11 = f32[128,128]{1,0:T(8,128)S(1)} collective-permute-done((f32[128,128]{1,0:T(8,128)S(1)}, f32[128,128]{1,0:T(8,128)S(1)}, u32[]{:S(2)}, u32[]{:S(2)}) %collective-permute-start.11) | collective-permute-done | bytes 65568 | tf_op jit(solution)/shard_map/ppermute | solution.py:102
  30.5 0.4 %collective-permute-done.12 = f32[128,128]{1,0:T(8,128)S(1)} collective-permute-done((f32[128,128]{1,0:T(8,128)S(1)}, f32[128,128]{1,0:T(8,128)S(1)}, u32[]{:S(2)}, u32[]{:S(2)}) %collective-permute-start.12) | collective-permute-done | bytes 65568 | tf_op jit(solution)/shard_map/ppermute | solution.py:102
  30.9 0.6 %add_add_fusion = f32[128,128]{1,0:T(8,128)} fusion(f32[128,128]{1,0:T(8,128)S(1)} %collective-permute-done.12, f32[128,128]{1,0:T(8,128)S(1)} %collective-permute-done.11, f32[128,128]{1,0:T(8,128)S(1)} %get-tuple-element.23, f32[128,128]{1,0:T(8,128)S(1)} %collective-permute-done.10), kind=kLoop, calls=%fused_computation | loop fusion | flops 49152 | bytes 327680 | tf_op jit(solution)/shard_map/add | solution.py:174
  (5 shorter events, 0.0 us)
Async XLA Ops:
  0.0 9.5 %copy-start.1 = (f32[128,128]{1,0:T(8,128)S(1)}, f32[128,128]{1,0:T(8,128)}, u32[]{:S(2)}) copy-start(f32[128,128]{1,0:T(8,128)} %in_ref.1) | copy-start | bytes 196612
  0.0 14.4 %collective-permute-start.1 = (f32[48,512]{1,0:T(8,128)}, f32[48,512]{1,0:T(8,128)S(1)}, u32[]{:S(2)}, u32[]{:S(2)}) collective-permute-start(f32[48,512]{1,0:T(8,128)} %refs_0_.1), channel_id=1, source_target_pairs={{0,2},{1,3},{2,0},{3,1},{4,6},{5,7},{6,4},{7,5},{8,10},{9,11},{10,... | collective-permute-start | bytes 294920 | tf_op jit(solution)/shard_map/ppermute | solution.py:102
  4.0 5.4 %collective-permute-start = (f32[48,512]{1,0:T(8,128)}, f32[48,512]{1,0:T(8,128)S(1)}, u32[]{:S(2)}, u32[]{:S(2)}) collective-permute-start(f32[48,512]{1,0:T(8,128)} %refs_0_.1), channel_id=1, source_target_pairs={{0,1},{1,0},{2,3},{3,2},{4,5},{5,4},{6,7},{7,6},{8,9},{9,8},{10,11... | collective-permute-start | bytes 294920 | tf_op jit(solution)/shard_map/ppermute | solution.py:102
  5.6 8.8 %collective-permute-start.2 = (f32[48,512]{1,0:T(8,128)}, f32[48,512]{1,0:T(8,128)S(1)}, u32[]{:S(2)}, u32[]{:S(2)}) collective-permute-start(f32[48,512]{1,0:T(8,128)} %refs_0_.1), channel_id=1, source_target_pairs={{0,3},{1,2},{2,1},{3,0},{4,7},{5,6},{6,5},{7,4},{8,11},{9,10},{10,... | collective-permute-start | bytes 294920 | tf_op jit(solution)/shard_map/ppermute | solution.py:102
  5.6 0.7 %copy-start.2 = (s32[4,8]{1,0:T(4,128)S(1)}, s32[4,8]{1,0:T(4,128)}, u32[]{:S(2)}) copy-start(s32[4,8]{1,0:T(4,128)} %list_ref.1) | copy-start | bytes 388
  6.3 0.7 %copy-start.3 = (s32[4]{0:T(128)S(1)}, s32[4]{0:T(128)}, u32[]{:S(2)}) copy-start(s32[4]{0:T(128)} %count_ref.1) | copy-start | bytes 52
  9.5 9.5 %copy-start = (f32[48,512]{1,0:T(8,128)S(1)}, f32[48,512]{1,0:T(8,128)}, u32[]{:S(2)}) copy-start(f32[48,512]{1,0:T(8,128)} %refs_0_.1) | copy-start | bytes 294916
  9.5 8.0 %collective-permute-start.8 = (f32[128,128]{1,0:T(8,128)S(1)}, f32[128,128]{1,0:T(8,128)S(1)}, u32[]{:S(2)}, u32[]{:S(2)}) collective-permute-start(f32[128,128]{1,0:T(8,128)S(1)} %shard_map.48.refs_7_), channel_id=1, source_target_pairs={{0,1},{1,0},{2,3},{3,2},{4,5},{5,4},{6,7},{7,6},{8,9},{9,8},{10,11... | collective-permute-start | bytes 196616 | tf_op jit(solution)/shard_map/ppermute | solution.py:102
  12.0 6.1 %collective-permute-start.7 = (f32[128,128]{1,0:T(8,128)S(1)}, f32[128,128]{1,0:T(8,128)S(1)}, u32[]{:S(2)}, u32[]{:S(2)}) collective-permute-start(f32[128,128]{1,0:T(8,128)S(1)} %shard_map.48.refs_7_), channel_id=1, source_target_pairs={{0,2},{1,3},{2,0},{3,1},{4,6},{5,7},{6,4},{7,5},{8,10},{9,11},{10,... | collective-permute-start | bytes 196616 | tf_op jit(solution)/shard_map/ppermute | solution.py:102
  12.8 6.2 %collective-permute-start.6 = (f32[128,128]{1,0:T(8,128)S(1)}, f32[128,128]{1,0:T(8,128)S(1)}, u32[]{:S(2)}, u32[]{:S(2)}) collective-permute-start(f32[128,128]{1,0:T(8,128)S(1)} %shard_map.48.refs_7_), channel_id=1, source_target_pairs={{0,3},{1,2},{2,1},{3,0},{4,7},{5,6},{6,5},{7,4},{8,11},{9,10},{10,... | collective-permute-start | bytes 196616 | tf_op jit(solution)/shard_map/ppermute | solution.py:102
  14.5 6.0 %collective-permute-start.5 = (f32[200,128]{1,0:T(8,128)S(1)}, f32[200,128]{1,0:T(8,128)S(1)}, u32[]{:S(2)}, u32[]{:S(2)}) collective-permute-start(f32[200,128]{1,0:T(8,128)S(1)} %constant_dynamic-update-slice_fusion.refs_0_), channel_id=1, source_target_pairs={{0,24},{4,28},{8,16},{12,20},{16,8},{20,12},{24,0},{28,4},{1,25},{... | collective-permute-start | bytes 307208 | tf_op jit(solution)/shard_map/ppermute | solution.py:102
  17.0 4.7 %collective-permute-start.4 = (f32[200,128]{1,0:T(8,128)S(1)}, f32[200,128]{1,0:T(8,128)S(1)}, u32[]{:S(2)}, u32[]{:S(2)}) collective-permute-start(f32[200,128]{1,0:T(8,128)S(1)} %constant_dynamic-update-slice_fusion.refs_0_), channel_id=1, source_target_pairs={{0,16},{4,20},{8,24},{12,28},{16,0},{20,4},{24,8},{28,12},{1,17},{... | collective-permute-start | bytes 307208 | tf_op jit(solution)/shard_map/ppermute | solution.py:102
  17.5 4.7 %collective-permute-start.3 = (f32[200,128]{1,0:T(8,128)S(1)}, f32[200,128]{1,0:T(8,128)S(1)}, u32[]{:S(2)}, u32[]{:S(2)}) collective-permute-start(f32[200,128]{1,0:T(8,128)S(1)} %constant_dynamic-update-slice_fusion.refs_0_), channel_id=1, source_target_pairs={{0,8},{4,12},{8,0},{12,4},{16,24},{20,28},{24,16},{28,20},{1,9},{5... | collective-permute-start | bytes 307208 | tf_op jit(solution)/shard_map/ppermute | solution.py:102
  19.0 3.3 %collective-permute-start.9 = (f32[320,512]{1,0:T(8,128)S(1)}, f32[320,512]{1,0:T(8,128)S(1)}, u32[]{:S(2)}, u32[]{:S(2)}) collective-permute-start(f32[320,512]{1,0:T(8,128)S(1)} %shard_map.49.group_ref), channel_id=1, source_target_pairs={{0,4},{4,0},{8,12},{12,8},{16,20},{20,16},{24,28},{28,24},{1,5},{5... | collective-permute-start | bytes 1966088 | tf_op jit(solution)/shard_map/ppermute | solution.py:102
  24.5 5.5 %collective-permute-start.10 = (f32[128,128]{1,0:T(8,128)S(1)}, f32[128,128]{1,0:T(8,128)S(1)}, u32[]{:S(2)}, u32[]{:S(2)}) collective-permute-start(f32[128,128]{1,0:T(8,128)S(1)} %get-tuple-element.24), channel_id=1, source_target_pairs={{0,24},{4,28},{8,16},{12,20},{16,8},{20,12},{24,0},{28,4},{1,25},{... | collective-permute-start | bytes 196616 | tf_op jit(solution)/shard_map/ppermute | solution.py:102
  26.1 4.5 %collective-permute-start.11 = (f32[128,128]{1,0:T(8,128)S(1)}, f32[128,128]{1,0:T(8,128)S(1)}, u32[]{:S(2)}, u32[]{:S(2)}) collective-permute-start(f32[128,128]{1,0:T(8,128)S(1)} %get-tuple-element.25), channel_id=1, source_target_pairs={{0,16},{4,20},{8,24},{12,28},{16,0},{20,4},{24,8},{28,12},{1,17},{... | collective-permute-start | bytes 196616 | tf_op jit(solution)/shard_map/ppermute | solution.py:102
  26.7 4.3 %collective-permute-start.12 = (f32[128,128]{1,0:T(8,128)S(1)}, f32[128,128]{1,0:T(8,128)S(1)}, u32[]{:S(2)}, u32[]{:S(2)}) collective-permute-start(f32[128,128]{1,0:T(8,128)S(1)} %get-tuple-element.26), channel_id=1, source_target_pairs={{0,8},{4,12},{8,0},{12,4},{16,24},{20,28},{24,16},{28,20},{1,9},{5... | collective-permute-start | bytes 196616 | tf_op jit(solution)/shard_map/ppermute | solution.py:102

commit v9 on v8

--- a/solution.py
+++ b/solution.py
@@ -16,9 +16,11 @@
     return high, (value - high.astype(jnp.float32)).astype(jnp.bfloat16)
 
 
-def stacked(value, order, axis):
-    high, low = halves(value)
-    return jnp.concatenate([{"h": high, "l": low}[letter] for letter in order], axis=axis)
+def three_pass(left_both, right_high, right_low):
+    size = left_both.shape[0] // 2
+    mul = functools.partial(jnp.dot, preferred_element_type=jnp.float32)
+    first = mul(left_both, right_high)
+    return (first[:size] + first[size:]) + mul(left_both[:size], right_low)
 
 
 def lists_kernel(list_ref, count_ref, out_ref):
@@ -46,16 +48,20 @@
 
 
 def columns_kernel(feat_count, group_ref, col_ref, vec_ref):
-    chunk = 2 * vec_ref.shape[0]
+    eig_count = vec_ref.shape[0] // 2
+    chunk = 2 * eig_count
     cols = group_ref[:feat_count, :]
-    col_ref[...] = stacked(cols.T, "hhl", 1)
+    flipped = cols.T
+    for start in range(0, cols.shape[1], chunk):
+        high, low = halves(flipped[start : start + chunk, :])
+        col_ref[2 * start : 2 * start + chunk, :] = high
+        col_ref[2 * start + chunk : 2 * (start + chunk), :] = low
     vecs = group_ref[feat_count:, :] * jnp.exp(jnp.sum(cols * cols, axis=0, keepdims=True) * (-1.0 / feat_count))
-    for start in range(0, cols.shape[1], chunk):
-        vec_ref[:, 3 * start : 3 * (start + chunk)] = stacked(vecs[:, start : start + chunk], "hhl", 1)
+    vec_ref[:eig_count, :], vec_ref[eig_count:, :] = halves(vecs)
 
 
 def rows_kernel(feat_count, *refs):
-    panel_refs, (row_ref, scale_ref, mask_ref) = refs[:-3], refs[-3:]
+    panel_refs, (high_ref, low_ref, scale_ref, mask_ref) = refs[:-4], refs[-4:]
     width = panel_refs[0].shape[1]
     group_blocks = mask_ref.shape[0] // 2
     blk_index = lax.axis_index("blk")
@@ -63,7 +69,7 @@
         span = slice(place * width, (place + 1) * width)
         rows = ref[:feat_count, :]
         scale_ref[:, span] = jnp.exp(jnp.sum(rows * rows, axis=0, keepdims=True) * (-1.0 / feat_count))
-        row_ref[:, span] = stacked(rows * (2.0 / feat_count), "hlh", 0)
+        high_ref[:, span], low_ref[:, span] = halves(rows * (2.0 / feat_count))
         lists = ref[feat_count:, :]
         for spot in range(2 * group_blocks):
             column = (blk_index ^ (spot // group_blocks)) * group_blocks + spot % group_blocks
@@ -71,10 +77,10 @@
             mask_ref[spot : spot + 1, span] = jnp.max(hits, axis=0, keepdims=True)
 
 
-def apply_kernel(row_ref, scale_ref, mask_ref, *refs):
+def apply_kernel(high_ref, low_ref, scale_ref, mask_ref, *refs):
     own_cols, own_vecs, sibling_cols, sibling_vecs, *out_refs = refs
     width = out_refs[0].shape[1]
-    group_cols = own_cols.shape[0]
+    group_cols = own_vecs.shape[1]
     chunk = 2 * width
     pairs = range(len(out_refs) // 2)
     totals = [None for _ in pairs]
@@ -83,13 +89,10 @@
             at = (group * group_cols + start) // width
             for pair in pairs:
                 span = slice(pair * chunk, (pair + 1) * chunk)
-                inner = jnp.dot(
-                    col_ref[start : start + chunk, :], row_ref[:, span], preferred_element_type=jnp.float32
-                )
+                inner = three_pass(col_ref[2 * start : 2 * (start + chunk), :], high_ref[:, span], low_ref[:, span])
                 both = [jnp.broadcast_to(mask_ref[spot : spot + 1, span], (width, chunk)) for spot in (at, at + 1)]
-                weight = stacked(jnp.exp(inner) * jnp.concatenate(both, axis=0), "hlh", 0)
-                vecs = vec_ref[:, 3 * start : 3 * (start + chunk)]
-                added = jnp.dot(vecs, weight, preferred_element_type=jnp.float32)
+                weight = jnp.exp(inner) * jnp.concatenate(both, axis=0)
+                added = three_pass(vec_ref[:, start : start + chunk], *halves(weight))
                 totals[pair] = added if totals[pair] is None else totals[pair] + added
     for pair in pairs:
         total = totals[pair] * scale_ref[:, pair * chunk : (pair + 1) * chunk]
@@ -148,7 +151,7 @@
     def columns_of(group):
         return pl.pallas_call(
             functools.partial(columns_kernel, feat_count),
-            out_shape=[shape((group_cols, 3 * feat_count), bf16), shape((eig_count, 3 * group_cols), bf16)],
+            out_shape=[shape((2 * group_cols, feat_count), bf16), shape((2 * eig_count, group_cols), bf16)],
             compiler_params=params,
         )(group)
 
@@ -156,7 +159,8 @@
     rows = pl.pallas_call(
         functools.partial(rows_kernel, feat_count),
         out_shape=[
-            shape((3 * feat_count, row_count), bf16),
+            shape((feat_count, row_count), bf16),
+            shape((feat_count, row_count), bf16),
             shape((1, row_count), f32),
             shape((2 * group_blocks, row_count), f32),
         ],

time: 31.9 us -> 33.5 us (1.050)
  Pallas kernels: 3.27 us -> 4.8 us
    pallas_call x1, Pallas kernels: 1.86 us -> 3.57 us  [shards(): pl.pallas_call(apply_kernel, out_shape=[shape((eig_count, width), f32)] *...]
  transfers between devices with their start and end apart: 13 -> 13, of which waited for: 8 -> 8; matrix products, arithmetic and copies ran while one was open for 2% -> 2% of each run, Pallas kernels for 4% -> 3%
where the time goes in v9:
time: 33.5 us; the launch traced here: 33.2 us
  starting transfers between devices  17.7 us (53%)
  waiting for transfers between devices  7.83 us (23%)
  Pallas kernels  4.8 us (14%)
  local copies, waits for them, and re-layouts  2.12 us (6%)
  other arithmetic  0.65 us (2%)
    ppermute x13, starting transfers between devices, swapped(): lax.ppermute(value, axis, [(source, source ^ step) for source in range(co...  17.7 us
    ppermute x13, waiting for transfers between devices, swapped(): lax.ppermute(value, axis, [(source, source ^ step) for source in range(co...  7.83 us
    pallas_call x1, Pallas kernels, shards(): pl.pallas_call(apply_kernel, out_shape=[shape((eig_count, width), f32)] *...  3.57 us
    unnamed x12, local copies, waits for them, and re-layouts  2.12 us
  transfers between devices with their start and end apart: 13, of which 8 were waited for; matrix products, arithmetic and copies ran while one was open for 2% of the time, Pallas kernels for 3%

profile of v9, /device:TPU:0, one launch (start us, length us, event | category | flops | bytes accessed | tf_op | source)
XLA Modules:
  0.0 33.2 jit_solution(678545160400354762)
XLA Ops:
  0.0 0.0 copy-start.1
  0.0 4.0 %collective-permute-start.1 = (f32[48,512]{1,0:T(8,128)}, f32[48,512]{1,0:T(8,128)S(1)}, u32[]{:S(2)}, u32[]{:S(2)}) collective-permute-start(f32[48,512]{1,0:T(8,128)} %refs_0_.1), channel_id=1, source_target_pairs={{0,2},{1,3},{2,0},{3,1},{4,6},{5,7},{6,4},{7,5},{8,10},{9,11},{10,... | collective-permute-start | bytes 294920 | tf_op jit(solution)/shard_map/ppermute | solution.py:105
  4.0 1.6 %collective-permute-start = (f32[48,512]{1,0:T(8,128)}, f32[48,512]{1,0:T(8,128)S(1)}, u32[]{:S(2)}, u32[]{:S(2)}) collective-permute-start(f32[48,512]{1,0:T(8,128)} %refs_0_.1), channel_id=1, source_target_pairs={{0,1},{1,0},{2,3},{3,2},{4,5},{5,4},{6,7},{7,6},{8,9},{9,8},{10,11... | collective-permute-start | bytes 294920 | tf_op jit(solution)/shard_map/ppermute | solution.py:105
  5.6 0.0 collective-permute-start.2
  5.6 0.0 copy-start.2
  5.6 0.7 %copy-done.2 = s32[4,8]{1,0:T(4,128)S(1)} copy-done((s32[4,8]{1,0:T(4,128)S(1)}, s32[4,8]{1,0:T(4,128)}, u32[]{:S(2)}) %copy-start.2) | copy-done | bytes 152
  6.3 0.0 copy-start.3
  6.3 0.7 %copy-done.3 = s32[4]{0:T(128)S(1)} copy-done((s32[4]{0:T(128)S(1)}, s32[4]{0:T(128)}, u32[]{:S(2)}) %copy-start.3) | copy-done | bytes 40
  7.0 0.6 %shard_map.46 = f32[8,128]{1,0:T(8,128)S(1)} custom-call(s32[4,8]{1,0:T(4,128)S(1)} %copy-done.2, s32[4]{0:T(128)S(1)} %copy-done.3), custom_call_target="tpu_custom_call" | custom-call | tf_op jit(solution)/shard_map/pallas_call | solution.py:132
  7.6 0.7 %dynamic-slice_dynamic-update-slice_fusion.3 = f32[200,128]{1,0:T(8,128)S(1)} fusion(f32[48,512]{1,0:T(8,128)} %refs_0_.1, s32[]{:T(128)S(6)} %select_n.2), kind=kLoop, calls=%fused_computation.4 | loop fusion | bytes 49156
  8.3 1.2 %collective-permute-done.before_ref.refs_1_ = f32[48,512]{1,0:T(8,128)S(1)} collective-permute-done((f32[48,512]{1,0:T(8,128)}, f32[48,512]{1,0:T(8,128)S(1)}, u32[]{:S(2)}, u32[]{:S(2)}) %collective-permute-start) | collective-permute-done | bytes 98336 | tf_op jit(solution)/shard_map/ppermute | solution.py:105
  9.5 0.0 copy-done.1
  9.5 0.0 copy-start
  9.5 2.4 %collective-permute-start.8 = (f32[128,128]{1,0:T(8,128)S(1)}, f32[128,128]{1,0:T(8,128)S(1)}, u32[]{:S(2)}, u32[]{:S(2)}) collective-permute-start(f32[128,128]{1,0:T(8,128)S(1)} %shard_map.48.refs_7_), channel_id=1, source_target_pairs={{0,1},{1,0},{2,3},{3,2},{4,5},{5,4},{6,7},{7,6},{8,9},{9,8},{10,11... | collective-permute-start | bytes 196616 | tf_op jit(solution)/shard_map/ppermute | solution.py:105
  12.0 0.8 %collective-permute-start.7 = (f32[128,128]{1,0:T(8,128)S(1)}, f32[128,128]{1,0:T(8,128)S(1)}, u32[]{:S(2)}, u32[]{:S(2)}) collective-permute-start(f32[128,128]{1,0:T(8,128)S(1)} %shard_map.48.refs_7_), channel_id=1, source_target_pairs={{0,2},{1,3},{2,0},{3,1},{4,6},{5,7},{6,4},{7,5},{8,10},{9,11},{10,... | collective-permute-start | bytes 196616 | tf_op jit(solution)/shard_map/ppermute | solution.py:105
  12.8 1.6 %collective-permute-start.6 = (f32[128,128]{1,0:T(8,128)S(1)}, f32[128,128]{1,0:T(8,128)S(1)}, u32[]{:S(2)}, u32[]{:S(2)}) collective-permute-start(f32[128,128]{1,0:T(8,128)S(1)} %shard_map.48.refs_7_), channel_id=1, source_target_pairs={{0,3},{1,2},{2,1},{3,0},{4,7},{5,6},{6,5},{7,4},{8,11},{9,10},{10,... | collective-permute-start | bytes 196616 | tf_op jit(solution)/shard_map/ppermute | solution.py:105
  14.4 0.0 collective-permute-done.1.refs_2_
  14.4 0.0 collective-permute-done.2.refs_3_
  14.5 2.5 %collective-permute-start.5 = (f32[200,128]{1,0:T(8,128)S(1)}, f32[200,128]{1,0:T(8,128)S(1)}, u32[]{:S(2)}, u32[]{:S(2)}) collective-permute-start(f32[200,128]{1,0:T(8,128)S(1)} %constant_dynamic-update-slice_fusion.refs_0_), channel_id=1, source_target_pairs={{0,24},{4,28},{8,16},{12,20},{16,8},{20,12},{24,0},{28,4},{1,25},{... | collective-permute-start | bytes 307208 | tf_op jit(solution)/shard_map/ppermute | solution.py:105
  17.0 0.5 %collective-permute-start.4 = (f32[200,128]{1,0:T(8,128)S(1)}, f32[200,128]{1,0:T(8,128)S(1)}, u32[]{:S(2)}, u32[]{:S(2)}) collective-permute-start(f32[200,128]{1,0:T(8,128)S(1)} %constant_dynamic-update-slice_fusion.refs_0_), channel_id=1, source_target_pairs={{0,16},{4,20},{8,24},{12,28},{16,0},{20,4},{24,8},{28,12},{1,17},{... | collective-permute-start | bytes 307208 | tf_op jit(solution)/shard_map/ppermute | solution.py:105
  17.5 0.0 collective-permute-done.8.refs_6_
  17.5 0.5 %collective-permute-start.3 = (f32[200,128]{1,0:T(8,128)S(1)}, f32[200,128]{1,0:T(8,128)S(1)}, u32[]{:S(2)}, u32[]{:S(2)}) collective-permute-start(f32[200,128]{1,0:T(8,128)S(1)} %constant_dynamic-update-slice_fusion.refs_0_), channel_id=1, source_target_pairs={{0,8},{4,12},{8,0},{12,4},{16,24},{20,28},{24,16},{28,20},{1,9},{5... | collective-permute-start | bytes 307208 | tf_op jit(solution)/shard_map/ppermute | solution.py:105
  18.0 0.0 collective-permute-done.7.refs_5_
  18.0 0.9 %collective-permute-done.6.refs_4_ = f32[128,128]{1,0:T(8,128)S(1)} collective-permute-done((f32[128,128]{1,0:T(8,128)S(1)}, f32[128,128]{1,0:T(8,128)S(1)}, u32[]{:S(2)}, u32[]{:S(2)}) %collective-permute-start.6) | collective-permute-done | bytes 65568 | tf_op jit(solution)/shard_map/ppermute | solution.py:105
  19.0 0.0 copy-done
  19.0 0.1 shard_map.49.group_ref
  19.0 0.1 collective-permute-start.9
  19.1 0.2 shard_map.50
  19.3 1.1 %collective-permute-done.5.refs_3_ = f32[200,128]{1,0:T(8,128)S(1)} collective-permute-done((f32[200,128]{1,0:T(8,128)S(1)}, f32[200,128]{1,0:T(8,128)S(1)}, u32[]{:S(2)}, u32[]{:S(2)}) %collective-permute-start.5) | collective-permute-done | bytes 102432 | tf_op jit(solution)/shard_map/ppermute | solution.py:105
  20.4 1.2 %collective-permute-done.4.refs_2_ = f32[200,128]{1,0:T(8,128)S(1)} collective-permute-done((f32[200,128]{1,0:T(8,128)S(1)}, f32[200,128]{1,0:T(8,128)S(1)}, u32[]{:S(2)}, u32[]{:S(2)}) %collective-permute-start.4) | collective-permute-done | bytes 102432 | tf_op jit(solution)/shard_map/ppermute | solution.py:105
  21.6 0.5 %collective-permute-done.3.refs_1_ = f32[200,128]{1,0:T(8,128)S(1)} collective-permute-done((f32[200,128]{1,0:T(8,128)S(1)}, f32[200,128]{1,0:T(8,128)S(1)}, u32[]{:S(2)}, u32[]{:S(2)}) %collective-permute-start.3) | collective-permute-done | bytes 102432 | tf_op jit(solution)/shard_map/ppermute | solution.py:105
  22.1 0.2 shard_map.47
  22.3 0.0 collective-permute-done.9.group_ref
  22.3 0.2 shard_map.51
  22.5 3.6 %shard_map.52 = (f32[128,128]{1,0:T(8,128)S(1)}, f32[128,128]{1,0:T(8,128)S(1)}, f32[128,128]{1,0:T(8,128)S(1)}, f32[128,128]{1,0:T(8,128)S(1)}) custom-call(bf16[192,512]{1,0:T(8,128)(2,1)S(1)} %get-tuple-element.17.high_ref, bf16[192,512]{1,0:T(8,128)(2,1)S(1)} %get-tuple-element.18.low_ref, f32[1,512]{1,0:T(1,128)S(1)} %get-tuple-element.19.scale_ref, ...), custom_call_target="tpu_custom_call" | custom-call | tf_op jit(solution)/shard_map/pallas_call | solution.py:171
  26.1 1.6 %collective-permute-start.10 = (f32[128,128]{1,0:T(8,128)S(1)}, f32[128,128]{1,0:T(8,128)S(1)}, u32[]{:S(2)}, u32[]{:S(2)}) collective-permute-start(f32[128,128]{1,0:T(8,128)S(1)} %get-tuple-element.26), channel_id=1, source_target_pairs={{0,24},{4,28},{8,16},{12,20},{16,8},{20,12},{24,0},{28,4},{1,25},{... | collective-permute-start | bytes 196616 | tf_op jit(solution)/shard_map/ppermute | solution.py:105
  27.7 0.6 %collective-permute-start.11 = (f32[128,128]{1,0:T(8,128)S(1)}, f32[128,128]{1,0:T(8,128)S(1)}, u32[]{:S(2)}, u32[]{:S(2)}) collective-permute-start(f32[128,128]{1,0:T(8,128)S(1)} %get-tuple-element.27), channel_id=1, source_target_pairs={{0,16},{4,20},{8,24},{12,28},{16,0},{20,4},{24,8},{28,12},{1,17},{... | collective-permute-start | bytes 196616 | tf_op jit(solution)/shard_map/ppermute | solution.py:105
  28.3 1.4 %collective-permute-start.12 = (f32[128,128]{1,0:T(8,128)S(1)}, f32[128,128]{1,0:T(8,128)S(1)}, u32[]{:S(2)}, u32[]{:S(2)}) collective-permute-start(f32[128,128]{1,0:T(8,128)S(1)} %get-tuple-element.28), channel_id=1, source_target_pairs={{0,8},{4,12},{8,0},{12,4},{16,24},{20,28},{24,16},{28,20},{1,9},{5... | collective-permute-start | bytes 196616 | tf_op jit(solution)/shard_map/ppermute | solution.py:105
  29.7 2.0 %collective-permute-done.10 = f32[128,128]{1,0:T(8,128)S(1)} collective-permute-done((f32[128,128]{1,0:T(8,128)S(1)}, f32[128,128]{1,0:T(8,128)S(1)}, u32[]{:S(2)}, u32[]{:S(2)}) %collective-permute-start.10) | collective-permute-done | bytes 65568 | tf_op jit(solution)/shard_map/ppermute | solution.py:105
  31.7 0.5 %collective-permute-done.11 = f32[128,128]{1,0:T(8,128)S(1)} collective-permute-done((f32[128,128]{1,0:T(8,128)S(1)}, f32[128,128]{1,0:T(8,128)S(1)}, u32[]{:S(2)}, u32[]{:S(2)}) %collective-permute-start.11) | collective-permute-done | bytes 65568 | tf_op jit(solution)/shard_map/ppermute | solution.py:105
  32.2 0.4 %collective-permute-done.12 = f32[128,128]{1,0:T(8,128)S(1)} collective-permute-done((f32[128,128]{1,0:T(8,128)S(1)}, f32[128,128]{1,0:T(8,128)S(1)}, u32[]{:S(2)}, u32[]{:S(2)}) %collective-permute-start.12) | collective-permute-done | bytes 65568 | tf_op jit(solution)/shard_map/ppermute | solution.py:105
  32.5 0.6 %add_add_fusion = f32[128,128]{1,0:T(8,128)} fusion(f32[128,128]{1,0:T(8,128)S(1)} %collective-permute-done.12, f32[128,128]{1,0:T(8,128)S(1)} %collective-permute-done.11, f32[128,128]{1,0:T(8,128)S(1)} %get-tuple-element.25, f32[128,128]{1,0:T(8,128)S(1)} %collective-permute-done.10), kind=kLoop, calls=%fused_computation | loop fusion | flops 49152 | bytes 327680 | tf_op jit(solution)/shard_map/add | solution.py:178
  (5 shorter events, 0.0 us)
Async XLA Ops:
  0.0 9.5 %copy-start.1 = (f32[128,128]{1,0:T(8,128)S(1)}, f32[128,128]{1,0:T(8,128)}, u32[]{:S(2)}) copy-start(f32[128,128]{1,0:T(8,128)} %in_ref.1) | copy-start | bytes 196612
  0.0 14.4 %collective-permute-start.1 = (f32[48,512]{1,0:T(8,128)}, f32[48,512]{1,0:T(8,128)S(1)}, u32[]{:S(2)}, u32[]{:S(2)}) collective-permute-start(f32[48,512]{1,0:T(8,128)} %refs_0_.1), channel_id=1, source_target_pairs={{0,2},{1,3},{2,0},{3,1},{4,6},{5,7},{6,4},{7,5},{8,10},{9,11},{10,... | collective-permute-start | bytes 294920 | tf_op jit(solution)/shard_map/ppermute | solution.py:105
  4.0 5.4 %collective-permute-start = (f32[48,512]{1,0:T(8,128)}, f32[48,512]{1,0:T(8,128)S(1)}, u32[]{:S(2)}, u32[]{:S(2)}) collective-permute-start(f32[48,512]{1,0:T(8,128)} %refs_0_.1), channel_id=1, source_target_pairs={{0,1},{1,0},{2,3},{3,2},{4,5},{5,4},{6,7},{7,6},{8,9},{9,8},{10,11... | collective-permute-start | bytes 294920 | tf_op jit(solution)/shard_map/ppermute | solution.py:105
  5.6 8.8 %collective-permute-start.2 = (f32[48,512]{1,0:T(8,128)}, f32[48,512]{1,0:T(8,128)S(1)}, u32[]{:S(2)}, u32[]{:S(2)}) collective-permute-start(f32[48,512]{1,0:T(8,128)} %refs_0_.1), channel_id=1, source_target_pairs={{0,3},{1,2},{2,1},{3,0},{4,7},{5,6},{6,5},{7,4},{8,11},{9,10},{10,... | collective-permute-start | bytes 294920 | tf_op jit(solution)/shard_map/ppermute | solution.py:105
  5.6 0.7 %copy-start.2 = (s32[4,8]{1,0:T(4,128)S(1)}, s32[4,8]{1,0:T(4,128)}, u32[]{:S(2)}) copy-start(s32[4,8]{1,0:T(4,128)} %list_ref.1) | copy-start | bytes 388
  6.3 0.7 %copy-start.3 = (s32[4]{0:T(128)S(1)}, s32[4]{0:T(128)}, u32[]{:S(2)}) copy-start(s32[4]{0:T(128)} %count_ref.1) | copy-start | bytes 52
  9.5 9.5 %copy-start = (f32[48,512]{1,0:T(8,128)S(1)}, f32[48,512]{1,0:T(8,128)}, u32[]{:S(2)}) copy-start(f32[48,512]{1,0:T(8,128)} %refs_0_.1) | copy-start | bytes 294916
  9.5 8.0 %collective-permute-start.8 = (f32[128,128]{1,0:T(8,128)S(1)}, f32[128,128]{1,0:T(8,128)S(1)}, u32[]{:S(2)}, u32[]{:S(2)}) collective-permute-start(f32[128,128]{1,0:T(8,128)S(1)} %shard_map.48.refs_7_), channel_id=1, source_target_pairs={{0,1},{1,0},{2,3},{3,2},{4,5},{5,4},{6,7},{7,6},{8,9},{9,8},{10,11... | collective-permute-start | bytes 196616 | tf_op jit(solution)/shard_map/ppermute | solution.py:105
  12.0 6.1 %collective-permute-start.7 = (f32[128,128]{1,0:T(8,128)S(1)}, f32[128,128]{1,0:T(8,128)S(1)}, u32[]{:S(2)}, u32[]{:S(2)}) collective-permute-start(f32[128,128]{1,0:T(8,128)S(1)} %shard_map.48.refs_7_), channel_id=1, source_target_pairs={{0,2},{1,3},{2,0},{3,1},{4,6},{5,7},{6,4},{7,5},{8,10},{9,11},{10,... | collective-permute-start | bytes 196616 | tf_op jit(solution)/shard_map/ppermute | solution.py:105
  12.8 6.2 %collective-permute-start.6 = (f32[128,128]{1,0:T(8,128)S(1)}, f32[128,128]{1,0:T(8,128)S(1)}, u32[]{:S(2)}, u32[]{:S(2)}) collective-permute-start(f32[128,128]{1,0:T(8,128)S(1)} %shard_map.48.refs_7_), channel_id=1, source_target_pairs={{0,3},{1,2},{2,1},{3,0},{4,7},{5,6},{6,5},{7,4},{8,11},{9,10},{10,... | collective-permute-start | bytes 196616 | tf_op jit(solution)/shard_map/ppermute | solution.py:105
  14.5 6.0 %collective-permute-start.5 = (f32[200,128]{1,0:T(8,128)S(1)}, f32[200,128]{1,0:T(8,128)S(1)}, u32[]{:S(2)}, u32[]{:S(2)}) collective-permute-start(f32[200,128]{1,0:T(8,128)S(1)} %constant_dynamic-update-slice_fusion.refs_0_), channel_id=1, source_target_pairs={{0,24},{4,28},{8,16},{12,20},{16,8},{20,12},{24,0},{28,4},{1,25},{... | collective-permute-start | bytes 307208 | tf_op jit(solution)/shard_map/ppermute | solution.py:105
  17.0 4.7 %collective-permute-start.4 = (f32[200,128]{1,0:T(8,128)S(1)}, f32[200,128]{1,0:T(8,128)S(1)}, u32[]{:S(2)}, u32[]{:S(2)}) collective-permute-start(f32[200,128]{1,0:T(8,128)S(1)} %constant_dynamic-update-slice_fusion.refs_0_), channel_id=1, source_target_pairs={{0,16},{4,20},{8,24},{12,28},{16,0},{20,4},{24,8},{28,12},{1,17},{... | collective-permute-start | bytes 307208 | tf_op jit(solution)/shard_map/ppermute | solution.py:105
  17.5 4.7 %collective-permute-start.3 = (f32[200,128]{1,0:T(8,128)S(1)}, f32[200,128]{1,0:T(8,128)S(1)}, u32[]{:S(2)}, u32[]{:S(2)}) collective-permute-start(f32[200,128]{1,0:T(8,128)S(1)} %constant_dynamic-update-slice_fusion.refs_0_), channel_id=1, source_target_pairs={{0,8},{4,12},{8,0},{12,4},{16,24},{20,28},{24,16},{28,20},{1,9},{5... | collective-permute-start | bytes 307208 | tf_op jit(solution)/shard_map/ppermute | solution.py:105
  19.0 3.3 %collective-permute-start.9 = (f32[320,512]{1,0:T(8,128)S(1)}, f32[320,512]{1,0:T(8,128)S(1)}, u32[]{:S(2)}, u32[]{:S(2)}) collective-permute-start(f32[320,512]{1,0:T(8,128)S(1)} %shard_map.49.group_ref), channel_id=1, source_target_pairs={{0,4},{4,0},{8,12},{12,8},{16,20},{20,16},{24,28},{28,24},{1,5},{5... | collective-permute-start | bytes 1966088 | tf_op jit(solution)/shard_map/ppermute | solution.py:105
  26.1 5.5 %collective-permute-start.10 = (f32[128,128]{1,0:T(8,128)S(1)}, f32[128,128]{1,0:T(8,128)S(1)}, u32[]{:S(2)}, u32[]{:S(2)}) collective-permute-start(f32[128,128]{1,0:T(8,128)S(1)} %get-tuple-element.26), channel_id=1, source_target_pairs={{0,24},{4,28},{8,16},{12,20},{16,8},{20,12},{24,0},{28,4},{1,25},{... | collective-permute-start | bytes 196616 | tf_op jit(solution)/shard_map/ppermute | solution.py:105
  27.7 4.5 %collective-permute-start.11 = (f32[128,128]{1,0:T(8,128)S(1)}, f32[128,128]{1,0:T(8,128)S(1)}, u32[]{:S(2)}, u32[]{:S(2)}) collective-permute-start(f32[128,128]{1,0:T(8,128)S(1)} %get-tuple-element.27), channel_id=1, source_target_pairs={{0,16},{4,20},{8,24},{12,28},{16,0},{20,4},{24,8},{28,12},{1,17},{... | collective-permute-start | bytes 196616 | tf_op jit(solution)/shard_map/ppermute | solution.py:105
  28.3 4.3 %collective-permute-start.12 = (f32[128,128]{1,0:T(8,128)S(1)}, f32[128,128]{1,0:T(8,128)S(1)}, u32[]{:S(2)}, u32[]{:S(2)}) collective-permute-start(f32[128,128]{1,0:T(8,128)S(1)} %get-tuple-element.28), channel_id=1, source_target_pairs={{0,8},{4,12},{8,0},{12,4},{16,24},{20,28},{24,16},{28,20},{1,9},{5... | collective-permute-start | bytes 196616 | tf_op jit(solution)/shard_map/ppermute | solution.py:105

commit v10 on v8

--- a/solution.py
+++ b/solution.py
@@ -46,7 +46,7 @@
 
 
 def columns_kernel(feat_count, group_ref, col_ref, vec_ref):
-    chunk = 2 * vec_ref.shape[0]
+    chunk = 4 * vec_ref.shape[0]
     cols = group_ref[:feat_count, :]
     col_ref[...] = stacked(cols.T, "hhl", 1)
     vecs = group_ref[feat_count:, :] * jnp.exp(jnp.sum(cols * cols, axis=0, keepdims=True) * (-1.0 / feat_count))
@@ -75,24 +75,23 @@
     own_cols, own_vecs, sibling_cols, sibling_vecs, *out_refs = refs
     width = out_refs[0].shape[1]
     group_cols = own_cols.shape[0]
-    chunk = 2 * width
-    pairs = range(len(out_refs) // 2)
+    chunk = 4 * width
+    pairs = [slice(first * width, (first + 2) * width) for first in range(0, len(out_refs), 2)]
     totals = [None for _ in pairs]
     for group, (col_ref, vec_ref) in enumerate(((own_cols, own_vecs), (sibling_cols, sibling_vecs))):
         for start in range(0, group_cols, chunk):
             at = (group * group_cols + start) // width
-            for pair in pairs:
-                span = slice(pair * chunk, (pair + 1) * chunk)
+            for pair, span in enumerate(pairs):
                 inner = jnp.dot(
                     col_ref[start : start + chunk, :], row_ref[:, span], preferred_element_type=jnp.float32
                 )
-                both = [jnp.broadcast_to(mask_ref[spot : spot + 1, span], (width, chunk)) for spot in (at, at + 1)]
-                weight = stacked(jnp.exp(inner) * jnp.concatenate(both, axis=0), "hlh", 0)
+                masks = [jnp.broadcast_to(mask_ref[at + spot : at + spot + 1, span], (width, 2 * width)) for spot in range(4)]
+                weight = stacked(jnp.exp(inner) * jnp.concatenate(masks, axis=0), "hlh", 0)
                 vecs = vec_ref[:, 3 * start : 3 * (start + chunk)]
                 added = jnp.dot(vecs, weight, preferred_element_type=jnp.float32)
                 totals[pair] = added if totals[pair] is None else totals[pair] + added
-    for pair in pairs:
-        total = totals[pair] * scale_ref[:, pair * chunk : (pair + 1) * chunk]
+    for pair, span in enumerate(pairs):
+        total = totals[pair] * scale_ref[:, span]
         out_refs[2 * pair][...] = total[:, :width]
         out_refs[2 * pair + 1][...] = total[:, width:]
 

time: 31.9 us -> 31.9 us (level)
  no operation moved by 1% of the time
where the time goes in v10:
time: 31.9 us; the launch traced here: 31.6 us
  starting transfers between devices  17.7 us (55%)
  waiting for transfers between devices  7.74 us (24%)
  Pallas kernels  3.3 us (10%)
  local copies, waits for them, and re-layouts  2.12 us (7%)
  other arithmetic  0.65 us (2%)
    ppermute x13, starting transfers between devices, swapped(): lax.ppermute(value, axis, [(source, source ^ step) for source in range(co...  17.7 us
    ppermute x13, waiting for transfers between devices, swapped(): lax.ppermute(value, axis, [(source, source ^ step) for source in range(co...  7.74 us
    unnamed x12, local copies, waits for them, and re-layouts  2.12 us
    pallas_call x1, Pallas kernels, shards(): pl.pallas_call(apply_kernel, out_shape=[shape((eig_count, width), f32)] *...  1.89 us
    add x1, other arithmetic, shards(): total = total + swapped(tiles[place], 'blk', steps[place])  0.65 us
  transfers between devices with their start and end apart: 13, of which 8 were waited for; matrix products, arithmetic and copies ran while one was open for 2% of the time, Pallas kernels for 4%

profile of v10, /device:TPU:0, one launch (start us, length us, event | category | flops | bytes accessed | tf_op | source)
XLA Modules:
  0.0 31.6 jit_solution(15349750354808566502)
XLA Ops:
  0.0 0.0 copy-start.1
  0.0 4.0 %collective-permute-start.1 = (f32[48,512]{1,0:T(8,128)}, f32[48,512]{1,0:T(8,128)S(1)}, u32[]{:S(2)}, u32[]{:S(2)}) collective-permute-start(f32[48,512]{1,0:T(8,128)} %refs_0_.1), channel_id=1, source_target_pairs={{0,2},{1,3},{2,0},{3,1},{4,6},{5,7},{6,4},{7,5},{8,10},{9,11},{10,... | collective-permute-start | bytes 294920 | tf_op jit(solution)/shard_map/ppermute | solution.py:101
  4.0 1.6 %collective-permute-start = (f32[48,512]{1,0:T(8,128)}, f32[48,512]{1,0:T(8,128)S(1)}, u32[]{:S(2)}, u32[]{:S(2)}) collective-permute-start(f32[48,512]{1,0:T(8,128)} %refs_0_.1), channel_id=1, source_target_pairs={{0,1},{1,0},{2,3},{3,2},{4,5},{5,4},{6,7},{7,6},{8,9},{9,8},{10,11... | collective-permute-start | bytes 294920 | tf_op jit(solution)/shard_map/ppermute | solution.py:101
  5.6 0.0 collective-permute-start.2
  5.6 0.0 copy-start.2
  5.6 0.7 %copy-done.2 = s32[4,8]{1,0:T(4,128)S(1)} copy-done((s32[4,8]{1,0:T(4,128)S(1)}, s32[4,8]{1,0:T(4,128)}, u32[]{:S(2)}) %copy-start.2) | copy-done | bytes 152
  6.3 0.0 copy-start.3
  6.3 0.7 %copy-done.3 = s32[4]{0:T(128)S(1)} copy-done((s32[4]{0:T(128)S(1)}, s32[4]{0:T(128)}, u32[]{:S(2)}) %copy-start.3) | copy-done | bytes 40
  7.0 0.6 %shard_map.46 = f32[8,128]{1,0:T(8,128)S(1)} custom-call(s32[4,8]{1,0:T(4,128)S(1)} %copy-done.2, s32[4]{0:T(128)S(1)} %copy-done.3), custom_call_target="tpu_custom_call" | custom-call | tf_op jit(solution)/shard_map/pallas_call | solution.py:128
  7.6 0.7 %dynamic-slice_dynamic-update-slice_fusion.3 = f32[200,128]{1,0:T(8,128)S(1)} fusion(f32[48,512]{1,0:T(8,128)} %refs_0_.1, s32[]{:T(128)S(6)} %select_n.2), kind=kLoop, calls=%fused_computation.4 | loop fusion | bytes 49156
  8.3 1.2 %collective-permute-done.before_ref.refs_1_ = f32[48,512]{1,0:T(8,128)S(1)} collective-permute-done((f32[48,512]{1,0:T(8,128)}, f32[48,512]{1,0:T(8,128)S(1)}, u32[]{:S(2)}, u32[]{:S(2)}) %collective-permute-start) | collective-permute-done | bytes 98336 | tf_op jit(solution)/shard_map/ppermute | solution.py:101
  9.5 0.0 copy-done.1
  9.5 0.0 copy-start
  9.5 2.4 %collective-permute-start.8 = (f32[128,128]{1,0:T(8,128)S(1)}, f32[128,128]{1,0:T(8,128)S(1)}, u32[]{:S(2)}, u32[]{:S(2)}) collective-permute-start(f32[128,128]{1,0:T(8,128)S(1)} %shard_map.48.refs_7_), channel_id=1, source_target_pairs={{0,1},{1,0},{2,3},{3,2},{4,5},{5,4},{6,7},{7,6},{8,9},{9,8},{10,11... | collective-permute-start | bytes 196616 | tf_op jit(solution)/shard_map/ppermute | solution.py:101
  12.0 0.8 %collective-permute-start.7 = (f32[128,128]{1,0:T(8,128)S(1)}, f32[128,128]{1,0:T(8,128)S(1)}, u32[]{:S(2)}, u32[]{:S(2)}) collective-permute-start(f32[128,128]{1,0:T(8,128)S(1)} %shard_map.48.refs_7_), channel_id=1, source_target_pairs={{0,2},{1,3},{2,0},{3,1},{4,6},{5,7},{6,4},{7,5},{8,10},{9,11},{10,... | collective-permute-start | bytes 196616 | tf_op jit(solution)/shard_map/ppermute | solution.py:101
  12.8 1.6 %collective-permute-start.6 = (f32[128,128]{1,0:T(8,128)S(1)}, f32[128,128]{1,0:T(8,128)S(1)}, u32[]{:S(2)}, u32[]{:S(2)}) collective-permute-start(f32[128,128]{1,0:T(8,128)S(1)} %shard_map.48.refs_7_), channel_id=1, source_target_pairs={{0,3},{1,2},{2,1},{3,0},{4,7},{5,6},{6,5},{7,4},{8,11},{9,10},{10,... | collective-permute-start | bytes 196616 | tf_op jit(solution)/shard_map/ppermute | solution.py:101
  14.4 0.0 collective-permute-done.1.refs_2_
  14.4 0.0 collective-permute-done.2.refs_3_
  14.5 2.5 %collective-permute-start.5 = (f32[200,128]{1,0:T(8,128)S(1)}, f32[200,128]{1,0:T(8,128)S(1)}, u32[]{:S(2)}, u32[]{:S(2)}) collective-permute-start(f32[200,128]{1,0:T(8,128)S(1)} %constant_dynamic-update-slice_fusion.refs_0_), channel_id=1, source_target_pairs={{0,24},{4,28},{8,16},{12,20},{16,8},{20,12},{24,0},{28,4},{1,25},{... | collective-permute-start | bytes 307208 | tf_op jit(solution)/shard_map/ppermute | solution.py:101
  17.0 0.5 %collective-permute-start.4 = (f32[200,128]{1,0:T(8,128)S(1)}, f32[200,128]{1,0:T(8,128)S(1)}, u32[]{:S(2)}, u32[]{:S(2)}) collective-permute-start(f32[200,128]{1,0:T(8,128)S(1)} %constant_dynamic-update-slice_fusion.refs_0_), channel_id=1, source_target_pairs={{0,16},{4,20},{8,24},{12,28},{16,0},{20,4},{24,8},{28,12},{1,17},{... | collective-permute-start | bytes 307208 | tf_op jit(solution)/shard_map/ppermute | solution.py:101
  17.5 0.0 collective-permute-done.8.refs_6_
  17.5 0.5 %collective-permute-start.3 = (f32[200,128]{1,0:T(8,128)S(1)}, f32[200,128]{1,0:T(8,128)S(1)}, u32[]{:S(2)}, u32[]{:S(2)}) collective-permute-start(f32[200,128]{1,0:T(8,128)S(1)} %constant_dynamic-update-slice_fusion.refs_0_), channel_id=1, source_target_pairs={{0,8},{4,12},{8,0},{12,4},{16,24},{20,28},{24,16},{28,20},{1,9},{5... | collective-permute-start | bytes 307208 | tf_op jit(solution)/shard_map/ppermute | solution.py:101
  18.0 0.0 collective-permute-done.7.refs_5_
  18.0 0.9 %collective-permute-done.6.refs_4_ = f32[128,128]{1,0:T(8,128)S(1)} collective-permute-done((f32[128,128]{1,0:T(8,128)S(1)}, f32[128,128]{1,0:T(8,128)S(1)}, u32[]{:S(2)}, u32[]{:S(2)}) %collective-permute-start.6) | collective-permute-done | bytes 65568 | tf_op jit(solution)/shard_map/ppermute | solution.py:101
  19.0 0.0 copy-done
  19.0 0.1 shard_map.49.group_ref
  19.0 0.1 collective-permute-start.9
  19.1 0.3 shard_map.50
  19.4 1.0 %collective-permute-done.5.refs_3_ = f32[200,128]{1,0:T(8,128)S(1)} collective-permute-done((f32[200,128]{1,0:T(8,128)S(1)}, f32[200,128]{1,0:T(8,128)S(1)}, u32[]{:S(2)}, u32[]{:S(2)}) %collective-permute-start.5) | collective-permute-done | bytes 102432 | tf_op jit(solution)/shard_map/ppermute | solution.py:101
  20.4 1.2 %collective-permute-done.4.refs_2_ = f32[200,128]{1,0:T(8,128)S(1)} collective-permute-done((f32[200,128]{1,0:T(8,128)S(1)}, f32[200,128]{1,0:T(8,128)S(1)}, u32[]{:S(2)}, u32[]{:S(2)}) %collective-permute-start.4) | collective-permute-done | bytes 102432 | tf_op jit(solution)/shard_map/ppermute | solution.py:101
  21.6 0.5 %collective-permute-done.3.refs_1_ = f32[200,128]{1,0:T(8,128)S(1)} collective-permute-done((f32[200,128]{1,0:T(8,128)S(1)}, f32[200,128]{1,0:T(8,128)S(1)}, u32[]{:S(2)}, u32[]{:S(2)}) %collective-permute-start.3) | collective-permute-done | bytes 102432 | tf_op jit(solution)/shard_map/ppermute | solution.py:101
  22.1 0.2 shard_map.47
  22.3 0.0 collective-permute-done.9.group_ref
  22.3 0.3 shard_map.51
  22.6 1.9 %shard_map.52 = (f32[128,128]{1,0:T(8,128)S(1)}, f32[128,128]{1,0:T(8,128)S(1)}, f32[128,128]{1,0:T(8,128)S(1)}, f32[128,128]{1,0:T(8,128)S(1)}) custom-call(bf16[576,512]{1,0:T(8,128)(2,1)S(1)} %get-tuple-element.16.row_ref, f32[1,512]{1,0:T(1,128)S(1)} %get-tuple-element.17.scale_ref, f32[8,512]{1,0:T(8,128)S(1)} %get-tuple-element.18.mask_ref, ...), custom_call_target="tpu_custom_call" | custom-call | tf_op jit(solution)/shard_map/pallas_call | solution.py:166
  24.5 1.6 %collective-permute-start.10 = (f32[128,128]{1,0:T(8,128)S(1)}, f32[128,128]{1,0:T(8,128)S(1)}, u32[]{:S(2)}, u32[]{:S(2)}) collective-permute-start(f32[128,128]{1,0:T(8,128)S(1)} %get-tuple-element.24), channel_id=1, source_target_pairs={{0,24},{4,28},{8,16},{12,20},{16,8},{20,12},{24,0},{28,4},{1,25},{... | collective-permute-start | bytes 196616 | tf_op jit(solution)/shard_map/ppermute | solution.py:101
  26.1 0.6 %collective-permute-start.11 = (f32[128,128]{1,0:T(8,128)S(1)}, f32[128,128]{1,0:T(8,128)S(1)}, u32[]{:S(2)}, u32[]{:S(2)}) collective-permute-start(f32[128,128]{1,0:T(8,128)S(1)} %get-tuple-element.25), channel_id=1, source_target_pairs={{0,16},{4,20},{8,24},{12,28},{16,0},{20,4},{24,8},{28,12},{1,17},{... | collective-permute-start | bytes 196616 | tf_op jit(solution)/shard_map/ppermute | solution.py:101
  26.7 1.4 %collective-permute-start.12 = (f32[128,128]{1,0:T(8,128)S(1)}, f32[128,128]{1,0:T(8,128)S(1)}, u32[]{:S(2)}, u32[]{:S(2)}) collective-permute-start(f32[128,128]{1,0:T(8,128)S(1)} %get-tuple-element.26), channel_id=1, source_target_pairs={{0,8},{4,12},{8,0},{12,4},{16,24},{20,28},{24,16},{28,20},{1,9},{5... | collective-permute-start | bytes 196616 | tf_op jit(solution)/shard_map/ppermute | solution.py:101
  28.1 2.0 %collective-permute-done.10 = f32[128,128]{1,0:T(8,128)S(1)} collective-permute-done((f32[128,128]{1,0:T(8,128)S(1)}, f32[128,128]{1,0:T(8,128)S(1)}, u32[]{:S(2)}, u32[]{:S(2)}) %collective-permute-start.10) | collective-permute-done | bytes 65568 | tf_op jit(solution)/shard_map/ppermute | solution.py:101
  30.1 0.5 %collective-permute-done.11 = f32[128,128]{1,0:T(8,128)S(1)} collective-permute-done((f32[128,128]{1,0:T(8,128)S(1)}, f32[128,128]{1,0:T(8,128)S(1)}, u32[]{:S(2)}, u32[]{:S(2)}) %collective-permute-start.11) | collective-permute-done | bytes 65568 | tf_op jit(solution)/shard_map/ppermute | solution.py:101
  30.6 0.4 %collective-permute-done.12 = f32[128,128]{1,0:T(8,128)S(1)} collective-permute-done((f32[128,128]{1,0:T(8,128)S(1)}, f32[128,128]{1,0:T(8,128)S(1)}, u32[]{:S(2)}, u32[]{:S(2)}) %collective-permute-start.12) | collective-permute-done | bytes 65568 | tf_op jit(solution)/shard_map/ppermute | solution.py:101
  31.0 0.6 %add_add_fusion = f32[128,128]{1,0:T(8,128)} fusion(f32[128,128]{1,0:T(8,128)S(1)} %collective-permute-done.12, f32[128,128]{1,0:T(8,128)S(1)} %collective-permute-done.11, f32[128,128]{1,0:T(8,128)S(1)} %get-tuple-element.23, f32[128,128]{1,0:T(8,128)S(1)} %collective-permute-done.10), kind=kLoop, calls=%fused_computation | loop fusion | flops 49152 | bytes 327680 | tf_op jit(solution)/shard_map/add | solution.py:173
  (5 shorter events, 0.0 us)
Async XLA Ops:
  0.0 9.5 %copy-start.1 = (f32[128,128]{1,0:T(8,128)S(1)}, f32[128,128]{1,0:T(8,128)}, u32[]{:S(2)}) copy-start(f32[128,128]{1,0:T(8,128)} %in_ref.1) | copy-start | bytes 196612
  0.0 14.4 %collective-permute-start.1 = (f32[48,512]{1,0:T(8,128)}, f32[48,512]{1,0:T(8,128)S(1)}, u32[]{:S(2)}, u32[]{:S(2)}) collective-permute-start(f32[48,512]{1,0:T(8,128)} %refs_0_.1), channel_id=1, source_target_pairs={{0,2},{1,3},{2,0},{3,1},{4,6},{5,7},{6,4},{7,5},{8,10},{9,11},{10,... | collective-permute-start | bytes 294920 | tf_op jit(solution)/shard_map/ppermute | solution.py:101
  4.0 5.4 %collective-permute-start = (f32[48,512]{1,0:T(8,128)}, f32[48,512]{1,0:T(8,128)S(1)}, u32[]{:S(2)}, u32[]{:S(2)}) collective-permute-start(f32[48,512]{1,0:T(8,128)} %refs_0_.1), channel_id=1, source_target_pairs={{0,1},{1,0},{2,3},{3,2},{4,5},{5,4},{6,7},{7,6},{8,9},{9,8},{10,11... | collective-permute-start | bytes 294920 | tf_op jit(solution)/shard_map/ppermute | solution.py:101
  5.6 8.8 %collective-permute-start.2 = (f32[48,512]{1,0:T(8,128)}, f32[48,512]{1,0:T(8,128)S(1)}, u32[]{:S(2)}, u32[]{:S(2)}) collective-permute-start(f32[48,512]{1,0:T(8,128)} %refs_0_.1), channel_id=1, source_target_pairs={{0,3},{1,2},{2,1},{3,0},{4,7},{5,6},{6,5},{7,4},{8,11},{9,10},{10,... | collective-permute-start | bytes 294920 | tf_op jit(solution)/shard_map/ppermute | solution.py:101
  5.6 0.7 %copy-start.2 = (s32[4,8]{1,0:T(4,128)S(1)}, s32[4,8]{1,0:T(4,128)}, u32[]{:S(2)}) copy-start(s32[4,8]{1,0:T(4,128)} %list_ref.1) | copy-start | bytes 388
  6.3 0.7 %copy-start.3 = (s32[4]{0:T(128)S(1)}, s32[4]{0:T(128)}, u32[]{:S(2)}) copy-start(s32[4]{0:T(128)} %count_ref.1) | copy-start | bytes 52
  9.5 9.5 %copy-start = (f32[48,512]{1,0:T(8,128)S(1)}, f32[48,512]{1,0:T(8,128)}, u32[]{:S(2)}) copy-start(f32[48,512]{1,0:T(8,128)} %refs_0_.1) | copy-start | bytes 294916
  9.5 8.0 %collective-permute-start.8 = (f32[128,128]{1,0:T(8,128)S(1)}, f32[128,128]{1,0:T(8,128)S(1)}, u32[]{:S(2)}, u32[]{:S(2)}) collective-permute-start(f32[128,128]{1,0:T(8,128)S(1)} %shard_map.48.refs_7_), channel_id=1, source_target_pairs={{0,1},{1,0},{2,3},{3,2},{4,5},{5,4},{6,7},{7,6},{8,9},{9,8},{10,11... | collective-permute-start | bytes 196616 | tf_op jit(solution)/shard_map/ppermute | solution.py:101
  12.0 6.1 %collective-permute-start.7 = (f32[128,128]{1,0:T(8,128)S(1)}, f32[128,128]{1,0:T(8,128)S(1)}, u32[]{:S(2)}, u32[]{:S(2)}) collective-permute-start(f32[128,128]{1,0:T(8,128)S(1)} %shard_map.48.refs_7_), channel_id=1, source_target_pairs={{0,2},{1,3},{2,0},{3,1},{4,6},{5,7},{6,4},{7,5},{8,10},{9,11},{10,... | collective-permute-start | bytes 196616 | tf_op jit(solution)/shard_map/ppermute | solution.py:101
  12.8 6.2 %collective-permute-start.6 = (f32[128,128]{1,0:T(8,128)S(1)}, f32[128,128]{1,0:T(8,128)S(1)}, u32[]{:S(2)}, u32[]{:S(2)}) collective-permute-start(f32[128,128]{1,0:T(8,128)S(1)} %shard_map.48.refs_7_), channel_id=1, source_target_pairs={{0,3},{1,2},{2,1},{3,0},{4,7},{5,6},{6,5},{7,4},{8,11},{9,10},{10,... | collective-permute-start | bytes 196616 | tf_op jit(solution)/shard_map/ppermute | solution.py:101
  14.5 6.0 %collective-permute-start.5 = (f32[200,128]{1,0:T(8,128)S(1)}, f32[200,128]{1,0:T(8,128)S(1)}, u32[]{:S(2)}, u32[]{:S(2)}) collective-permute-start(f32[200,128]{1,0:T(8,128)S(1)} %constant_dynamic-update-slice_fusion.refs_0_), channel_id=1, source_target_pairs={{0,24},{4,28},{8,16},{12,20},{16,8},{20,12},{24,0},{28,4},{1,25},{... | collective-permute-start | bytes 307208 | tf_op jit(solution)/shard_map/ppermute | solution.py:101
  17.0 4.7 %collective-permute-start.4 = (f32[200,128]{1,0:T(8,128)S(1)}, f32[200,128]{1,0:T(8,128)S(1)}, u32[]{:S(2)}, u32[]{:S(2)}) collective-permute-start(f32[200,128]{1,0:T(8,128)S(1)} %constant_dynamic-update-slice_fusion.refs_0_), channel_id=1, source_target_pairs={{0,16},{4,20},{8,24},{12,28},{16,0},{20,4},{24,8},{28,12},{1,17},{... | collective-permute-start | bytes 307208 | tf_op jit(solution)/shard_map/ppermute | solution.py:101
  17.5 4.7 %collective-permute-start.3 = (f32[200,128]{1,0:T(8,128)S(1)}, f32[200,128]{1,0:T(8,128)S(1)}, u32[]{:S(2)}, u32[]{:S(2)}) collective-permute-start(f32[200,128]{1,0:T(8,128)S(1)} %constant_dynamic-update-slice_fusion.refs_0_), channel_id=1, source_target_pairs={{0,8},{4,12},{8,0},{12,4},{16,24},{20,28},{24,16},{28,20},{1,9},{5... | collective-permute-start | bytes 307208 | tf_op jit(solution)/shard_map/ppermute | solution.py:101
  19.0 3.3 %collective-permute-start.9 = (f32[320,512]{1,0:T(8,128)S(1)}, f32[320,512]{1,0:T(8,128)S(1)}, u32[]{:S(2)}, u32[]{:S(2)}) collective-permute-start(f32[320,512]{1,0:T(8,128)S(1)} %shard_map.49.group_ref), channel_id=1, source_target_pairs={{0,4},{4,0},{8,12},{12,8},{16,20},{20,16},{24,28},{28,24},{1,5},{5... | collective-permute-start | bytes 1966088 | tf_op jit(solution)/shard_map/ppermute | solution.py:101
  24.5 5.5 %collective-permute-start.10 = (f32[128,128]{1,0:T(8,128)S(1)}, f32[128,128]{1,0:T(8,128)S(1)}, u32[]{:S(2)}, u32[]{:S(2)}) collective-permute-start(f32[128,128]{1,0:T(8,128)S(1)} %get-tuple-element.24), channel_id=1, source_target_pairs={{0,24},{4,28},{8,16},{12,20},{16,8},{20,12},{24,0},{28,4},{1,25},{... | collective-permute-start | bytes 196616 | tf_op jit(solution)/shard_map/ppermute | solution.py:101
  26.1 4.5 %collective-permute-start.11 = (f32[128,128]{1,0:T(8,128)S(1)}, f32[128,128]{1,0:T(8,128)S(1)}, u32[]{:S(2)}, u32[]{:S(2)}) collective-permute-start(f32[128,128]{1,0:T(8,128)S(1)} %get-tuple-element.25), channel_id=1, source_target_pairs={{0,16},{4,20},{8,24},{12,28},{16,0},{20,4},{24,8},{28,12},{1,17},{... | collective-permute-start | bytes 196616 | tf_op jit(solution)/shard_map/ppermute | solution.py:101
  26.7 4.3 %collective-permute-start.12 = (f32[128,128]{1,0:T(8,128)S(1)}, f32[128,128]{1,0:T(8,128)S(1)}, u32[]{:S(2)}, u32[]{:S(2)}) collective-permute-start(f32[128,128]{1,0:T(8,128)S(1)} %get-tuple-element.26), channel_id=1, source_target_pairs={{0,8},{4,12},{8,0},{12,4},{16,24},{20,28},{24,16},{28,20},{1,9},{5... | collective-permute-start | bytes 196616 | tf_op jit(solution)/shard_map/ppermute | solution.py:101

commit v11 on v6

--- a/solution.py
+++ b/solution.py
@@ -144,6 +144,8 @@
     own_block = [lax.dynamic_slice_in_dim(piece, rep_index * width, width, 1) for piece in pieces]
     panel = jnp.concatenate([*own_block, lists], axis=0)
     steps = list(range(0, cycle_size, 2))
+    half = len(steps) // 2
+    steps[half:] = steps[: half - 1 : -1]
     panels = [panel] + [swapped(panel, "blk", step) for step in steps[1:]]
 
     own_group = pl.pallas_call(
@@ -160,7 +162,6 @@
             compiler_params=params,
         )(group)
 
-    half = len(steps) // 2
 
     def rows_of(first, **estimate):
         return pl.pallas_call(

time: 33 us -> 32.7 us (level)
  waiting for transfers between devices: 7.04 us -> 6.61 us
    ppermute x13, waiting for transfers between devices: 7.04 us -> 6.61 us  [swapped(): lax.ppermute(value, axis, [(source, source ^ step) for source in range(co...]
  transfers between devices with their start and end apart: 13 -> 13, of which waited for: 6 -> 7; matrix products, arithmetic and copies ran while one was open for 2% -> 2% of each run, Pallas kernels for 12% -> 13%
where the time goes in v11:
time: 32.7 us; the launch traced here: 32.4 us
  starting transfers between devices  18.8 us (57%)
  waiting for transfers between devices  6.61 us (20%)
  Pallas kernels  4.09 us (13%)
  local copies, waits for them, and re-layouts  2.12 us (6%)
  other arithmetic  0.64 us (2%)
    ppermute x13, starting transfers between devices, swapped(): lax.ppermute(value, axis, [(source, source ^ step) for source in range(co...  18.8 us
    ppermute x13, waiting for transfers between devices, swapped(): lax.ppermute(value, axis, [(source, source ^ step) for source in range(co...  6.61 us
    pallas_call x3, Pallas kernels, tiles_of(): pl.pallas_call(functools.partial(apply_kernel, groups), in_specs=[anywher...  2.67 us
    unnamed x12, local copies, waits for them, and re-layouts  2.12 us
  transfers between devices with their start and end apart: 13, of which 7 were waited for; matrix products, arithmetic and copies ran while one was open for 2% of the time, Pallas kernels for 13%

profile of v11, /device:TPU:0, one launch (start us, length us, event | category | flops | bytes accessed | tf_op | source)
XLA Modules:
  0.0 32.4 jit_solution(6713672139663438467)
XLA Ops:
  0.0 0.0 copy-start.1
  0.0 4.0 %collective-permute-start = (f32[48,512]{1,0:T(8,128)}, f32[48,512]{1,0:T(8,128)S(1)}, u32[]{:S(2)}, u32[]{:S(2)}) collective-permute-start(f32[48,512]{1,0:T(8,128)} %refs_0_.1), channel_id=1, source_target_pairs={{0,2},{1,3},{2,0},{3,1},{4,6},{5,7},{6,4},{7,5},{8,10},{9,11},{10,... | collective-permute-start | bytes 294920 | tf_op jit(solution)/shard_map/ppermute | solution.py:108
  4.0 1.6 %collective-permute-start.1 = (f32[48,512]{1,0:T(8,128)}, f32[48,512]{1,0:T(8,128)S(1)}, u32[]{:S(2)}, u32[]{:S(2)}) collective-permute-start(f32[48,512]{1,0:T(8,128)} %refs_0_.1), channel_id=1, source_target_pairs={{0,1},{1,0},{2,3},{3,2},{4,5},{5,4},{6,7},{7,6},{8,9},{9,8},{10,11... | collective-permute-start | bytes 294920 | tf_op jit(solution)/shard_map/ppermute | solution.py:108
  5.6 0.0 collective-permute-start.2
  5.6 0.0 copy-start.2
  5.6 0.7 %copy-done.2 = s32[4,8]{1,0:T(4,128)S(1)} copy-done((s32[4,8]{1,0:T(4,128)S(1)}, s32[4,8]{1,0:T(4,128)}, u32[]{:S(2)}) %copy-start.2) | copy-done | bytes 152
  6.3 0.0 copy-start.3
  6.3 0.7 %copy-done.3 = s32[4]{0:T(128)S(1)} copy-done((s32[4]{0:T(128)S(1)}, s32[4]{0:T(128)}, u32[]{:S(2)}) %copy-start.3) | copy-done | bytes 40
  7.0 0.6 %shard_map.46 = f32[8,128]{1,0:T(8,128)S(1)} custom-call(s32[4,8]{1,0:T(4,128)S(1)} %copy-done.2, s32[4]{0:T(128)S(1)} %copy-done.3), custom_call_target="tpu_custom_call" | custom-call | tf_op jit(solution)/shard_map/pallas_call | solution.py:137
  7.6 0.7 %dynamic-slice_dynamic-update-slice_fusion.3 = f32[200,128]{1,0:T(8,128)S(1)} fusion(f32[48,512]{1,0:T(8,128)} %refs_0_.1, s32[]{:T(128)S(6)} %select_n.2), kind=kLoop, calls=%fused_computation.4 | loop fusion | bytes 49156
  8.3 1.2 %collective-permute-done.1.before_ref.refs_2_ = f32[48,512]{1,0:T(8,128)S(1)} collective-permute-done((f32[48,512]{1,0:T(8,128)}, f32[48,512]{1,0:T(8,128)S(1)}, u32[]{:S(2)}, u32[]{:S(2)}) %collective-permute-start.1) | collective-permute-done | bytes 98336 | tf_op jit(solution)/shard_map/ppermute | solution.py:108
  9.5 0.0 copy-done.1
  9.5 0.0 copy-start
  9.5 2.4 %collective-permute-start.5 = (f32[128,128]{1,0:T(8,128)S(1)}, f32[128,128]{1,0:T(8,128)S(1)}, u32[]{:S(2)}, u32[]{:S(2)}) collective-permute-start(f32[128,128]{1,0:T(8,128)S(1)} %shard_map.48.refs_4_), channel_id=1, source_target_pairs={{0,1},{1,0},{2,3},{3,2},{4,5},{5,4},{6,7},{7,6},{8,9},{9,8},{10,11... | collective-permute-start | bytes 196616 | tf_op jit(solution)/shard_map/ppermute | solution.py:108
  12.0 0.8 %collective-permute-start.6 = (f32[128,128]{1,0:T(8,128)S(1)}, f32[128,128]{1,0:T(8,128)S(1)}, u32[]{:S(2)}, u32[]{:S(2)}) collective-permute-start(f32[128,128]{1,0:T(8,128)S(1)} %shard_map.48.refs_4_), channel_id=1, source_target_pairs={{0,2},{1,3},{2,0},{3,1},{4,6},{5,7},{6,4},{7,5},{8,10},{9,11},{10,... | collective-permute-start | bytes 196616 | tf_op jit(solution)/shard_map/ppermute | solution.py:108
  12.8 1.6 %collective-permute-start.7 = (f32[128,128]{1,0:T(8,128)S(1)}, f32[128,128]{1,0:T(8,128)S(1)}, u32[]{:S(2)}, u32[]{:S(2)}) collective-permute-start(f32[128,128]{1,0:T(8,128)S(1)} %shard_map.48.refs_4_), channel_id=1, source_target_pairs={{0,3},{1,2},{2,1},{3,0},{4,7},{5,6},{6,5},{7,4},{8,11},{9,10},{10,... | collective-permute-start | bytes 196616 | tf_op jit(solution)/shard_map/ppermute | solution.py:108
  14.4 0.0 collective-permute-done.refs_1_
  14.4 0.0 collective-permute-done.2.refs_3_
  14.5 2.5 %collective-permute-start.3 = (f32[200,128]{1,0:T(8,128)S(1)}, f32[200,128]{1,0:T(8,128)S(1)}, u32[]{:S(2)}, u32[]{:S(2)}) collective-permute-start(f32[200,128]{1,0:T(8,128)S(1)} %constant_dynamic-update-slice_fusion.refs_0_), channel_id=1, source_target_pairs={{0,24},{4,28},{8,16},{12,20},{16,8},{20,12},{24,0},{28,4},{1,25},{... | collective-permute-start | bytes 307208 | tf_op jit(solution)/shard_map/ppermute | solution.py:108
  17.0 0.5 %collective-permute-start.4 = (f32[200,128]{1,0:T(8,128)S(1)}, f32[200,128]{1,0:T(8,128)S(1)}, u32[]{:S(2)}, u32[]{:S(2)}) collective-permute-start(f32[200,128]{1,0:T(8,128)S(1)} %constant_dynamic-update-slice_fusion.refs_0_), channel_id=1, source_target_pairs={{0,16},{4,20},{8,24},{12,28},{16,0},{20,4},{24,8},{28,12},{1,17},{... | collective-permute-start | bytes 307208 | tf_op jit(solution)/shard_map/ppermute | solution.py:108
  17.5 0.0 collective-permute-done.5.refs_5_
  17.5 0.2 collective-permute-done.6.refs_6_
  17.7 1.2 %collective-permute-done.7.refs_7_ = f32[128,128]{1,0:T(8,128)S(1)} collective-permute-done((f32[128,128]{1,0:T(8,128)S(1)}, f32[128,128]{1,0:T(8,128)S(1)}, u32[]{:S(2)}, u32[]{:S(2)}) %collective-permute-start.7) | collective-permute-done | bytes 65568 | tf_op jit(solution)/shard_map/ppermute | solution.py:108
  19.0 0.0 copy-done
  19.0 0.1 shard_map.49.group_ref
  19.0 0.1 collective-permute-start.8
  19.1 1.6 %collective-permute-start.9 = (f32[200,128]{1,0:T(8,128)S(1)}, f32[200,128]{1,0:T(8,128)S(1)}, u32[]{:S(2)}, u32[]{:S(2)}) collective-permute-start(f32[200,128]{1,0:T(8,128)S(1)} %constant_dynamic-update-slice_fusion.refs_0_), channel_id=1, source_target_pairs={{0,8},{4,12},{8,0},{12,4},{16,24},{20,28},{24,16},{28,20},{1,9},{5... | collective-permute-start | bytes 307208 | tf_op jit(solution)/shard_map/ppermute | solution.py:108
  20.6 0.3 shard_map.50
  20.9 0.0 collective-permute-done.3.refs_0_
  21.0 0.7 %collective-permute-done.4.refs_1_ = f32[200,128]{1,0:T(8,128)S(1)} collective-permute-done((f32[200,128]{1,0:T(8,128)S(1)}, f32[200,128]{1,0:T(8,128)S(1)}, u32[]{:S(2)}, u32[]{:S(2)}) %collective-permute-start.4) | collective-permute-done | bytes 102432 | tf_op jit(solution)/shard_map/ppermute | solution.py:108
  21.6 0.1 shard_map.47
  21.7 0.8 %shard_map.51 = (f32[128,128]{1,0:T(8,128)S(1)}, f32[128,128]{1,0:T(8,128)S(1)}) custom-call(f32[1,256]{1,0:T(1,128)S(1)} %get-tuple-element.21.before_ref.scale_ref, bf16[576,256]{1,0:T(8,128)(2,1)S(1)} %get-tuple-element.22.row_ref, f32[1,256]{1,0:T(1,128)S(1)} %get-tuple-element.21.before_ref.scale_ref, f32[8,256]{1,0:T(8,128)S(1)} %get-tuple-element.23.mask_ref, ...), custom_call_target="tpu_custom_call" | custom-call | tf_op jit(solution)/shard_map/pallas_call | solution.py:179
  22.5 0.0 collective-permute-done.8.group_ref
  22.5 0.3 shard_map.52
  22.8 0.8 %shard_map.53 = (f32[128,128]{1,0:T(8,128)S(1)}, f32[128,128]{1,0:T(8,128)S(1)}) custom-call(f32[128,128]{1,0:T(8,128)S(1)} %get-tuple-element.26.before_ref.refs_2_, bf16[576,256]{1,0:T(8,128)(2,1)S(1)} %get-tuple-element.22.row_ref, f32[1,256]{1,0:T(1,128)S(1)} %get-tuple-element.21.before_ref.scale_ref, f32[8,256]{1,0:T(8,128)S(1)} %get-tuple-element.23.mask_ref, ...), custom_call_target="tpu_custom_call" | custom-call | tf_op jit(solution)/shard_map/pallas_call | solution.py:179
  23.7 1.6 %collective-permute-start.11 = (f32[128,128]{1,0:T(8,128)S(1)}, f32[128,128]{1,0:T(8,128)S(1)}, u32[]{:S(2)}, u32[]{:S(2)}) collective-permute-start(f32[128,128]{1,0:T(8,128)S(1)} %get-tuple-element.30.before_ref), channel_id=1, source_target_pairs={{0,24},{4,28},{8,16},{12,20},{16,8},{20,12},{24,0},{28,4},{1,25},{... | collective-permute-start | bytes 196616 | tf_op jit(solution)/shard_map/ppermute | solution.py:108
  25.3 0.9 %collective-permute-start.12 = (f32[128,128]{1,0:T(8,128)S(1)}, f32[128,128]{1,0:T(8,128)S(1)}, u32[]{:S(2)}, u32[]{:S(2)}) collective-permute-start(f32[128,128]{1,0:T(8,128)S(1)} %get-tuple-element.36), channel_id=1, source_target_pairs={{0,16},{4,20},{8,24},{12,28},{16,0},{20,4},{24,8},{28,12},{1,17},{... | collective-permute-start | bytes 196616 | tf_op jit(solution)/shard_map/ppermute | solution.py:108
  26.2 0.0 collective-permute-done.9.refs_1_
  26.2 0.1 shard_map.54
  26.3 1.1 %shard_map.55 = (f32[128,128]{1,0:T(8,128)S(1)}, f32[128,128]{1,0:T(8,128)S(1)}) custom-call(f32[128,128]{1,0:T(8,128)S(1)} %get-tuple-element.30.before_ref, bf16[576,256]{1,0:T(8,128)(2,1)S(1)} %get-tuple-element.31.row_ref, f32[1,256]{1,0:T(1,128)S(1)} %get-tuple-element.32.scale_ref, f32[8,256]{1,0:T(8,128)S(1)} %get-tuple-element.33.mask_ref, ...), custom_call_target="tpu_custom_call" | custom-call | tf_op jit(solution)/shard_map/pallas_call | solution.py:179
  27.4 1.1 %collective-permute-start.10 = (f32[128,128]{1,0:T(8,128)S(1)}, f32[128,128]{1,0:T(8,128)S(1)}, u32[]{:S(2)}, u32[]{:S(2)}) collective-permute-start(f32[128,128]{1,0:T(8,128)S(1)} %get-tuple-element.35), channel_id=1, source_target_pairs={{0,8},{4,12},{8,0},{12,4},{16,24},{20,28},{24,16},{28,20},{1,9},{5... | collective-permute-start | bytes 196616 | tf_op jit(solution)/shard_map/ppermute | solution.py:108
  28.4 0.4 %collective-permute-done.11.refs_0_ = f32[128,128]{1,0:T(8,128)S(1)} collective-permute-done((f32[128,128]{1,0:T(8,128)S(1)}, f32[128,128]{1,0:T(8,128)S(1)}, u32[]{:S(2)}, u32[]{:S(2)}) %collective-permute-start.11) | collective-permute-done | bytes 65568 | tf_op jit(solution)/shard_map/ppermute | solution.py:108
  28.9 0.7 %collective-permute-done.12.refs_1_ = f32[128,128]{1,0:T(8,128)S(1)} collective-permute-done((f32[128,128]{1,0:T(8,128)S(1)}, f32[128,128]{1,0:T(8,128)S(1)}, u32[]{:S(2)}, u32[]{:S(2)}) %collective-permute-start.12) | collective-permute-done | bytes 65568 | tf_op jit(solution)/shard_map/ppermute | solution.py:108
  29.6 2.1 %collective-permute-done.10 = f32[128,128]{1,0:T(8,128)S(1)} collective-permute-done((f32[128,128]{1,0:T(8,128)S(1)}, f32[128,128]{1,0:T(8,128)S(1)}, u32[]{:S(2)}, u32[]{:S(2)}) %collective-permute-start.10) | collective-permute-done | bytes 65568 | tf_op jit(solution)/shard_map/ppermute | solution.py:108
  31.7 0.6 %add_add_fusion = f32[128,128]{1,0:T(8,128)} fusion(f32[128,128]{1,0:T(8,128)S(1)} %shard_map.56, f32[128,128]{1,0:T(8,128)S(1)} %get-tuple-element.34, f32[128,128]{1,0:T(8,128)S(1)} %collective-permute-done.10), kind=kLoop, calls=%fused_computation | loop fusion | flops 32768 | bytes 262144 | tf_op jit(solution)/shard_map/add | solution.py:203
  (6 shorter events, 0.0 us)
Async XLA Ops:
  0.0 9.5 %copy-start.1 = (f32[128,128]{1,0:T(8,128)S(1)}, f32[128,128]{1,0:T(8,128)}, u32[]{:S(2)}) copy-start(f32[128,128]{1,0:T(8,128)} %in_ref.1) | copy-start | bytes 196612
  0.0 14.4 %collective-permute-start = (f32[48,512]{1,0:T(8,128)}, f32[48,512]{1,0:T(8,128)S(1)}, u32[]{:S(2)}, u32[]{:S(2)}) collective-permute-start(f32[48,512]{1,0:T(8,128)} %refs_0_.1), channel_id=1, source_target_pairs={{0,2},{1,3},{2,0},{3,1},{4,6},{5,7},{6,4},{7,5},{8,10},{9,11},{10,... | collective-permute-start | bytes 294920 | tf_op jit(solution)/shard_map/ppermute | solution.py:108
  4.0 5.4 %collective-permute-start.1 = (f32[48,512]{1,0:T(8,128)}, f32[48,512]{1,0:T(8,128)S(1)}, u32[]{:S(2)}, u32[]{:S(2)}) collective-permute-start(f32[48,512]{1,0:T(8,128)} %refs_0_.1), channel_id=1, source_target_pairs={{0,1},{1,0},{2,3},{3,2},{4,5},{5,4},{6,7},{7,6},{8,9},{9,8},{10,11... | collective-permute-start | bytes 294920 | tf_op jit(solution)/shard_map/ppermute | solution.py:108
  5.6 8.8 %collective-permute-start.2 = (f32[48,512]{1,0:T(8,128)}, f32[48,512]{1,0:T(8,128)S(1)}, u32[]{:S(2)}, u32[]{:S(2)}) collective-permute-start(f32[48,512]{1,0:T(8,128)} %refs_0_.1), channel_id=1, source_target_pairs={{0,3},{1,2},{2,1},{3,0},{4,7},{5,6},{6,5},{7,4},{8,11},{9,10},{10,... | collective-permute-start | bytes 294920 | tf_op jit(solution)/shard_map/ppermute | solution.py:108
  5.6 0.7 %copy-start.2 = (s32[4,8]{1,0:T(4,128)S(1)}, s32[4,8]{1,0:T(4,128)}, u32[]{:S(2)}) copy-start(s32[4,8]{1,0:T(4,128)} %list_ref.1) | copy-start | bytes 388
  6.3 0.7 %copy-start.3 = (s32[4]{0:T(128)S(1)}, s32[4]{0:T(128)}, u32[]{:S(2)}) copy-start(s32[4]{0:T(128)} %count_ref.1) | copy-start | bytes 52
  9.5 9.5 %copy-start = (f32[48,512]{1,0:T(8,128)S(1)}, f32[48,512]{1,0:T(8,128)}, u32[]{:S(2)}) copy-start(f32[48,512]{1,0:T(8,128)} %refs_0_.1) | copy-start | bytes 294916
  9.5 8.0 %collective-permute-start.5 = (f32[128,128]{1,0:T(8,128)S(1)}, f32[128,128]{1,0:T(8,128)S(1)}, u32[]{:S(2)}, u32[]{:S(2)}) collective-permute-start(f32[128,128]{1,0:T(8,128)S(1)} %shard_map.48.refs_4_), channel_id=1, source_target_pairs={{0,1},{1,0},{2,3},{3,2},{4,5},{5,4},{6,7},{7,6},{8,9},{9,8},{10,11... | collective-permute-start | bytes 196616 | tf_op jit(solution)/shard_map/ppermute | solution.py:108
  12.0 5.8 %collective-permute-start.6 = (f32[128,128]{1,0:T(8,128)S(1)}, f32[128,128]{1,0:T(8,128)S(1)}, u32[]{:S(2)}, u32[]{:S(2)}) collective-permute-start(f32[128,128]{1,0:T(8,128)S(1)} %shard_map.48.refs_4_), channel_id=1, source_target_pairs={{0,2},{1,3},{2,0},{3,1},{4,6},{5,7},{6,4},{7,5},{8,10},{9,11},{10,... | collective-permute-start | bytes 196616 | tf_op jit(solution)/shard_map/ppermute | solution.py:108
  12.8 6.2 %collective-permute-start.7 = (f32[128,128]{1,0:T(8,128)S(1)}, f32[128,128]{1,0:T(8,128)S(1)}, u32[]{:S(2)}, u32[]{:S(2)}) collective-permute-start(f32[128,128]{1,0:T(8,128)S(1)} %shard_map.48.refs_4_), channel_id=1, source_target_pairs={{0,3},{1,2},{2,1},{3,0},{4,7},{5,6},{6,5},{7,4},{8,11},{9,10},{10,... | collective-permute-start | bytes 196616 | tf_op jit(solution)/shard_map/ppermute | solution.py:108
  14.5 6.5 %collective-permute-start.3 = (f32[200,128]{1,0:T(8,128)S(1)}, f32[200,128]{1,0:T(8,128)S(1)}, u32[]{:S(2)}, u32[]{:S(2)}) collective-permute-start(f32[200,128]{1,0:T(8,128)S(1)} %constant_dynamic-update-slice_fusion.refs_0_), channel_id=1, source_target_pairs={{0,24},{4,28},{8,16},{12,20},{16,8},{20,12},{24,0},{28,4},{1,25},{... | collective-permute-start | bytes 307208 | tf_op jit(solution)/shard_map/ppermute | solution.py:108
  17.0 4.7 %collective-permute-start.4 = (f32[200,128]{1,0:T(8,128)S(1)}, f32[200,128]{1,0:T(8,128)S(1)}, u32[]{:S(2)}, u32[]{:S(2)}) collective-permute-start(f32[200,128]{1,0:T(8,128)S(1)} %constant_dynamic-update-slice_fusion.refs_0_), channel_id=1, source_target_pairs={{0,16},{4,20},{8,24},{12,28},{16,0},{20,4},{24,8},{28,12},{1,17},{... | collective-permute-start | bytes 307208 | tf_op jit(solution)/shard_map/ppermute | solution.py:108
  19.0 3.5 %collective-permute-start.8 = (f32[320,512]{1,0:T(8,128)S(1)}, f32[320,512]{1,0:T(8,128)S(1)}, u32[]{:S(2)}, u32[]{:S(2)}) collective-permute-start(f32[320,512]{1,0:T(8,128)S(1)} %shard_map.49.group_ref), channel_id=1, source_target_pairs={{0,4},{4,0},{8,12},{12,8},{16,20},{20,16},{24,28},{28,24},{1,5},{5... | collective-permute-start | bytes 1966088 | tf_op jit(solution)/shard_map/ppermute | solution.py:108
  19.1 7.1 %collective-permute-start.9 = (f32[200,128]{1,0:T(8,128)S(1)}, f32[200,128]{1,0:T(8,128)S(1)}, u32[]{:S(2)}, u32[]{:S(2)}) collective-permute-start(f32[200,128]{1,0:T(8,128)S(1)} %constant_dynamic-update-slice_fusion.refs_0_), channel_id=1, source_target_pairs={{0,8},{4,12},{8,0},{12,4},{16,24},{20,28},{24,16},{28,20},{1,9},{5... | collective-permute-start | bytes 307208 | tf_op jit(solution)/shard_map/ppermute | solution.py:108
  23.7 5.2 %collective-permute-start.11 = (f32[128,128]{1,0:T(8,128)S(1)}, f32[128,128]{1,0:T(8,128)S(1)}, u32[]{:S(2)}, u32[]{:S(2)}) collective-permute-start(f32[128,128]{1,0:T(8,128)S(1)} %get-tuple-element.30.before_ref), channel_id=1, source_target_pairs={{0,24},{4,28},{8,16},{12,20},{16,8},{20,12},{24,0},{28,4},{1,25},{... | collective-permute-start | bytes 196616 | tf_op jit(solution)/shard_map/ppermute | solution.py:108
  25.3 4.3 %collective-permute-start.12 = (f32[128,128]{1,0:T(8,128)S(1)}, f32[128,128]{1,0:T(8,128)S(1)}, u32[]{:S(2)}, u32[]{:S(2)}) collective-permute-start(f32[128,128]{1,0:T(8,128)S(1)} %get-tuple-element.36), channel_id=1, source_target_pairs={{0,16},{4,20},{8,24},{12,28},{16,0},{20,4},{24,8},{28,12},{1,17},{... | collective-permute-start | bytes 196616 | tf_op jit(solution)/shard_map/ppermute | solution.py:108
  27.4 4.3 %collective-permute-start.10 = (f32[128,128]{1,0:T(8,128)S(1)}, f32[128,128]{1,0:T(8,128)S(1)}, u32[]{:S(2)}, u32[]{:S(2)}) collective-permute-start(f32[128,128]{1,0:T(8,128)S(1)} %get-tuple-element.35), channel_id=1, source_target_pairs={{0,8},{4,12},{8,0},{12,4},{16,24},{20,28},{24,16},{28,20},{1,9},{5... | collective-permute-start | bytes 196616 | tf_op jit(solution)/shard_map/ppermute | solution.py:108

commit v12 on v8

--- a/solution.py
+++ b/solution.py
@@ -125,7 +125,8 @@
         out_shape=shape(eigvecs.shape, f32),
         compiler_params=params,
     )(pieces[1], eigvecs)
-    vecs = [swapped(late_vecs, "rep", step) for step in range(rep_size - 1, 0, -1)] + [late_vecs]
+    vecs = [swapped(late_vecs if step > 1 else eigvecs, "rep", step) for step in range(rep_size - 1, 0, -1)]
+    vecs = [*vecs, late_vecs]
     lists = pl.pallas_call(
         lists_kernel,
         in_specs=[smem, smem],

time: 31.9 us -> 32.6 us (1.022)
  the two profiles are of different devices: /device:TPU:0 before, /device:TPU:16 now
where the time goes in v12:
time: 32.6 us; the launch traced here: 32.4 us
  starting transfers between devices  14.6 us (45%)
  waiting for transfers between devices  11.7 us (36%)
  Pallas kernels  3.27 us (10%)
  local copies, waits for them, and re-layouts  2.11 us (6%)
  other arithmetic  0.65 us (2%)
    ppermute x13, starting transfers between devices, swapped(): lax.ppermute(value, axis, [(source, source ^ step) for source in range(co...  14.6 us
    ppermute x13, waiting for transfers between devices, swapped(): lax.ppermute(value, axis, [(source, source ^ step) for source in range(co...  11.7 us
    unnamed x12, local copies, waits for them, and re-layouts  2.11 us
    pallas_call x1, Pallas kernels, shards(): pl.pallas_call(apply_kernel, out_shape=[shape((eig_count, width), f32)] *...  1.86 us
  transfers between devices with their start and end apart: 13, of which 7 were waited for; matrix products, arithmetic and copies ran while one was open for 2% of the time, Pallas kernels for 3%

profile of v12, /device:TPU:16, one launch (start us, length us, event | category | flops | bytes accessed | tf_op | source)
XLA Modules:
  0.0 32.4 jit_solution(12115609671622040589)
XLA Ops:
  0.0 0.0 copy-start.1
  0.0 0.0 collective-permute-start.1
  0.0 1.9 %collective-permute-start = (f32[48,512]{1,0:T(8,128)}, f32[48,512]{1,0:T(8,128)S(1)}, u32[]{:S(2)}, u32[]{:S(2)}) collective-permute-start(f32[48,512]{1,0:T(8,128)} %refs_0_.1), channel_id=1, source_target_pairs={{0,1},{1,0},{2,3},{3,2},{4,5},{5,4},{6,7},{7,6},{8,9},{9,8},{10,11... | collective-permute-start | bytes 294920 | tf_op jit(solution)/shard_map/ppermute | solution.py:102
  1.9 1.6 %collective-permute-start.2 = (f32[48,512]{1,0:T(8,128)}, f32[48,512]{1,0:T(8,128)S(1)}, u32[]{:S(2)}, u32[]{:S(2)}) collective-permute-start(f32[48,512]{1,0:T(8,128)} %refs_0_.1), channel_id=1, source_target_pairs={{0,3},{1,2},{2,1},{3,0},{4,7},{5,6},{6,5},{7,4},{8,11},{9,10},{10,... | collective-permute-start | bytes 294920 | tf_op jit(solution)/shard_map/ppermute | solution.py:102
  3.5 2.5 %collective-permute-start.8 = (f32[128,128]{1,0:T(8,128)}, f32[128,128]{1,0:T(8,128)S(1)}, u32[]{:S(2)}, u32[]{:S(2)}) collective-permute-start(f32[128,128]{1,0:T(8,128)} %in_ref.1), channel_id=1, source_target_pairs={{0,1},{1,0},{2,3},{3,2},{4,5},{5,4},{6,7},{7,6},{8,9},{9,8},{10,11... | collective-permute-start | bytes 196616 | tf_op jit(solution)/shard_map/ppermute | solution.py:102
  6.0 0.0 copy-start.2
  6.0 0.7 %copy-done.2 = s32[4,8]{1,0:T(4,128)S(1)} copy-done((s32[4,8]{1,0:T(4,128)S(1)}, s32[4,8]{1,0:T(4,128)}, u32[]{:S(2)}) %copy-start.2) | copy-done | bytes 152
  6.7 0.0 copy-start.3
  6.7 0.7 %copy-done.3 = s32[4]{0:T(128)S(1)} copy-done((s32[4]{0:T(128)S(1)}, s32[4]{0:T(128)}, u32[]{:S(2)}) %copy-start.3) | copy-done | bytes 40
  7.3 0.6 %shard_map.46 = f32[8,128]{1,0:T(8,128)S(1)} custom-call(s32[4,8]{1,0:T(4,128)S(1)} %copy-done.2, s32[4]{0:T(128)S(1)} %copy-done.3), custom_call_target="tpu_custom_call" | custom-call | tf_op jit(solution)/shard_map/pallas_call | solution.py:130
  7.9 0.7 %dynamic-slice_dynamic-update-slice_fusion.3 = f32[200,128]{1,0:T(8,128)S(1)} fusion(f32[48,512]{1,0:T(8,128)} %refs_0_.1, s32[]{:T(128)S(6)} %select_n.2), kind=kLoop, calls=%fused_computation.4 | loop fusion | bytes 49156
  8.7 0.0 collective-permute-done.before_ref.refs_1_
  8.7 0.0 copy-done.1
  8.7 0.0 copy-start
  8.7 1.0 %collective-permute-start.7 = (f32[128,128]{1,0:T(8,128)S(1)}, f32[128,128]{1,0:T(8,128)S(1)}, u32[]{:S(2)}, u32[]{:S(2)}) collective-permute-start(f32[128,128]{1,0:T(8,128)S(1)} %shard_map.48.refs_7_), channel_id=1, source_target_pairs={{0,2},{1,3},{2,0},{3,1},{4,6},{5,7},{6,4},{7,5},{8,10},{9,11},{10,... | collective-permute-start | bytes 196616 | tf_op jit(solution)/shard_map/ppermute | solution.py:102
  9.7 0.5 %collective-permute-start.6 = (f32[128,128]{1,0:T(8,128)S(1)}, f32[128,128]{1,0:T(8,128)S(1)}, u32[]{:S(2)}, u32[]{:S(2)}) collective-permute-start(f32[128,128]{1,0:T(8,128)S(1)} %shard_map.48.refs_7_), channel_id=1, source_target_pairs={{0,3},{1,2},{2,1},{3,0},{4,7},{5,6},{6,5},{7,4},{8,11},{9,10},{10,... | collective-permute-start | bytes 196616 | tf_op jit(solution)/shard_map/ppermute | solution.py:102
  10.2 0.0 collective-permute-done.1.refs_2_
  10.2 4.0 %collective-permute-done.2.refs_3_ = f32[48,512]{1,0:T(8,128)S(1)} collective-permute-done((f32[48,512]{1,0:T(8,128)}, f32[48,512]{1,0:T(8,128)S(1)}, u32[]{:S(2)}, u32[]{:S(2)}) %collective-permute-start.2) | collective-permute-done | bytes 98336 | tf_op jit(solution)/shard_map/ppermute | solution.py:102
  14.2 2.4 %collective-permute-start.5 = (f32[200,128]{1,0:T(8,128)S(1)}, f32[200,128]{1,0:T(8,128)S(1)}, u32[]{:S(2)}, u32[]{:S(2)}) collective-permute-start(f32[200,128]{1,0:T(8,128)S(1)} %constant_dynamic-update-slice_fusion.refs_0_), channel_id=1, source_target_pairs={{0,24},{4,28},{8,16},{12,20},{16,8},{20,12},{24,0},{28,4},{1,25},{... | collective-permute-start | bytes 307208 | tf_op jit(solution)/shard_map/ppermute | solution.py:102
  16.7 0.5 %collective-permute-start.4 = (f32[200,128]{1,0:T(8,128)S(1)}, f32[200,128]{1,0:T(8,128)S(1)}, u32[]{:S(2)}, u32[]{:S(2)}) collective-permute-start(f32[200,128]{1,0:T(8,128)S(1)} %constant_dynamic-update-slice_fusion.refs_0_), channel_id=1, source_target_pairs={{0,16},{4,20},{8,24},{12,28},{16,0},{20,4},{24,8},{28,12},{1,17},{... | collective-permute-start | bytes 307208 | tf_op jit(solution)/shard_map/ppermute | solution.py:102
  17.2 0.0 collective-permute-done.8.refs_6_
  17.2 0.5 %collective-permute-start.3 = (f32[200,128]{1,0:T(8,128)S(1)}, f32[200,128]{1,0:T(8,128)S(1)}, u32[]{:S(2)}, u32[]{:S(2)}) collective-permute-start(f32[200,128]{1,0:T(8,128)S(1)} %constant_dynamic-update-slice_fusion.refs_0_), channel_id=1, source_target_pairs={{0,8},{4,12},{8,0},{12,4},{16,24},{20,28},{24,16},{28,20},{1,9},{5... | collective-permute-start | bytes 307208 | tf_op jit(solution)/shard_map/ppermute | solution.py:102
  17.7 0.0 collective-permute-done.7.refs_5_
  17.7 0.0 collective-permute-done.6.refs_4_
  17.7 0.0 copy-done
  17.7 0.1 shard_map.49.group_ref
  17.8 0.1 collective-permute-start.9
  17.9 0.3 shard_map.50
  18.2 1.8 %collective-permute-done.5.refs_3_ = f32[200,128]{1,0:T(8,128)S(1)} collective-permute-done((f32[200,128]{1,0:T(8,128)S(1)}, f32[200,128]{1,0:T(8,128)S(1)}, u32[]{:S(2)}, u32[]{:S(2)}) %collective-permute-start.5) | collective-permute-done | bytes 102432 | tf_op jit(solution)/shard_map/ppermute | solution.py:102
  19.9 2.1 %collective-permute-done.4.refs_2_ = f32[200,128]{1,0:T(8,128)S(1)} collective-permute-done((f32[200,128]{1,0:T(8,128)S(1)}, f32[200,128]{1,0:T(8,128)S(1)}, u32[]{:S(2)}, u32[]{:S(2)}) %collective-permute-start.4) | collective-permute-done | bytes 102432 | tf_op jit(solution)/shard_map/ppermute | solution.py:102
  22.0 0.1 collective-permute-done.3.refs_1_
  22.1 0.2 shard_map.47
  22.3 0.0 collective-permute-done.9.group_ref
  22.3 0.3 shard_map.51
  22.6 1.9 %shard_map.52 = (f32[128,128]{1,0:T(8,128)S(1)}, f32[128,128]{1,0:T(8,128)S(1)}, f32[128,128]{1,0:T(8,128)S(1)}, f32[128,128]{1,0:T(8,128)S(1)}) custom-call(bf16[576,512]{1,0:T(8,128)(2,1)S(1)} %get-tuple-element.16.row_ref, f32[1,512]{1,0:T(1,128)S(1)} %get-tuple-element.17.scale_ref, f32[8,512]{1,0:T(8,128)S(1)} %get-tuple-element.18.mask_ref, ...), custom_call_target="tpu_custom_call" | custom-call | tf_op jit(solution)/shard_map/pallas_call | solution.py:168
  24.4 1.8 %collective-permute-start.10 = (f32[128,128]{1,0:T(8,128)S(1)}, f32[128,128]{1,0:T(8,128)S(1)}, u32[]{:S(2)}, u32[]{:S(2)}) collective-permute-start(f32[128,128]{1,0:T(8,128)S(1)} %get-tuple-element.24), channel_id=1, source_target_pairs={{0,24},{4,28},{8,16},{12,20},{16,8},{20,12},{24,0},{28,4},{1,25},{... | collective-permute-start | bytes 196616 | tf_op jit(solution)/shard_map/ppermute | solution.py:102
  26.2 1.3 %collective-permute-start.11 = (f32[128,128]{1,0:T(8,128)S(1)}, f32[128,128]{1,0:T(8,128)S(1)}, u32[]{:S(2)}, u32[]{:S(2)}) collective-permute-start(f32[128,128]{1,0:T(8,128)S(1)} %get-tuple-element.25), channel_id=1, source_target_pairs={{0,16},{4,20},{8,24},{12,28},{16,0},{20,4},{24,8},{28,12},{1,17},{... | collective-permute-start | bytes 196616 | tf_op jit(solution)/shard_map/ppermute | solution.py:102
  27.5 0.5 %collective-permute-start.12 = (f32[128,128]{1,0:T(8,128)S(1)}, f32[128,128]{1,0:T(8,128)S(1)}, u32[]{:S(2)}, u32[]{:S(2)}) collective-permute-start(f32[128,128]{1,0:T(8,128)S(1)} %get-tuple-element.26), channel_id=1, source_target_pairs={{0,8},{4,12},{8,0},{12,4},{16,24},{20,28},{24,16},{28,20},{1,9},{5... | collective-permute-start | bytes 196616 | tf_op jit(solution)/shard_map/ppermute | solution.py:102
  28.0 2.1 %collective-permute-done.10 = f32[128,128]{1,0:T(8,128)S(1)} collective-permute-done((f32[128,128]{1,0:T(8,128)S(1)}, f32[128,128]{1,0:T(8,128)S(1)}, u32[]{:S(2)}, u32[]{:S(2)}) %collective-permute-start.10) | collective-permute-done | bytes 65568 | tf_op jit(solution)/shard_map/ppermute | solution.py:102
  30.1 0.5 %collective-permute-done.11 = f32[128,128]{1,0:T(8,128)S(1)} collective-permute-done((f32[128,128]{1,0:T(8,128)S(1)}, f32[128,128]{1,0:T(8,128)S(1)}, u32[]{:S(2)}, u32[]{:S(2)}) %collective-permute-start.11) | collective-permute-done | bytes 65568 | tf_op jit(solution)/shard_map/ppermute | solution.py:102
  30.7 1.1 %collective-permute-done.12 = f32[128,128]{1,0:T(8,128)S(1)} collective-permute-done((f32[128,128]{1,0:T(8,128)S(1)}, f32[128,128]{1,0:T(8,128)S(1)}, u32[]{:S(2)}, u32[]{:S(2)}) %collective-permute-start.12) | collective-permute-done | bytes 65568 | tf_op jit(solution)/shard_map/ppermute | solution.py:102
  31.8 0.6 %add_add_fusion = f32[128,128]{1,0:T(8,128)} fusion(f32[128,128]{1,0:T(8,128)S(1)} %collective-permute-done.12, f32[128,128]{1,0:T(8,128)S(1)} %collective-permute-done.11, f32[128,128]{1,0:T(8,128)S(1)} %get-tuple-element.23, f32[128,128]{1,0:T(8,128)S(1)} %collective-permute-done.10), kind=kLoop, calls=%fused_computation | loop fusion | flops 49152 | bytes 327680 | tf_op jit(solution)/shard_map/add | solution.py:175
  (5 shorter events, 0.0 us)
Async XLA Ops:
  0.0 8.7 %copy-start.1 = (f32[128,128]{1,0:T(8,128)S(1)}, f32[128,128]{1,0:T(8,128)}, u32[]{:S(2)}) copy-start(f32[128,128]{1,0:T(8,128)} %in_ref.1) | copy-start | bytes 196612
  0.0 10.2 %collective-permute-start.1 = (f32[48,512]{1,0:T(8,128)}, f32[48,512]{1,0:T(8,128)S(1)}, u32[]{:S(2)}, u32[]{:S(2)}) collective-permute-start(f32[48,512]{1,0:T(8,128)} %refs_0_.1), channel_id=1, source_target_pairs={{0,2},{1,3},{2,0},{3,1},{4,6},{5,7},{6,4},{7,5},{8,10},{9,11},{10,... | collective-permute-start | bytes 294920 | tf_op jit(solution)/shard_map/ppermute | solution.py:102
  0.0 8.6 %collective-permute-start = (f32[48,512]{1,0:T(8,128)}, f32[48,512]{1,0:T(8,128)S(1)}, u32[]{:S(2)}, u32[]{:S(2)}) collective-permute-start(f32[48,512]{1,0:T(8,128)} %refs_0_.1), channel_id=1, source_target_pairs={{0,1},{1,0},{2,3},{3,2},{4,5},{5,4},{6,7},{7,6},{8,9},{9,8},{10,11... | collective-permute-start | bytes 294920 | tf_op jit(solution)/shard_map/ppermute | solution.py:102
  1.9 12.3 %collective-permute-start.2 = (f32[48,512]{1,0:T(8,128)}, f32[48,512]{1,0:T(8,128)S(1)}, u32[]{:S(2)}, u32[]{:S(2)}) collective-permute-start(f32[48,512]{1,0:T(8,128)} %refs_0_.1), channel_id=1, source_target_pairs={{0,3},{1,2},{2,1},{3,0},{4,7},{5,6},{6,5},{7,4},{8,11},{9,10},{10,... | collective-permute-start | bytes 294920 | tf_op jit(solution)/shard_map/ppermute | solution.py:102
  3.5 13.7 %collective-permute-start.8 = (f32[128,128]{1,0:T(8,128)}, f32[128,128]{1,0:T(8,128)S(1)}, u32[]{:S(2)}, u32[]{:S(2)}) collective-permute-start(f32[128,128]{1,0:T(8,128)} %in_ref.1), channel_id=1, source_target_pairs={{0,1},{1,0},{2,3},{3,2},{4,5},{5,4},{6,7},{7,6},{8,9},{9,8},{10,11... | collective-permute-start | bytes 196616 | tf_op jit(solution)/shard_map/ppermute | solution.py:102
  6.0 0.7 %copy-start.2 = (s32[4,8]{1,0:T(4,128)S(1)}, s32[4,8]{1,0:T(4,128)}, u32[]{:S(2)}) copy-start(s32[4,8]{1,0:T(4,128)} %list_ref.1) | copy-start | bytes 388
  6.7 0.7 %copy-start.3 = (s32[4]{0:T(128)S(1)}, s32[4]{0:T(128)}, u32[]{:S(2)}) copy-start(s32[4]{0:T(128)} %count_ref.1) | copy-start | bytes 52
  8.7 9.1 %copy-start = (f32[48,512]{1,0:T(8,128)S(1)}, f32[48,512]{1,0:T(8,128)}, u32[]{:S(2)}) copy-start(f32[48,512]{1,0:T(8,128)} %refs_0_.1) | copy-start | bytes 294916
  8.7 9.0 %collective-permute-start.7 = (f32[128,128]{1,0:T(8,128)S(1)}, f32[128,128]{1,0:T(8,128)S(1)}, u32[]{:S(2)}, u32[]{:S(2)}) collective-permute-start(f32[128,128]{1,0:T(8,128)S(1)} %shard_map.48.refs_7_), channel_id=1, source_target_pairs={{0,2},{1,3},{2,0},{3,1},{4,6},{5,7},{6,4},{7,5},{8,10},{9,11},{10,... | collective-permute-start | bytes 196616 | tf_op jit(solution)/shard_map/ppermute | solution.py:102
  9.7 8.0 %collective-permute-start.6 = (f32[128,128]{1,0:T(8,128)S(1)}, f32[128,128]{1,0:T(8,128)S(1)}, u32[]{:S(2)}, u32[]{:S(2)}) collective-permute-start(f32[128,128]{1,0:T(8,128)S(1)} %shard_map.48.refs_7_), channel_id=1, source_target_pairs={{0,3},{1,2},{2,1},{3,0},{4,7},{5,6},{6,5},{7,4},{8,11},{9,10},{10,... | collective-permute-start | bytes 196616 | tf_op jit(solution)/shard_map/ppermute | solution.py:102
  14.2 5.7 %collective-permute-start.5 = (f32[200,128]{1,0:T(8,128)S(1)}, f32[200,128]{1,0:T(8,128)S(1)}, u32[]{:S(2)}, u32[]{:S(2)}) collective-permute-start(f32[200,128]{1,0:T(8,128)S(1)} %constant_dynamic-update-slice_fusion.refs_0_), channel_id=1, source_target_pairs={{0,24},{4,28},{8,16},{12,20},{16,8},{20,12},{24,0},{28,4},{1,25},{... | collective-permute-start | bytes 307208 | tf_op jit(solution)/shard_map/ppermute | solution.py:102
  16.7 5.4 %collective-permute-start.4 = (f32[200,128]{1,0:T(8,128)S(1)}, f32[200,128]{1,0:T(8,128)S(1)}, u32[]{:S(2)}, u32[]{:S(2)}) collective-permute-start(f32[200,128]{1,0:T(8,128)S(1)} %constant_dynamic-update-slice_fusion.refs_0_), channel_id=1, source_target_pairs={{0,16},{4,20},{8,24},{12,28},{16,0},{20,4},{24,8},{28,12},{1,17},{... | collective-permute-start | bytes 307208 | tf_op jit(solution)/shard_map/ppermute | solution.py:102
  17.2 4.9 %collective-permute-start.3 = (f32[200,128]{1,0:T(8,128)S(1)}, f32[200,128]{1,0:T(8,128)S(1)}, u32[]{:S(2)}, u32[]{:S(2)}) collective-permute-start(f32[200,128]{1,0:T(8,128)S(1)} %constant_dynamic-update-slice_fusion.refs_0_), channel_id=1, source_target_pairs={{0,8},{4,12},{8,0},{12,4},{16,24},{20,28},{24,16},{28,20},{1,9},{5... | collective-permute-start | bytes 307208 | tf_op jit(solution)/shard_map/ppermute | solution.py:102
  17.8 4.5 %collective-permute-start.9 = (f32[320,512]{1,0:T(8,128)S(1)}, f32[320,512]{1,0:T(8,128)S(1)}, u32[]{:S(2)}, u32[]{:S(2)}) collective-permute-start(f32[320,512]{1,0:T(8,128)S(1)} %shard_map.49.group_ref), channel_id=1, source_target_pairs={{0,4},{4,0},{8,12},{12,8},{16,20},{20,16},{24,28},{28,24},{1,5},{5... | collective-permute-start | bytes 1966088 | tf_op jit(solution)/shard_map/ppermute | solution.py:102
  24.4 5.7 %collective-permute-start.10 = (f32[128,128]{1,0:T(8,128)S(1)}, f32[128,128]{1,0:T(8,128)S(1)}, u32[]{:S(2)}, u32[]{:S(2)}) collective-permute-start(f32[128,128]{1,0:T(8,128)S(1)} %get-tuple-element.24), channel_id=1, source_target_pairs={{0,24},{4,28},{8,16},{12,20},{16,8},{20,12},{24,0},{28,4},{1,25},{... | collective-permute-start | bytes 196616 | tf_op jit(solution)/shard_map/ppermute | solution.py:102
  26.2 4.5 %collective-permute-start.11 = (f32[128,128]{1,0:T(8,128)S(1)}, f32[128,128]{1,0:T(8,128)S(1)}, u32[]{:S(2)}, u32[]{:S(2)}) collective-permute-start(f32[128,128]{1,0:T(8,128)S(1)} %get-tuple-element.25), channel_id=1, source_target_pairs={{0,16},{4,20},{8,24},{12,28},{16,0},{20,4},{24,8},{28,12},{1,17},{... | collective-permute-start | bytes 196616 | tf_op jit(solution)/shard_map/ppermute | solution.py:102
  27.5 4.3 %collective-permute-start.12 = (f32[128,128]{1,0:T(8,128)S(1)}, f32[128,128]{1,0:T(8,128)S(1)}, u32[]{:S(2)}, u32[]{:S(2)}) collective-permute-start(f32[128,128]{1,0:T(8,128)S(1)} %get-tuple-element.26), channel_id=1, source_target_pairs={{0,8},{4,12},{8,0},{12,4},{16,24},{20,28},{24,16},{28,20},{1,9},{5... | collective-permute-start | bytes 196616 | tf_op jit(solution)/shard_map/ppermute | solution.py:102

commit v13 on v8

--- a/solution.py
+++ b/solution.py
@@ -9,6 +9,7 @@
 
 
 TRANSFER_FLOPS = 62 * 10**8
+LOG2_E = 1.4426950408889634
 
 
 def halves(value):
@@ -45,49 +46,51 @@
         out_ref[feat_count:, span] = ref[...]
 
 
-def columns_kernel(feat_count, group_ref, col_ref, vec_ref):
+def columns_kernel(feat_count, first, group_ref, col_ref, vec_ref):
     chunk = 2 * vec_ref.shape[0]
     cols = group_ref[:feat_count, :]
-    col_ref[...] = stacked(cols.T, "hhl", 1)
+    col_ref[:, : 3 * feat_count] = stacked(cols.T, "hhl", 1)
+    flags = (col_ref.shape[0], col_ref.shape[1] - 3 * feat_count)
+    block = lax.broadcasted_iota(jnp.int32, flags, 0) // vec_ref.shape[0] + first
+    here = lax.broadcasted_iota(jnp.int32, flags, 1) == block
+    col_ref[:, 3 * feat_count :] = jnp.where(here, 1.0, 0.0).astype(jnp.bfloat16)
     vecs = group_ref[feat_count:, :] * jnp.exp(jnp.sum(cols * cols, axis=0, keepdims=True) * (-1.0 / feat_count))
     for start in range(0, cols.shape[1], chunk):
         vec_ref[:, 3 * start : 3 * (start + chunk)] = stacked(vecs[:, start : start + chunk], "hhl", 1)
 
 
-def rows_kernel(feat_count, *refs):
-    panel_refs, (row_ref, scale_ref, mask_ref) = refs[:-3], refs[-3:]
+def rows_kernel(feat_count, group_blocks, *refs):
+    panel_refs, (row_ref, scale_ref, listed_ref) = refs[:-3], refs[-3:]
     width = panel_refs[0].shape[1]
-    group_blocks = mask_ref.shape[0] // 2
     blk_index = lax.axis_index("blk")
+    listed_ref[...] = jnp.ones_like(listed_ref)
     for place, ref in enumerate(panel_refs):
         span = slice(place * width, (place + 1) * width)
         rows = ref[:feat_count, :]
         scale_ref[:, span] = jnp.exp(jnp.sum(rows * rows, axis=0, keepdims=True) * (-1.0 / feat_count))
-        row_ref[:, span] = stacked(rows * (2.0 / feat_count), "hlh", 0)
+        row_ref[: 3 * feat_count, span] = stacked(rows * (2.0 * LOG2_E / feat_count), "hlh", 0)
         lists = ref[feat_count:, :]
         for spot in range(2 * group_blocks):
             column = (blk_index ^ (spot // group_blocks)) * group_blocks + spot % group_blocks
             hits = jnp.where(lists == column.astype(jnp.float32), 1.0, 0.0)
-            mask_ref[spot : spot + 1, span] = jnp.max(hits, axis=0, keepdims=True)
+            listed_ref[spot : spot + 1, span] = jnp.max(hits, axis=0, keepdims=True)
+    row_ref[3 * feat_count :, :] = ((listed_ref[...] - 1.0) * 16384.0).astype(jnp.bfloat16)
 
 
-def apply_kernel(row_ref, scale_ref, mask_ref, *refs):
+def apply_kernel(row_ref, scale_ref, *refs):
     own_cols, own_vecs, sibling_cols, sibling_vecs, *out_refs = refs
     width = out_refs[0].shape[1]
-    group_cols = own_cols.shape[0]
     chunk = 2 * width
     pairs = range(len(out_refs) // 2)
     totals = [None for _ in pairs]
-    for group, (col_ref, vec_ref) in enumerate(((own_cols, own_vecs), (sibling_cols, sibling_vecs))):
-        for start in range(0, group_cols, chunk):
-            at = (group * group_cols + start) // width
+    for col_ref, vec_ref in ((own_cols, own_vecs), (sibling_cols, sibling_vecs)):
+        for start in range(0, col_ref.shape[0], chunk):
             for pair in pairs:
                 span = slice(pair * chunk, (pair + 1) * chunk)
                 inner = jnp.dot(
                     col_ref[start : start + chunk, :], row_ref[:, span], preferred_element_type=jnp.float32
                 )
-                both = [jnp.broadcast_to(mask_ref[spot : spot + 1, span], (width, chunk)) for spot in (at, at + 1)]
-                weight = stacked(jnp.exp(inner) * jnp.concatenate(both, axis=0), "hlh", 0)
+                weight = stacked(jnp.exp2(inner), "hlh", 0)
                 vecs = vec_ref[:, 3 * start : 3 * (start + chunk)]
                 added = jnp.dot(vecs, weight, preferred_element_type=jnp.float32)
                 totals[pair] = added if totals[pair] is None else totals[pair] + added
@@ -145,25 +148,24 @@
     )(*pieces, *vecs)
     sibling_group = swapped(own_group, "blk", 1)
 
-    def columns_of(group):
+    depth = 3 * feat_count + max(16, 2 * group_blocks)
+
+    def columns_of(group, first):
         return pl.pallas_call(
-            functools.partial(columns_kernel, feat_count),
-            out_shape=[shape((group_cols, 3 * feat_count), bf16), shape((eig_count, 3 * group_cols), bf16)],
+            functools.partial(columns_kernel, feat_count, first),
+            out_shape=[shape((group_cols, depth), bf16), shape((eig_count, 3 * group_cols), bf16)],
             compiler_params=params,
         )(group)
 
     row_count = len(panels) * width
     rows = pl.pallas_call(
-        functools.partial(rows_kernel, feat_count),
-        out_shape=[
-            shape((3 * feat_count, row_count), bf16),
-            shape((1, row_count), f32),
-            shape((2 * group_blocks, row_count), f32),
-        ],
+        functools.partial(rows_kernel, feat_count, group_blocks),
+        out_shape=[shape((depth, row_count), bf16), shape((1, row_count), f32)],
+        scratch_shapes=[pltpu.VMEM((depth - 3 * feat_count, row_count), f32)],
         compiler_params=params,
         cost_estimate=hint,
     )(*panels)
-    columns = [*columns_of(own_group), *columns_of(sibling_group)]
+    columns = [*columns_of(own_group, 0), *columns_of(sibling_group, group_blocks)]
     tiles = pl.pallas_call(
         apply_kernel,
         out_shape=[shape((eig_count, width), f32)] * len(panels),

time: 31.9 us -> 31.9 us (level)
  no operation moved by 1% of the time
where the time goes in v13:
time: 31.9 us; the launch traced here: 31.7 us
  starting transfers between devices  17.7 us (55%)
  waiting for transfers between devices  7.68 us (24%)
  Pallas kernels  3.42 us (11%)
  local copies, waits for them, and re-layouts  2.12 us (7%)
  other arithmetic  0.65 us (2%)
    ppermute x13, starting transfers between devices, swapped(): lax.ppermute(value, axis, [(source, source ^ step) for source in range(co...  17.7 us
    ppermute x13, waiting for transfers between devices, swapped(): lax.ppermute(value, axis, [(source, source ^ step) for source in range(co...  7.68 us
    unnamed x12, local copies, waits for them, and re-layouts  2.12 us
    pallas_call x1, Pallas kernels, shards(): pl.pallas_call(apply_kernel, out_shape=[shape((eig_count, width), f32)] *...  1.86 us
    pallas_call x2, Pallas kernels, columns_of(): pl.pallas_call(functools.partial(columns_kernel, feat_count, first), out_...  0.72 us
    add x1, other arithmetic, shards(): total = total + swapped(tiles[place], 'blk', steps[place])  0.65 us
  transfers between devices with their start and end apart: 13, of which 8 were waited for; matrix products, arithmetic and copies ran while one was open for 2% of the time, Pallas kernels for 4%

profile of v13, /device:TPU:0, one launch (start us, length us, event | category | flops | bytes accessed | tf_op | source)
XLA Modules:
  0.0 31.7 jit_solution(2351511703558487266)
XLA Ops:
  0.0 0.0 copy-start.1
  0.0 4.0 %collective-permute-start.1 = (f32[48,512]{1,0:T(8,128)}, f32[48,512]{1,0:T(8,128)S(1)}, u32[]{:S(2)}, u32[]{:S(2)}) collective-permute-start(f32[48,512]{1,0:T(8,128)} %refs_0_.1), channel_id=1, source_target_pairs={{0,2},{1,3},{2,0},{3,1},{4,6},{5,7},{6,4},{7,5},{8,10},{9,11},{10,... | collective-permute-start | bytes 294920 | tf_op jit(solution)/shard_map/ppermute | solution.py:105
  4.0 1.6 %collective-permute-start = (f32[48,512]{1,0:T(8,128)}, f32[48,512]{1,0:T(8,128)S(1)}, u32[]{:S(2)}, u32[]{:S(2)}) collective-permute-start(f32[48,512]{1,0:T(8,128)} %refs_0_.1), channel_id=1, source_target_pairs={{0,1},{1,0},{2,3},{3,2},{4,5},{5,4},{6,7},{7,6},{8,9},{9,8},{10,11... | collective-permute-start | bytes 294920 | tf_op jit(solution)/shard_map/ppermute | solution.py:105
  5.6 0.0 collective-permute-start.2
  5.6 0.0 copy-start.2
  5.6 0.7 %copy-done.2 = s32[4,8]{1,0:T(4,128)S(1)} copy-done((s32[4,8]{1,0:T(4,128)S(1)}, s32[4,8]{1,0:T(4,128)}, u32[]{:S(2)}) %copy-start.2) | copy-done | bytes 152
  6.3 0.0 copy-start.3
  6.3 0.7 %copy-done.3 = s32[4]{0:T(128)S(1)} copy-done((s32[4]{0:T(128)S(1)}, s32[4]{0:T(128)}, u32[]{:S(2)}) %copy-start.3) | copy-done | bytes 40
  7.0 0.6 %shard_map.46 = f32[8,128]{1,0:T(8,128)S(1)} custom-call(s32[4,8]{1,0:T(4,128)S(1)} %copy-done.2, s32[4]{0:T(128)S(1)} %copy-done.3), custom_call_target="tpu_custom_call" | custom-call | tf_op jit(solution)/shard_map/pallas_call | solution.py:132
  7.6 0.7 %dynamic-slice_dynamic-update-slice_fusion.3 = f32[200,128]{1,0:T(8,128)S(1)} fusion(f32[48,512]{1,0:T(8,128)} %refs_0_.1, s32[]{:T(128)S(6)} %select_n.2), kind=kLoop, calls=%fused_computation.4 | loop fusion | bytes 49156
  8.3 1.2 %collective-permute-done.before_ref.refs_1_ = f32[48,512]{1,0:T(8,128)S(1)} collective-permute-done((f32[48,512]{1,0:T(8,128)}, f32[48,512]{1,0:T(8,128)S(1)}, u32[]{:S(2)}, u32[]{:S(2)}) %collective-permute-start) | collective-permute-done | bytes 98336 | tf_op jit(solution)/shard_map/ppermute | solution.py:105
  9.5 0.0 copy-done.1
  9.5 0.0 copy-start
  9.5 2.4 %collective-permute-start.8 = (f32[128,128]{1,0:T(8,128)S(1)}, f32[128,128]{1,0:T(8,128)S(1)}, u32[]{:S(2)}, u32[]{:S(2)}) collective-permute-start(f32[128,128]{1,0:T(8,128)S(1)} %shard_map.48.refs_7_), channel_id=1, source_target_pairs={{0,1},{1,0},{2,3},{3,2},{4,5},{5,4},{6,7},{7,6},{8,9},{9,8},{10,11... | collective-permute-start | bytes 196616 | tf_op jit(solution)/shard_map/ppermute | solution.py:105
  12.0 0.8 %collective-permute-start.7 = (f32[128,128]{1,0:T(8,128)S(1)}, f32[128,128]{1,0:T(8,128)S(1)}, u32[]{:S(2)}, u32[]{:S(2)}) collective-permute-start(f32[128,128]{1,0:T(8,128)S(1)} %shard_map.48.refs_7_), channel_id=1, source_target_pairs={{0,2},{1,3},{2,0},{3,1},{4,6},{5,7},{6,4},{7,5},{8,10},{9,11},{10,... | collective-permute-start | bytes 196616 | tf_op jit(solution)/shard_map/ppermute | solution.py:105
  12.8 1.6 %collective-permute-start.6 = (f32[128,128]{1,0:T(8,128)S(1)}, f32[128,128]{1,0:T(8,128)S(1)}, u32[]{:S(2)}, u32[]{:S(2)}) collective-permute-start(f32[128,128]{1,0:T(8,128)S(1)} %shard_map.48.refs_7_), channel_id=1, source_target_pairs={{0,3},{1,2},{2,1},{3,0},{4,7},{5,6},{6,5},{7,4},{8,11},{9,10},{10,... | collective-permute-start | bytes 196616 | tf_op jit(solution)/shard_map/ppermute | solution.py:105
  14.4 0.0 collective-permute-done.1.refs_2_
  14.4 0.0 collective-permute-done.2.refs_3_
  14.5 2.5 %collective-permute-start.5 = (f32[200,128]{1,0:T(8,128)S(1)}, f32[200,128]{1,0:T(8,128)S(1)}, u32[]{:S(2)}, u32[]{:S(2)}) collective-permute-start(f32[200,128]{1,0:T(8,128)S(1)} %constant_dynamic-update-slice_fusion.refs_0_), channel_id=1, source_target_pairs={{0,24},{4,28},{8,16},{12,20},{16,8},{20,12},{24,0},{28,4},{1,25},{... | collective-permute-start | bytes 307208 | tf_op jit(solution)/shard_map/ppermute | solution.py:105
  17.0 0.5 %collective-permute-start.4 = (f32[200,128]{1,0:T(8,128)S(1)}, f32[200,128]{1,0:T(8,128)S(1)}, u32[]{:S(2)}, u32[]{:S(2)}) collective-permute-start(f32[200,128]{1,0:T(8,128)S(1)} %constant_dynamic-update-slice_fusion.refs_0_), channel_id=1, source_target_pairs={{0,16},{4,20},{8,24},{12,28},{16,0},{20,4},{24,8},{28,12},{1,17},{... | collective-permute-start | bytes 307208 | tf_op jit(solution)/shard_map/ppermute | solution.py:105
  17.5 0.0 collective-permute-done.8.refs_6_
  17.5 0.5 %collective-permute-start.3 = (f32[200,128]{1,0:T(8,128)S(1)}, f32[200,128]{1,0:T(8,128)S(1)}, u32[]{:S(2)}, u32[]{:S(2)}) collective-permute-start(f32[200,128]{1,0:T(8,128)S(1)} %constant_dynamic-update-slice_fusion.refs_0_), channel_id=1, source_target_pairs={{0,8},{4,12},{8,0},{12,4},{16,24},{20,28},{24,16},{28,20},{1,9},{5... | collective-permute-start | bytes 307208 | tf_op jit(solution)/shard_map/ppermute | solution.py:105
  18.0 0.0 collective-permute-done.7.refs_5_
  18.0 0.9 %collective-permute-done.6.refs_4_ = f32[128,128]{1,0:T(8,128)S(1)} collective-permute-done((f32[128,128]{1,0:T(8,128)S(1)}, f32[128,128]{1,0:T(8,128)S(1)}, u32[]{:S(2)}, u32[]{:S(2)}) %collective-permute-start.6) | collective-permute-done | bytes 65568 | tf_op jit(solution)/shard_map/ppermute | solution.py:105
  19.0 0.0 copy-done
  19.0 0.1 shard_map.49.group_ref
  19.0 0.1 collective-permute-start.9
  19.1 0.4 %shard_map.50 = (bf16[512,592]{1,0:T(8,128)(2,1)S(1)}, bf16[128,1536]{1,0:T(8,128)(2,1)S(1)}) custom-call(f32[320,512]{1,0:T(8,128)S(1)} %shard_map.49.group_ref), custom_call_target="tpu_custom_call" | custom-call | tf_op jit(solution)/shard_map/pallas_call | solution.py:154
  19.5 1.0 %collective-permute-done.5.refs_3_ = f32[200,128]{1,0:T(8,128)S(1)} collective-permute-done((f32[200,128]{1,0:T(8,128)S(1)}, f32[200,128]{1,0:T(8,128)S(1)}, u32[]{:S(2)}, u32[]{:S(2)}) %collective-permute-start.5) | collective-permute-done | bytes 102432 | tf_op jit(solution)/shard_map/ppermute | solution.py:105
  20.4 1.2 %collective-permute-done.4.refs_2_ = f32[200,128]{1,0:T(8,128)S(1)} collective-permute-done((f32[200,128]{1,0:T(8,128)S(1)}, f32[200,128]{1,0:T(8,128)S(1)}, u32[]{:S(2)}, u32[]{:S(2)}) %collective-permute-start.4) | collective-permute-done | bytes 102432 | tf_op jit(solution)/shard_map/ppermute | solution.py:105
  21.6 0.5 %collective-permute-done.3.refs_1_ = f32[200,128]{1,0:T(8,128)S(1)} collective-permute-done((f32[200,128]{1,0:T(8,128)S(1)}, f32[200,128]{1,0:T(8,128)S(1)}, u32[]{:S(2)}, u32[]{:S(2)}) %collective-permute-start.3) | collective-permute-done | bytes 102432 | tf_op jit(solution)/shard_map/ppermute | solution.py:105
  22.1 0.2 shard_map.47
  22.3 0.0 collective-permute-done.9.group_ref
  22.3 0.4 %shard_map.51 = (bf16[512,592]{1,0:T(8,128)(2,1)S(1)}, bf16[128,1536]{1,0:T(8,128)(2,1)S(1)}) custom-call(f32[320,512]{1,0:T(8,128)S(1)} %collective-permute-done.9.group_ref), custom_call_target="tpu_custom_call" | custom-call | tf_op jit(solution)/shard_map/pallas_call | solution.py:154
  22.7 1.9 %shard_map.52 = (f32[128,128]{1,0:T(8,128)S(1)}, f32[128,128]{1,0:T(8,128)S(1)}, f32[128,128]{1,0:T(8,128)S(1)}, f32[128,128]{1,0:T(8,128)S(1)}) custom-call(bf16[592,512]{1,0:T(8,128)(2,1)S(1)} %get-tuple-element.15.row_ref, f32[1,512]{1,0:T(1,128)S(1)} %get-tuple-element.16.scale_ref, bf16[512,592]{1,0:T(8,128)(2,1)S(1)} %get-tuple-element.17.refs_0_, ...), custom_call_target="tpu_custom_call" | custom-call | tf_op jit(solution)/shard_map/pallas_call | solution.py:169
  24.6 1.6 %collective-permute-start.10 = (f32[128,128]{1,0:T(8,128)S(1)}, f32[128,128]{1,0:T(8,128)S(1)}, u32[]{:S(2)}, u32[]{:S(2)}) collective-permute-start(f32[128,128]{1,0:T(8,128)S(1)} %get-tuple-element.22), channel_id=1, source_target_pairs={{0,24},{4,28},{8,16},{12,20},{16,8},{20,12},{24,0},{28,4},{1,25},{... | collective-permute-start | bytes 196616 | tf_op jit(solution)/shard_map/ppermute | solution.py:105
  26.1 0.6 %collective-permute-start.11 = (f32[128,128]{1,0:T(8,128)S(1)}, f32[128,128]{1,0:T(8,128)S(1)}, u32[]{:S(2)}, u32[]{:S(2)}) collective-permute-start(f32[128,128]{1,0:T(8,128)S(1)} %get-tuple-element.23), channel_id=1, source_target_pairs={{0,16},{4,20},{8,24},{12,28},{16,0},{20,4},{24,8},{28,12},{1,17},{... | collective-permute-start | bytes 196616 | tf_op jit(solution)/shard_map/ppermute | solution.py:105
  26.7 1.4 %collective-permute-start.12 = (f32[128,128]{1,0:T(8,128)S(1)}, f32[128,128]{1,0:T(8,128)S(1)}, u32[]{:S(2)}, u32[]{:S(2)}) collective-permute-start(f32[128,128]{1,0:T(8,128)S(1)} %get-tuple-element.24), channel_id=1, source_target_pairs={{0,8},{4,12},{8,0},{12,4},{16,24},{20,28},{24,16},{28,20},{1,9},{5... | collective-permute-start | bytes 196616 | tf_op jit(solution)/shard_map/ppermute | solution.py:105
  28.1 2.0 %collective-permute-done.10 = f32[128,128]{1,0:T(8,128)S(1)} collective-permute-done((f32[128,128]{1,0:T(8,128)S(1)}, f32[128,128]{1,0:T(8,128)S(1)}, u32[]{:S(2)}, u32[]{:S(2)}) %collective-permute-start.10) | collective-permute-done | bytes 65568 | tf_op jit(solution)/shard_map/ppermute | solution.py:105
  30.1 0.5 %collective-permute-done.11 = f32[128,128]{1,0:T(8,128)S(1)} collective-permute-done((f32[128,128]{1,0:T(8,128)S(1)}, f32[128,128]{1,0:T(8,128)S(1)}, u32[]{:S(2)}, u32[]{:S(2)}) %collective-permute-start.11) | collective-permute-done | bytes 65568 | tf_op jit(solution)/shard_map/ppermute | solution.py:105
  30.6 0.4 %collective-permute-done.12 = f32[128,128]{1,0:T(8,128)S(1)} collective-permute-done((f32[128,128]{1,0:T(8,128)S(1)}, f32[128,128]{1,0:T(8,128)S(1)}, u32[]{:S(2)}, u32[]{:S(2)}) %collective-permute-start.12) | collective-permute-done | bytes 65568 | tf_op jit(solution)/shard_map/ppermute | solution.py:105
  31.0 0.6 %add_add_fusion = f32[128,128]{1,0:T(8,128)} fusion(f32[128,128]{1,0:T(8,128)S(1)} %collective-permute-done.12, f32[128,128]{1,0:T(8,128)S(1)} %collective-permute-done.11, f32[128,128]{1,0:T(8,128)S(1)} %get-tuple-element.21, f32[128,128]{1,0:T(8,128)S(1)} %collective-permute-done.10), kind=kLoop, calls=%fused_computation | loop fusion | flops 49152 | bytes 327680 | tf_op jit(solution)/shard_map/add | solution.py:176
  (5 shorter events, 0.0 us)
Async XLA Ops:
  0.0 9.5 %copy-start.1 = (f32[128,128]{1,0:T(8,128)S(1)}, f32[128,128]{1,0:T(8,128)}, u32[]{:S(2)}) copy-start(f32[128,128]{1,0:T(8,128)} %in_ref.1) | copy-start | bytes 196612
  0.0 14.4 %collective-permute-start.1 = (f32[48,512]{1,0:T(8,128)}, f32[48,512]{1,0:T(8,128)S(1)}, u32[]{:S(2)}, u32[]{:S(2)}) collective-permute-start(f32[48,512]{1,0:T(8,128)} %refs_0_.1), channel_id=1, source_target_pairs={{0,2},{1,3},{2,0},{3,1},{4,6},{5,7},{6,4},{7,5},{8,10},{9,11},{10,... | collective-permute-start | bytes 294920 | tf_op jit(solution)/shard_map/ppermute | solution.py:105
  4.0 5.4 %collective-permute-start = (f32[48,512]{1,0:T(8,128)}, f32[48,512]{1,0:T(8,128)S(1)}, u32[]{:S(2)}, u32[]{:S(2)}) collective-permute-start(f32[48,512]{1,0:T(8,128)} %refs_0_.1), channel_id=1, source_target_pairs={{0,1},{1,0},{2,3},{3,2},{4,5},{5,4},{6,7},{7,6},{8,9},{9,8},{10,11... | collective-permute-start | bytes 294920 | tf_op jit(solution)/shard_map/ppermute | solution.py:105
  5.6 8.8 %collective-permute-start.2 = (f32[48,512]{1,0:T(8,128)}, f32[48,512]{1,0:T(8,128)S(1)}, u32[]{:S(2)}, u32[]{:S(2)}) collective-permute-start(f32[48,512]{1,0:T(8,128)} %refs_0_.1), channel_id=1, source_target_pairs={{0,3},{1,2},{2,1},{3,0},{4,7},{5,6},{6,5},{7,4},{8,11},{9,10},{10,... | collective-permute-start | bytes 294920 | tf_op jit(solution)/shard_map/ppermute | solution.py:105
  5.6 0.7 %copy-start.2 = (s32[4,8]{1,0:T(4,128)S(1)}, s32[4,8]{1,0:T(4,128)}, u32[]{:S(2)}) copy-start(s32[4,8]{1,0:T(4,128)} %list_ref.1) | copy-start | bytes 388
  6.3 0.7 %copy-start.3 = (s32[4]{0:T(128)S(1)}, s32[4]{0:T(128)}, u32[]{:S(2)}) copy-start(s32[4]{0:T(128)} %count_ref.1) | copy-start | bytes 52
  9.5 9.5 %copy-start = (f32[48,512]{1,0:T(8,128)S(1)}, f32[48,512]{1,0:T(8,128)}, u32[]{:S(2)}) copy-start(f32[48,512]{1,0:T(8,128)} %refs_0_.1) | copy-start | bytes 294916
  9.5 8.0 %collective-permute-start.8 = (f32[128,128]{1,0:T(8,128)S(1)}, f32[128,128]{1,0:T(8,128)S(1)}, u32[]{:S(2)}, u32[]{:S(2)}) collective-permute-start(f32[128,128]{1,0:T(8,128)S(1)} %shard_map.48.refs_7_), channel_id=1, source_target_pairs={{0,1},{1,0},{2,3},{3,2},{4,5},{5,4},{6,7},{7,6},{8,9},{9,8},{10,11... | collective-permute-start | bytes 196616 | tf_op jit(solution)/shard_map/ppermute | solution.py:105
  12.0 6.1 %collective-permute-start.7 = (f32[128,128]{1,0:T(8,128)S(1)}, f32[128,128]{1,0:T(8,128)S(1)}, u32[]{:S(2)}, u32[]{:S(2)}) collective-permute-start(f32[128,128]{1,0:T(8,128)S(1)} %shard_map.48.refs_7_), channel_id=1, source_target_pairs={{0,2},{1,3},{2,0},{3,1},{4,6},{5,7},{6,4},{7,5},{8,10},{9,11},{10,... | collective-permute-start | bytes 196616 | tf_op jit(solution)/shard_map/ppermute | solution.py:105
  12.8 6.2 %collective-permute-start.6 = (f32[128,128]{1,0:T(8,128)S(1)}, f32[128,128]{1,0:T(8,128)S(1)}, u32[]{:S(2)}, u32[]{:S(2)}) collective-permute-start(f32[128,128]{1,0:T(8,128)S(1)} %shard_map.48.refs_7_), channel_id=1, source_target_pairs={{0,3},{1,2},{2,1},{3,0},{4,7},{5,6},{6,5},{7,4},{8,11},{9,10},{10,... | collective-permute-start | bytes 196616 | tf_op jit(solution)/shard_map/ppermute | solution.py:105
  14.5 6.0 %collective-permute-start.5 = (f32[200,128]{1,0:T(8,128)S(1)}, f32[200,128]{1,0:T(8,128)S(1)}, u32[]{:S(2)}, u32[]{:S(2)}) collective-permute-start(f32[200,128]{1,0:T(8,128)S(1)} %constant_dynamic-update-slice_fusion.refs_0_), channel_id=1, source_target_pairs={{0,24},{4,28},{8,16},{12,20},{16,8},{20,12},{24,0},{28,4},{1,25},{... | collective-permute-start | bytes 307208 | tf_op jit(solution)/shard_map/ppermute | solution.py:105
  17.0 4.7 %collective-permute-start.4 = (f32[200,128]{1,0:T(8,128)S(1)}, f32[200,128]{1,0:T(8,128)S(1)}, u32[]{:S(2)}, u32[]{:S(2)}) collective-permute-start(f32[200,128]{1,0:T(8,128)S(1)} %constant_dynamic-update-slice_fusion.refs_0_), channel_id=1, source_target_pairs={{0,16},{4,20},{8,24},{12,28},{16,0},{20,4},{24,8},{28,12},{1,17},{... | collective-permute-start | bytes 307208 | tf_op jit(solution)/shard_map/ppermute | solution.py:105
  17.5 4.7 %collective-permute-start.3 = (f32[200,128]{1,0:T(8,128)S(1)}, f32[200,128]{1,0:T(8,128)S(1)}, u32[]{:S(2)}, u32[]{:S(2)}) collective-permute-start(f32[200,128]{1,0:T(8,128)S(1)} %constant_dynamic-update-slice_fusion.refs_0_), channel_id=1, source_target_pairs={{0,8},{4,12},{8,0},{12,4},{16,24},{20,28},{24,16},{28,20},{1,9},{5... | collective-permute-start | bytes 307208 | tf_op jit(solution)/shard_map/ppermute | solution.py:105
  19.0 3.3 %collective-permute-start.9 = (f32[320,512]{1,0:T(8,128)S(1)}, f32[320,512]{1,0:T(8,128)S(1)}, u32[]{:S(2)}, u32[]{:S(2)}) collective-permute-start(f32[320,512]{1,0:T(8,128)S(1)} %shard_map.49.group_ref), channel_id=1, source_target_pairs={{0,4},{4,0},{8,12},{12,8},{16,20},{20,16},{24,28},{28,24},{1,5},{5... | collective-permute-start | bytes 1966088 | tf_op jit(solution)/shard_map/ppermute | solution.py:105
  24.6 5.6 %collective-permute-start.10 = (f32[128,128]{1,0:T(8,128)S(1)}, f32[128,128]{1,0:T(8,128)S(1)}, u32[]{:S(2)}, u32[]{:S(2)}) collective-permute-start(f32[128,128]{1,0:T(8,128)S(1)} %get-tuple-element.22), channel_id=1, source_target_pairs={{0,24},{4,28},{8,16},{12,20},{16,8},{20,12},{24,0},{28,4},{1,25},{... | collective-permute-start | bytes 196616 | tf_op jit(solution)/shard_map/ppermute | solution.py:105
  26.1 4.5 %collective-permute-start.11 = (f32[128,128]{1,0:T(8,128)S(1)}, f32[128,128]{1,0:T(8,128)S(1)}, u32[]{:S(2)}, u32[]{:S(2)}) collective-permute-start(f32[128,128]{1,0:T(8,128)S(1)} %get-tuple-element.23), channel_id=1, source_target_pairs={{0,16},{4,20},{8,24},{12,28},{16,0},{20,4},{24,8},{28,12},{1,17},{... | collective-permute-start | bytes 196616 | tf_op jit(solution)/shard_map/ppermute | solution.py:105
  26.7 4.3 %collective-permute-start.12 = (f32[128,128]{1,0:T(8,128)S(1)}, f32[128,128]{1,0:T(8,128)S(1)}, u32[]{:S(2)}, u32[]{:S(2)}) collective-permute-start(f32[128,128]{1,0:T(8,128)S(1)} %get-tuple-element.24), channel_id=1, source_target_pairs={{0,8},{4,12},{8,0},{12,4},{16,24},{20,28},{24,16},{28,20},{1,9},{5... | collective-permute-start | bytes 196616 | tf_op jit(solution)/shard_map/ppermute | solution.py:105

commit v14 on v8

--- a/solution.py
+++ b/solution.py
@@ -32,7 +32,7 @@
     out_ref[...] = in_ref[...]
 
 
-def group_kernel(piece_count, *refs):
+def group_kernel(piece_count, order, *refs):
     piece_refs, vec_refs, out_ref = refs[:piece_count], refs[piece_count:-1], refs[-1]
     piece_feats = piece_refs[0].shape[0]
     width = vec_refs[0].shape[1]
@@ -40,7 +40,7 @@
     rank = lax.axis_index("rep")
     for piece, ref in enumerate(piece_refs):
         out_ref[piece * piece_feats : (piece + 1) * piece_feats, :] = ref[...]
-    for spot, ref in enumerate(vec_refs[::-1]):
+    for spot, ref in zip(order, vec_refs):
         span = pl.ds(pl.multiple_of((rank ^ spot) * width, width), width)
         out_ref[feat_count:, span] = ref[...]
 
@@ -125,7 +125,8 @@
         out_shape=shape(eigvecs.shape, f32),
         compiler_params=params,
     )(pieces[1], eigvecs)
-    vecs = [swapped(late_vecs, "rep", step) for step in range(rep_size - 1, 0, -1)] + [late_vecs]
+    order = [*range(2, rep_size), 1, 0]
+    vecs = [swapped(late_vecs, "rep", step) for step in order[:-1]] + [late_vecs]
     lists = pl.pallas_call(
         lists_kernel,
         in_specs=[smem, smem],
@@ -139,7 +140,7 @@
     panels = [panel] + [swapped(panel, "blk", step) for step in steps[1:]]
 
     own_group = pl.pallas_call(
-        functools.partial(group_kernel, rep_size),
+        functools.partial(group_kernel, rep_size, order),
         out_shape=shape((feat_count + eig_count, group_cols), f32),
         compiler_params=params,
     )(*pieces, *vecs)

time: 31.9 us -> 31.9 us (level)
  waiting for transfers between devices: 7.75 us -> 8.81 us
  starting transfers between devices: 17.7 us -> 16.8 us
    ppermute x13, waiting for transfers between devices: 7.75 us -> 8.81 us  [swapped(): lax.ppermute(value, axis, [(source, source ^ step) for source in range(co...]
    ppermute x13, starting transfers between devices: 17.7 us -> 16.8 us  [swapped(): lax.ppermute(value, axis, [(source, source ^ step) for source in range(co...]
  transfers between devices with their start and end apart: 13 -> 13, of which waited for: 8 -> 9; matrix products, arithmetic and copies ran while one was open for 2% -> 2% of each run, Pallas kernels for 4% -> 3%
where the time goes in v14:
time: 31.9 us; the launch traced here: 31.7 us
  starting transfers between devices  16.8 us (53%)
  waiting for transfers between devices  8.81 us (28%)
  Pallas kernels  3.26 us (10%)
  local copies, waits for them, and re-layouts  2.12 us (7%)
  other arithmetic  0.65 us (2%)
    ppermute x13, starting transfers between devices, swapped(): lax.ppermute(value, axis, [(source, source ^ step) for source in range(co...  16.8 us
    ppermute x13, waiting for transfers between devices, swapped(): lax.ppermute(value, axis, [(source, source ^ step) for source in range(co...  8.81 us
    unnamed x12, local copies, waits for them, and re-layouts  2.12 us
    pallas_call x1, Pallas kernels, shards(): pl.pallas_call(apply_kernel, out_shape=[shape((eig_count, width), f32)] *...  1.86 us
    add x1, other arithmetic, shards(): total = total + swapped(tiles[place], 'blk', steps[place])  0.65 us
  transfers between devices with their start and end apart: 13, of which 9 were waited for; matrix products, arithmetic and copies ran while one was open for 2% of the time, Pallas kernels for 3%

profile of v14, /device:TPU:0, one launch (start us, length us, event | category | flops | bytes accessed | tf_op | source)
XLA Modules:
  0.0 31.7 jit_solution(9410994245980836547)
XLA Ops:
  0.0 0.0 copy-start.1
  0.0 4.0 %collective-permute-start.1 = (f32[48,512]{1,0:T(8,128)}, f32[48,512]{1,0:T(8,128)S(1)}, u32[]{:S(2)}, u32[]{:S(2)}) collective-permute-start(f32[48,512]{1,0:T(8,128)} %refs_0_.1), channel_id=1, source_target_pairs={{0,2},{1,3},{2,0},{3,1},{4,6},{5,7},{6,4},{7,5},{8,10},{9,11},{10,... | collective-permute-start | bytes 294920 | tf_op jit(solution)/shard_map/ppermute | solution.py:102
  4.0 1.6 %collective-permute-start = (f32[48,512]{1,0:T(8,128)}, f32[48,512]{1,0:T(8,128)S(1)}, u32[]{:S(2)}, u32[]{:S(2)}) collective-permute-start(f32[48,512]{1,0:T(8,128)} %refs_0_.1), channel_id=1, source_target_pairs={{0,1},{1,0},{2,3},{3,2},{4,5},{5,4},{6,7},{7,6},{8,9},{9,8},{10,11... | collective-permute-start | bytes 294920 | tf_op jit(solution)/shard_map/ppermute | solution.py:102
  5.6 0.0 collective-permute-start.2
  5.6 0.0 copy-start.2
  5.6 0.7 %copy-done.2 = s32[4,8]{1,0:T(4,128)S(1)} copy-done((s32[4,8]{1,0:T(4,128)S(1)}, s32[4,8]{1,0:T(4,128)}, u32[]{:S(2)}) %copy-start.2) | copy-done | bytes 152
  6.3 0.0 copy-start.3
  6.3 0.7 %copy-done.3 = s32[4]{0:T(128)S(1)} copy-done((s32[4]{0:T(128)S(1)}, s32[4]{0:T(128)}, u32[]{:S(2)}) %copy-start.3) | copy-done | bytes 40
  7.0 0.6 %shard_map.46 = f32[8,128]{1,0:T(8,128)S(1)} custom-call(s32[4,8]{1,0:T(4,128)S(1)} %copy-done.2, s32[4]{0:T(128)S(1)} %copy-done.3), custom_call_target="tpu_custom_call" | custom-call | tf_op jit(solution)/shard_map/pallas_call | solution.py:130
  7.6 0.7 %dynamic-slice_dynamic-update-slice_fusion.3 = f32[200,128]{1,0:T(8,128)S(1)} fusion(f32[48,512]{1,0:T(8,128)} %refs_0_.1, s32[]{:T(128)S(6)} %select_n.2), kind=kLoop, calls=%fused_computation.4 | loop fusion | bytes 49156
  8.3 1.2 %collective-permute-done.before_ref.refs_1_ = f32[48,512]{1,0:T(8,128)S(1)} collective-permute-done((f32[48,512]{1,0:T(8,128)}, f32[48,512]{1,0:T(8,128)S(1)}, u32[]{:S(2)}, u32[]{:S(2)}) %collective-permute-start) | collective-permute-done | bytes 98336 | tf_op jit(solution)/shard_map/ppermute | solution.py:102
  9.5 0.0 copy-done.1
  9.5 0.0 copy-start
  9.5 2.4 %collective-permute-start.8 = (f32[128,128]{1,0:T(8,128)S(1)}, f32[128,128]{1,0:T(8,128)S(1)}, u32[]{:S(2)}, u32[]{:S(2)}) collective-permute-start(f32[128,128]{1,0:T(8,128)S(1)} %shard_map.48.refs_7_), channel_id=1, source_target_pairs={{0,1},{1,0},{2,3},{3,2},{4,5},{5,4},{6,7},{7,6},{8,9},{9,8},{10,11... | collective-permute-start | bytes 196616 | tf_op jit(solution)/shard_map/ppermute | solution.py:102
  12.0 1.1 %collective-permute-start.7 = (f32[128,128]{1,0:T(8,128)S(1)}, f32[128,128]{1,0:T(8,128)S(1)}, u32[]{:S(2)}, u32[]{:S(2)}) collective-permute-start(f32[128,128]{1,0:T(8,128)S(1)} %shard_map.48.refs_7_), channel_id=1, source_target_pairs={{0,3},{1,2},{2,1},{3,0},{4,7},{5,6},{6,5},{7,4},{8,11},{9,10},{10,... | collective-permute-start | bytes 196616 | tf_op jit(solution)/shard_map/ppermute | solution.py:102
  13.1 0.4 %collective-permute-start.6 = (f32[128,128]{1,0:T(8,128)S(1)}, f32[128,128]{1,0:T(8,128)S(1)}, u32[]{:S(2)}, u32[]{:S(2)}) collective-permute-start(f32[128,128]{1,0:T(8,128)S(1)} %shard_map.48.refs_7_), channel_id=1, source_target_pairs={{0,2},{1,3},{2,0},{3,1},{4,6},{5,7},{6,4},{7,5},{8,10},{9,11},{10,... | collective-permute-start | bytes 196616 | tf_op jit(solution)/shard_map/ppermute | solution.py:102
  13.5 0.0 collective-permute-done.1.refs_2_
  13.5 0.0 collective-permute-done.2.refs_3_
  13.6 2.5 %collective-permute-start.5 = (f32[200,128]{1,0:T(8,128)S(1)}, f32[200,128]{1,0:T(8,128)S(1)}, u32[]{:S(2)}, u32[]{:S(2)}) collective-permute-start(f32[200,128]{1,0:T(8,128)S(1)} %constant_dynamic-update-slice_fusion.refs_0_), channel_id=1, source_target_pairs={{0,24},{4,28},{8,16},{12,20},{16,8},{20,12},{24,0},{28,4},{1,25},{... | collective-permute-start | bytes 307208 | tf_op jit(solution)/shard_map/ppermute | solution.py:102
  16.1 0.5 %collective-permute-start.4 = (f32[200,128]{1,0:T(8,128)S(1)}, f32[200,128]{1,0:T(8,128)S(1)}, u32[]{:S(2)}, u32[]{:S(2)}) collective-permute-start(f32[200,128]{1,0:T(8,128)S(1)} %constant_dynamic-update-slice_fusion.refs_0_), channel_id=1, source_target_pairs={{0,16},{4,20},{8,24},{12,28},{16,0},{20,4},{24,8},{28,12},{1,17},{... | collective-permute-start | bytes 307208 | tf_op jit(solution)/shard_map/ppermute | solution.py:102
  16.6 0.0 collective-permute-done.8.refs_6_
  16.6 0.5 %collective-permute-start.3 = (f32[200,128]{1,0:T(8,128)S(1)}, f32[200,128]{1,0:T(8,128)S(1)}, u32[]{:S(2)}, u32[]{:S(2)}) collective-permute-start(f32[200,128]{1,0:T(8,128)S(1)} %constant_dynamic-update-slice_fusion.refs_0_), channel_id=1, source_target_pairs={{0,8},{4,12},{8,0},{12,4},{16,24},{20,28},{24,16},{28,20},{1,9},{5... | collective-permute-start | bytes 307208 | tf_op jit(solution)/shard_map/ppermute | solution.py:102
  17.1 0.9 %collective-permute-done.7.refs_5_ = f32[128,128]{1,0:T(8,128)S(1)} collective-permute-done((f32[128,128]{1,0:T(8,128)S(1)}, f32[128,128]{1,0:T(8,128)S(1)}, u32[]{:S(2)}, u32[]{:S(2)}) %collective-permute-start.7) | collective-permute-done | bytes 65568 | tf_op jit(solution)/shard_map/ppermute | solution.py:102
  18.1 1.4 %collective-permute-done.6.refs_4_ = f32[128,128]{1,0:T(8,128)S(1)} collective-permute-done((f32[128,128]{1,0:T(8,128)S(1)}, f32[128,128]{1,0:T(8,128)S(1)}, u32[]{:S(2)}, u32[]{:S(2)}) %collective-permute-start.6) | collective-permute-done | bytes 65568 | tf_op jit(solution)/shard_map/ppermute | solution.py:102
  19.4 0.0 copy-done
  19.5 0.1 collective-permute-start.9
  19.6 0.3 shard_map.50
  19.9 0.0 collective-permute-done.5.refs_3_
  19.9 0.9 %collective-permute-done.4.refs_2_ = f32[200,128]{1,0:T(8,128)S(1)} collective-permute-done((f32[200,128]{1,0:T(8,128)S(1)}, f32[200,128]{1,0:T(8,128)S(1)}, u32[]{:S(2)}, u32[]{:S(2)}) %collective-permute-start.4) | collective-permute-done | bytes 102432 | tf_op jit(solution)/shard_map/ppermute | solution.py:102
  20.7 0.5 %collective-permute-done.3.refs_1_ = f32[200,128]{1,0:T(8,128)S(1)} collective-permute-done((f32[200,128]{1,0:T(8,128)S(1)}, f32[200,128]{1,0:T(8,128)S(1)}, u32[]{:S(2)}, u32[]{:S(2)}) %collective-permute-start.3) | collective-permute-done | bytes 102432 | tf_op jit(solution)/shard_map/ppermute | solution.py:102
  21.2 0.2 shard_map.47
  21.4 0.2 collective-permute-done.9.group_ref
  21.6 0.3 shard_map.51
  21.9 1.9 %shard_map.52 = (f32[128,128]{1,0:T(8,128)S(1)}, f32[128,128]{1,0:T(8,128)S(1)}, f32[128,128]{1,0:T(8,128)S(1)}, f32[128,128]{1,0:T(8,128)S(1)}) custom-call(bf16[576,512]{1,0:T(8,128)(2,1)S(1)} %get-tuple-element.16.row_ref, f32[1,512]{1,0:T(1,128)S(1)} %get-tuple-element.17.scale_ref, f32[8,512]{1,0:T(8,128)S(1)} %get-tuple-element.18.mask_ref, ...), custom_call_target="tpu_custom_call" | custom-call | tf_op jit(solution)/shard_map/pallas_call | solution.py:168
  23.8 2.5 %collective-permute-start.10 = (f32[128,128]{1,0:T(8,128)S(1)}, f32[128,128]{1,0:T(8,128)S(1)}, u32[]{:S(2)}, u32[]{:S(2)}) collective-permute-start(f32[128,128]{1,0:T(8,128)S(1)} %get-tuple-element.24), channel_id=1, source_target_pairs={{0,24},{4,28},{8,16},{12,20},{16,8},{20,12},{24,0},{28,4},{1,25},{... | collective-permute-start | bytes 196616 | tf_op jit(solution)/shard_map/ppermute | solution.py:102
  26.3 0.5 %collective-permute-start.11 = (f32[128,128]{1,0:T(8,128)S(1)}, f32[128,128]{1,0:T(8,128)S(1)}, u32[]{:S(2)}, u32[]{:S(2)}) collective-permute-start(f32[128,128]{1,0:T(8,128)S(1)} %get-tuple-element.25), channel_id=1, source_target_pairs={{0,16},{4,20},{8,24},{12,28},{16,0},{20,4},{24,8},{28,12},{1,17},{... | collective-permute-start | bytes 196616 | tf_op jit(solution)/shard_map/ppermute | solution.py:102
  26.8 0.5 %collective-permute-start.12 = (f32[128,128]{1,0:T(8,128)S(1)}, f32[128,128]{1,0:T(8,128)S(1)}, u32[]{:S(2)}, u32[]{:S(2)}) collective-permute-start(f32[128,128]{1,0:T(8,128)S(1)} %get-tuple-element.26), channel_id=1, source_target_pairs={{0,8},{4,12},{8,0},{12,4},{16,24},{20,28},{24,16},{28,20},{1,9},{5... | collective-permute-start | bytes 196616 | tf_op jit(solution)/shard_map/ppermute | solution.py:102
  27.4 1.7 %collective-permute-done.10 = f32[128,128]{1,0:T(8,128)S(1)} collective-permute-done((f32[128,128]{1,0:T(8,128)S(1)}, f32[128,128]{1,0:T(8,128)S(1)}, u32[]{:S(2)}, u32[]{:S(2)}) %collective-permute-start.10) | collective-permute-done | bytes 65568 | tf_op jit(solution)/shard_map/ppermute | solution.py:102
  29.1 1.5 %collective-permute-done.11 = f32[128,128]{1,0:T(8,128)S(1)} collective-permute-done((f32[128,128]{1,0:T(8,128)S(1)}, f32[128,128]{1,0:T(8,128)S(1)}, u32[]{:S(2)}, u32[]{:S(2)}) %collective-permute-start.11) | collective-permute-done | bytes 65568 | tf_op jit(solution)/shard_map/ppermute | solution.py:102
  30.6 0.5 %collective-permute-done.12 = f32[128,128]{1,0:T(8,128)S(1)} collective-permute-done((f32[128,128]{1,0:T(8,128)S(1)}, f32[128,128]{1,0:T(8,128)S(1)}, u32[]{:S(2)}, u32[]{:S(2)}) %collective-permute-start.12) | collective-permute-done | bytes 65568 | tf_op jit(solution)/shard_map/ppermute | solution.py:102
  31.1 0.6 %add_add_fusion = f32[128,128]{1,0:T(8,128)} fusion(f32[128,128]{1,0:T(8,128)S(1)} %collective-permute-done.12, f32[128,128]{1,0:T(8,128)S(1)} %collective-permute-done.11, f32[128,128]{1,0:T(8,128)S(1)} %get-tuple-element.23, f32[128,128]{1,0:T(8,128)S(1)} %collective-permute-done.10), kind=kLoop, calls=%fused_computation | loop fusion | flops 49152 | bytes 327680 | tf_op jit(solution)/shard_map/add | solution.py:175
  (6 shorter events, 0.1 us)
Async XLA Ops:
  0.0 9.5 %copy-start.1 = (f32[128,128]{1,0:T(8,128)S(1)}, f32[128,128]{1,0:T(8,128)}, u32[]{:S(2)}) copy-start(f32[128,128]{1,0:T(8,128)} %in_ref.1) | copy-start | bytes 196612
  0.0 13.5 %collective-permute-start.1 = (f32[48,512]{1,0:T(8,128)}, f32[48,512]{1,0:T(8,128)S(1)}, u32[]{:S(2)}, u32[]{:S(2)}) collective-permute-start(f32[48,512]{1,0:T(8,128)} %refs_0_.1), channel_id=1, source_target_pairs={{0,2},{1,3},{2,0},{3,1},{4,6},{5,7},{6,4},{7,5},{8,10},{9,11},{10,... | collective-permute-start | bytes 294920 | tf_op jit(solution)/shard_map/ppermute | solution.py:102
  4.0 5.4 %collective-permute-start = (f32[48,512]{1,0:T(8,128)}, f32[48,512]{1,0:T(8,128)S(1)}, u32[]{:S(2)}, u32[]{:S(2)}) collective-permute-start(f32[48,512]{1,0:T(8,128)} %refs_0_.1), channel_id=1, source_target_pairs={{0,1},{1,0},{2,3},{3,2},{4,5},{5,4},{6,7},{7,6},{8,9},{9,8},{10,11... | collective-permute-start | bytes 294920 | tf_op jit(solution)/shard_map/ppermute | solution.py:102
  5.6 7.9 %collective-permute-start.2 = (f32[48,512]{1,0:T(8,128)}, f32[48,512]{1,0:T(8,128)S(1)}, u32[]{:S(2)}, u32[]{:S(2)}) collective-permute-start(f32[48,512]{1,0:T(8,128)} %refs_0_.1), channel_id=1, source_target_pairs={{0,3},{1,2},{2,1},{3,0},{4,7},{5,6},{6,5},{7,4},{8,11},{9,10},{10,... | collective-permute-start | bytes 294920 | tf_op jit(solution)/shard_map/ppermute | solution.py:102
  5.6 0.7 %copy-start.2 = (s32[4,8]{1,0:T(4,128)S(1)}, s32[4,8]{1,0:T(4,128)}, u32[]{:S(2)}) copy-start(s32[4,8]{1,0:T(4,128)} %list_ref.1) | copy-start | bytes 388
  6.3 0.7 %copy-start.3 = (s32[4]{0:T(128)S(1)}, s32[4]{0:T(128)}, u32[]{:S(2)}) copy-start(s32[4]{0:T(128)} %count_ref.1) | copy-start | bytes 52
  9.5 9.9 %copy-start = (f32[48,512]{1,0:T(8,128)S(1)}, f32[48,512]{1,0:T(8,128)}, u32[]{:S(2)}) copy-start(f32[48,512]{1,0:T(8,128)} %refs_0_.1) | copy-start | bytes 294916
  9.5 7.1 %collective-permute-start.8 = (f32[128,128]{1,0:T(8,128)S(1)}, f32[128,128]{1,0:T(8,128)S(1)}, u32[]{:S(2)}, u32[]{:S(2)}) collective-permute-start(f32[128,128]{1,0:T(8,128)S(1)} %shard_map.48.refs_7_), channel_id=1, source_target_pairs={{0,1},{1,0},{2,3},{3,2},{4,5},{5,4},{6,7},{7,6},{8,9},{9,8},{10,11... | collective-permute-start | bytes 196616 | tf_op jit(solution)/shard_map/ppermute | solution.py:102
  12.0 6.1 %collective-permute-start.7 = (f32[128,128]{1,0:T(8,128)S(1)}, f32[128,128]{1,0:T(8,128)S(1)}, u32[]{:S(2)}, u32[]{:S(2)}) collective-permute-start(f32[128,128]{1,0:T(8,128)S(1)} %shard_map.48.refs_7_), channel_id=1, source_target_pairs={{0,3},{1,2},{2,1},{3,0},{4,7},{5,6},{6,5},{7,4},{8,11},{9,10},{10,... | collective-permute-start | bytes 196616 | tf_op jit(solution)/shard_map/ppermute | solution.py:102
  13.1 6.3 %collective-permute-start.6 = (f32[128,128]{1,0:T(8,128)S(1)}, f32[128,128]{1,0:T(8,128)S(1)}, u32[]{:S(2)}, u32[]{:S(2)}) collective-permute-start(f32[128,128]{1,0:T(8,128)S(1)} %shard_map.48.refs_7_), channel_id=1, source_target_pairs={{0,2},{1,3},{2,0},{3,1},{4,6},{5,7},{6,4},{7,5},{8,10},{9,11},{10,... | collective-permute-start | bytes 196616 | tf_op jit(solution)/shard_map/ppermute | solution.py:102
  13.6 6.3 %collective-permute-start.5 = (f32[200,128]{1,0:T(8,128)S(1)}, f32[200,128]{1,0:T(8,128)S(1)}, u32[]{:S(2)}, u32[]{:S(2)}) collective-permute-start(f32[200,128]{1,0:T(8,128)S(1)} %constant_dynamic-update-slice_fusion.refs_0_), channel_id=1, source_target_pairs={{0,24},{4,28},{8,16},{12,20},{16,8},{20,12},{24,0},{28,4},{1,25},{... | collective-permute-start | bytes 307208 | tf_op jit(solution)/shard_map/ppermute | solution.py:102
  16.1 4.7 %collective-permute-start.4 = (f32[200,128]{1,0:T(8,128)S(1)}, f32[200,128]{1,0:T(8,128)S(1)}, u32[]{:S(2)}, u32[]{:S(2)}) collective-permute-start(f32[200,128]{1,0:T(8,128)S(1)} %constant_dynamic-update-slice_fusion.refs_0_), channel_id=1, source_target_pairs={{0,16},{4,20},{8,24},{12,28},{16,0},{20,4},{24,8},{28,12},{1,17},{... | collective-permute-start | bytes 307208 | tf_op jit(solution)/shard_map/ppermute | solution.py:102
  16.6 4.7 %collective-permute-start.3 = (f32[200,128]{1,0:T(8,128)S(1)}, f32[200,128]{1,0:T(8,128)S(1)}, u32[]{:S(2)}, u32[]{:S(2)}) collective-permute-start(f32[200,128]{1,0:T(8,128)S(1)} %constant_dynamic-update-slice_fusion.refs_0_), channel_id=1, source_target_pairs={{0,8},{4,12},{8,0},{12,4},{16,24},{20,28},{24,16},{28,20},{1,9},{5... | collective-permute-start | bytes 307208 | tf_op jit(solution)/shard_map/ppermute | solution.py:102
  19.5 2.2 %collective-permute-start.9 = (f32[320,512]{1,0:T(8,128)S(1)}, f32[320,512]{1,0:T(8,128)S(1)}, u32[]{:S(2)}, u32[]{:S(2)}) collective-permute-start(f32[320,512]{1,0:T(8,128)S(1)} %shard_map.49.group_ref), channel_id=1, source_target_pairs={{0,4},{4,0},{8,12},{12,8},{16,20},{20,16},{24,28},{28,24},{1,5},{5... | collective-permute-start | bytes 1966088 | tf_op jit(solution)/shard_map/ppermute | solution.py:102
  23.8 5.3 %collective-permute-start.10 = (f32[128,128]{1,0:T(8,128)S(1)}, f32[128,128]{1,0:T(8,128)S(1)}, u32[]{:S(2)}, u32[]{:S(2)}) collective-permute-start(f32[128,128]{1,0:T(8,128)S(1)} %get-tuple-element.24), channel_id=1, source_target_pairs={{0,24},{4,28},{8,16},{12,20},{16,8},{20,12},{24,0},{28,4},{1,25},{... | collective-permute-start | bytes 196616 | tf_op jit(solution)/shard_map/ppermute | solution.py:102
  26.3 4.3 %collective-permute-start.11 = (f32[128,128]{1,0:T(8,128)S(1)}, f32[128,128]{1,0:T(8,128)S(1)}, u32[]{:S(2)}, u32[]{:S(2)}) collective-permute-start(f32[128,128]{1,0:T(8,128)S(1)} %get-tuple-element.25), channel_id=1, source_target_pairs={{0,16},{4,20},{8,24},{12,28},{16,0},{20,4},{24,8},{28,12},{1,17},{... | collective-permute-start | bytes 196616 | tf_op jit(solution)/shard_map/ppermute | solution.py:102
  26.8 4.3 %collective-permute-start.12 = (f32[128,128]{1,0:T(8,128)S(1)}, f32[128,128]{1,0:T(8,128)S(1)}, u32[]{:S(2)}, u32[]{:S(2)}) collective-permute-start(f32[128,128]{1,0:T(8,128)S(1)} %get-tuple-element.26), channel_id=1, source_target_pairs={{0,8},{4,12},{8,0},{12,4},{16,24},{20,28},{24,16},{28,20},{1,9},{5... | collective-permute-start | bytes 196616 | tf_op jit(solution)/shard_map/ppermute | solution.py:102

commit v15 on v14

--- a/solution.py
+++ b/solution.py
@@ -126,7 +126,7 @@
         compiler_params=params,
     )(pieces[1], eigvecs)
     order = [*range(2, rep_size), 1, 0]
-    vecs = [swapped(late_vecs, "rep", step) for step in order[:-1]] + [late_vecs]
+    vecs = [swapped(late_vecs if step > 1 else eigvecs, "rep", step) for step in order[:-1]] + [late_vecs]
     lists = pl.pallas_call(
         lists_kernel,
         in_specs=[smem, smem],

time: 31.9 us -> 33.3 us (1.044)
  the two profiles are of different devices: /device:TPU:0 before, /device:TPU:16 now
where the time goes in v15:
time: 33.3 us; the launch traced here: 33.1 us
  starting transfers between devices  15.5 us (47%)
  waiting for transfers between devices  11.5 us (35%)
  Pallas kernels  3.27 us (10%)
  local copies, waits for them, and re-layouts  2.11 us (6%)
  other arithmetic  0.65 us (2%)
    ppermute x13, starting transfers between devices, swapped(): lax.ppermute(value, axis, [(source, source ^ step) for source in range(co...  15.5 us
    ppermute x13, waiting for transfers between devices, swapped(): lax.ppermute(value, axis, [(source, source ^ step) for source in range(co...  11.5 us
    unnamed x12, local copies, waits for them, and re-layouts  2.11 us
    pallas_call x1, Pallas kernels, shards(): pl.pallas_call(apply_kernel, out_shape=[shape((eig_count, width), f32)] *...  1.86 us
  transfers between devices with their start and end apart: 13, of which 7 were waited for; matrix products, arithmetic and copies ran while one was open for 2% of the time, Pallas kernels for 3%

profile of v15, /device:TPU:16, one launch (start us, length us, event | category | flops | bytes accessed | tf_op | source)
XLA Modules:
  0.0 33.1 jit_solution(8608455295498116895)
XLA Ops:
  0.0 0.0 copy-start.1
  0.0 0.0 collective-permute-start.1
  0.0 1.9 %collective-permute-start = (f32[48,512]{1,0:T(8,128)}, f32[48,512]{1,0:T(8,128)S(1)}, u32[]{:S(2)}, u32[]{:S(2)}) collective-permute-start(f32[48,512]{1,0:T(8,128)} %refs_0_.1), channel_id=1, source_target_pairs={{0,1},{1,0},{2,3},{3,2},{4,5},{5,4},{6,7},{7,6},{8,9},{9,8},{10,11... | collective-permute-start | bytes 294920 | tf_op jit(solution)/shard_map/ppermute | solution.py:102
  1.9 1.6 %collective-permute-start.2 = (f32[48,512]{1,0:T(8,128)}, f32[48,512]{1,0:T(8,128)S(1)}, u32[]{:S(2)}, u32[]{:S(2)}) collective-permute-start(f32[48,512]{1,0:T(8,128)} %refs_0_.1), channel_id=1, source_target_pairs={{0,3},{1,2},{2,1},{3,0},{4,7},{5,6},{6,5},{7,4},{8,11},{9,10},{10,... | collective-permute-start | bytes 294920 | tf_op jit(solution)/shard_map/ppermute | solution.py:102
  3.5 2.5 %collective-permute-start.8 = (f32[128,128]{1,0:T(8,128)}, f32[128,128]{1,0:T(8,128)S(1)}, u32[]{:S(2)}, u32[]{:S(2)}) collective-permute-start(f32[128,128]{1,0:T(8,128)} %in_ref.1), channel_id=1, source_target_pairs={{0,1},{1,0},{2,3},{3,2},{4,5},{5,4},{6,7},{7,6},{8,9},{9,8},{10,11... | collective-permute-start | bytes 196616 | tf_op jit(solution)/shard_map/ppermute | solution.py:102
  6.0 0.0 copy-start.2
  6.0 0.7 %copy-done.2 = s32[4,8]{1,0:T(4,128)S(1)} copy-done((s32[4,8]{1,0:T(4,128)S(1)}, s32[4,8]{1,0:T(4,128)}, u32[]{:S(2)}) %copy-start.2) | copy-done | bytes 152
  6.7 0.0 copy-start.3
  6.7 0.7 %copy-done.3 = s32[4]{0:T(128)S(1)} copy-done((s32[4]{0:T(128)S(1)}, s32[4]{0:T(128)}, u32[]{:S(2)}) %copy-start.3) | copy-done | bytes 40
  7.3 0.6 %shard_map.46 = f32[8,128]{1,0:T(8,128)S(1)} custom-call(s32[4,8]{1,0:T(4,128)S(1)} %copy-done.2, s32[4]{0:T(128)S(1)} %copy-done.3), custom_call_target="tpu_custom_call" | custom-call | tf_op jit(solution)/shard_map/pallas_call | solution.py:130
  7.9 0.7 %dynamic-slice_dynamic-update-slice_fusion.3 = f32[200,128]{1,0:T(8,128)S(1)} fusion(f32[48,512]{1,0:T(8,128)} %refs_0_.1, s32[]{:T(128)S(6)} %select_n.2), kind=kLoop, calls=%fused_computation.4 | loop fusion | bytes 49156
  8.7 0.0 collective-permute-done.before_ref.refs_1_
  8.7 0.0 copy-done.1
  8.7 0.0 copy-start
  8.7 0.7 %collective-permute-start.7 = (f32[128,128]{1,0:T(8,128)S(1)}, f32[128,128]{1,0:T(8,128)S(1)}, u32[]{:S(2)}, u32[]{:S(2)}) collective-permute-start(f32[128,128]{1,0:T(8,128)S(1)} %shard_map.48.refs_7_), channel_id=1, source_target_pairs={{0,3},{1,2},{2,1},{3,0},{4,7},{5,6},{6,5},{7,4},{8,11},{9,10},{10,... | collective-permute-start | bytes 196616 | tf_op jit(solution)/shard_map/ppermute | solution.py:102
  9.4 1.7 %collective-permute-start.6 = (f32[128,128]{1,0:T(8,128)S(1)}, f32[128,128]{1,0:T(8,128)S(1)}, u32[]{:S(2)}, u32[]{:S(2)}) collective-permute-start(f32[128,128]{1,0:T(8,128)S(1)} %shard_map.48.refs_7_), channel_id=1, source_target_pairs={{0,2},{1,3},{2,0},{3,1},{4,6},{5,7},{6,4},{7,5},{8,10},{9,11},{10,... | collective-permute-start | bytes 196616 | tf_op jit(solution)/shard_map/ppermute | solution.py:102
  11.1 0.0 collective-permute-done.1.refs_2_
  11.1 3.8 %collective-permute-done.2.refs_3_ = f32[48,512]{1,0:T(8,128)S(1)} collective-permute-done((f32[48,512]{1,0:T(8,128)}, f32[48,512]{1,0:T(8,128)S(1)}, u32[]{:S(2)}, u32[]{:S(2)}) %collective-permute-start.2) | collective-permute-done | bytes 98336 | tf_op jit(solution)/shard_map/ppermute | solution.py:102
  14.9 2.4 %collective-permute-start.5 = (f32[200,128]{1,0:T(8,128)S(1)}, f32[200,128]{1,0:T(8,128)S(1)}, u32[]{:S(2)}, u32[]{:S(2)}) collective-permute-start(f32[200,128]{1,0:T(8,128)S(1)} %constant_dynamic-update-slice_fusion.refs_0_), channel_id=1, source_target_pairs={{0,24},{4,28},{8,16},{12,20},{16,8},{20,12},{24,0},{28,4},{1,25},{... | collective-permute-start | bytes 307208 | tf_op jit(solution)/shard_map/ppermute | solution.py:102
  17.4 0.5 %collective-permute-start.4 = (f32[200,128]{1,0:T(8,128)S(1)}, f32[200,128]{1,0:T(8,128)S(1)}, u32[]{:S(2)}, u32[]{:S(2)}) collective-permute-start(f32[200,128]{1,0:T(8,128)S(1)} %constant_dynamic-update-slice_fusion.refs_0_), channel_id=1, source_target_pairs={{0,16},{4,20},{8,24},{12,28},{16,0},{20,4},{24,8},{28,12},{1,17},{... | collective-permute-start | bytes 307208 | tf_op jit(solution)/shard_map/ppermute | solution.py:102
  17.9 0.0 collective-permute-done.8.refs_6_
  17.9 0.5 %collective-permute-start.3 = (f32[200,128]{1,0:T(8,128)S(1)}, f32[200,128]{1,0:T(8,128)S(1)}, u32[]{:S(2)}, u32[]{:S(2)}) collective-permute-start(f32[200,128]{1,0:T(8,128)S(1)} %constant_dynamic-update-slice_fusion.refs_0_), channel_id=1, source_target_pairs={{0,8},{4,12},{8,0},{12,4},{16,24},{20,28},{24,16},{28,20},{1,9},{5... | collective-permute-start | bytes 307208 | tf_op jit(solution)/shard_map/ppermute | solution.py:102
  18.4 0.0 collective-permute-done.7.refs_5_
  18.4 0.0 collective-permute-done.6.refs_4_
  18.4 0.0 copy-done
  18.5 0.1 collective-permute-start.9
  18.6 0.3 shard_map.50
  18.9 1.8 %collective-permute-done.5.refs_3_ = f32[200,128]{1,0:T(8,128)S(1)} collective-permute-done((f32[200,128]{1,0:T(8,128)S(1)}, f32[200,128]{1,0:T(8,128)S(1)}, u32[]{:S(2)}, u32[]{:S(2)}) %collective-permute-start.5) | collective-permute-done | bytes 102432 | tf_op jit(solution)/shard_map/ppermute | solution.py:102
  20.6 2.1 %collective-permute-done.4.refs_2_ = f32[200,128]{1,0:T(8,128)S(1)} collective-permute-done((f32[200,128]{1,0:T(8,128)S(1)}, f32[200,128]{1,0:T(8,128)S(1)}, u32[]{:S(2)}, u32[]{:S(2)}) %collective-permute-start.4) | collective-permute-done | bytes 102432 | tf_op jit(solution)/shard_map/ppermute | solution.py:102
  22.7 0.1 collective-permute-done.3.refs_1_
  22.8 0.2 shard_map.47
  23.0 0.0 collective-permute-done.9.group_ref
  23.0 0.3 shard_map.51
  23.3 1.9 %shard_map.52 = (f32[128,128]{1,0:T(8,128)S(1)}, f32[128,128]{1,0:T(8,128)S(1)}, f32[128,128]{1,0:T(8,128)S(1)}, f32[128,128]{1,0:T(8,128)S(1)}) custom-call(bf16[576,512]{1,0:T(8,128)(2,1)S(1)} %get-tuple-element.16.row_ref, f32[1,512]{1,0:T(1,128)S(1)} %get-tuple-element.17.scale_ref, f32[8,512]{1,0:T(8,128)S(1)} %get-tuple-element.18.mask_ref, ...), custom_call_target="tpu_custom_call" | custom-call | tf_op jit(solution)/shard_map/pallas_call | solution.py:168
  25.1 1.8 %collective-permute-start.10 = (f32[128,128]{1,0:T(8,128)S(1)}, f32[128,128]{1,0:T(8,128)S(1)}, u32[]{:S(2)}, u32[]{:S(2)}) collective-permute-start(f32[128,128]{1,0:T(8,128)S(1)} %get-tuple-element.24), channel_id=1, source_target_pairs={{0,24},{4,28},{8,16},{12,20},{16,8},{20,12},{24,0},{28,4},{1,25},{... | collective-permute-start | bytes 196616 | tf_op jit(solution)/shard_map/ppermute | solution.py:102
  26.9 1.3 %collective-permute-start.11 = (f32[128,128]{1,0:T(8,128)S(1)}, f32[128,128]{1,0:T(8,128)S(1)}, u32[]{:S(2)}, u32[]{:S(2)}) collective-permute-start(f32[128,128]{1,0:T(8,128)S(1)} %get-tuple-element.25), channel_id=1, source_target_pairs={{0,16},{4,20},{8,24},{12,28},{16,0},{20,4},{24,8},{28,12},{1,17},{... | collective-permute-start | bytes 196616 | tf_op jit(solution)/shard_map/ppermute | solution.py:102
  28.2 0.5 %collective-permute-start.12 = (f32[128,128]{1,0:T(8,128)S(1)}, f32[128,128]{1,0:T(8,128)S(1)}, u32[]{:S(2)}, u32[]{:S(2)}) collective-permute-start(f32[128,128]{1,0:T(8,128)S(1)} %get-tuple-element.26), channel_id=1, source_target_pairs={{0,8},{4,12},{8,0},{12,4},{16,24},{20,28},{24,16},{28,20},{1,9},{5... | collective-permute-start | bytes 196616 | tf_op jit(solution)/shard_map/ppermute | solution.py:102
  28.7 2.1 %collective-permute-done.10 = f32[128,128]{1,0:T(8,128)S(1)} collective-permute-done((f32[128,128]{1,0:T(8,128)S(1)}, f32[128,128]{1,0:T(8,128)S(1)}, u32[]{:S(2)}, u32[]{:S(2)}) %collective-permute-start.10) | collective-permute-done | bytes 65568 | tf_op jit(solution)/shard_map/ppermute | solution.py:102
  30.8 0.5 %collective-permute-done.11 = f32[128,128]{1,0:T(8,128)S(1)} collective-permute-done((f32[128,128]{1,0:T(8,128)S(1)}, f32[128,128]{1,0:T(8,128)S(1)}, u32[]{:S(2)}, u32[]{:S(2)}) %collective-permute-start.11) | collective-permute-done | bytes 65568 | tf_op jit(solution)/shard_map/ppermute | solution.py:102
  31.4 1.1 %collective-permute-done.12 = f32[128,128]{1,0:T(8,128)S(1)} collective-permute-done((f32[128,128]{1,0:T(8,128)S(1)}, f32[128,128]{1,0:T(8,128)S(1)}, u32[]{:S(2)}, u32[]{:S(2)}) %collective-permute-start.12) | collective-permute-done | bytes 65568 | tf_op jit(solution)/shard_map/ppermute | solution.py:102
  32.5 0.6 %add_add_fusion = f32[128,128]{1,0:T(8,128)} fusion(f32[128,128]{1,0:T(8,128)S(1)} %collective-permute-done.12, f32[128,128]{1,0:T(8,128)S(1)} %collective-permute-done.11, f32[128,128]{1,0:T(8,128)S(1)} %get-tuple-element.23, f32[128,128]{1,0:T(8,128)S(1)} %collective-permute-done.10), kind=kLoop, calls=%fused_computation | loop fusion | flops 49152 | bytes 327680 | tf_op jit(solution)/shard_map/add | solution.py:175
  (6 shorter events, 0.1 us)
Async XLA Ops:
  0.0 8.7 %copy-start.1 = (f32[128,128]{1,0:T(8,128)S(1)}, f32[128,128]{1,0:T(8,128)}, u32[]{:S(2)}) copy-start(f32[128,128]{1,0:T(8,128)} %in_ref.1) | copy-start | bytes 196612
  0.0 11.1 %collective-permute-start.1 = (f32[48,512]{1,0:T(8,128)}, f32[48,512]{1,0:T(8,128)S(1)}, u32[]{:S(2)}, u32[]{:S(2)}) collective-permute-start(f32[48,512]{1,0:T(8,128)} %refs_0_.1), channel_id=1, source_target_pairs={{0,2},{1,3},{2,0},{3,1},{4,6},{5,7},{6,4},{7,5},{8,10},{9,11},{10,... | collective-permute-start | bytes 294920 | tf_op jit(solution)/shard_map/ppermute | solution.py:102
  0.0 8.6 %collective-permute-start = (f32[48,512]{1,0:T(8,128)}, f32[48,512]{1,0:T(8,128)S(1)}, u32[]{:S(2)}, u32[]{:S(2)}) collective-permute-start(f32[48,512]{1,0:T(8,128)} %refs_0_.1), channel_id=1, source_target_pairs={{0,1},{1,0},{2,3},{3,2},{4,5},{5,4},{6,7},{7,6},{8,9},{9,8},{10,11... | collective-permute-start | bytes 294920 | tf_op jit(solution)/shard_map/ppermute | solution.py:102
  1.9 13.0 %collective-permute-start.2 = (f32[48,512]{1,0:T(8,128)}, f32[48,512]{1,0:T(8,128)S(1)}, u32[]{:S(2)}, u32[]{:S(2)}) collective-permute-start(f32[48,512]{1,0:T(8,128)} %refs_0_.1), channel_id=1, source_target_pairs={{0,3},{1,2},{2,1},{3,0},{4,7},{5,6},{6,5},{7,4},{8,11},{9,10},{10,... | collective-permute-start | bytes 294920 | tf_op jit(solution)/shard_map/ppermute | solution.py:102
  3.5 14.4 %collective-permute-start.8 = (f32[128,128]{1,0:T(8,128)}, f32[128,128]{1,0:T(8,128)S(1)}, u32[]{:S(2)}, u32[]{:S(2)}) collective-permute-start(f32[128,128]{1,0:T(8,128)} %in_ref.1), channel_id=1, source_target_pairs={{0,1},{1,0},{2,3},{3,2},{4,5},{5,4},{6,7},{7,6},{8,9},{9,8},{10,11... | collective-permute-start | bytes 196616 | tf_op jit(solution)/shard_map/ppermute | solution.py:102
  6.0 0.7 %copy-start.2 = (s32[4,8]{1,0:T(4,128)S(1)}, s32[4,8]{1,0:T(4,128)}, u32[]{:S(2)}) copy-start(s32[4,8]{1,0:T(4,128)} %list_ref.1) | copy-start | bytes 388
  6.7 0.7 %copy-start.3 = (s32[4]{0:T(128)S(1)}, s32[4]{0:T(128)}, u32[]{:S(2)}) copy-start(s32[4]{0:T(128)} %count_ref.1) | copy-start | bytes 52
  8.7 9.8 %copy-start = (f32[48,512]{1,0:T(8,128)S(1)}, f32[48,512]{1,0:T(8,128)}, u32[]{:S(2)}) copy-start(f32[48,512]{1,0:T(8,128)} %refs_0_.1) | copy-start | bytes 294916
  8.7 9.7 %collective-permute-start.7 = (f32[128,128]{1,0:T(8,128)S(1)}, f32[128,128]{1,0:T(8,128)S(1)}, u32[]{:S(2)}, u32[]{:S(2)}) collective-permute-start(f32[128,128]{1,0:T(8,128)S(1)} %shard_map.48.refs_7_), channel_id=1, source_target_pairs={{0,3},{1,2},{2,1},{3,0},{4,7},{5,6},{6,5},{7,4},{8,11},{9,10},{10,... | collective-permute-start | bytes 196616 | tf_op jit(solution)/shard_map/ppermute | solution.py:102
  9.4 9.0 %collective-permute-start.6 = (f32[128,128]{1,0:T(8,128)S(1)}, f32[128,128]{1,0:T(8,128)S(1)}, u32[]{:S(2)}, u32[]{:S(2)}) collective-permute-start(f32[128,128]{1,0:T(8,128)S(1)} %shard_map.48.refs_7_), channel_id=1, source_target_pairs={{0,2},{1,3},{2,0},{3,1},{4,6},{5,7},{6,4},{7,5},{8,10},{9,11},{10,... | collective-permute-start | bytes 196616 | tf_op jit(solution)/shard_map/ppermute | solution.py:102
  14.9 5.7 %collective-permute-start.5 = (f32[200,128]{1,0:T(8,128)S(1)}, f32[200,128]{1,0:T(8,128)S(1)}, u32[]{:S(2)}, u32[]{:S(2)}) collective-permute-start(f32[200,128]{1,0:T(8,128)S(1)} %constant_dynamic-update-slice_fusion.refs_0_), channel_id=1, source_target_pairs={{0,24},{4,28},{8,16},{12,20},{16,8},{20,12},{24,0},{28,4},{1,25},{... | collective-permute-start | bytes 307208 | tf_op jit(solution)/shard_map/ppermute | solution.py:102
  17.4 5.4 %collective-permute-start.4 = (f32[200,128]{1,0:T(8,128)S(1)}, f32[200,128]{1,0:T(8,128)S(1)}, u32[]{:S(2)}, u32[]{:S(2)}) collective-permute-start(f32[200,128]{1,0:T(8,128)S(1)} %constant_dynamic-update-slice_fusion.refs_0_), channel_id=1, source_target_pairs={{0,16},{4,20},{8,24},{12,28},{16,0},{20,4},{24,8},{28,12},{1,17},{... | collective-permute-start | bytes 307208 | tf_op jit(solution)/shard_map/ppermute | solution.py:102
  17.9 4.9 %collective-permute-start.3 = (f32[200,128]{1,0:T(8,128)S(1)}, f32[200,128]{1,0:T(8,128)S(1)}, u32[]{:S(2)}, u32[]{:S(2)}) collective-permute-start(f32[200,128]{1,0:T(8,128)S(1)} %constant_dynamic-update-slice_fusion.refs_0_), channel_id=1, source_target_pairs={{0,8},{4,12},{8,0},{12,4},{16,24},{20,28},{24,16},{28,20},{1,9},{5... | collective-permute-start | bytes 307208 | tf_op jit(solution)/shard_map/ppermute | solution.py:102
  18.5 4.5 %collective-permute-start.9 = (f32[320,512]{1,0:T(8,128)S(1)}, f32[320,512]{1,0:T(8,128)S(1)}, u32[]{:S(2)}, u32[]{:S(2)}) collective-permute-start(f32[320,512]{1,0:T(8,128)S(1)} %shard_map.49.group_ref), channel_id=1, source_target_pairs={{0,4},{4,0},{8,12},{12,8},{16,20},{20,16},{24,28},{28,24},{1,5},{5... | collective-permute-start | bytes 1966088 | tf_op jit(solution)/shard_map/ppermute | solution.py:102
  25.1 5.7 %collective-permute-start.10 = (f32[128,128]{1,0:T(8,128)S(1)}, f32[128,128]{1,0:T(8,128)S(1)}, u32[]{:S(2)}, u32[]{:S(2)}) collective-permute-start(f32[128,128]{1,0:T(8,128)S(1)} %get-tuple-element.24), channel_id=1, source_target_pairs={{0,24},{4,28},{8,16},{12,20},{16,8},{20,12},{24,0},{28,4},{1,25},{... | collective-permute-start | bytes 196616 | tf_op jit(solution)/shard_map/ppermute | solution.py:102
  26.9 4.5 %collective-permute-start.11 = (f32[128,128]{1,0:T(8,128)S(1)}, f32[128,128]{1,0:T(8,128)S(1)}, u32[]{:S(2)}, u32[]{:S(2)}) collective-permute-start(f32[128,128]{1,0:T(8,128)S(1)} %get-tuple-element.25), channel_id=1, source_target_pairs={{0,16},{4,20},{8,24},{12,28},{16,0},{20,4},{24,8},{28,12},{1,17},{... | collective-permute-start | bytes 196616 | tf_op jit(solution)/shard_map/ppermute | solution.py:102
  28.2 4.3 %collective-permute-start.12 = (f32[128,128]{1,0:T(8,128)S(1)}, f32[128,128]{1,0:T(8,128)S(1)}, u32[]{:S(2)}, u32[]{:S(2)}) collective-permute-start(f32[128,128]{1,0:T(8,128)S(1)} %get-tuple-element.26), channel_id=1, source_target_pairs={{0,8},{4,12},{8,0},{12,4},{16,24},{20,28},{24,16},{28,20},{1,9},{5... | collective-permute-start | bytes 196616 | tf_op jit(solution)/shard_map/ppermute | solution.py:102

commit v16 on v13

--- a/solution.py
+++ b/solution.py
@@ -33,7 +33,7 @@
     out_ref[...] = in_ref[...]
 
 
-def group_kernel(piece_count, *refs):
+def group_kernel(piece_count, order, *refs):
     piece_refs, vec_refs, out_ref = refs[:piece_count], refs[piece_count:-1], refs[-1]
     piece_feats = piece_refs[0].shape[0]
     width = vec_refs[0].shape[1]
@@ -41,7 +41,7 @@
     rank = lax.axis_index("rep")
     for piece, ref in enumerate(piece_refs):
         out_ref[piece * piece_feats : (piece + 1) * piece_feats, :] = ref[...]
-    for spot, ref in enumerate(vec_refs[::-1]):
+    for spot, ref in zip(order, vec_refs):
         span = pl.ds(pl.multiple_of((rank ^ spot) * width, width), width)
         out_ref[feat_count:, span] = ref[...]
 
@@ -128,7 +128,8 @@
         out_shape=shape(eigvecs.shape, f32),
         compiler_params=params,
     )(pieces[1], eigvecs)
-    vecs = [swapped(late_vecs, "rep", step) for step in range(rep_size - 1, 0, -1)] + [late_vecs]
+    order = [*range(2, rep_size), 1, 0]
+    vecs = [swapped(late_vecs, "rep", step) for step in order[:-1]] + [late_vecs]
     lists = pl.pallas_call(
         lists_kernel,
         in_specs=[smem, smem],
@@ -142,7 +143,7 @@
     panels = [panel] + [swapped(panel, "blk", step) for step in steps[1:]]
 
     own_group = pl.pallas_call(
-        functools.partial(group_kernel, rep_size),
+        functools.partial(group_kernel, rep_size, order),
         out_shape=shape((feat_count + eig_count, group_cols), f32),
         compiler_params=params,
     )(*pieces, *vecs)

time: 31.9 us -> 32 us (level)
  waiting for transfers between devices: 7.68 us -> 8.74 us
  starting transfers between devices: 17.7 us -> 16.8 us
    ppermute x13, waiting for transfers between devices: 7.68 us -> 8.74 us  [swapped(): lax.ppermute(value, axis, [(source, source ^ step) for source in range(co...]
    ppermute x13, starting transfers between devices: 17.7 us -> 16.8 us  [swapped(): lax.ppermute(value, axis, [(source, source ^ step) for source in range(co...]
  transfers between devices with their start and end apart: 13 -> 13, of which waited for: 8 -> 9; matrix products, arithmetic and copies ran while one was open for 2% -> 2% of each run, Pallas kernels for 4% -> 4%
where the time goes in v16:
time: 32 us; the launch traced here: 31.8 us
  starting transfers between devices  16.8 us (52%)
  waiting for transfers between devices  8.74 us (27%)
  Pallas kernels  3.41 us (11%)
  local copies, waits for them, and re-layouts  2.12 us (7%)
  other arithmetic  0.65 us (2%)
    ppermute x13, starting transfers between devices, swapped(): lax.ppermute(value, axis, [(source, source ^ step) for source in range(co...  16.8 us
    ppermute x13, waiting for transfers between devices, swapped(): lax.ppermute(value, axis, [(source, source ^ step) for source in range(co...  8.74 us
    unnamed x12, local copies, waits for them, and re-layouts  2.12 us
    pallas_call x1, Pallas kernels, shards(): pl.pallas_call(apply_kernel, out_shape=[shape((eig_count, width), f32)] *...  1.85 us
    pallas_call x2, Pallas kernels, columns_of(): pl.pallas_call(functools.partial(columns_kernel, feat_count, first), out_...  0.72 us
    add x1, other arithmetic, shards(): total = total + swapped(tiles[place], 'blk', steps[place])  0.65 us
  transfers between devices with their start and end apart: 13, of which 9 were waited for; matrix products, arithmetic and copies ran while one was open for 2% of the time, Pallas kernels for 4%

profile of v16, /device:TPU:0, one launch (start us, length us, event | category | flops | bytes accessed | tf_op | source)
XLA Modules:
  0.0 31.8 jit_solution(10419435542100782551)
XLA Ops:
  0.0 0.0 copy-start.1
  0.0 4.0 %collective-permute-start.1 = (f32[48,512]{1,0:T(8,128)}, f32[48,512]{1,0:T(8,128)S(1)}, u32[]{:S(2)}, u32[]{:S(2)}) collective-permute-start(f32[48,512]{1,0:T(8,128)} %refs_0_.1), channel_id=1, source_target_pairs={{0,2},{1,3},{2,0},{3,1},{4,6},{5,7},{6,4},{7,5},{8,10},{9,11},{10,... | collective-permute-start | bytes 294920 | tf_op jit(solution)/shard_map/ppermute | solution.py:105
  4.0 1.6 %collective-permute-start = (f32[48,512]{1,0:T(8,128)}, f32[48,512]{1,0:T(8,128)S(1)}, u32[]{:S(2)}, u32[]{:S(2)}) collective-permute-start(f32[48,512]{1,0:T(8,128)} %refs_0_.1), channel_id=1, source_target_pairs={{0,1},{1,0},{2,3},{3,2},{4,5},{5,4},{6,7},{7,6},{8,9},{9,8},{10,11... | collective-permute-start | bytes 294920 | tf_op jit(solution)/shard_map/ppermute | solution.py:105
  5.6 0.0 collective-permute-start.2
  5.6 0.0 copy-start.2
  5.6 0.7 %copy-done.2 = s32[4,8]{1,0:T(4,128)S(1)} copy-done((s32[4,8]{1,0:T(4,128)S(1)}, s32[4,8]{1,0:T(4,128)}, u32[]{:S(2)}) %copy-start.2) | copy-done | bytes 152
  6.3 0.0 copy-start.3
  6.3 0.7 %copy-done.3 = s32[4]{0:T(128)S(1)} copy-done((s32[4]{0:T(128)S(1)}, s32[4]{0:T(128)}, u32[]{:S(2)}) %copy-start.3) | copy-done | bytes 40
  7.0 0.6 %shard_map.46 = f32[8,128]{1,0:T(8,128)S(1)} custom-call(s32[4,8]{1,0:T(4,128)S(1)} %copy-done.2, s32[4]{0:T(128)S(1)} %copy-done.3), custom_call_target="tpu_custom_call" | custom-call | tf_op jit(solution)/shard_map/pallas_call | solution.py:133
  7.6 0.7 %dynamic-slice_dynamic-update-slice_fusion.3 = f32[200,128]{1,0:T(8,128)S(1)} fusion(f32[48,512]{1,0:T(8,128)} %refs_0_.1, s32[]{:T(128)S(6)} %select_n.2), kind=kLoop, calls=%fused_computation.4 | loop fusion | bytes 49156
  8.3 1.2 %collective-permute-done.before_ref.refs_1_ = f32[48,512]{1,0:T(8,128)S(1)} collective-permute-done((f32[48,512]{1,0:T(8,128)}, f32[48,512]{1,0:T(8,128)S(1)}, u32[]{:S(2)}, u32[]{:S(2)}) %collective-permute-start) | collective-permute-done | bytes 98336 | tf_op jit(solution)/shard_map/ppermute | solution.py:105
  9.5 0.0 copy-done.1
  9.5 0.0 copy-start
  9.5 2.4 %collective-permute-start.8 = (f32[128,128]{1,0:T(8,128)S(1)}, f32[128,128]{1,0:T(8,128)S(1)}, u32[]{:S(2)}, u32[]{:S(2)}) collective-permute-start(f32[128,128]{1,0:T(8,128)S(1)} %shard_map.48.refs_7_), channel_id=1, source_target_pairs={{0,1},{1,0},{2,3},{3,2},{4,5},{5,4},{6,7},{7,6},{8,9},{9,8},{10,11... | collective-permute-start | bytes 196616 | tf_op jit(solution)/shard_map/ppermute | solution.py:105
  12.0 1.1 %collective-permute-start.7 = (f32[128,128]{1,0:T(8,128)S(1)}, f32[128,128]{1,0:T(8,128)S(1)}, u32[]{:S(2)}, u32[]{:S(2)}) collective-permute-start(f32[128,128]{1,0:T(8,128)S(1)} %shard_map.48.refs_7_), channel_id=1, source_target_pairs={{0,3},{1,2},{2,1},{3,0},{4,7},{5,6},{6,5},{7,4},{8,11},{9,10},{10,... | collective-permute-start | bytes 196616 | tf_op jit(solution)/shard_map/ppermute | solution.py:105
  13.1 0.4 %collective-permute-start.6 = (f32[128,128]{1,0:T(8,128)S(1)}, f32[128,128]{1,0:T(8,128)S(1)}, u32[]{:S(2)}, u32[]{:S(2)}) collective-permute-start(f32[128,128]{1,0:T(8,128)S(1)} %shard_map.48.refs_7_), channel_id=1, source_target_pairs={{0,2},{1,3},{2,0},{3,1},{4,6},{5,7},{6,4},{7,5},{8,10},{9,11},{10,... | collective-permute-start | bytes 196616 | tf_op jit(solution)/shard_map/ppermute | solution.py:105
  13.5 0.0 collective-permute-done.1.refs_2_
  13.5 0.0 collective-permute-done.2.refs_3_
  13.6 2.5 %collective-permute-start.5 = (f32[200,128]{1,0:T(8,128)S(1)}, f32[200,128]{1,0:T(8,128)S(1)}, u32[]{:S(2)}, u32[]{:S(2)}) collective-permute-start(f32[200,128]{1,0:T(8,128)S(1)} %constant_dynamic-update-slice_fusion.refs_0_), channel_id=1, source_target_pairs={{0,24},{4,28},{8,16},{12,20},{16,8},{20,12},{24,0},{28,4},{1,25},{... | collective-permute-start | bytes 307208 | tf_op jit(solution)/shard_map/ppermute | solution.py:105
  16.1 0.5 %collective-permute-start.4 = (f32[200,128]{1,0:T(8,128)S(1)}, f32[200,128]{1,0:T(8,128)S(1)}, u32[]{:S(2)}, u32[]{:S(2)}) collective-permute-start(f32[200,128]{1,0:T(8,128)S(1)} %constant_dynamic-update-slice_fusion.refs_0_), channel_id=1, source_target_pairs={{0,16},{4,20},{8,24},{12,28},{16,0},{20,4},{24,8},{28,12},{1,17},{... | collective-permute-start | bytes 307208 | tf_op jit(solution)/shard_map/ppermute | solution.py:105
  16.6 0.0 collective-permute-done.8.refs_6_
  16.6 0.5 %collective-permute-start.3 = (f32[200,128]{1,0:T(8,128)S(1)}, f32[200,128]{1,0:T(8,128)S(1)}, u32[]{:S(2)}, u32[]{:S(2)}) collective-permute-start(f32[200,128]{1,0:T(8,128)S(1)} %constant_dynamic-update-slice_fusion.refs_0_), channel_id=1, source_target_pairs={{0,8},{4,12},{8,0},{12,4},{16,24},{20,28},{24,16},{28,20},{1,9},{5... | collective-permute-start | bytes 307208 | tf_op jit(solution)/shard_map/ppermute | solution.py:105
  17.1 0.9 %collective-permute-done.7.refs_5_ = f32[128,128]{1,0:T(8,128)S(1)} collective-permute-done((f32[128,128]{1,0:T(8,128)S(1)}, f32[128,128]{1,0:T(8,128)S(1)}, u32[]{:S(2)}, u32[]{:S(2)}) %collective-permute-start.7) | collective-permute-done | bytes 65568 | tf_op jit(solution)/shard_map/ppermute | solution.py:105
  18.1 1.4 %collective-permute-done.6.refs_4_ = f32[128,128]{1,0:T(8,128)S(1)} collective-permute-done((f32[128,128]{1,0:T(8,128)S(1)}, f32[128,128]{1,0:T(8,128)S(1)}, u32[]{:S(2)}, u32[]{:S(2)}) %collective-permute-start.6) | collective-permute-done | bytes 65568 | tf_op jit(solution)/shard_map/ppermute | solution.py:105
  19.4 0.0 copy-done
  19.5 0.1 collective-permute-start.9
  19.6 0.4 %shard_map.50 = (bf16[512,592]{1,0:T(8,128)(2,1)S(1)}, bf16[128,1536]{1,0:T(8,128)(2,1)S(1)}) custom-call(f32[320,512]{1,0:T(8,128)S(1)} %shard_map.49.group_ref), custom_call_target="tpu_custom_call" | custom-call | tf_op jit(solution)/shard_map/pallas_call | solution.py:155
  19.9 0.0 collective-permute-done.5.refs_3_
  19.9 0.8 %collective-permute-done.4.refs_2_ = f32[200,128]{1,0:T(8,128)S(1)} collective-permute-done((f32[200,128]{1,0:T(8,128)S(1)}, f32[200,128]{1,0:T(8,128)S(1)}, u32[]{:S(2)}, u32[]{:S(2)}) %collective-permute-start.4) | collective-permute-done | bytes 102432 | tf_op jit(solution)/shard_map/ppermute | solution.py:105
  20.7 0.5 %collective-permute-done.3.refs_1_ = f32[200,128]{1,0:T(8,128)S(1)} collective-permute-done((f32[200,128]{1,0:T(8,128)S(1)}, f32[200,128]{1,0:T(8,128)S(1)}, u32[]{:S(2)}, u32[]{:S(2)}) %collective-permute-start.3) | collective-permute-done | bytes 102432 | tf_op jit(solution)/shard_map/ppermute | solution.py:105
  21.2 0.2 shard_map.47
  21.4 0.2 collective-permute-done.9.group_ref
  21.6 0.4 %shard_map.51 = (bf16[512,592]{1,0:T(8,128)(2,1)S(1)}, bf16[128,1536]{1,0:T(8,128)(2,1)S(1)}) custom-call(f32[320,512]{1,0:T(8,128)S(1)} %collective-permute-done.9.group_ref), custom_call_target="tpu_custom_call" | custom-call | tf_op jit(solution)/shard_map/pallas_call | solution.py:155
  22.0 1.9 %shard_map.52 = (f32[128,128]{1,0:T(8,128)S(1)}, f32[128,128]{1,0:T(8,128)S(1)}, f32[128,128]{1,0:T(8,128)S(1)}, f32[128,128]{1,0:T(8,128)S(1)}) custom-call(bf16[592,512]{1,0:T(8,128)(2,1)S(1)} %get-tuple-element.15.row_ref, f32[1,512]{1,0:T(1,128)S(1)} %get-tuple-element.16.scale_ref, bf16[512,592]{1,0:T(8,128)(2,1)S(1)} %get-tuple-element.17.refs_0_, ...), custom_call_target="tpu_custom_call" | custom-call | tf_op jit(solution)/shard_map/pallas_call | solution.py:170
  23.9 2.5 %collective-permute-start.10 = (f32[128,128]{1,0:T(8,128)S(1)}, f32[128,128]{1,0:T(8,128)S(1)}, u32[]{:S(2)}, u32[]{:S(2)}) collective-permute-start(f32[128,128]{1,0:T(8,128)S(1)} %get-tuple-element.22), channel_id=1, source_target_pairs={{0,24},{4,28},{8,16},{12,20},{16,8},{20,12},{24,0},{28,4},{1,25},{... | collective-permute-start | bytes 196616 | tf_op jit(solution)/shard_map/ppermute | solution.py:105
  26.4 0.5 %collective-permute-start.11 = (f32[128,128]{1,0:T(8,128)S(1)}, f32[128,128]{1,0:T(8,128)S(1)}, u32[]{:S(2)}, u32[]{:S(2)}) collective-permute-start(f32[128,128]{1,0:T(8,128)S(1)} %get-tuple-element.23), channel_id=1, source_target_pairs={{0,16},{4,20},{8,24},{12,28},{16,0},{20,4},{24,8},{28,12},{1,17},{... | collective-permute-start | bytes 196616 | tf_op jit(solution)/shard_map/ppermute | solution.py:105
  26.9 0.5 %collective-permute-start.12 = (f32[128,128]{1,0:T(8,128)S(1)}, f32[128,128]{1,0:T(8,128)S(1)}, u32[]{:S(2)}, u32[]{:S(2)}) collective-permute-start(f32[128,128]{1,0:T(8,128)S(1)} %get-tuple-element.24), channel_id=1, source_target_pairs={{0,8},{4,12},{8,0},{12,4},{16,24},{20,28},{24,16},{28,20},{1,9},{5... | collective-permute-start | bytes 196616 | tf_op jit(solution)/shard_map/ppermute | solution.py:105
  27.4 1.7 %collective-permute-done.10 = f32[128,128]{1,0:T(8,128)S(1)} collective-permute-done((f32[128,128]{1,0:T(8,128)S(1)}, f32[128,128]{1,0:T(8,128)S(1)}, u32[]{:S(2)}, u32[]{:S(2)}) %collective-permute-start.10) | collective-permute-done | bytes 65568 | tf_op jit(solution)/shard_map/ppermute | solution.py:105
  29.1 1.5 %collective-permute-done.11 = f32[128,128]{1,0:T(8,128)S(1)} collective-permute-done((f32[128,128]{1,0:T(8,128)S(1)}, f32[128,128]{1,0:T(8,128)S(1)}, u32[]{:S(2)}, u32[]{:S(2)}) %collective-permute-start.11) | collective-permute-done | bytes 65568 | tf_op jit(solution)/shard_map/ppermute | solution.py:105
  30.6 0.5 %collective-permute-done.12 = f32[128,128]{1,0:T(8,128)S(1)} collective-permute-done((f32[128,128]{1,0:T(8,128)S(1)}, f32[128,128]{1,0:T(8,128)S(1)}, u32[]{:S(2)}, u32[]{:S(2)}) %collective-permute-start.12) | collective-permute-done | bytes 65568 | tf_op jit(solution)/shard_map/ppermute | solution.py:105
  31.2 0.6 %add_add_fusion = f32[128,128]{1,0:T(8,128)} fusion(f32[128,128]{1,0:T(8,128)S(1)} %collective-permute-done.12, f32[128,128]{1,0:T(8,128)S(1)} %collective-permute-done.11, f32[128,128]{1,0:T(8,128)S(1)} %get-tuple-element.21, f32[128,128]{1,0:T(8,128)S(1)} %collective-permute-done.10), kind=kLoop, calls=%fused_computation | loop fusion | flops 49152 | bytes 327680 | tf_op jit(solution)/shard_map/add | solution.py:177
  (6 shorter events, 0.1 us)
Async XLA Ops:
  0.0 9.5 %copy-start.1 = (f32[128,128]{1,0:T(8,128)S(1)}, f32[128,128]{1,0:T(8,128)}, u32[]{:S(2)}) copy-start(f32[128,128]{1,0:T(8,128)} %in_ref.1) | copy-start | bytes 196612
  0.0 13.5 %collective-permute-start.1 = (f32[48,512]{1,0:T(8,128)}, f32[48,512]{1,0:T(8,128)S(1)}, u32[]{:S(2)}, u32[]{:S(2)}) collective-permute-start(f32[48,512]{1,0:T(8,128)} %refs_0_.1), channel_id=1, source_target_pairs={{0,2},{1,3},{2,0},{3,1},{4,6},{5,7},{6,4},{7,5},{8,10},{9,11},{10,... | collective-permute-start | bytes 294920 | tf_op jit(solution)/shard_map/ppermute | solution.py:105
  4.0 5.4 %collective-permute-start = (f32[48,512]{1,0:T(8,128)}, f32[48,512]{1,0:T(8,128)S(1)}, u32[]{:S(2)}, u32[]{:S(2)}) collective-permute-start(f32[48,512]{1,0:T(8,128)} %refs_0_.1), channel_id=1, source_target_pairs={{0,1},{1,0},{2,3},{3,2},{4,5},{5,4},{6,7},{7,6},{8,9},{9,8},{10,11... | collective-permute-start | bytes 294920 | tf_op jit(solution)/shard_map/ppermute | solution.py:105
  5.6 7.9 %collective-permute-start.2 = (f32[48,512]{1,0:T(8,128)}, f32[48,512]{1,0:T(8,128)S(1)}, u32[]{:S(2)}, u32[]{:S(2)}) collective-permute-start(f32[48,512]{1,0:T(8,128)} %refs_0_.1), channel_id=1, source_target_pairs={{0,3},{1,2},{2,1},{3,0},{4,7},{5,6},{6,5},{7,4},{8,11},{9,10},{10,... | collective-permute-start | bytes 294920 | tf_op jit(solution)/shard_map/ppermute | solution.py:105
  5.6 0.7 %copy-start.2 = (s32[4,8]{1,0:T(4,128)S(1)}, s32[4,8]{1,0:T(4,128)}, u32[]{:S(2)}) copy-start(s32[4,8]{1,0:T(4,128)} %list_ref.1) | copy-start | bytes 388
  6.3 0.7 %copy-start.3 = (s32[4]{0:T(128)S(1)}, s32[4]{0:T(128)}, u32[]{:S(2)}) copy-start(s32[4]{0:T(128)} %count_ref.1) | copy-start | bytes 52
  9.5 9.9 %copy-start = (f32[48,512]{1,0:T(8,128)S(1)}, f32[48,512]{1,0:T(8,128)}, u32[]{:S(2)}) copy-start(f32[48,512]{1,0:T(8,128)} %refs_0_.1) | copy-start | bytes 294916
  9.5 7.1 %collective-permute-start.8 = (f32[128,128]{1,0:T(8,128)S(1)}, f32[128,128]{1,0:T(8,128)S(1)}, u32[]{:S(2)}, u32[]{:S(2)}) collective-permute-start(f32[128,128]{1,0:T(8,128)S(1)} %shard_map.48.refs_7_), channel_id=1, source_target_pairs={{0,1},{1,0},{2,3},{3,2},{4,5},{5,4},{6,7},{7,6},{8,9},{9,8},{10,11... | collective-permute-start | bytes 196616 | tf_op jit(solution)/shard_map/ppermute | solution.py:105
  12.0 6.1 %collective-permute-start.7 = (f32[128,128]{1,0:T(8,128)S(1)}, f32[128,128]{1,0:T(8,128)S(1)}, u32[]{:S(2)}, u32[]{:S(2)}) collective-permute-start(f32[128,128]{1,0:T(8,128)S(1)} %shard_map.48.refs_7_), channel_id=1, source_target_pairs={{0,3},{1,2},{2,1},{3,0},{4,7},{5,6},{6,5},{7,4},{8,11},{9,10},{10,... | collective-permute-start | bytes 196616 | tf_op jit(solution)/shard_map/ppermute | solution.py:105
  13.1 6.3 %collective-permute-start.6 = (f32[128,128]{1,0:T(8,128)S(1)}, f32[128,128]{1,0:T(8,128)S(1)}, u32[]{:S(2)}, u32[]{:S(2)}) collective-permute-start(f32[128,128]{1,0:T(8,128)S(1)} %shard_map.48.refs_7_), channel_id=1, source_target_pairs={{0,2},{1,3},{2,0},{3,1},{4,6},{5,7},{6,4},{7,5},{8,10},{9,11},{10,... | collective-permute-start | bytes 196616 | tf_op jit(solution)/shard_map/ppermute | solution.py:105
  13.6 6.4 %collective-permute-start.5 = (f32[200,128]{1,0:T(8,128)S(1)}, f32[200,128]{1,0:T(8,128)S(1)}, u32[]{:S(2)}, u32[]{:S(2)}) collective-permute-start(f32[200,128]{1,0:T(8,128)S(1)} %constant_dynamic-update-slice_fusion.refs_0_), channel_id=1, source_target_pairs={{0,24},{4,28},{8,16},{12,20},{16,8},{20,12},{24,0},{28,4},{1,25},{... | collective-permute-start | bytes 307208 | tf_op jit(solution)/shard_map/ppermute | solution.py:105
  16.1 4.7 %collective-permute-start.4 = (f32[200,128]{1,0:T(8,128)S(1)}, f32[200,128]{1,0:T(8,128)S(1)}, u32[]{:S(2)}, u32[]{:S(2)}) collective-permute-start(f32[200,128]{1,0:T(8,128)S(1)} %constant_dynamic-update-slice_fusion.refs_0_), channel_id=1, source_target_pairs={{0,16},{4,20},{8,24},{12,28},{16,0},{20,4},{24,8},{28,12},{1,17},{... | collective-permute-start | bytes 307208 | tf_op jit(solution)/shard_map/ppermute | solution.py:105
  16.6 4.7 %collective-permute-start.3 = (f32[200,128]{1,0:T(8,128)S(1)}, f32[200,128]{1,0:T(8,128)S(1)}, u32[]{:S(2)}, u32[]{:S(2)}) collective-permute-start(f32[200,128]{1,0:T(8,128)S(1)} %constant_dynamic-update-slice_fusion.refs_0_), channel_id=1, source_target_pairs={{0,8},{4,12},{8,0},{12,4},{16,24},{20,28},{24,16},{28,20},{1,9},{5... | collective-permute-start | bytes 307208 | tf_op jit(solution)/shard_map/ppermute | solution.py:105
  19.5 2.2 %collective-permute-start.9 = (f32[320,512]{1,0:T(8,128)S(1)}, f32[320,512]{1,0:T(8,128)S(1)}, u32[]{:S(2)}, u32[]{:S(2)}) collective-permute-start(f32[320,512]{1,0:T(8,128)S(1)} %shard_map.49.group_ref), channel_id=1, source_target_pairs={{0,4},{4,0},{8,12},{12,8},{16,20},{20,16},{24,28},{28,24},{1,5},{5... | collective-permute-start | bytes 1966088 | tf_op jit(solution)/shard_map/ppermute | solution.py:105
  23.9 5.3 %collective-permute-start.10 = (f32[128,128]{1,0:T(8,128)S(1)}, f32[128,128]{1,0:T(8,128)S(1)}, u32[]{:S(2)}, u32[]{:S(2)}) collective-permute-start(f32[128,128]{1,0:T(8,128)S(1)} %get-tuple-element.22), channel_id=1, source_target_pairs={{0,24},{4,28},{8,16},{12,20},{16,8},{20,12},{24,0},{28,4},{1,25},{... | collective-permute-start | bytes 196616 | tf_op jit(solution)/shard_map/ppermute | solution.py:105
  26.4 4.3 %collective-permute-start.11 = (f32[128,128]{1,0:T(8,128)S(1)}, f32[128,128]{1,0:T(8,128)S(1)}, u32[]{:S(2)}, u32[]{:S(2)}) collective-permute-start(f32[128,128]{1,0:T(8,128)S(1)} %get-tuple-element.23), channel_id=1, source_target_pairs={{0,16},{4,20},{8,24},{12,28},{16,0},{20,4},{24,8},{28,12},{1,17},{... | collective-permute-start | bytes 196616 | tf_op jit(solution)/shard_map/ppermute | solution.py:105
  26.9 4.3 %collective-permute-start.12 = (f32[128,128]{1,0:T(8,128)S(1)}, f32[128,128]{1,0:T(8,128)S(1)}, u32[]{:S(2)}, u32[]{:S(2)}) collective-permute-start(f32[128,128]{1,0:T(8,128)S(1)} %get-tuple-element.24), channel_id=1, source_target_pairs={{0,8},{4,12},{8,0},{12,4},{16,24},{20,28},{24,16},{28,20},{1,9},{5... | collective-permute-start | bytes 196616 | tf_op jit(solution)/shard_map/ppermute | solution.py:105
